TPU v7x, 32 devices: a whole 2x2x4 slice. The times are simulated.
32 devices in a mesh: gx: 2 (over y), gy: 4 (over x, core), gz: 4 (over z).
Axes of the slice: x: 2, y: 2, z: 4, core: 2. Of those that a mesh axis runs over, the one named last changes fastest.
Arguments:
- level_set: float32 [32, 64, 512], P('gx', 'gy', 'gz'), may hold values from 0 to 1
- velocity: float32 [3, 32, 64, 512], P(None, 'gx', 'gy', 'gz'), may hold values from -6 to 6
- source: float32 [32, 64, 512], P('gx', 'gy', 'gz'), may hold values from -6 to 6
- coarse_factor: float32 [32, 32], P(('gx', 'gy', 'gz')), may hold values from -0.2 to 0.2
Outputs:
- level_set_new: float32 [32, 64, 512], P('gx', 'gy', 'gz')
- pressure: float32 [32, 64, 512], P('gx', 'gy', 'gz')
All inputs are finite; a program needn't handle non-finite values.
Results may differ from a plain program's by a relative error of at most 0.029.
Values sent between devices are 32-bit elements; how exact they have to be, the bound alone decides.
No kernel may reach another device: no remote copies, remote signals or barrier semaphores. Data moves between devices by JAX's collectives and lax.ppermute only.
A program may use at most 64 MiB of HBM per device.

v0:
```python
import jax
import jax.numpy as jnp
import numpy as np
from jax import lax
from jax.sharding import PartitionSpec as P

NP = 8
RSWEEPS = 2
ITERS = 6


GLL_POINTS = (
    -1.0,
    -0.8717401485096066,
    -0.5917001814331423,
    -0.2092992179024789,
    0.2092992179024789,
    0.5917001814331423,
    0.8717401485096066,
    1.0,
)
GLL_WEIGHTS = (
    0.03571428571428571,
    0.21070422714350603,
    0.3411226924835044,
    0.4124587946587038,
    0.4124587946587038,
    0.3411226924835044,
    0.21070422714350603,
    0.03571428571428571,
)
HIGHEST = lax.Precision.HIGHEST
TIME_STEP = 0.02
PSEUDO_STEP = 0.004
INTERFACE_WIDTH = 0.5
GAS_DENSITY = 0.1
SOURCE_SCALE = 20.0


def extended(cells, sides, width):
    for axis, dim in sides:
        count = lax.axis_size(axis)
        ends = count - 1
        head = lax.slice_in_dim(cells, 0, width, axis=dim)
        tail = lax.slice_in_dim(cells, cells.shape[dim] - width, cells.shape[dim], axis=dim)
        cells = jnp.concatenate(
            [
                lax.ppermute(tail, axis, [(i, (i + 1) % count) for i in range(ends)]),
                cells,
                lax.ppermute(head, axis, [((i + 1) % count, i) for i in range(ends)]),
            ],
            axis=dim,
        )
    return cells


def node_tables():
    points = np.array(GLL_POINTS)
    amount = points.shape[0]
    barycentric = np.ones(amount)
    for target in range(amount):
        for partner in range(amount):
            if partner != target:
                barycentric[target] = barycentric[target] / (points[target] - points[partner])
    derivative = np.zeros((amount, amount))
    for target in range(amount):
        for partner in range(amount):
            if partner != target:
                derivative[target, partner] = (
                    barycentric[partner] / barycentric[target] / (points[target] - points[partner])
                )
        derivative[target, target] = -np.sum(derivative[target])
    return derivative


def apply_axis(values, matrix, which_axis):
    if which_axis == 0:
        return jnp.einsum("ap,pqr->aqr", matrix, values, precision=HIGHEST)
    if which_axis == 1:
        return jnp.einsum("aq,pqr->par", matrix, values, precision=HIGHEST)
    return jnp.einsum("pqr,ar->pqa", values, matrix, precision=HIGHEST)


def edge_passes(padded):
    summed = padded
    for which_axis in (1, 2, 3):
        amount = summed.shape[which_axis] - 2
        center = lax.slice_in_dim(summed, 1, amount + 1, axis=which_axis)
        upper_side = lax.slice_in_dim(summed, 2, amount + 2, axis=which_axis)
        lower_side = lax.slice_in_dim(summed, 0, amount, axis=which_axis)
        shape_list = [1, 1, 1, 1]
        shape_list[which_axis] = amount
        position = (jnp.arange(amount) % NP).reshape(shape_list)
        summed = (
            center
            + jnp.where(position == NP - 1, upper_side, 0.0)
            + jnp.where(position == 0, lower_side, 0.0)
        )
    return summed


def assemble(stacked):
    padded = extended(stacked, (("gx", 1), ("gy", 2), ("gz", 3)), 1)
    return edge_passes(padded)


def body(level_set, velocity, source, coarse_factor):
    shape_tuple = level_set.shape
    derivative = node_tables()
    deriv_tables = [
        jnp.asarray(np.kron(np.eye(extent // NP), derivative), jnp.float32)
        for extent in shape_tuple
    ]
    trans_tables = [
        jnp.asarray(np.kron(np.eye(extent // NP), derivative.T), jnp.float32)
        for extent in shape_tuple
    ]
    square_tables = [
        jnp.asarray(np.kron(np.eye(extent // NP), (derivative * derivative).T), jnp.float32)
        for extent in shape_tuple
    ]
    weights = jnp.asarray(np.array(GLL_WEIGHTS), jnp.float32)
    along_x = jnp.tile(weights, shape_tuple[0] // NP)
    along_y = jnp.tile(weights, shape_tuple[1] // NP)
    along_z = jnp.tile(weights, shape_tuple[2] // NP)
    bmass = along_x[:, None, None] * along_y[None, :, None] * along_z[None, None, :]
    gradient = [
        apply_axis(level_set, deriv_tables[which_axis], which_axis) for which_axis in range(3)
    ]
    advect = velocity[0] * gradient[0] + velocity[1] * gradient[1] + velocity[2] * gradient[2]
    divergence = (
        apply_axis(bmass * velocity[0], trans_tables[0], 0)
        + apply_axis(bmass * velocity[1], trans_tables[1], 1)
        + apply_axis(bmass * velocity[2], trans_tables[2], 2)
        + bmass * source
    )
    assembled = assemble(jnp.stack([bmass * advect, bmass, divergence]))
    mass_sum = assembled[1]
    weight = bmass / mass_sum
    level_now = level_set - TIME_STEP * assembled[0] / mass_sum
    rhs_field = SOURCE_SCALE * assembled[2]
    for sweep in range(RSWEEPS):
        gradient = [
            apply_axis(level_now, deriv_tables[which_axis], which_axis) for which_axis in range(3)
        ]
        inv_norm = 1.0 / jnp.sqrt(
            1.0 + gradient[0] * gradient[0] + gradient[1] * gradient[1] + gradient[2] * gradient[2]
        )
        compress = level_now * (1.0 - level_now) * inv_norm
        weak_form = apply_axis(
            bmass * (compress * gradient[0] - INTERFACE_WIDTH * gradient[0]), trans_tables[0], 0
        )
        weak_form = weak_form + apply_axis(
            bmass * (compress * gradient[1] - INTERFACE_WIDTH * gradient[1]), trans_tables[1], 1
        )
        weak_form = weak_form + apply_axis(
            bmass * (compress * gradient[2] - INTERFACE_WIDTH * gradient[2]), trans_tables[2], 2
        )
        level_now = level_now + PSEUDO_STEP * assemble(weak_form[None])[0] / mass_sum
    inverse_density = 1.0 / (GAS_DENSITY + (1.0 - GAS_DENSITY) * jnp.clip(level_now, 0.0, 1.0))
    scaled = bmass * inverse_density
    diag_local = (
        apply_axis(scaled, square_tables[0], 0)
        + apply_axis(scaled, square_tables[1], 1)
        + apply_axis(scaled, square_tables[2], 2)
        + bmass
    )
    diagonal = assemble(diag_local[None])[0]
    own_row = coarse_factor[0]

    def precondition(residual):
        jacobi = residual / diagonal
        restricted = jnp.sum(weight * residual)
        coarse_mid = lax.psum(restricted * own_row, ("gx", "gy", "gz"))
        coarse_value = jnp.dot(own_row, coarse_mid, precision=HIGHEST)
        result = jacobi + assemble((weight * coarse_value)[None])[0]
        return (result, lax.psum(jnp.sum(weight * residual * result), ("gx", "gy", "gz")))

    pressure = jnp.zeros_like(rhs_field)
    residual = rhs_field
    direction, inner_now = precondition(residual)
    for step in range(ITERS):
        local_part = bmass * direction
        for element_which_axis in range(3):
            local_part = local_part + apply_axis(
                scaled
                * apply_axis(direction, deriv_tables[element_which_axis], element_which_axis),
                trans_tables[element_which_axis],
                element_which_axis,
            )
        image = assemble(local_part[None])[0]
        curvature = lax.psum(jnp.sum(weight * direction * image), ("gx", "gy", "gz"))
        step_size = inner_now / curvature
        pressure = pressure + step_size * direction
        residual = residual - step_size * image
        if step + 1 < ITERS:
            preconditioned, inner_next = precondition(residual)
            direction = preconditioned + inner_next / inner_now * direction
            inner_now = inner_next
    return (level_now, pressure)


def solution(mesh):
    in_specs = (
        P("gx", "gy", "gz"),
        P(None, "gx", "gy", "gz"),
        P("gx", "gy", "gz"),
        P(("gx", "gy", "gz"), None),
    )
    out_specs = (P("gx", "gy", "gz"), P("gx", "gy", "gz"))
    return jax.shard_map(body, mesh=mesh, in_specs=in_specs, out_specs=out_specs, check_vma=False)
```

profile of v0, /device:TPU:0, one launch (start us, length us, event | category | flops | bytes accessed | tf_op | source)
XLA Modules:
  0.0 1162.9 jit_solution(6111673692743623964)
XLA Ops:
  6.2 4.9 collective-permute-start
  12.6 4.2 collective-permute-done.1
  29.5 3.9 collective-permute-done.5
  40.5 4.3 collective-permute-done.7
  48.1 3.8 collective-permute-done.9
  59.7 4.7 collective-permute-done.11
  70.0 4.2 collective-permute-done.13
  87.9 4.7 collective-permute-done.17
  94.6 37.5 %psum.126 = f32[32]{0:T(128)S(1)} all-reduce(f32[32]{0:T(128)S(1)} %bitcast_multiply_fusion.24), channel_id=1, replica_groups=mesh['gx'=2,'gy'=4,'gz'=4] {'gx','gy','gz'}, use_global_device_ids=true, to_apply=%region_1.2 | all-reduce | flops 32 | bytes 256 | tf_op jit(solution)/shard_map/psum | solution.py:174
  133.5 4.2 collective-permute-start.24
  139.8 4.5 collective-permute-start.18
  154.6 4.1 collective-permute-start.28
  160.2 4.6 collective-permute-start.22
  169.7 4.7 collective-permute-done.23
  177.1 4.5 collective-permute-start.30
  183.0 4.2 collective-permute-done.31
  189.9 4.1 collective-permute-done.33
  200.9 4.7 collective-permute-done.35
  207.0 37.7 %all-reduce = (f32[]{:T(128)}, f32[]{:T(128)}) all-reduce(f32[]{:T(128)} %get-tuple-element.9, f32[]{:T(128)} %get-tuple-element.8), channel_id=1, replica_groups=mesh['gx'=2,'gy'=4,'gz'=4] {'gx','gy','gz'}, use_global_device_ids=true, to_apply=%region_3.4 | all-reduce | flops 2 | bytes 16 | tf_op jit(solution)/shard_map/psum | solution.py:177
  247.4 41.7 %psum.129 = f32[32]{0:T(128)S(1)} all-reduce(f32[32]{0:T(128)S(1)} %bitcast_multiply_fusion.22), channel_id=1, replica_groups=mesh['gx'=2,'gy'=4,'gz'=4] {'gx','gy','gz'}, use_global_device_ids=true, to_apply=%region_7.8 | all-reduce | flops 32 | bytes 256 | tf_op jit(solution)/shard_map/psum | solution.py:174
  290.5 4.2 collective-permute-start.36
  296.0 4.2 collective-permute-done.37
  311.9 4.7 collective-permute-done.41
  318.0 39.3 %psum.130 = f32[]{:T(128)} all-reduce(f32[]{:T(128)} %get-tuple-element.36), channel_id=1, replica_groups=mesh['gx'=2,'gy'=4,'gz'=4] {'gx','gy','gz'}, use_global_device_ids=true, to_apply=%region_9.10 | all-reduce | flops 1 | bytes 8 | tf_op jit(solution)/shard_map/psum | solution.py:177
  360.3 4.4 collective-permute-start.42
  366.1 4.2 collective-permute-done.43
  383.1 4.7 collective-permute-done.47
  389.2 39.3 %psum.131 = f32[]{:T(128)} all-reduce(f32[]{:T(128)} %get-tuple-element.34), channel_id=1, replica_groups=mesh['gx'=2,'gy'=4,'gz'=4] {'gx','gy','gz'}, use_global_device_ids=true, to_apply=%region_11.12 | all-reduce | flops 1 | bytes 8 | tf_op jit(solution)/shard_map/psum | solution.py:192
  431.1 40.1 %psum.132 = f32[32]{0:T(128)S(1)} all-reduce(f32[32]{0:T(128)S(1)} %bitcast_multiply_fusion.20), channel_id=1, replica_groups=mesh['gx'=2,'gy'=4,'gz'=4] {'gx','gy','gz'}, use_global_device_ids=true, to_apply=%region_13.14 | all-reduce | flops 32 | bytes 256 | tf_op jit(solution)/shard_map/psum | solution.py:174
  472.6 4.2 collective-permute-start.48
  478.1 4.2 collective-permute-done.49
  495.4 4.7 collective-permute-done.53
  501.5 39.3 %psum.133 = f32[]{:T(128)} all-reduce(f32[]{:T(128)} %get-tuple-element.30), channel_id=1, replica_groups=mesh['gx'=2,'gy'=4,'gz'=4] {'gx','gy','gz'}, use_global_device_ids=true, to_apply=%region_15.16 | all-reduce | flops 1 | bytes 8 | tf_op jit(solution)/shard_map/psum | solution.py:177
  543.9 4.4 collective-permute-start.54
  549.6 4.2 collective-permute-done.55
  566.6 4.7 collective-permute-done.59
  572.7 38.5 %psum.134 = f32[]{:T(128)} all-reduce(f32[]{:T(128)} %get-tuple-element.28), channel_id=1, replica_groups=mesh['gx'=2,'gy'=4,'gz'=4] {'gx','gy','gz'}, use_global_device_ids=true, to_apply=%region_17.18 | all-reduce | flops 1 | bytes 8 | tf_op jit(solution)/shard_map/psum | solution.py:192
  613.9 40.8 %psum.135 = f32[32]{0:T(128)S(1)} all-reduce(f32[32]{0:T(128)S(1)} %bitcast_multiply_fusion.18), channel_id=1, replica_groups=mesh['gx'=2,'gy'=4,'gz'=4] {'gx','gy','gz'}, use_global_device_ids=true, to_apply=%region_19.20 | all-reduce | flops 32 | bytes 256 | tf_op jit(solution)/shard_map/psum | solution.py:174
  656.1 4.2 collective-permute-start.60
  661.6 4.2 collective-permute-done.61
  678.2 4.7 collective-permute-done.65
  684.3 39.3 %psum.136 = f32[]{:T(128)} all-reduce(f32[]{:T(128)} %get-tuple-element.24), channel_id=1, replica_groups=mesh['gx'=2,'gy'=4,'gz'=4] {'gx','gy','gz'}, use_global_device_ids=true, to_apply=%region_21.22 | all-reduce | flops 1 | bytes 8 | tf_op jit(solution)/shard_map/psum | solution.py:177
  726.7 4.4 collective-permute-start.66
  732.4 4.2 collective-permute-done.67
  749.4 4.7 collective-permute-done.71
  755.5 38.5 %psum.137 = f32[]{:T(128)} all-reduce(f32[]{:T(128)} %get-tuple-element.22), channel_id=1, replica_groups=mesh['gx'=2,'gy'=4,'gz'=4] {'gx','gy','gz'}, use_global_device_ids=true, to_apply=%region_23.24 | all-reduce | flops 1 | bytes 8 | tf_op jit(solution)/shard_map/psum | solution.py:192
  796.8 40.8 %psum.138 = f32[32]{0:T(128)S(1)} all-reduce(f32[32]{0:T(128)S(1)} %bitcast_multiply_fusion.16), channel_id=1, replica_groups=mesh['gx'=2,'gy'=4,'gz'=4] {'gx','gy','gz'}, use_global_device_ids=true, to_apply=%region_25.26 | all-reduce | flops 32 | bytes 256 | tf_op jit(solution)/shard_map/psum | solution.py:174
  838.9 4.2 collective-permute-start.72
  844.4 4.2 collective-permute-done.73
  861.1 4.7 collective-permute-done.77
  867.1 39.3 %psum.139 = f32[]{:T(128)} all-reduce(f32[]{:T(128)} %get-tuple-element.18), channel_id=1, replica_groups=mesh['gx'=2,'gy'=4,'gz'=4] {'gx','gy','gz'}, use_global_device_ids=true, to_apply=%region_27.28 | all-reduce | flops 1 | bytes 8 | tf_op jit(solution)/shard_map/psum | solution.py:177
  909.5 4.4 collective-permute-start.78
  915.3 4.2 collective-permute-done.79
  932.3 4.7 collective-permute-done.83
  938.3 38.5 %psum.140 = f32[]{:T(128)} all-reduce(f32[]{:T(128)} %get-tuple-element.16), channel_id=1, replica_groups=mesh['gx'=2,'gy'=4,'gz'=4] {'gx','gy','gz'}, use_global_device_ids=true, to_apply=%region_29.30 | all-reduce | flops 1 | bytes 8 | tf_op jit(solution)/shard_map/psum | solution.py:192
  979.6 40.8 %psum.141 = f32[32]{0:T(128)S(1)} all-reduce(f32[32]{0:T(128)S(1)} %bitcast_multiply_fusion.14), channel_id=1, replica_groups=mesh['gx'=2,'gy'=4,'gz'=4] {'gx','gy','gz'}, use_global_device_ids=true, to_apply=%region_31.32 | all-reduce | flops 32 | bytes 256 | tf_op jit(solution)/shard_map/psum | solution.py:174
  1021.7 4.2 collective-permute-start.84
  1027.3 4.2 collective-permute-done.85
  1043.9 4.7 collective-permute-done.89
  1049.9 39.3 %psum.142 = f32[]{:T(128)} all-reduce(f32[]{:T(128)} %get-tuple-element.12), channel_id=1, replica_groups=mesh['gx'=2,'gy'=4,'gz'=4] {'gx','gy','gz'}, use_global_device_ids=true, to_apply=%region_33.34 | all-reduce | flops 1 | bytes 8 | tf_op jit(solution)/shard_map/psum | solution.py:177
  1092.3 4.4 collective-permute-start.90
  1098.0 4.2 collective-permute-done.91
  1115.1 4.7 collective-permute-done.95
  1121.9 38.5 %psum.143 = f32[]{:T(128)} all-reduce(f32[]{:T(128)} %fusion.92), channel_id=1, replica_groups=mesh['gx'=2,'gy'=4,'gz'=4] {'gx','gy','gz'}, use_global_device_ids=true, to_apply=%region_35.36 | all-reduce | flops 1 | bytes 8 | tf_op jit(solution)/shard_map/psum | solution.py:192
  (397 shorter events, 269.4 us)
Async XLA Ops:
  6.2 6.4 collective-permute-start
  11.1 5.7 collective-permute-start.1
  27.7 5.7 collective-permute-start.5
  39.1 5.6 collective-permute-start.7
  52.0 7.8 collective-permute-start.10
  55.5 9.0 collective-permute-start.11
  68.6 5.5 collective-permute-start.13
  80.2 7.7 collective-permute-start.16
  83.7 9.0 collective-permute-start.17
  133.5 12.2 %collective-permute-start.24 = (f32[1,1,16,128]{3,1,2,0:T(1,128)S(1)}, f32[1,1,16,128]{3,1,2,0:T(1,128)S(1)}, u32[]{:S(2)}, u32[]{:S(2)}) collective-permute-start(f32[1,1,16,128]{3,1,2,0:T(1,128)S(1)} %get-tuple-element.143), channel_id=1, source_target_pairs={{0,16},{1,17},{2,18},{3,19},{4,20},{5,21},{6,22},{7,23},{8,24},{9,... | collective-permute-start | bytes 24584 | tf_op jit(solution)/shard_map/ppermute | solution.py:48
  137.7 8.0 collective-permute-start.25
  139.8 8.5 collective-permute-start.18
  144.4 5.5 collective-permute-start.19
  145.7 8.7 collective-permute-start.26
  147.0 7.4 collective-permute-start.27
  149.9 10.1 collective-permute-start.20
  153.1 6.9 collective-permute-start.21
  154.6 11.5 collective-permute-start.28
  158.7 9.1 collective-permute-start.29
  160.2 9.5 collective-permute-start.22
  164.8 9.7 collective-permute-start.23
  177.1 5.9 collective-permute-start.30
  181.7 5.5 collective-permute-start.31
  194.1 6.8 collective-permute-start.34
  196.7 9.0 collective-permute-start.35
  290.5 5.5 collective-permute-start.36
  294.6 5.5 collective-permute-start.37
  305.8 6.1 collective-permute-start.40
  307.6 9.0 collective-permute-start.41
  360.3 5.7 collective-permute-start.42
  364.7 5.5 collective-permute-start.43
  376.3 6.8 collective-permute-start.46
  378.9 9.0 collective-permute-start.47
  472.6 5.5 collective-permute-start.48
  476.7 5.5 collective-permute-start.49
  487.9 7.5 collective-permute-start.52
  491.2 9.0 collective-permute-start.53
  543.9 5.7 collective-permute-start.54
  548.2 5.5 collective-permute-start.55
  559.8 6.8 collective-permute-start.58
  562.4 9.0 collective-permute-start.59
  656.1 5.5 collective-permute-start.60
  660.3 5.5 collective-permute-start.61
  671.4 6.8 collective-permute-start.64
  674.0 9.0 collective-permute-start.65
  726.7 5.7 collective-permute-start.66
  731.1 5.5 collective-permute-start.67
  742.6 6.8 collective-permute-start.70
  745.2 9.0 collective-permute-start.71
  838.9 5.5 collective-permute-start.72
  843.1 5.5 collective-permute-start.73
  854.2 6.8 collective-permute-start.76
  856.8 9.0 collective-permute-start.77
  909.5 5.7 collective-permute-start.78
  913.9 5.5 collective-permute-start.79
  925.4 6.8 collective-permute-start.82
  928.0 9.0 collective-permute-start.83
  1025.9 5.5 collective-permute-start.85
  1037.1 6.8 collective-permute-start.88
  1039.6 9.0 collective-permute-start.89
  1092.3 5.7 collective-permute-start.90
  1096.7 5.5 collective-permute-start.91
  1108.2 6.8 collective-permute-start.94
  1110.8 9.0 collective-permute-start.95
  (41 other events, 232.2 us)
where the time goes:
time: 1180 us; the launch traced here: 1160 us
  blocking collectives  669 us (57%)
  waiting for transfers between devices  217 us (18%)
  starting transfers between devices  197 us (17%)
  other arithmetic  36.4 us (3%)
  between operations  18.2 us (2%)
  matrix products  16.5 us (1%)
    psum x6, blocking collectives, precondition(): coarse_mid = lax.psum(restricted * own_row, ('gx', 'gy', 'gz'))  242 us
    psum x6, blocking collectives, precondition(): lax.psum(jnp.sum(weight * residual * result), ('gx', 'gy', 'gz'))  234 us
    psum x5, blocking collectives, body(): lax.psum(jnp.sum(weight * direction * image), ('gx', 'gy', 'gz'))  193 us
    ppermute x48, waiting for transfers between devices, extended(): lax.ppermute(head, axis, [((i + 1) % count, i) for i in range(ends)])  177 us
    ppermute x48, starting transfers between devices, extended(): lax.ppermute(tail, axis, [(i, (i + 1) % count) for i in range(ends)])  135 us
    ppermute x48, starting transfers between devices, extended(): lax.ppermute(head, axis, [((i + 1) % count, i) for i in range(ends)])  62.5 us
    ppermute x48, waiting for transfers between devices, extended(): lax.ppermute(tail, axis, [(i, (i + 1) % count) for i in range(ends)])  40.5 us
  transfers between devices with their start and end apart: 96, of which 60 were waited for; matrix products, arithmetic and copies ran while one was open for 0% of the time, Pallas kernels for 0%

commit v1 on v0

v1 whole, which is shorter than its diff:
```python
import jax
import jax.numpy as jnp
import ml_dtypes
import numpy as np
from jax import lax
from jax.experimental import pallas as pl
from jax.experimental.pallas import tpu as pltpu
from jax.sharding import PartitionSpec as P

NP = 8
RSWEEPS = 2
ITERS = 6
AXES = ("gx", "gy", "gz")

GLL_POINTS = (
    -1.0,
    -0.8717401485096066,
    -0.5917001814331423,
    -0.2092992179024789,
    0.2092992179024789,
    0.5917001814331423,
    0.8717401485096066,
    1.0,
)
GLL_WEIGHTS = (
    0.03571428571428571,
    0.21070422714350603,
    0.3411226924835044,
    0.4124587946587038,
    0.4124587946587038,
    0.3411226924835044,
    0.21070422714350603,
    0.03571428571428571,
)
HIGHEST = lax.Precision.HIGHEST
TIME_STEP = 0.02
PSEUDO_STEP = 0.004
INTERFACE_WIDTH = 0.5
GAS_DENSITY = 0.1
SOURCE_SCALE = 20.0
F32 = jnp.float32
BF16 = jnp.bfloat16


def node_tables():
    points = np.array(GLL_POINTS)
    amount = points.shape[0]
    barycentric = np.ones(amount)
    for target in range(amount):
        for partner in range(amount):
            if partner != target:
                barycentric[target] = barycentric[target] / (points[target] - points[partner])
    derivative = np.zeros((amount, amount))
    for target in range(amount):
        for partner in range(amount):
            if partner != target:
                derivative[target, partner] = (
                    barycentric[partner] / barycentric[target] / (points[target] - points[partner])
                )
        derivative[target, target] = -np.sum(derivative[target])
    return derivative


DERIV = node_tables()
TRANS = DERIV.T.copy()
SQUARE = (DERIV * DERIV).T.copy()
WEIGHTS = np.array(GLL_WEIGHTS)

BX, BY, BZ = 16, 16, 128
ROWS = BX * BY


def split_bf16(matrix):
    full = matrix.astype(np.float32)
    high = full.astype(ml_dtypes.bfloat16)
    low = (full - high.astype(np.float32)).astype(ml_dtypes.bfloat16)
    return high, low


def const_tables():
    parts = []
    for matrix in (DERIV, TRANS, SQUARE):
        for shift in range(NP):
            column = np.array([matrix[s, (s - shift) % NP] for s in range(NP)])
            parts.append(np.repeat(column[:, None], BZ, axis=1))
    wy = np.tile(WEIGHTS, BY // NP)
    wz = np.tile(WEIGHTS, BZ // NP)
    parts.append(wy[:, None] * wz[None, :])
    parts.append(1.0 / (wy[:, None] * wz[None, :]))
    return np.concatenate(parts, axis=0).astype(np.float32)


def z_tables():
    out = []
    for matrix in (DERIV, TRANS, SQUARE):
        high, low = split_bf16(np.kron(np.eye(BZ // NP), matrix.T))
        out += [high, low]
    return np.concatenate(out, axis=0)


KIND = {"d": 0, "t": 1, "s": 2}
MATS = {"d": DERIV, "t": TRANS, "s": SQUARE}


def along_x(v, kind):
    matrix = MATS[kind]
    sign = 1.0 if abs(matrix[7, 7] - matrix[0, 0]) < abs(matrix[7, 7] + matrix[0, 0]) else -1.0
    out = [None] * BX
    for e in range(BX // NP):
        part = [v[(e * NP + i) * BY : (e * NP + i + 1) * BY] for i in range(NP)]
        even = [part[j] + part[7 - j] for j in range(4)]
        odd = [part[j] - part[7 - j] for j in range(4)]
        for i in range(4):
            a = b = None
            for j in range(4):
                ca = float(0.5 * (matrix[i, j] + matrix[i, 7 - j]))
                cb = float(0.5 * (matrix[i, j] - matrix[i, 7 - j]))
                a = ca * even[j] if a is None else a + ca * even[j]
                b = cb * odd[j] if b is None else b + cb * odd[j]
            out[e * NP + i] = a + b
            out[e * NP + 7 - i] = a - b if sign > 0 else b - a
    return jnp.concatenate(out, axis=0)


def along_y(v, kind, tab):
    v3 = v.reshape(ROWS // NP, NP, BZ)
    base = KIND[kind] * NP * NP
    total = None
    for shift in range(NP):
        coef = tab[base + shift * NP : base + (shift + 1) * NP, :][None]
        rolled = v3 if shift == 0 else pltpu.roll(v3, shift, 1)
        total = coef * rolled if total is None else total + coef * rolled
    return total.reshape(ROWS, BZ)


def along_z(v, kind, zt):
    base = KIND[kind] * 2 * BZ
    high = zt[base : base + BZ, :]
    low = zt[base + BZ : base + 2 * BZ, :]
    vh = v.astype(BF16)
    vl = (v - vh.astype(F32)).astype(BF16)

    def dot(a, b):
        return jnp.dot(a, b, preferred_element_type=F32)

    return dot(vh, high) + (dot(vl, high) + dot(vh, low))


def bmass_of(tab):
    base = 3 * NP * NP
    yz = tab[base : base + BY, :]
    return jnp.concatenate([yz * float(WEIGHTS[x % NP]) for x in range(BX)], axis=0)


def local_sum(v):
    parts = [v[x * BY : (x + 1) * BY] for x in range(BX)]
    for x in range(NP, BX, NP):
        both = parts[x - 1] + parts[x]
        parts[x - 1] = both
        parts[x] = both
    sub = lax.broadcasted_iota(jnp.int32, (NP, BZ), 0)
    out = []
    for x in range(BX):
        a, b = parts[x][:NP], parts[x][NP:]
        out.append(jnp.where(sub == NP - 1, a + pltpu.roll(b, NP - 1, 0), a))
        out.append(jnp.where(sub == 0, b + pltpu.roll(a, 1, 0), b))
    v = jnp.concatenate(out, axis=0)
    lane = lax.broadcasted_iota(jnp.int32, (NP, BZ), 1)
    last = (lane % NP == NP - 1) & (lane < BZ - 1)
    first = (lane % NP == 0) & (lane > 0)
    v3 = v.reshape(ROWS // NP, NP, BZ)
    up = pltpu.roll(v3, BZ - 1, 2)
    down = pltpu.roll(v3, 1, 2)
    v3 = v3 + jnp.where(last[None], up, jnp.where(first[None], down, 0.0))
    return v3.reshape(ROWS, BZ)


class Geometry:
    def __init__(self, sizes):
        self.sizes = sizes
        self.at = [lax.axis_index(a) for a in AXES]
        self.low = [g > 0 for g in self.at]
        self.high = [g < n - 1 for g, n in zip(self.at, sizes)]
        self.me = (self.at[0] * sizes[1] + self.at[1]) * sizes[2] + self.at[2]

    def neighbour(self, *step):
        ok = None
        number = self.me
        strides = (self.sizes[1] * self.sizes[2], self.sizes[2], 1)
        for a in range(3):
            if step[a]:
                there = self.high[a] if step[a] > 0 else self.low[a]
                ok = there if ok is None else jnp.logical_and(ok, there)
                number = number + step[a] * strides[a]
        return jnp.where(ok, number, self.me)

    def half(self, flag):
        return jnp.where(flag, 0.5, 1.0).astype(F32)

    def x_share(self, x):
        if x == 0:
            return self.half(self.low[0])
        if x == BX - 1:
            return self.half(self.high[0])
        return None

    def y_share(self):
        row = lax.broadcasted_iota(jnp.int32, (BY, BZ), 0)
        one = jnp.where(row == 0, self.half(self.low[1]), 1.0)
        return jnp.where(row == BY - 1, self.half(self.high[1]), one)

    def z_share(self, shape, dim):
        lane = lax.broadcasted_iota(jnp.int32, shape, dim)
        one = jnp.where(lane == 0, self.half(self.low[2]), 1.0)
        return jnp.where(lane == BZ - 1, self.half(self.high[2]), one)

    def yz_weight(self):
        row = lax.broadcasted_iota(jnp.int32, (BY, BZ), 0)
        lane = lax.broadcasted_iota(jnp.int32, (BY, BZ), 1)
        inside_y = ((row % NP == 0) & (row > 0)) | ((row % NP == NP - 1) & (row < BY - 1))
        inside_z = ((lane % NP == 0) & (lane > 0)) | ((lane % NP == NP - 1) & (lane < BZ - 1))
        wy = jnp.where(inside_y, 0.5, self.y_share())
        wz = jnp.where(inside_z, 0.5, self.z_share((BY, BZ), 1))
        return wy * wz

    def x_weight(self, x):
        if x in (0, BX - 1):
            return self.x_share(x)
        return 0.5 if x % NP in (0, NP - 1) else 1.0


def inverse_mass(geo, tab):
    base = 3 * NP * NP + BY
    yz = tab[base : base + BY, :] * geo.yz_weight()
    return jnp.concatenate(
        [yz * (geo.x_weight(x) * float(1.0 / WEIGHTS[x % NP])) for x in range(BX)], axis=0
    )


def face_steps(n):
    return ("swap",) if n == 2 else ("up", "down")


class Layout:
    def __init__(self, sizes):
        self.sizes = sizes
        self.devices = sizes[0] * sizes[1] * sizes[2]
        self.lanes = -(-(self.devices + 3) // 128) * 128
        self.scalar_rows = self.lanes // 128

    def slot_rows(self, fields):
        need = self.scalar_rows + 2 * fields
        if fields == 2:
            need += self.scalar_rows
        return 4 if need <= 4 else -(-need // 8) * 8


def pick_faces(geo, axis, n, low, high):
    if n == 2:
        return [jnp.where(geo.at[axis] == 0, high, low)]
    return [high, low]


def send_fields(geo, lay, f_refs, scalars, send_ref, xs, ys, fields, extra=None):
    rows = lay.slot_rows(fields)
    base = [scalars[:, i * 128 : (i + 1) * 128] for i in range(lay.scalar_rows)]
    used = lay.scalar_rows
    if extra is not None:
        base.append(jnp.zeros((2 * fields, 128), F32))
        base += [extra[:, i * 128 : (i + 1) * 128] for i in range(lay.scalar_rows)]
        used += 2 * fields + lay.scalar_rows
    base.append(jnp.zeros((rows - used, 128), F32))
    base = jnp.concatenate([b for b in base if b.shape[0]], axis=0)
    send_ref[...] = jnp.broadcast_to(base[None], (lay.devices, rows, 128))
    picker = lax.broadcasted_iota(jnp.int32, (8, BZ), 0)
    lane = lax.broadcasted_iota(jnp.int32, (8, BZ), 1)
    picker = jnp.where(
        ((picker == 0) & (lane == 0)) | ((picker == 1) & (lane == BZ - 1)), 1.0, 0.0
    ).astype(F32)
    for k, f_ref in enumerate(f_refs):
        at = lay.scalar_rows + 2 * k
        halves = [
            lax.dot_general(
                picker,
                f_ref[h * 128 : (h + 1) * 128, :],
                (((1,), (1,)), ((), ())),
                precision=HIGHEST,
                preferred_element_type=F32,
            )
            for h in range(2)
        ]
        for dz in (-1, 1):
            side = 0 if dz < 0 else 1
            pair = jnp.concatenate([halves[0][side : side + 1], halves[1][side : side + 1]], axis=0)
            for dx in (-1, 0, 1):
                for dy in (-1, 0, 1):
                    send_ref[geo.neighbour(dx, dy, dz), at : at + 2, :] = pair
        for dx in (-1, 1):
            for dy in (-1, 1):
                row = (BX - 1 if dx > 0 else 0) * BY + (BY - 1 if dy > 0 else 0)
                send_ref[geo.neighbour(dx, dy, 0), at : at + 1, :] = f_ref[row : row + 1, :]
        lowx, highx = f_ref[0:BY, :], f_ref[ROWS - BY : ROWS, :]
        for ref, face in zip(xs, pick_faces(geo, 0, lay.sizes[0], lowx, highx)):
            ref[k * BY : (k + 1) * BY, :] = face
        lowy = f_ref[pl.ds(0, BX, stride=BY), :]
        highy = f_ref[pl.ds(BY - 1, BX, stride=BY), :]
        for ref, face in zip(ys, pick_faces(geo, 1, lay.sizes[1], lowy, highy)):
            ref[k * BX : (k + 1) * BX, :] = face
    send_ref[geo.me] = base


def came_from(geo, axis, n, refs, k, size):
    if n == 2:
        face = refs[0][k * size : (k + 1) * size, :]
        return (
            jnp.where(geo.low[axis], face, 0.0),
            jnp.where(geo.high[axis], face, 0.0),
        )
    up = refs[0][k * size : (k + 1) * size, :]
    down = refs[1][k * size : (k + 1) * size, :]
    return jnp.where(geo.low[axis], up, 0.0), jnp.where(geo.high[axis], down, 0.0)


def received(geo, lay, f, recv_ref, xs, ys, w_ref, k):
    at = lay.scalar_rows + 2 * k
    lane = lax.broadcasted_iota(jnp.int32, (2, 128), 1)
    row = lax.broadcasted_iota(jnp.int32, (2, 128), 0)
    sides = []
    for dz in (-1, 1):
        total = None
        for dx in (-1, 0, 1):
            for dy in (-1, 0, 1):
                pair = recv_ref[geo.neighbour(dx, dy, dz), at : at + 2, :]
                shift = 0
                keep = None
                if dx:
                    pair = jnp.concatenate([pair[1:2], pair[0:1]], axis=0)
                    shift += 112 * dx
                    want = (lane >= 112) & (row == 1) if dx > 0 else (lane < 16) & (row == 0)
                    keep = want
                if dy:
                    shift += 15 * dy
                    want = lane % 16 == (15 if dy > 0 else 0)
                    keep = want if keep is None else keep & want
                if shift % 128:
                    pair = pltpu.roll(pair, shift % 128, 1)
                if keep is not None:
                    pair = jnp.where(keep, pair, 0.0)
                total = pair if total is None else total + pair
        sides.append(total)
    placer_row = lax.broadcasted_iota(jnp.int32, (8, BZ), 0)
    placer_lane = lax.broadcasted_iota(jnp.int32, (8, BZ), 1)
    placer = jnp.where(
        ((placer_row == 0) & (placer_lane == 0)) | ((placer_row == 1) & (placer_lane == BZ - 1)),
        1.0,
        0.0,
    ).astype(F32)
    halves = []
    for h in range(2):
        stack = jnp.concatenate(
            [sides[0][h : h + 1], sides[1][h : h + 1], jnp.zeros((6, 128), F32)], axis=0
        )
        halves.append(
            lax.dot_general(
                stack,
                placer,
                (((0,), (0,)), ((), ())),
                precision=HIGHEST,
                preferred_element_type=F32,
            )
        )
    w_ref[...] = f + jnp.concatenate(halves, axis=0)
    lowx, highx = came_from(geo, 0, lay.sizes[0], xs, k, BY)
    w_ref[0:BY, :] += lowx
    w_ref[ROWS - BY : ROWS, :] += highx
    lowy, highy = came_from(geo, 1, lay.sizes[1], ys, k, BX)
    w_ref[pl.ds(0, BX, stride=BY), :] += lowy
    w_ref[pl.ds(BY - 1, BX, stride=BY), :] += highy
    for dx in (-1, 1):
        for dy in (-1, 1):
            row = (BX - 1 if dx > 0 else 0) * BY + (BY - 1 if dy > 0 else 0)
            w_ref[row : row + 1, :] += recv_ref[geo.neighbour(dx, dy, 0), at : at + 1, :]


def received_scalars(lay, recv_ref):
    total = jnp.sum(recv_ref[...], axis=0)
    return jnp.concatenate([total[i : i + 1] for i in range(lay.scalar_rows)], axis=1)


def coarse_tables(geo, lay, places):
    steps = [places[a : a + 1, :] - geo.at[a].astype(F32) for a in range(3)]
    z = lax.broadcasted_iota(jnp.int32, (BZ, lay.lanes), 0)
    lane = lax.broadcasted_iota(jnp.int32, (1, lay.lanes), 1)
    dz = jnp.broadcast_to(steps[2], (BZ, lay.lanes))
    zmat = jnp.where(dz == 0.0, geo.z_share((BZ, lay.lanes), 0), 0.0)
    zmat = jnp.where((dz == 1.0) & (z == BZ - 1), 0.5, zmat)
    zmat = jnp.where((dz == -1.0) & (z == 0), 0.5, zmat)
    zmat = jnp.where(jnp.broadcast_to(lane, (BZ, lay.lanes)) >= lay.devices, 1.0, zmat)
    row = lax.broadcasted_iota(jnp.int32, (16, lay.lanes), 0)
    near = (jnp.abs(steps[0]) <= 1.0) & (jnp.abs(steps[1]) <= 1.0)
    own = (steps[0] + 1.0) * 3.0 + steps[1] + 1.0
    own = jnp.where(near & (lane < lay.devices), own, -1.0)
    own = jnp.where(
        (lane >= lay.devices) & (lane < lay.devices + 3),
        (lane - lay.devices + 9).astype(F32),
        own,
    )
    msel = jnp.where(row.astype(F32) == jnp.broadcast_to(own, (16, lay.lanes)), 1.0, 0.0)
    return zmat, msel.astype(F32)


def partial_sums(geo, v, sums, q_ref, zmat, msel):
    first, last = v[0:BY], v[ROWS - BY : ROWS]
    middle = first * geo.x_share(0) + last * geo.x_share(BX - 1)
    for x in range(1, BX - 1):
        middle = middle + v[x * BY : (x + 1) * BY]
    share = geo.y_share()
    for i, part in enumerate((0.5 * first, middle, 0.5 * last)):
        q_ref[3 * i : 3 * i + 1, :] = 0.5 * part[0:1]
        q_ref[3 * i + 1 : 3 * i + 2, :] = jnp.sum(part * share, axis=0, keepdims=True)
        q_ref[3 * i + 2 : 3 * i + 3, :] = 0.5 * part[BY - 1 : BY]
    q_ref[9:16, :] = jnp.zeros((7, BZ), F32)
    for i, total in enumerate(sums):
        q_ref[9 + i : 10 + i, :] = total
    rows = jnp.dot(q_ref[...], zmat, precision=HIGHEST, preferred_element_type=F32)
    return jnp.sum(rows * msel, axis=0, keepdims=True)


def spread(geo, values, zmat, msel):
    rows = lax.dot_general(
        msel * values,
        zmat,
        (((1,), (1,)), ((), ())),
        precision=HIGHEST,
        preferred_element_type=F32,
    )
    y = lax.broadcasted_iota(jnp.int32, (BY, BZ), 0)
    share = geo.y_share()
    planes = []
    for i in range(3):
        plane = share * rows[3 * i + 1 : 3 * i + 2]
        plane = plane + jnp.where(y == 0, 0.5 * rows[3 * i : 3 * i + 1], 0.0)
        planes.append(plane + jnp.where(y == BY - 1, 0.5 * rows[3 * i + 2 : 3 * i + 3], 0.0))
    out = [planes[1]] * BX
    out[0] = planes[1] * geo.x_share(0) + 0.5 * planes[0]
    out[BX - 1] = planes[1] * geo.x_share(BX - 1) + 0.5 * planes[2]
    return out


def all_rows(v):
    total = v[0:8]
    for i in range(1, ROWS // 8):
        total = total + v[8 * i : 8 * i + 8]
    return jnp.sum(total, axis=0, keepdims=True)


def weighted_rows(geo, v):
    yz = geo.yz_weight()
    total = None
    for x in range(BX):
        weight = geo.x_weight(x)
        part = v[x * BY : (x + 1) * BY]
        if not (isinstance(weight, float) and weight == 1.0):
            part = part * weight
        total = part if total is None else total + part
    return jnp.sum(total * yz, axis=0, keepdims=True)


def weak_form(level, tab, zt):
    gx, gy, gz = along_x(level, "d"), along_y(level, "d", tab), along_z(level, "d", zt)
    inv_norm = 1.0 / jnp.sqrt(1.0 + gx * gx + gy * gy + gz * gz)
    coef = bmass_of(tab) * (level * (1.0 - level) * inv_norm - INTERFACE_WIDTH)
    return (
        along_x(coef * gx, "t") + along_y(coef * gy, "t", tab) + along_z(coef * gz, "t", zt)
    )


def stiffness(v, scaled, tab, zt):
    out = bmass_of(tab) * v
    out = out + along_x(scaled * along_x(v, "d"), "t")
    out = out + along_y(scaled * along_y(v, "d", tab), "t", tab)
    return out + along_z(scaled * along_z(v, "d", zt), "t", zt)


def local_step(geo, lay, residual, dinv, scaled, state, p_old, refs):
    tab, zt, zmat, msel, gram, u_ref, f_ref, send_ref, xs, ys, q_ref, state_ref, final = refs
    s_row, ts_row, gamma, curvature = state
    values = jnp.dot(s_row, gram, precision=HIGHEST, preferred_element_type=F32)
    coarse = jnp.sum(s_row * values, axis=1, keepdims=True)
    jacobi = residual * dinv
    planes = spread(geo, values, zmat, msel)
    u = jnp.concatenate([jacobi[x * BY : (x + 1) * BY] + planes[x] for x in range(BX)], axis=0)
    u_ref[...] = u
    local = stiffness(u, scaled, tab, zt)
    sums = [weighted_rows(geo, residual * jacobi), all_rows(u * local)]
    sums.append(jnp.zeros((1, BZ), F32) if p_old is None else all_rows(p_old * local))
    scalars = partial_sums(geo, local, sums, q_ref, zmat, msel)
    ones = jnp.ones_like(s_row)
    state_ref[...] = jnp.concatenate(
        [s_row, ts_row, ones * gamma, ones * curvature, ones * coarse, jnp.zeros((3, lay.lanes), F32)],
        axis=0,
    )
    if final:
        rows = [scalars[:, i * 128 : (i + 1) * 128] for i in range(lay.scalar_rows)]
        rows = jnp.concatenate(rows, axis=0)
        send_ref[...] = jnp.broadcast_to(rows[None], send_ref.shape)
        return
    f_ref[...] = local_sum(local)
    send_fields(geo, lay, [f_ref], scalars, send_ref, xs, ys, 1)


def step_sizes(lay, recv_ref, state_ref, first):
    row = received_scalars(lay, recv_ref)
    lane = lax.broadcasted_iota(jnp.int32, row.shape, 1)

    def pick(which):
        return jnp.sum(jnp.where(lane == lay.devices + which, row, 0.0), axis=1, keepdims=True)

    gamma = pick(0) + state_ref[4:5, 0:1]
    if first:
        curvature = pick(1)
        beta = None
    else:
        beta = gamma / state_ref[2:3, 0:1]
        curvature = pick(1) + beta * (2.0 * pick(2) + beta * state_ref[3:4, 0:1])
    return row, gamma, curvature, beta, gamma / curvature


def build(mesh):
    sizes = tuple(int(mesh.shape[a]) for a in AXES)
    lay = Layout(sizes)
    steps = [face_steps(sizes[0]), face_steps(sizes[1])]
    nx, ny = len(steps[0]), len(steps[1])
    tab_np, zt_np = const_tables(), z_tables()
    number = np.arange(lay.lanes)
    places_np = np.full((8, lay.lanes), -9.0, np.float32)
    places_np[0, : lay.devices] = (number // (sizes[1] * sizes[2]))[: lay.devices]
    places_np[1, : lay.devices] = (number // sizes[2] % sizes[1])[: lay.devices]
    places_np[2, : lay.devices] = (number % sizes[2])[: lay.devices]
    block = jax.ShapeDtypeStruct((ROWS, BZ), F32)

    def like(*shape):
        return jax.ShapeDtypeStruct(shape, F32)

    def outgoing(fields):
        return (
            [like(lay.devices, lay.slot_rows(fields), 128)]
            + [like(BY * fields, BZ)] * nx
            + [like(BX * fields, BZ)] * ny
        )

    def call(kernel, ins, outs, scratch, name):
        spec = pl.BlockSpec(memory_space=pltpu.VMEM)
        return pl.pallas_call(
            kernel,
            out_shape=outs,
            in_specs=[spec] * len(ins),
            out_specs=[spec] * len(outs),
            scratch_shapes=scratch,
            compiler_params=pltpu.CompilerParams(vmem_limit_bytes=48 * 1024 * 1024),
            name=name,
        )(*ins)

    work = pltpu.VMEM((ROWS, BZ), F32)
    qrows = pltpu.VMEM((16, BZ), F32)

    def ring(v, axis, n, step):
        if step == "swap":
            pairs = [(0, 1), (1, 0)]
        else:
            d = 1 if step == "up" else n - 1
            pairs = [(i, (i + d) % n) for i in range(n)]
        return lax.ppermute(v, axis, pairs)

    def exchange(out):
        send, faces = out[0], out[1:]
        recv = lax.all_to_all(send, AXES, 0, 0, tiled=True)
        xs = [ring(faces[i], "gx", sizes[0], s) for i, s in enumerate(steps[0])]
        ys = [ring(faces[nx + i], "gy", sizes[1], s) for i, s in enumerate(steps[1])]
        return [recv, *xs, *ys]

    n_out = 1 + nx + ny

    def split(refs):
        return refs[0], refs[1 : 1 + nx], refs[1 + nx : 1 + nx + ny]

    def start_kernel(level_ref, vel_ref, source_ref, factor_ref, tab_ref, zt_ref, places_ref, *rest):
        send, xs, ys = split(rest[:n_out])
        fa_ref, fd_ref, zmat_ref, msel_ref, q_ref = rest[n_out:]
        geo = Geometry(sizes)
        level = level_ref[...]
        bm = bmass_of(tab_ref)
        advect = vel_ref[0] * along_x(level, "d")
        advect = advect + vel_ref[1] * along_y(level, "d", tab_ref)
        advect = advect + vel_ref[2] * along_z(level, "d", zt_ref)
        fa_ref[...] = local_sum(bm * advect)
        div = bm * source_ref[...] + along_x(bm * vel_ref[0], "t")
        div = div + along_y(bm * vel_ref[1], "t", tab_ref)
        div = div + along_z(bm * vel_ref[2], "t", zt_ref)
        fd_ref[...] = local_sum(div)
        zmat, msel = coarse_tables(geo, lay, places_ref)
        zmat_ref[...] = zmat
        msel_ref[...] = msel
        scalars = partial_sums(geo, div, [], q_ref, zmat, msel)
        send_fields(geo, lay, [fa_ref, fd_ref], scalars, send, xs, ys, 2, factor_ref[...])

    def first_kernel(recv, *rest):
        xs, ys = rest[:nx], rest[nx : nx + ny]
        level_ref, fa_ref, fd_ref, tab_ref, zt_ref = rest[nx + ny : nx + ny + 5]
        out = rest[nx + ny + 5 :]
        send, oxs, oys = split(out[:n_out])
        level_out, f_ref, r_ref, s_ref, gram_ref, w_ref = out[n_out:]
        geo = Geometry(sizes)
        at = lay.scalar_rows + 4
        factor = [recv[:, at + i, :] for i in range(lay.scalar_rows)]
        factor = jnp.concatenate(factor, axis=1)
        if lay.lanes > lay.devices:
            pad = jnp.zeros((lay.lanes - lay.devices, lay.lanes), F32)
            factor = jnp.concatenate([factor, pad], axis=0)
        gram_ref[...] = lax.dot_general(
            factor,
            factor,
            (((1,), (1,)), ((), ())),
            precision=HIGHEST,
            preferred_element_type=F32,
        )
        received(geo, lay, fd_ref[...], recv, xs, ys, w_ref, 1)
        r_ref[...] = SOURCE_SCALE * w_ref[...]
        row = received_scalars(lay, recv)
        s_ref[...] = jnp.broadcast_to(SOURCE_SCALE * row, s_ref.shape)
        received(geo, lay, fa_ref[...], recv, xs, ys, w_ref, 0)
        level = level_ref[...] - TIME_STEP * w_ref[...] * inverse_mass(geo, tab_ref)
        level_out[...] = level
        f_ref[...] = local_sum(weak_form(level, tab_ref, zt_ref))
        send_fields(geo, lay, [f_ref], jnp.zeros((1, lay.lanes), F32), send, oxs, oys, 1)

    def new_level(geo, recv, xs, ys, level_ref, f_ref, tab_ref, w_ref):
        received(geo, lay, f_ref[...], recv, xs, ys, w_ref, 0)
        return level_ref[...] + PSEUDO_STEP * w_ref[...] * inverse_mass(geo, tab_ref)

    def sweep_kernel(recv, *rest):
        xs, ys = rest[:nx], rest[nx : nx + ny]
        level_ref, fin_ref, tab_ref, zt_ref = rest[nx + ny : nx + ny + 4]
        out = rest[nx + ny + 4 :]
        send, oxs, oys = split(out[:n_out])
        level_out, f_ref, w_ref = out[n_out:]
        geo = Geometry(sizes)
        level = new_level(geo, recv, xs, ys, level_ref, fin_ref, tab_ref, w_ref)
        level_out[...] = level
        f_ref[...] = local_sum(weak_form(level, tab_ref, zt_ref))
        send_fields(geo, lay, [f_ref], jnp.zeros((1, lay.lanes), F32), send, oxs, oys, 1)

    def diagonal_kernel(recv, *rest):
        xs, ys = rest[:nx], rest[nx : nx + ny]
        level_ref, fin_ref, tab_ref, zt_ref = rest[nx + ny : nx + ny + 4]
        out = rest[nx + ny + 4 :]
        send, oxs, oys = split(out[:n_out])
        level_out, f_ref, scaled_ref, w_ref = out[n_out:]
        geo = Geometry(sizes)
        level = new_level(geo, recv, xs, ys, level_ref, fin_ref, tab_ref, w_ref)
        level_out[...] = level
        bm = bmass_of(tab_ref)
        scaled = bm / (GAS_DENSITY + (1.0 - GAS_DENSITY) * jnp.clip(level, 0.0, 1.0))
        scaled_ref[...] = scaled
        diag = bm + along_x(scaled, "s") + along_y(scaled, "s", tab_ref) + along_z(scaled, "s", zt_ref)
        f_ref[...] = local_sum(diag)
        send_fields(geo, lay, [f_ref], jnp.zeros((1, lay.lanes), F32), send, oxs, oys, 1)

    def solve_kernel(recv, *rest):
        xs, ys = rest[:nx], rest[nx : nx + ny]
        fin_ref, r_ref, scaled_ref, s_ref, tab_ref, zt_ref, zmat_ref, msel_ref, gram_ref = rest[
            nx + ny : nx + ny + 9
        ]
        out = rest[nx + ny + 9 :]
        send, oxs, oys = split(out[:n_out])
        dinv_ref, u_ref, f_ref, state_ref, w_ref, q_ref = out[n_out:]
        geo = Geometry(sizes)
        received(geo, lay, fin_ref[...], recv, xs, ys, w_ref, 0)
        dinv = 1.0 / w_ref[...]
        dinv_ref[...] = dinv
        zero = jnp.zeros((1, 1), F32)
        s_row = s_ref[0:1, :]
        state = (s_row, jnp.zeros_like(s_row), zero, zero)
        refs = (tab_ref, zt_ref, zmat_ref[...], msel_ref[...], gram_ref[...], u_ref, f_ref, send, oxs, oys)
        local_step(
            geo, lay, r_ref[...], dinv, scaled_ref[...], state, None, (*refs, q_ref, state_ref, False)
        )

    def make_iterate(first, final):
        def iterate_kernel(recv, *rest):
            xs, ys = rest[:nx], rest[nx : nx + ny]
            n_in = 10 + (0 if first else 3)
            ins = rest[nx + ny : nx + ny + n_in]
            fin_ref, r_ref, u_in, dinv_ref, scaled_ref, state_in = ins[:6]
            tab_ref, zt_ref, zmat_ref, msel_ref = ins[6:10]
            gram_ref = rest[nx + ny + n_in]
            p_in, si_in, x_in = (None, None, None) if first else ins[10:13]
            out = rest[nx + ny + n_in + 1 :]
            if final:
                send, oxs, oys = out[0], (), ()
                out = out[1:]
                u_ref, state_ref, p_ref, x_ref, w_ref, q_ref = out
                f_ref = r_out = si_ref = None
            else:
                send, oxs, oys = split(out[:n_out])
                u_ref, state_ref, p_ref, x_ref, r_out, si_ref, f_ref, w_ref, q_ref = out[n_out:]
            geo = Geometry(sizes)
            row, gamma, curvature, beta, alpha = step_sizes(lay, recv, state_in, first)
            received(geo, lay, fin_ref[...], recv, xs, ys, w_ref, 0)
            image = w_ref[...]
            p = u_in[...]
            s_row, ts_row = state_in[0:1, :], row
            if not first:
                p = p + beta * p_in[...]
                image = image + beta * si_in[...]
                ts_row = ts_row + beta * state_in[1:2, :]
            p_ref[...] = p
            x_ref[...] = alpha * p if first else x_in[...] + alpha * p
            residual = r_ref[...] - alpha * image
            if not final:
                si_ref[...] = image
                r_out[...] = residual
            lane = lax.broadcasted_iota(jnp.int32, row.shape, 1)
            ts_row = jnp.where(lane < lay.devices, ts_row, 0.0)
            state = (s_row - alpha * ts_row, ts_row, gamma, curvature)
            refs = (tab_ref, zt_ref, zmat_ref[...], msel_ref[...], gram_ref[...], u_ref, f_ref, send)
            local_step(
                geo,
                lay,
                residual,
                dinv_ref[...],
                scaled_ref[...],
                state,
                p,
                (*refs, oxs, oys, q_ref, state_ref, final),
            )

        return iterate_kernel

    def last_kernel(recv, state_in, u_in, p_in, x_in, out_ref):
        _, _, _, beta, alpha = step_sizes(lay, recv, state_in, False)
        out_ref[...] = x_in[...] + alpha * (u_in[...] + beta * p_in[...])

    def body(level_set, velocity, source, coarse_factor):
        level = level_set.reshape(ROWS, BZ)
        vel = velocity.reshape(3, ROWS, BZ)
        src = source.reshape(ROWS, BZ)
        tab, zt, places = jnp.asarray(tab_np), jnp.asarray(zt_np), jnp.asarray(places_np)
        factor = jnp.pad(coarse_factor, ((0, 0), (0, lay.lanes - lay.devices)))

        out = call(
            start_kernel,
            [level, vel, src, factor, tab, zt, places],
            outgoing(2) + [block, block, like(BZ, lay.lanes), like(16, lay.lanes)],
            [qrows],
            "advect",
        )
        fa, fd, zmat, msel = out[n_out:]
        got = exchange(out[:n_out])
        out = call(
            first_kernel,
            [*got, level, fa, fd, tab, zt],
            outgoing(1) + [block, block, block, like(8, lay.lanes), like(lay.lanes, lay.lanes)],
            [work],
            "sweep_first",
        )
        level, f, residual, s_rows, gram = out[n_out:]
        for _ in range(RSWEEPS - 1):
            got = exchange(out[:n_out])
            out = call(
                sweep_kernel, [*got, level, f, tab, zt], outgoing(1) + [block, block], [work], "sweep"
            )
            level, f = out[n_out:]
        got = exchange(out[:n_out])
        out = call(
            diagonal_kernel,
            [*got, level, f, tab, zt],
            outgoing(1) + [block, block, block],
            [work],
            "diagonal",
        )
        level, f, scaled = out[n_out:]
        got = exchange(out[:n_out])
        out = call(
            solve_kernel,
            [*got, f, residual, scaled, s_rows, tab, zt, zmat, msel, gram],
            outgoing(1) + [block, block, block, like(8, lay.lanes)],
            [work, qrows],
            "solve_start",
        )
        dinv, u, f, state = out[n_out:]
        p = image = x = None
        for step in range(ITERS - 1):
            first, final = step == 0, step == ITERS - 2
            got = exchange(out[:n_out])
            ins = [*got, f, residual, u, dinv, scaled, state, tab, zt, zmat, msel]
            if not first:
                ins += [p, image, x]
            ins.append(gram)
            fields = [block, like(8, lay.lanes), block, block]
            if final:
                outs = [like(lay.devices, lay.scalar_rows, 128)] + fields
            else:
                outs = outgoing(1) + fields + [block, block, block]
            out = call(make_iterate(first, final), ins, outs, [work, qrows], "iterate")
            if final:
                u, state, p, x = out[1:]
            else:
                u, state, p, x, residual, image, f = out[n_out:]
        recv = lax.all_to_all(out[0], AXES, 0, 0, tiled=True)
        (x,) = call(last_kernel, [recv, state, u, p, x], [block], [], "pressure")
        return level.reshape(BX, BY, BZ), x.reshape(BX, BY, BZ)

    return body


def solution(mesh):
    in_specs = (
        P("gx", "gy", "gz"),
        P(None, "gx", "gy", "gz"),
        P("gx", "gy", "gz"),
        P(("gx", "gy", "gz"), None),
    )
    out_specs = (P("gx", "gy", "gz"), P("gx", "gy", "gz"))
    return jax.shard_map(
        build(mesh), mesh=mesh, in_specs=in_specs, out_specs=out_specs, check_vma=False
    )
```

time: 1180 us -> 134 us (0.11); the launches traced: 1160 us -> 133 us
  blocking collectives: 669 us -> 9.31 us
  waiting for transfers between devices: 217 us -> 37 us
  starting transfers between devices: 197 us -> 59.2 us
  other arithmetic: 36.4 us -> 0 us
  Pallas kernels: 0 us -> 21.7 us
  between operations: 18.2 us -> 0.77 us
  matrix products: 16.5 us -> 0 us
    psum x17 -> x0, blocking collectives: 669 us -> none  [the longest x6 242 us: precondition(): coarse_mid = lax.psum(restricted * own_row, ('gx', 'gy', 'gz'))]
    ppermute x96 -> x27, waiting for transfers between devices: 217 us -> 12.4 us  [ring(): return lax.ppermute(v, axis, pairs)]
    ppermute x96 -> x27, starting transfers between devices: 197 us -> 31.1 us  [ring(): return lax.ppermute(v, axis, pairs)]
    all_to_all x0 -> x9, starting transfers between devices: none -> 28 us  [exchange(): recv = lax.all_to_all(send, AXES, 0, 0, tiled=True)]
    all_to_all x0 -> x9, waiting for transfers between devices: none -> 24.6 us  [exchange(): recv = lax.all_to_all(send, AXES, 0, 0, tiled=True)]
    pallas_call x0 -> x11, Pallas kernels: none -> 21.7 us  [call(): pl.pallas_call(kernel, out_shape=outs, in_specs=[spec] * len(ins), out_sp...]
    dot_general x57 -> x0, matrix products: 16.5 us -> none  [the longest x19 5.91 us: apply_axis(): return jnp.einsum('aq,pqr->par', matrix, values, precision=HIGHEST)]
    reduce_sum x16 -> x0, other arithmetic: 12.1 us -> none  [the longest x6 4.69 us: body(): jnp.sum(weight * direction * image)]
  transfers between devices with their start and end apart: 96 -> 36, of which waited for: 60 -> 27; matrix products, arithmetic and copies ran while one was open for 0% -> 0% of each run, Pallas kernels for 0% -> 0%
where the time goes in v1:
time: 134 us; the launch traced here: 133 us
  starting transfers between devices  59.2 us (44%)
  waiting for transfers between devices  37 us (28%)
  Pallas kernels  21.7 us (16%)
  blocking collectives  9.31 us (7%)
  local copies, waits for them, and re-layouts  5.32 us (4%)
    ppermute x27, starting transfers between devices, ring(): return lax.ppermute(v, axis, pairs)  31.1 us
    all_to_all x9, starting transfers between devices, exchange(): recv = lax.all_to_all(send, AXES, 0, 0, tiled=True)  28 us
    all_to_all x9, waiting for transfers between devices, exchange(): recv = lax.all_to_all(send, AXES, 0, 0, tiled=True)  24.6 us
    pallas_call x11, Pallas kernels, call(): pl.pallas_call(kernel, out_shape=outs, in_specs=[spec] * len(ins), out_sp...  21.7 us
    ppermute x27, waiting for transfers between devices, ring(): return lax.ppermute(v, axis, pairs)  12.4 us
    all_to_all x1, blocking collectives, body(): recv = lax.all_to_all(out[0], AXES, 0, 0, tiled=True)  9.31 us
    unnamed x18, local copies, waits for them, and re-layouts  4.65 us
  transfers between devices with their start and end apart: 36, of which 27 were waited for; matrix products, arithmetic and copies ran while one was open for 0% of the time, Pallas kernels for 0%

profile of v1, /device:TPU:0, one launch (start us, length us, event | category | flops | bytes accessed | tf_op | source)
XLA Modules:
  0.0 133.3 jit_solution(4856412689529505059)
XLA Ops:
  0.6 0.7 pad.4.factor_ref
  1.3 0.9 copy-done
  2.2 0.9 copy-done.2
  3.1 0.9 copy-done.4
  4.1 1.0 copy-done.6
  5.0 0.9 copy-done.7
  6.0 1.8 %advect.1 = (f32[32,8,128]{2,1,0:T(8,128)}, f32[32,128]{1,0:T(8,128)S(1)}, f32[32,128]{1,0:T(8,128)S(1)}, f32[32,128]{1,0:T(8,128)S(1)}, f32[256,128]{1,0:T(8,12...) custom-call(f32[256,128]{1,0:T(8,128)S(1)} %bitcast.5, f32[3,256,128]{2,1,0:T(8,128)S(1)} %bitcast.7, ...), custom_call_target="tpu_custom_call" | custom-call | tf_op jit(solution)/shard_map/advect/pallas_call | solution.py:554
  7.8 7.3 %all-to-all-start = ((f32[32,8,128]{2,1,0:T(8,128)}), f32[32,8,128]{2,1,0:T(8,128)S(1)}, u32[]{:S(2)}, u32[]{:S(2)}) async-start(f32[32,8,128]{2,1,0:T(8,128)} %get-tuple-element.89), calls=%async_computation | async-start | bytes 262144 | tf_op jit(solution)/shard_map/all_to_all | solution.py:577
  15.1 1.8 %collective-permute-start = (f32[32,128]{1,0:T(8,128)S(1)}, f32[32,128]{1,0:T(8,128)S(1)}, u32[]{:S(2)}, u32[]{:S(2)}) collective-permute-start(f32[32,128]{1,0:T(8,128)S(1)} %get-tuple-element.90), channel_id=1, source_target_pairs={{0,16},{16,0},{1,17},{17,1},{2,18},{18,2},{3,19},{19,3},{4,20},{20... | collective-permute-start | bytes 49160 | tf_op jit(solution)/shard_map/ppermute | solution.py:573
  16.9 1.7 %collective-permute-start.2 = (f32[32,128]{1,0:T(8,128)S(1)}, f32[32,128]{1,0:T(8,128)S(1)}, u32[]{:S(2)}, u32[]{:S(2)}) collective-permute-start(f32[32,128]{1,0:T(8,128)S(1)} %get-tuple-element.92), channel_id=1, source_target_pairs={{0,12},{4,0},{8,4},{12,8},{1,13},{5,1},{9,5},{13,9},{2,14},{6,2},{... | collective-permute-start | bytes 49160 | tf_op jit(solution)/shard_map/ppermute | solution.py:573
  18.9 1.3 collective-permute-done.1.rest_1_
  20.2 3.3 %all-to-all-done.recv = f32[32,8,128]{2,1,0:T(8,128)S(1)} async-done(((f32[32,8,128]{2,1,0:T(8,128)}), f32[32,8,128]{2,1,0:T(8,128)S(1)}, u32[]{:S(2)}, u32[]{:S(2)}) %all-to-all-start) | async-done | bytes 131104 | tf_op jit(solution)/shard_map/all_to_all | solution.py:577
  23.5 2.2 %sweep_first.1 = (f32[32,4,128]{2,1,0:T(4,128)}, f32[16,128]{1,0:T(8,128)S(1)}, f32[16,128]{1,0:T(8,128)S(1)}, f32[16,128]{1,0:T(8,128)S(1)}, f32[256,128]{1,0:T...) custom-call(f32[32,8,128]{2,1,0:T(8,128)S(1)} %all-to-all-done.recv,, ...), custom_call_target="tpu_custom_call" | custom-call | tf_op jit(solution)/shard_map/sweep_first/pallas_call | solution.py:554
  25.7 2.6 %all-to-all-start.1 = ((f32[32,4,128]{2,1,0:T(4,128)}), f32[32,4,128]{2,1,0:T(4,128)S(1)}, u32[]{:S(2)}, u32[]{:S(2)}) async-start(f32[32,4,128]{2,1,0:T(4,128)} %get-tuple-element.95), calls=%async_computation.1 | async-start | bytes 131072 | tf_op jit(solution)/shard_map/all_to_all | solution.py:577
  28.2 1.7 %collective-permute-start.3 = (f32[16,128]{1,0:T(8,128)S(1)}, f32[16,128]{1,0:T(8,128)S(1)}, u32[]{:S(2)}, u32[]{:S(2)}) collective-permute-start(f32[16,128]{1,0:T(8,128)S(1)} %get-tuple-element.96), channel_id=1, source_target_pairs={{0,16},{16,0},{1,17},{17,1},{2,18},{18,2},{3,19},{19,3},{4,20},{20... | collective-permute-start | bytes 24584 | tf_op jit(solution)/shard_map/ppermute | solution.py:573
  30.0 1.7 %collective-permute-start.5 = (f32[16,128]{1,0:T(8,128)S(1)}, f32[16,128]{1,0:T(8,128)S(1)}, u32[]{:S(2)}, u32[]{:S(2)}) collective-permute-start(f32[16,128]{1,0:T(8,128)S(1)} %get-tuple-element.98), channel_id=1, source_target_pairs={{0,12},{4,0},{8,4},{12,8},{1,13},{5,1},{9,5},{13,9},{2,14},{6,2},{... | collective-permute-start | bytes 24584 | tf_op jit(solution)/shard_map/ppermute | solution.py:573
  32.0 1.1 collective-permute-done.4.rest_1_
  33.1 2.7 %all-to-all-done.1.recv = f32[32,4,128]{2,1,0:T(4,128)S(1)} async-done(((f32[32,4,128]{2,1,0:T(4,128)}), f32[32,4,128]{2,1,0:T(4,128)S(1)}, u32[]{:S(2)}, u32[]{:S(2)}) %all-to-all-start.1) | async-done | bytes 65568 | tf_op jit(solution)/shard_map/all_to_all | solution.py:577
  35.7 2.0 %sweep.1 = (f32[32,4,128]{2,1,0:T(4,128)}, f32[16,128]{1,0:T(8,128)S(1)}, f32[16,128]{1,0:T(8,128)S(1)}, f32[16,128]{1,0:T(8,128)S(1)}, f32[256,128]{1,0:T(8,128)S(1)}, /*index=5*/f32[256,128]{1,0:T(8,128)S(1)}) custom-call(f32[32,4,128]{2,1,0:T(4,128)S(1)} %all-to-all-done.1.recv, f32[16,128]{1,0:T(8,128)S(1)} %collective-permute-done.3.rest_0_, ...), custom_call_target="tpu_custom_call" | custom-call | tf_op jit(solution)/shard_map/sweep/pallas_call | solution.py:554
  37.7 2.6 %all-to-all-start.2 = ((f32[32,4,128]{2,1,0:T(4,128)}), f32[32,4,128]{2,1,0:T(4,128)S(1)}, u32[]{:S(2)}, u32[]{:S(2)}) async-start(f32[32,4,128]{2,1,0:T(4,128)} %get-tuple-element.101), calls=%async_computation.2 | async-start | bytes 131072 | tf_op jit(solution)/shard_map/all_to_all | solution.py:577
  40.3 1.7 %collective-permute-start.6 = (f32[16,128]{1,0:T(8,128)S(1)}, f32[16,128]{1,0:T(8,128)S(1)}, u32[]{:S(2)}, u32[]{:S(2)}) collective-permute-start(f32[16,128]{1,0:T(8,128)S(1)} %get-tuple-element.102), channel_id=1, source_target_pairs={{0,16},{16,0},{1,17},{17,1},{2,18},{18,2},{3,19},{19,3},{4,20},{20... | collective-permute-start | bytes 24584 | tf_op jit(solution)/shard_map/ppermute | solution.py:573
  42.0 1.7 %collective-permute-start.8 = (f32[16,128]{1,0:T(8,128)S(1)}, f32[16,128]{1,0:T(8,128)S(1)}, u32[]{:S(2)}, u32[]{:S(2)}) collective-permute-start(f32[16,128]{1,0:T(8,128)S(1)} %get-tuple-element.104), channel_id=1, source_target_pairs={{0,12},{4,0},{8,4},{12,8},{1,13},{5,1},{9,5},{13,9},{2,14},{6,2},{... | collective-permute-start | bytes 24584 | tf_op jit(solution)/shard_map/ppermute | solution.py:573
  44.0 1.1 collective-permute-done.7.rest_1_
  45.1 2.7 %all-to-all-done.2.recv = f32[32,4,128]{2,1,0:T(4,128)S(1)} async-done(((f32[32,4,128]{2,1,0:T(4,128)}), f32[32,4,128]{2,1,0:T(4,128)S(1)}, u32[]{:S(2)}, u32[]{:S(2)}) %all-to-all-start.2) | async-done | bytes 65568 | tf_op jit(solution)/shard_map/all_to_all | solution.py:577
  47.8 1.7 %diagonal.1 = (f32[32,4,128]{2,1,0:T(4,128)}, f32[16,128]{1,0:T(8,128)S(1)}, f32[16,128]{1,0:T(8,128)S(1)}, f32[16,128]{1,0:T(8,128)S(1)}, f32[256,128]{1,0:T(8,...) custom-call(f32[32,4,128]{2,1,0:T(4,128)S(1)} %all-to-all-done.2.recv, ...), custom_call_target="tpu_custom_call" | custom-call | tf_op jit(solution)/shard_map/diagonal/pallas_call | solution.py:554
  49.5 2.6 %all-to-all-start.3 = ((f32[32,4,128]{2,1,0:T(4,128)}), f32[32,4,128]{2,1,0:T(4,128)S(1)}, u32[]{:S(2)}, u32[]{:S(2)}) async-start(f32[32,4,128]{2,1,0:T(4,128)} %get-tuple-element.108), calls=%async_computation.3 | async-start | bytes 131072 | tf_op jit(solution)/shard_map/all_to_all | solution.py:577
  52.1 1.7 %collective-permute-start.9 = (f32[16,128]{1,0:T(8,128)S(1)}, f32[16,128]{1,0:T(8,128)S(1)}, u32[]{:S(2)}, u32[]{:S(2)}) collective-permute-start(f32[16,128]{1,0:T(8,128)S(1)} %get-tuple-element.109), channel_id=1, source_target_pairs={{0,16},{16,0},{1,17},{17,1},{2,18},{18,2},{3,19},{19,3},{4,20},{20... | collective-permute-start | bytes 24584 | tf_op jit(solution)/shard_map/ppermute | solution.py:573
  53.8 1.7 %collective-permute-start.11 = (f32[16,128]{1,0:T(8,128)S(1)}, f32[16,128]{1,0:T(8,128)S(1)}, u32[]{:S(2)}, u32[]{:S(2)}) collective-permute-start(f32[16,128]{1,0:T(8,128)S(1)} %get-tuple-element.111), channel_id=1, source_target_pairs={{0,12},{4,0},{8,4},{12,8},{1,13},{5,1},{9,5},{13,9},{2,14},{6,2},{... | collective-permute-start | bytes 24584 | tf_op jit(solution)/shard_map/ppermute | solution.py:573
  55.8 1.1 collective-permute-done.10.rest_1_
  56.9 2.7 %all-to-all-done.3.recv = f32[32,4,128]{2,1,0:T(4,128)S(1)} async-done(((f32[32,4,128]{2,1,0:T(4,128)}), f32[32,4,128]{2,1,0:T(4,128)S(1)}, u32[]{:S(2)}, u32[]{:S(2)}) %all-to-all-start.3) | async-done | bytes 65568 | tf_op jit(solution)/shard_map/all_to_all | solution.py:577
  59.6 2.3 %solve_start.1 = (f32[32,4,128]{2,1,0:T(4,128)}, f32[16,128]{1,0:T(8,128)S(1)}, f32[16,128]{1,0:T(8,128)S(1)}, f32[16,128]{1,0:T(8,128)S(1)}, f32[256,128]{1,0:T...) custom-call(f32[32,4,128]{2,1,0:T(4,128)S(1)} %all-to-all-done.3.recv, ...), custom_call_target="tpu_custom_call" | custom-call | tf_op jit(solution)/shard_map/solve_start/pallas_call | solution.py:554
  61.9 2.6 %all-to-all-start.4 = ((f32[32,4,128]{2,1,0:T(4,128)}), f32[32,4,128]{2,1,0:T(4,128)S(1)}, u32[]{:S(2)}, u32[]{:S(2)}) async-start(f32[32,4,128]{2,1,0:T(4,128)} %get-tuple-element.119), calls=%async_computation.4 | async-start | bytes 131072 | tf_op jit(solution)/shard_map/all_to_all | solution.py:577
  64.4 1.7 %collective-permute-start.12 = (f32[16,128]{1,0:T(8,128)S(1)}, f32[16,128]{1,0:T(8,128)S(1)}, u32[]{:S(2)}, u32[]{:S(2)}) collective-permute-start(f32[16,128]{1,0:T(8,128)S(1)} %get-tuple-element.120), channel_id=1, source_target_pairs={{0,16},{16,0},{1,17},{17,1},{2,18},{18,2},{3,19},{19,3},{4,20},{20... | collective-permute-start | bytes 24584 | tf_op jit(solution)/shard_map/ppermute | solution.py:573
  66.2 1.7 %collective-permute-start.14 = (f32[16,128]{1,0:T(8,128)S(1)}, f32[16,128]{1,0:T(8,128)S(1)}, u32[]{:S(2)}, u32[]{:S(2)}) collective-permute-start(f32[16,128]{1,0:T(8,128)S(1)} %get-tuple-element.122), channel_id=1, source_target_pairs={{0,12},{4,0},{8,4},{12,8},{1,13},{5,1},{9,5},{13,9},{2,14},{6,2},{... | collective-permute-start | bytes 24584 | tf_op jit(solution)/shard_map/ppermute | solution.py:573
  68.2 1.1 collective-permute-done.13.rest_1_
  69.3 2.7 %all-to-all-done.4.recv = f32[32,4,128]{2,1,0:T(4,128)S(1)} async-done(((f32[32,4,128]{2,1,0:T(4,128)}), f32[32,4,128]{2,1,0:T(4,128)S(1)}, u32[]{:S(2)}, u32[]{:S(2)}) %all-to-all-start.4) | async-done | bytes 65568 | tf_op jit(solution)/shard_map/all_to_all | solution.py:577
  71.9 2.4 %iterate.5 = (f32[32,4,128]{2,1,0:T(4,128)}, f32[16,128]{1,0:T(8,128)S(1)}, f32[16,128]{1,0:T(8,128)S(1)}, f32[16,128]{1,0:T(8,128)S(1)}, f32[256,128]{1,0:T(8,1...) custom-call(f32[32,4,128]{2,1,0:T(4,128)S(1)} %all-to-all-done.4.rec, ...), custom_call_target="tpu_custom_call" | custom-call | tf_op jit(solution)/shard_map/iterate/pallas_call | solution.py:554
  74.3 2.6 %all-to-all-start.5 = ((f32[32,4,128]{2,1,0:T(4,128)}), f32[32,4,128]{2,1,0:T(4,128)S(1)}, u32[]{:S(2)}, u32[]{:S(2)}) async-start(f32[32,4,128]{2,1,0:T(4,128)} %get-tuple-element.127), calls=%async_computation.5 | async-start | bytes 131072 | tf_op jit(solution)/shard_map/all_to_all | solution.py:577
  76.9 1.7 %collective-permute-start.15 = (f32[16,128]{1,0:T(8,128)S(1)}, f32[16,128]{1,0:T(8,128)S(1)}, u32[]{:S(2)}, u32[]{:S(2)}) collective-permute-start(f32[16,128]{1,0:T(8,128)S(1)} %get-tuple-element.128), channel_id=1, source_target_pairs={{0,16},{16,0},{1,17},{17,1},{2,18},{18,2},{3,19},{19,3},{4,20},{20... | collective-permute-start | bytes 24584 | tf_op jit(solution)/shard_map/ppermute | solution.py:573
  78.6 1.7 %collective-permute-start.17 = (f32[16,128]{1,0:T(8,128)S(1)}, f32[16,128]{1,0:T(8,128)S(1)}, u32[]{:S(2)}, u32[]{:S(2)}) collective-permute-start(f32[16,128]{1,0:T(8,128)S(1)} %get-tuple-element.130), channel_id=1, source_target_pairs={{0,12},{4,0},{8,4},{12,8},{1,13},{5,1},{9,5},{13,9},{2,14},{6,2},{... | collective-permute-start | bytes 24584 | tf_op jit(solution)/shard_map/ppermute | solution.py:573
  80.6 1.1 collective-permute-done.16.rest_1_
  81.7 2.7 %all-to-all-done.5.recv = f32[32,4,128]{2,1,0:T(4,128)S(1)} async-done(((f32[32,4,128]{2,1,0:T(4,128)}), f32[32,4,128]{2,1,0:T(4,128)S(1)}, u32[]{:S(2)}, u32[]{:S(2)}) %all-to-all-start.5) | async-done | bytes 65568 | tf_op jit(solution)/shard_map/all_to_all | solution.py:577
  84.4 2.4 %iterate.6 = (f32[32,4,128]{2,1,0:T(4,128)}, f32[16,128]{1,0:T(8,128)S(1)}, f32[16,128]{1,0:T(8,128)S(1)}, f32[16,128]{1,0:T(8,128)S(1)}, f32[256,128]{1,0:T(8,1...) custom-call(f32[32,4,128]{2,1,0:T(4,128)S(1)} %all-to-all-done.5.rec, ...), custom_call_target="tpu_custom_call" | custom-call | tf_op jit(solution)/shard_map/iterate/pallas_call | solution.py:554
  86.7 2.6 %all-to-all-start.6 = ((f32[32,4,128]{2,1,0:T(4,128)}), f32[32,4,128]{2,1,0:T(4,128)S(1)}, u32[]{:S(2)}, u32[]{:S(2)}) async-start(f32[32,4,128]{2,1,0:T(4,128)} %get-tuple-element.138), calls=%async_computation.6 | async-start | bytes 131072 | tf_op jit(solution)/shard_map/all_to_all | solution.py:577
  89.3 1.7 %collective-permute-start.18 = (f32[16,128]{1,0:T(8,128)S(1)}, f32[16,128]{1,0:T(8,128)S(1)}, u32[]{:S(2)}, u32[]{:S(2)}) collective-permute-start(f32[16,128]{1,0:T(8,128)S(1)} %get-tuple-element.139), channel_id=1, source_target_pairs={{0,16},{16,0},{1,17},{17,1},{2,18},{18,2},{3,19},{19,3},{4,20},{20... | collective-permute-start | bytes 24584 | tf_op jit(solution)/shard_map/ppermute | solution.py:573
  91.0 1.7 %collective-permute-start.20 = (f32[16,128]{1,0:T(8,128)S(1)}, f32[16,128]{1,0:T(8,128)S(1)}, u32[]{:S(2)}, u32[]{:S(2)}) collective-permute-start(f32[16,128]{1,0:T(8,128)S(1)} %get-tuple-element.141), channel_id=1, source_target_pairs={{0,12},{4,0},{8,4},{12,8},{1,13},{5,1},{9,5},{13,9},{2,14},{6,2},{... | collective-permute-start | bytes 24584 | tf_op jit(solution)/shard_map/ppermute | solution.py:573
  93.0 1.1 collective-permute-done.19.rest_1_
  94.1 2.7 %all-to-all-done.6.recv = f32[32,4,128]{2,1,0:T(4,128)S(1)} async-done(((f32[32,4,128]{2,1,0:T(4,128)}), f32[32,4,128]{2,1,0:T(4,128)S(1)}, u32[]{:S(2)}, u32[]{:S(2)}) %all-to-all-start.6) | async-done | bytes 65568 | tf_op jit(solution)/shard_map/all_to_all | solution.py:577
  96.8 2.4 %iterate.7 = (f32[32,4,128]{2,1,0:T(4,128)}, f32[16,128]{1,0:T(8,128)S(1)}, f32[16,128]{1,0:T(8,128)S(1)}, f32[16,128]{1,0:T(8,128)S(1)}, f32[256,128]{1,0:T(8,1...) custom-call(f32[32,4,128]{2,1,0:T(4,128)S(1)} %all-to-all-done.6.rec, ...), custom_call_target="tpu_custom_call" | custom-call | tf_op jit(solution)/shard_map/iterate/pallas_call | solution.py:554
  99.1 2.8 %all-to-all-start.7 = ((f32[32,4,128]{2,1,0:T(4,128)}), f32[32,4,128]{2,1,0:T(4,128)S(1)}, u32[]{:S(2)}, u32[]{:S(2)}) async-start(f32[32,4,128]{2,1,0:T(4,128)} %get-tuple-element.149), calls=%async_computation.7 | async-start | bytes 131072 | tf_op jit(solution)/shard_map/all_to_all | solution.py:577
  101.9 1.5 %collective-permute-start.21 = (f32[16,128]{1,0:T(8,128)S(1)}, f32[16,128]{1,0:T(8,128)S(1)}, u32[]{:S(2)}, u32[]{:S(2)}) collective-permute-start(f32[16,128]{1,0:T(8,128)S(1)} %get-tuple-element.150), channel_id=1, source_target_pairs={{0,16},{16,0},{1,17},{17,1},{2,18},{18,2},{3,19},{19,3},{4,20},{20... | collective-permute-start | bytes 24584 | tf_op jit(solution)/shard_map/ppermute | solution.py:573
  103.5 1.7 %collective-permute-start.23 = (f32[16,128]{1,0:T(8,128)S(1)}, f32[16,128]{1,0:T(8,128)S(1)}, u32[]{:S(2)}, u32[]{:S(2)}) collective-permute-start(f32[16,128]{1,0:T(8,128)S(1)} %get-tuple-element.152), channel_id=1, source_target_pairs={{0,12},{4,0},{8,4},{12,8},{1,13},{5,1},{9,5},{13,9},{2,14},{6,2},{... | collective-permute-start | bytes 24584 | tf_op jit(solution)/shard_map/ppermute | solution.py:573
  105.2 0.4 collective-permute-done.21.rest_0_
  105.6 0.9 collective-permute-done.22.rest_1_
  106.6 2.7 %all-to-all-done.7.recv = f32[32,4,128]{2,1,0:T(4,128)S(1)} async-done(((f32[32,4,128]{2,1,0:T(4,128)}), f32[32,4,128]{2,1,0:T(4,128)S(1)}, u32[]{:S(2)}, u32[]{:S(2)}) %all-to-all-start.7) | async-done | bytes 65568 | tf_op jit(solution)/shard_map/all_to_all | solution.py:577
  109.2 2.4 %iterate.8 = (f32[32,4,128]{2,1,0:T(4,128)}, f32[16,128]{1,0:T(8,128)S(1)}, f32[16,128]{1,0:T(8,128)S(1)}, f32[16,128]{1,0:T(8,128)S(1)}, f32[256,128]{1,0:T(8,1...) custom-call(f32[32,4,128]{2,1,0:T(4,128)S(1)} %all-to-all-done.7.rec, ...), custom_call_target="tpu_custom_call" | custom-call | tf_op jit(solution)/shard_map/iterate/pallas_call | solution.py:554
  111.6 2.6 %all-to-all-start.8 = ((f32[32,4,128]{2,1,0:T(4,128)}), f32[32,4,128]{2,1,0:T(4,128)S(1)}, u32[]{:S(2)}, u32[]{:S(2)}) async-start(f32[32,4,128]{2,1,0:T(4,128)} %get-tuple-element.160), calls=%async_computation.8 | async-start | bytes 131072 | tf_op jit(solution)/shard_map/all_to_all | solution.py:577
  114.2 1.7 %collective-permute-start.24 = (f32[16,128]{1,0:T(8,128)S(1)}, f32[16,128]{1,0:T(8,128)S(1)}, u32[]{:S(2)}, u32[]{:S(2)}) collective-permute-start(f32[16,128]{1,0:T(8,128)S(1)} %get-tuple-element.161), channel_id=1, source_target_pairs={{0,16},{16,0},{1,17},{17,1},{2,18},{18,2},{3,19},{19,3},{4,20},{20... | collective-permute-start | bytes 24584 | tf_op jit(solution)/shard_map/ppermute | solution.py:573
  115.9 1.7 %collective-permute-start.26 = (f32[16,128]{1,0:T(8,128)S(1)}, f32[16,128]{1,0:T(8,128)S(1)}, u32[]{:S(2)}, u32[]{:S(2)}) collective-permute-start(f32[16,128]{1,0:T(8,128)S(1)} %get-tuple-element.163), channel_id=1, source_target_pairs={{0,12},{4,0},{8,4},{12,8},{1,13},{5,1},{9,5},{13,9},{2,14},{6,2},{... | collective-permute-start | bytes 24584 | tf_op jit(solution)/shard_map/ppermute | solution.py:573
  117.9 1.1 collective-permute-done.25.rest_1_
  119.0 2.7 %all-to-all-done.8.recv = f32[32,4,128]{2,1,0:T(4,128)S(1)} async-done(((f32[32,4,128]{2,1,0:T(4,128)}), f32[32,4,128]{2,1,0:T(4,128)S(1)}, u32[]{:S(2)}, u32[]{:S(2)}) %all-to-all-start.8) | async-done | bytes 65568 | tf_op jit(solution)/shard_map/all_to_all | solution.py:577
  121.6 1.5 %iterate.9 = (f32[32,1,128]{2,1,0:T(1,128)S(1)}, f32[256,128]{1,0:T(8,128)S(1)}, f32[8,128]{1,0:T(8,128)S(1)}, f32[256,128]{1,0:T(8,128)S(1)}, f32[256,128]{1,0:T(8,128)S(1)}) custom-call(f32[32,4,128]{2,1,0:T(4,128)S(1)} %all-to-all-done.8.recv, f32[16,128]{1,0:T(8,128)S(1)} %collective-permute-done.24.rest_0_, ...), custom_call_target="tpu_custom_call" | custom-call | tf_op jit(solution)/shard_map/iterate/pallas_call | solution.py:554
  123.2 9.3 %all_to_all.50.recv = f32[32,1,128]{2,1,0:T(1,128)S(1)} all-to-all(f32[32,1,128]{2,1,0:T(1,128)S(1)} %get-tuple-element.171), channel_id=1, replica_groups=mesh['gx'=2,'gy'=4,'gz'=4] {'gx','gy','gz'}, dimensions={0} | all-to-all | bytes 32768 | tf_op jit(solution)/shard_map/all_to_all | solution.py:810
  132.5 0.8 pressure.1
  (39 shorter events, 2.3 us)
Async XLA Ops:
  0.6 0.7 copy-start.8
  1.3 0.9 copy-start
  2.2 0.9 copy-start.2
  3.1 0.9 copy-start.4
  4.1 1.0 copy-start.6
  5.0 0.9 copy-start.7
  6.0 17.5 %copy-start.3 = (f32[224,128]{1,0:T(8,128)S(1)}, f32[224,128]{1,0:T(8,128)}, u32[]{:S(2)}) copy-start(f32[224,128]{1,0:T(8,128)} %constant.9.clone.tab_ref.rest_6_.rest_5_.rest_7_.rest_9_) | copy-start | bytes 344068
  6.0 17.5 %copy-start.5 = (f32[16,16,128]{2,1,0:T(8,128)S(1)}, f32[16,16,128]{2,1,0:T(8,128)}, u32[]{:S(2)}) copy-start(f32[16,16,128]{2,1,0:T(8,128)} %param.7) | copy-start | bytes 393220
  7.8 15.7 %copy-start.1 = (bf16[768,128]{1,0:T(8,128)(2,1)S(1)}, bf16[768,128]{1,0:T(8,128)(2,1)}, u32[]{:S(2)}) copy-start(bf16[768,128]{1,0:T(8,128)(2,1)} %constant.10.clone.zt_ref.rest_7_.rest_6_.rest_8_.rest_10_) | copy-start | bytes 589828
  7.8 15.7 %all-to-all-start = ((f32[32,8,128]{2,1,0:T(8,128)}), f32[32,8,128]{2,1,0:T(8,128)S(1)}, u32[]{:S(2)}, u32[]{:S(2)}) async-start(f32[32,8,128]{2,1,0:T(8,128)} %get-tuple-element.89), calls=%async_computation | async-start | bytes 262144 | tf_op jit(solution)/shard_map/all_to_all | solution.py:577
  15.1 3.8 %collective-permute-start = (f32[32,128]{1,0:T(8,128)S(1)}, f32[32,128]{1,0:T(8,128)S(1)}, u32[]{:S(2)}, u32[]{:S(2)}) collective-permute-start(f32[32,128]{1,0:T(8,128)S(1)} %get-tuple-element.90), channel_id=1, source_target_pairs={{0,16},{16,0},{1,17},{17,1},{2,18},{18,2},{3,19},{19,3},{4,20},{20... | collective-permute-start | bytes 49160 | tf_op jit(solution)/shard_map/ppermute | solution.py:573
  16.9 3.3 %collective-permute-start.1 = (f32[32,128]{1,0:T(8,128)S(1)}, f32[32,128]{1,0:T(8,128)S(1)}, u32[]{:S(2)}, u32[]{:S(2)}) collective-permute-start(f32[32,128]{1,0:T(8,128)S(1)} %get-tuple-element.91), channel_id=1, source_target_pairs={{0,4},{4,8},{8,12},{12,0},{1,5},{5,9},{9,13},{13,1},{2,6},{6,10},{... | collective-permute-start | bytes 49160 | tf_op jit(solution)/shard_map/ppermute | solution.py:573
  16.9 3.3 %collective-permute-start.2 = (f32[32,128]{1,0:T(8,128)S(1)}, f32[32,128]{1,0:T(8,128)S(1)}, u32[]{:S(2)}, u32[]{:S(2)}) collective-permute-start(f32[32,128]{1,0:T(8,128)S(1)} %get-tuple-element.92), channel_id=1, source_target_pairs={{0,12},{4,0},{8,4},{12,8},{1,13},{5,1},{9,5},{13,9},{2,14},{6,2},{... | collective-permute-start | bytes 49160 | tf_op jit(solution)/shard_map/ppermute | solution.py:573
  25.7 10.1 %all-to-all-start.1 = ((f32[32,4,128]{2,1,0:T(4,128)}), f32[32,4,128]{2,1,0:T(4,128)S(1)}, u32[]{:S(2)}, u32[]{:S(2)}) async-start(f32[32,4,128]{2,1,0:T(4,128)} %get-tuple-element.95), calls=%async_computation.1 | async-start | bytes 131072 | tf_op jit(solution)/shard_map/all_to_all | solution.py:577
  28.2 3.7 %collective-permute-start.3 = (f32[16,128]{1,0:T(8,128)S(1)}, f32[16,128]{1,0:T(8,128)S(1)}, u32[]{:S(2)}, u32[]{:S(2)}) collective-permute-start(f32[16,128]{1,0:T(8,128)S(1)} %get-tuple-element.96), channel_id=1, source_target_pairs={{0,16},{16,0},{1,17},{17,1},{2,18},{18,2},{3,19},{19,3},{4,20},{20... | collective-permute-start | bytes 24584 | tf_op jit(solution)/shard_map/ppermute | solution.py:573
  30.0 3.1 %collective-permute-start.4 = (f32[16,128]{1,0:T(8,128)S(1)}, f32[16,128]{1,0:T(8,128)S(1)}, u32[]{:S(2)}, u32[]{:S(2)}) collective-permute-start(f32[16,128]{1,0:T(8,128)S(1)} %get-tuple-element.97), channel_id=1, source_target_pairs={{0,4},{4,8},{8,12},{12,0},{1,5},{5,9},{9,13},{13,1},{2,6},{6,10},{... | collective-permute-start | bytes 24584 | tf_op jit(solution)/shard_map/ppermute | solution.py:573
  30.0 3.1 %collective-permute-start.5 = (f32[16,128]{1,0:T(8,128)S(1)}, f32[16,128]{1,0:T(8,128)S(1)}, u32[]{:S(2)}, u32[]{:S(2)}) collective-permute-start(f32[16,128]{1,0:T(8,128)S(1)} %get-tuple-element.98), channel_id=1, source_target_pairs={{0,12},{4,0},{8,4},{12,8},{1,13},{5,1},{9,5},{13,9},{2,14},{6,2},{... | collective-permute-start | bytes 24584 | tf_op jit(solution)/shard_map/ppermute | solution.py:573
  37.7 10.1 %all-to-all-start.2 = ((f32[32,4,128]{2,1,0:T(4,128)}), f32[32,4,128]{2,1,0:T(4,128)S(1)}, u32[]{:S(2)}, u32[]{:S(2)}) async-start(f32[32,4,128]{2,1,0:T(4,128)} %get-tuple-element.101), calls=%async_computation.2 | async-start | bytes 131072 | tf_op jit(solution)/shard_map/all_to_all | solution.py:577
  40.3 3.7 %collective-permute-start.6 = (f32[16,128]{1,0:T(8,128)S(1)}, f32[16,128]{1,0:T(8,128)S(1)}, u32[]{:S(2)}, u32[]{:S(2)}) collective-permute-start(f32[16,128]{1,0:T(8,128)S(1)} %get-tuple-element.102), channel_id=1, source_target_pairs={{0,16},{16,0},{1,17},{17,1},{2,18},{18,2},{3,19},{19,3},{4,20},{20... | collective-permute-start | bytes 24584 | tf_op jit(solution)/shard_map/ppermute | solution.py:573
  42.0 3.1 %collective-permute-start.7 = (f32[16,128]{1,0:T(8,128)S(1)}, f32[16,128]{1,0:T(8,128)S(1)}, u32[]{:S(2)}, u32[]{:S(2)}) collective-permute-start(f32[16,128]{1,0:T(8,128)S(1)} %get-tuple-element.103), channel_id=1, source_target_pairs={{0,4},{4,8},{8,12},{12,0},{1,5},{5,9},{9,13},{13,1},{2,6},{6,10},{... | collective-permute-start | bytes 24584 | tf_op jit(solution)/shard_map/ppermute | solution.py:573
  42.0 3.1 %collective-permute-start.8 = (f32[16,128]{1,0:T(8,128)S(1)}, f32[16,128]{1,0:T(8,128)S(1)}, u32[]{:S(2)}, u32[]{:S(2)}) collective-permute-start(f32[16,128]{1,0:T(8,128)S(1)} %get-tuple-element.104), channel_id=1, source_target_pairs={{0,12},{4,0},{8,4},{12,8},{1,13},{5,1},{9,5},{13,9},{2,14},{6,2},{... | collective-permute-start | bytes 24584 | tf_op jit(solution)/shard_map/ppermute | solution.py:573
  49.5 10.1 %all-to-all-start.3 = ((f32[32,4,128]{2,1,0:T(4,128)}), f32[32,4,128]{2,1,0:T(4,128)S(1)}, u32[]{:S(2)}, u32[]{:S(2)}) async-start(f32[32,4,128]{2,1,0:T(4,128)} %get-tuple-element.108), calls=%async_computation.3 | async-start | bytes 131072 | tf_op jit(solution)/shard_map/all_to_all | solution.py:577
  52.1 3.7 %collective-permute-start.9 = (f32[16,128]{1,0:T(8,128)S(1)}, f32[16,128]{1,0:T(8,128)S(1)}, u32[]{:S(2)}, u32[]{:S(2)}) collective-permute-start(f32[16,128]{1,0:T(8,128)S(1)} %get-tuple-element.109), channel_id=1, source_target_pairs={{0,16},{16,0},{1,17},{17,1},{2,18},{18,2},{3,19},{19,3},{4,20},{20... | collective-permute-start | bytes 24584 | tf_op jit(solution)/shard_map/ppermute | solution.py:573
  53.8 3.1 %collective-permute-start.10 = (f32[16,128]{1,0:T(8,128)S(1)}, f32[16,128]{1,0:T(8,128)S(1)}, u32[]{:S(2)}, u32[]{:S(2)}) collective-permute-start(f32[16,128]{1,0:T(8,128)S(1)} %get-tuple-element.110), channel_id=1, source_target_pairs={{0,4},{4,8},{8,12},{12,0},{1,5},{5,9},{9,13},{13,1},{2,6},{6,10},{... | collective-permute-start | bytes 24584 | tf_op jit(solution)/shard_map/ppermute | solution.py:573
  53.8 3.1 %collective-permute-start.11 = (f32[16,128]{1,0:T(8,128)S(1)}, f32[16,128]{1,0:T(8,128)S(1)}, u32[]{:S(2)}, u32[]{:S(2)}) collective-permute-start(f32[16,128]{1,0:T(8,128)S(1)} %get-tuple-element.111), channel_id=1, source_target_pairs={{0,12},{4,0},{8,4},{12,8},{1,13},{5,1},{9,5},{13,9},{2,14},{6,2},{... | collective-permute-start | bytes 24584 | tf_op jit(solution)/shard_map/ppermute | solution.py:573
  61.9 10.1 %all-to-all-start.4 = ((f32[32,4,128]{2,1,0:T(4,128)}), f32[32,4,128]{2,1,0:T(4,128)S(1)}, u32[]{:S(2)}, u32[]{:S(2)}) async-start(f32[32,4,128]{2,1,0:T(4,128)} %get-tuple-element.119), calls=%async_computation.4 | async-start | bytes 131072 | tf_op jit(solution)/shard_map/all_to_all | solution.py:577
  64.4 3.7 %collective-permute-start.12 = (f32[16,128]{1,0:T(8,128)S(1)}, f32[16,128]{1,0:T(8,128)S(1)}, u32[]{:S(2)}, u32[]{:S(2)}) collective-permute-start(f32[16,128]{1,0:T(8,128)S(1)} %get-tuple-element.120), channel_id=1, source_target_pairs={{0,16},{16,0},{1,17},{17,1},{2,18},{18,2},{3,19},{19,3},{4,20},{20... | collective-permute-start | bytes 24584 | tf_op jit(solution)/shard_map/ppermute | solution.py:573
  66.2 3.1 %collective-permute-start.13 = (f32[16,128]{1,0:T(8,128)S(1)}, f32[16,128]{1,0:T(8,128)S(1)}, u32[]{:S(2)}, u32[]{:S(2)}) collective-permute-start(f32[16,128]{1,0:T(8,128)S(1)} %get-tuple-element.121), channel_id=1, source_target_pairs={{0,4},{4,8},{8,12},{12,0},{1,5},{5,9},{9,13},{13,1},{2,6},{6,10},{... | collective-permute-start | bytes 24584 | tf_op jit(solution)/shard_map/ppermute | solution.py:573
  66.2 3.1 %collective-permute-start.14 = (f32[16,128]{1,0:T(8,128)S(1)}, f32[16,128]{1,0:T(8,128)S(1)}, u32[]{:S(2)}, u32[]{:S(2)}) collective-permute-start(f32[16,128]{1,0:T(8,128)S(1)} %get-tuple-element.122), channel_id=1, source_target_pairs={{0,12},{4,0},{8,4},{12,8},{1,13},{5,1},{9,5},{13,9},{2,14},{6,2},{... | collective-permute-start | bytes 24584 | tf_op jit(solution)/shard_map/ppermute | solution.py:573
  74.3 10.1 %all-to-all-start.5 = ((f32[32,4,128]{2,1,0:T(4,128)}), f32[32,4,128]{2,1,0:T(4,128)S(1)}, u32[]{:S(2)}, u32[]{:S(2)}) async-start(f32[32,4,128]{2,1,0:T(4,128)} %get-tuple-element.127), calls=%async_computation.5 | async-start | bytes 131072 | tf_op jit(solution)/shard_map/all_to_all | solution.py:577
  76.9 3.7 %collective-permute-start.15 = (f32[16,128]{1,0:T(8,128)S(1)}, f32[16,128]{1,0:T(8,128)S(1)}, u32[]{:S(2)}, u32[]{:S(2)}) collective-permute-start(f32[16,128]{1,0:T(8,128)S(1)} %get-tuple-element.128), channel_id=1, source_target_pairs={{0,16},{16,0},{1,17},{17,1},{2,18},{18,2},{3,19},{19,3},{4,20},{20... | collective-permute-start | bytes 24584 | tf_op jit(solution)/shard_map/ppermute | solution.py:573
  78.6 3.1 %collective-permute-start.16 = (f32[16,128]{1,0:T(8,128)S(1)}, f32[16,128]{1,0:T(8,128)S(1)}, u32[]{:S(2)}, u32[]{:S(2)}) collective-permute-start(f32[16,128]{1,0:T(8,128)S(1)} %get-tuple-element.129), channel_id=1, source_target_pairs={{0,4},{4,8},{8,12},{12,0},{1,5},{5,9},{9,13},{13,1},{2,6},{6,10},{... | collective-permute-start | bytes 24584 | tf_op jit(solution)/shard_map/ppermute | solution.py:573
  78.6 3.1 %collective-permute-start.17 = (f32[16,128]{1,0:T(8,128)S(1)}, f32[16,128]{1,0:T(8,128)S(1)}, u32[]{:S(2)}, u32[]{:S(2)}) collective-permute-start(f32[16,128]{1,0:T(8,128)S(1)} %get-tuple-element.130), channel_id=1, source_target_pairs={{0,12},{4,0},{8,4},{12,8},{1,13},{5,1},{9,5},{13,9},{2,14},{6,2},{... | collective-permute-start | bytes 24584 | tf_op jit(solution)/shard_map/ppermute | solution.py:573
  86.7 10.1 %all-to-all-start.6 = ((f32[32,4,128]{2,1,0:T(4,128)}), f32[32,4,128]{2,1,0:T(4,128)S(1)}, u32[]{:S(2)}, u32[]{:S(2)}) async-start(f32[32,4,128]{2,1,0:T(4,128)} %get-tuple-element.138), calls=%async_computation.6 | async-start | bytes 131072 | tf_op jit(solution)/shard_map/all_to_all | solution.py:577
  89.3 3.7 %collective-permute-start.18 = (f32[16,128]{1,0:T(8,128)S(1)}, f32[16,128]{1,0:T(8,128)S(1)}, u32[]{:S(2)}, u32[]{:S(2)}) collective-permute-start(f32[16,128]{1,0:T(8,128)S(1)} %get-tuple-element.139), channel_id=1, source_target_pairs={{0,16},{16,0},{1,17},{17,1},{2,18},{18,2},{3,19},{19,3},{4,20},{20... | collective-permute-start | bytes 24584 | tf_op jit(solution)/shard_map/ppermute | solution.py:573
  91.0 3.1 %collective-permute-start.19 = (f32[16,128]{1,0:T(8,128)S(1)}, f32[16,128]{1,0:T(8,128)S(1)}, u32[]{:S(2)}, u32[]{:S(2)}) collective-permute-start(f32[16,128]{1,0:T(8,128)S(1)} %get-tuple-element.140), channel_id=1, source_target_pairs={{0,4},{4,8},{8,12},{12,0},{1,5},{5,9},{9,13},{13,1},{2,6},{6,10},{... | collective-permute-start | bytes 24584 | tf_op jit(solution)/shard_map/ppermute | solution.py:573
  91.0 3.1 %collective-permute-start.20 = (f32[16,128]{1,0:T(8,128)S(1)}, f32[16,128]{1,0:T(8,128)S(1)}, u32[]{:S(2)}, u32[]{:S(2)}) collective-permute-start(f32[16,128]{1,0:T(8,128)S(1)} %get-tuple-element.141), channel_id=1, source_target_pairs={{0,12},{4,0},{8,4},{12,8},{1,13},{5,1},{9,5},{13,9},{2,14},{6,2},{... | collective-permute-start | bytes 24584 | tf_op jit(solution)/shard_map/ppermute | solution.py:573
  99.1 10.1 %all-to-all-start.7 = ((f32[32,4,128]{2,1,0:T(4,128)}), f32[32,4,128]{2,1,0:T(4,128)S(1)}, u32[]{:S(2)}, u32[]{:S(2)}) async-start(f32[32,4,128]{2,1,0:T(4,128)} %get-tuple-element.149), calls=%async_computation.7 | async-start | bytes 131072 | tf_op jit(solution)/shard_map/all_to_all | solution.py:577
  101.9 3.7 %collective-permute-start.21 = (f32[16,128]{1,0:T(8,128)S(1)}, f32[16,128]{1,0:T(8,128)S(1)}, u32[]{:S(2)}, u32[]{:S(2)}) collective-permute-start(f32[16,128]{1,0:T(8,128)S(1)} %get-tuple-element.150), channel_id=1, source_target_pairs={{0,16},{16,0},{1,17},{17,1},{2,18},{18,2},{3,19},{19,3},{4,20},{20... | collective-permute-start | bytes 24584 | tf_op jit(solution)/shard_map/ppermute | solution.py:573
  103.4 3.1 %collective-permute-start.22 = (f32[16,128]{1,0:T(8,128)S(1)}, f32[16,128]{1,0:T(8,128)S(1)}, u32[]{:S(2)}, u32[]{:S(2)}) collective-permute-start(f32[16,128]{1,0:T(8,128)S(1)} %get-tuple-element.151), channel_id=1, source_target_pairs={{0,4},{4,8},{8,12},{12,0},{1,5},{5,9},{9,13},{13,1},{2,6},{6,10},{... | collective-permute-start | bytes 24584 | tf_op jit(solution)/shard_map/ppermute | solution.py:573
  103.5 3.1 %collective-permute-start.23 = (f32[16,128]{1,0:T(8,128)S(1)}, f32[16,128]{1,0:T(8,128)S(1)}, u32[]{:S(2)}, u32[]{:S(2)}) collective-permute-start(f32[16,128]{1,0:T(8,128)S(1)} %get-tuple-element.152), channel_id=1, source_target_pairs={{0,12},{4,0},{8,4},{12,8},{1,13},{5,1},{9,5},{13,9},{2,14},{6,2},{... | collective-permute-start | bytes 24584 | tf_op jit(solution)/shard_map/ppermute | solution.py:573
  111.6 10.1 %all-to-all-start.8 = ((f32[32,4,128]{2,1,0:T(4,128)}), f32[32,4,128]{2,1,0:T(4,128)S(1)}, u32[]{:S(2)}, u32[]{:S(2)}) async-start(f32[32,4,128]{2,1,0:T(4,128)} %get-tuple-element.160), calls=%async_computation.8 | async-start | bytes 131072 | tf_op jit(solution)/shard_map/all_to_all | solution.py:577
  114.2 3.7 %collective-permute-start.24 = (f32[16,128]{1,0:T(8,128)S(1)}, f32[16,128]{1,0:T(8,128)S(1)}, u32[]{:S(2)}, u32[]{:S(2)}) collective-permute-start(f32[16,128]{1,0:T(8,128)S(1)} %get-tuple-element.161), channel_id=1, source_target_pairs={{0,16},{16,0},{1,17},{17,1},{2,18},{18,2},{3,19},{19,3},{4,20},{20... | collective-permute-start | bytes 24584 | tf_op jit(solution)/shard_map/ppermute | solution.py:573
  115.9 3.1 %collective-permute-start.25 = (f32[16,128]{1,0:T(8,128)S(1)}, f32[16,128]{1,0:T(8,128)S(1)}, u32[]{:S(2)}, u32[]{:S(2)}) collective-permute-start(f32[16,128]{1,0:T(8,128)S(1)} %get-tuple-element.162), channel_id=1, source_target_pairs={{0,4},{4,8},{8,12},{12,0},{1,5},{5,9},{9,13},{13,1},{2,6},{6,10},{... | collective-permute-start | bytes 24584 | tf_op jit(solution)/shard_map/ppermute | solution.py:573
  115.9 3.1 %collective-permute-start.26 = (f32[16,128]{1,0:T(8,128)S(1)}, f32[16,128]{1,0:T(8,128)S(1)}, u32[]{:S(2)}, u32[]{:S(2)}) collective-permute-start(f32[16,128]{1,0:T(8,128)S(1)} %get-tuple-element.163), channel_id=1, source_target_pairs={{0,12},{4,0},{8,4},{12,8},{1,13},{5,1},{9,5},{13,9},{2,14},{6,2},{... | collective-permute-start | bytes 24584 | tf_op jit(solution)/shard_map/ppermute | solution.py:573

commit v2 on v1

v2 whole, which is shorter than its diff:
```python
import jax
import jax.numpy as jnp
import ml_dtypes
import numpy as np
from jax import lax
from jax.experimental import pallas as pl
from jax.experimental.pallas import tpu as pltpu
from jax.sharding import PartitionSpec as P

NP = 8
RSWEEPS = 2
ITERS = 6
AXES = ("gx", "gy", "gz")

GLL_POINTS = (
    -1.0,
    -0.8717401485096066,
    -0.5917001814331423,
    -0.2092992179024789,
    0.2092992179024789,
    0.5917001814331423,
    0.8717401485096066,
    1.0,
)
GLL_WEIGHTS = (
    0.03571428571428571,
    0.21070422714350603,
    0.3411226924835044,
    0.4124587946587038,
    0.4124587946587038,
    0.3411226924835044,
    0.21070422714350603,
    0.03571428571428571,
)
HIGHEST = lax.Precision.HIGHEST
TIME_STEP = 0.02
PSEUDO_STEP = 0.004
INTERFACE_WIDTH = 0.5
GAS_DENSITY = 0.1
SOURCE_SCALE = 20.0
F32 = jnp.float32
BF16 = jnp.bfloat16


def node_tables():
    points = np.array(GLL_POINTS)
    amount = points.shape[0]
    barycentric = np.ones(amount)
    for target in range(amount):
        for partner in range(amount):
            if partner != target:
                barycentric[target] = barycentric[target] / (points[target] - points[partner])
    derivative = np.zeros((amount, amount))
    for target in range(amount):
        for partner in range(amount):
            if partner != target:
                derivative[target, partner] = (
                    barycentric[partner] / barycentric[target] / (points[target] - points[partner])
                )
        derivative[target, target] = -np.sum(derivative[target])
    return derivative


DERIV = node_tables()
TRANS = DERIV.T.copy()
SQUARE = (DERIV * DERIV).T.copy()
WEIGHTS = np.array(GLL_WEIGHTS)

BX, BY, BZ = 16, 16, 128
ROWS = BX * BY


def split_bf16(matrix):
    full = matrix.astype(np.float32)
    high = full.astype(ml_dtypes.bfloat16)
    low = (full - high.astype(np.float32)).astype(ml_dtypes.bfloat16)
    return high, low


def const_tables():
    parts = []
    for matrix in (DERIV, TRANS, SQUARE):
        for column in matrix.T:
            parts.append(np.repeat(column[:, None], BZ, axis=1))
    wy = np.tile(WEIGHTS, BY // NP)
    wz = np.tile(WEIGHTS, BZ // NP)
    parts.append(wy[:, None] * wz[None, :])
    parts.append(1.0 / (wy[:, None] * wz[None, :]))
    return np.concatenate(parts, axis=0).astype(np.float32)


def z_tables():
    out = []
    for matrix in (DERIV, TRANS, SQUARE):
        high, low = split_bf16(np.kron(np.eye(BZ // NP), matrix.T))
        top = np.concatenate([high, low], axis=1)
        out += [top, np.concatenate([high, np.zeros_like(low)], axis=1)]
    return np.concatenate(out, axis=0)


KIND = {"d": 0, "t": 1, "s": 2}
MATS = {"d": DERIV, "t": TRANS, "s": SQUARE}


def along_x(v, kind):
    matrix = MATS[kind]
    sign = 1.0 if abs(matrix[7, 7] - matrix[0, 0]) < abs(matrix[7, 7] + matrix[0, 0]) else -1.0
    out = [None] * BX
    for e in range(BX // NP):
        part = [v[(e * NP + i) * BY : (e * NP + i + 1) * BY] for i in range(NP)]
        even = [part[j] + part[7 - j] for j in range(4)]
        odd = [part[j] - part[7 - j] for j in range(4)]
        for i in range(4):
            a = b = None
            for j in range(4):
                ca = float(0.5 * (matrix[i, j] + matrix[i, 7 - j]))
                cb = float(0.5 * (matrix[i, j] - matrix[i, 7 - j]))
                a = ca * even[j] if a is None else a + ca * even[j]
                b = cb * odd[j] if b is None else b + cb * odd[j]
            out[e * NP + i] = a + b
            out[e * NP + 7 - i] = a - b if sign > 0 else b - a
    return jnp.concatenate(out, axis=0)


def along_y(v, kind, tab, work):
    work[...] = v
    base = KIND[kind] * NP * NP
    columns = [tab[base + s * NP : base + (s + 1) * NP, :] for s in range(NP)]
    out = []
    for q in range(ROWS // NP):
        total = None
        for s in range(NP):
            part = columns[s] * work[NP * q + s : NP * q + s + 1, :]
            total = part if total is None else total + part
        out.append(total)
    return jnp.concatenate(out, axis=0)


def along_z(v, kind, zt):
    base = KIND[kind] * 2 * BZ
    vh = v.astype(BF16)
    vl = (v - vh.astype(F32)).astype(BF16)
    both = jnp.dot(
        jnp.concatenate([vh, vl], axis=1), zt[base : base + 2 * BZ, :], preferred_element_type=F32
    )
    return both[:, :BZ] + both[:, BZ:]


def bmass_of(tab):
    base = 3 * NP * NP
    yz = tab[base : base + BY, :]
    return jnp.concatenate([yz * float(WEIGHTS[x % NP]) for x in range(BX)], axis=0)


def local_sum_xy(v):
    parts = [v[x * BY : (x + 1) * BY] for x in range(BX)]
    for x in range(NP, BX, NP):
        both = parts[x - 1] + parts[x]
        parts[x - 1] = both
        parts[x] = both
    sub = lax.broadcasted_iota(jnp.int32, (NP, BZ), 0)
    out = []
    for x in range(BX):
        a, b = parts[x][:NP], parts[x][NP:]
        out.append(jnp.where(sub == NP - 1, a + pltpu.roll(b, NP - 1, 0), a))
        out.append(jnp.where(sub == 0, b + pltpu.roll(a, 1, 0), b))
    return jnp.concatenate(out, axis=0)


def local_sum_z(v):
    lane = lax.broadcasted_iota(jnp.int32, (NP, BZ), 1)
    last = (lane % NP == NP - 1) & (lane < BZ - 1)
    first = (lane % NP == 0) & (lane > 0)
    v3 = v.reshape(ROWS // NP, NP, BZ)
    up = pltpu.roll(v3, BZ - 1, 2)
    down = pltpu.roll(v3, 1, 2)
    v3 = v3 + jnp.where(last[None], up, jnp.where(first[None], down, 0.0))
    return v3.reshape(ROWS, BZ)


class Geometry:
    def __init__(self, sizes):
        self.sizes = sizes
        self.at = [lax.axis_index(a) for a in AXES]
        self.low = [g > 0 for g in self.at]
        self.high = [g < n - 1 for g, n in zip(self.at, sizes)]
        self.me = (self.at[0] * sizes[1] + self.at[1]) * sizes[2] + self.at[2]

    def neighbour(self, *step):
        ok = None
        number = self.me
        strides = (self.sizes[1] * self.sizes[2], self.sizes[2], 1)
        for a in range(3):
            if step[a]:
                there = self.high[a] if step[a] > 0 else self.low[a]
                ok = there if ok is None else jnp.logical_and(ok, there)
                number = number + step[a] * strides[a]
        return jnp.where(ok, number, self.me)

    def half(self, flag):
        return jnp.where(flag, 0.5, 1.0).astype(F32)

    def x_share(self, x):
        if x == 0:
            return self.half(self.low[0])
        if x == BX - 1:
            return self.half(self.high[0])
        return None

    def y_share(self):
        row = lax.broadcasted_iota(jnp.int32, (BY, BZ), 0)
        one = jnp.where(row == 0, self.half(self.low[1]), 1.0)
        return jnp.where(row == BY - 1, self.half(self.high[1]), one)

    def z_share(self, shape, dim):
        lane = lax.broadcasted_iota(jnp.int32, shape, dim)
        one = jnp.where(lane == 0, self.half(self.low[2]), 1.0)
        return jnp.where(lane == BZ - 1, self.half(self.high[2]), one)

    def yz_weight(self):
        row = lax.broadcasted_iota(jnp.int32, (BY, BZ), 0)
        lane = lax.broadcasted_iota(jnp.int32, (BY, BZ), 1)
        inside_y = ((row % NP == 0) & (row > 0)) | ((row % NP == NP - 1) & (row < BY - 1))
        inside_z = ((lane % NP == 0) & (lane > 0)) | ((lane % NP == NP - 1) & (lane < BZ - 1))
        wy = jnp.where(inside_y, 0.5, self.y_share())
        wz = jnp.where(inside_z, 0.5, self.z_share((BY, BZ), 1))
        return wy * wz

    def x_weight(self, x):
        if x in (0, BX - 1):
            return self.x_share(x)
        return 0.5 if x % NP in (0, NP - 1) else 1.0


def inverse_mass(geo, tab):
    base = 3 * NP * NP + BY
    yz = tab[base : base + BY, :] * geo.yz_weight()
    return jnp.concatenate(
        [yz * (geo.x_weight(x) * float(1.0 / WEIGHTS[x % NP])) for x in range(BX)], axis=0
    )


def face_steps(n):
    return ("swap",) if n == 2 else ("up", "down")


class Layout:
    def __init__(self, sizes):
        self.sizes = sizes
        self.devices = sizes[0] * sizes[1] * sizes[2]
        self.plain = self.devices
        self.offset = self.devices + 8
        self.lanes = -(-(self.offset + self.devices) // 128) * 128
        self.scalar_rows = self.lanes // 128

    def slot_rows(self, fields):
        need = self.scalar_rows + 2 * fields
        if fields == 2:
            need += self.scalar_rows
        return 4 if need <= 4 else -(-need // 8) * 8


def pick_faces(geo, axis, n, low, high):
    if n == 2:
        return [jnp.where(geo.at[axis] == 0, high, low)]
    return [high, low]


def tile_iota():
    return lax.broadcasted_iota(jnp.int32, (8, BZ), 0), lax.broadcasted_iota(jnp.int32, (8, BZ), 1)


def pack_z_faces(v, work):
    sub, lane = tile_iota()
    tile = None
    for q in range(ROWS // 8):
        part = pltpu.roll(v[8 * q : 8 * q + 8], (2 * q + 1) % BZ, 1)
        if tile is None:
            tile = part
        else:
            tile = jnp.where(lane >= 2 * q, part, tile)
    turns = (-1, 0, 1, 63, 64, 65)
    for i, a in enumerate(turns):
        work[8 * i : 8 * i + 8, :] = tile if a == 0 else pltpu.roll(tile, a % BZ, 1)
    line = lane[0:1]
    out = []
    for side in (1, 0):
        pair = []
        for r in range(2):
            total = None
            for g in range(4):
                e, h = g % 2, g // 2
                at = 8 * turns.index(e - side + 64 * h) + 4 * r + g
                part = work[at : at + 1, :]
                keep = (line % 2 == e) & (line // 64 == h)
                total = part if total is None else jnp.where(keep, part, total)
            pair.append(total)
        out.append(pair)
    return out


def unpack_z_faces(sides):
    sub, lane = tile_iota()
    low, high = [
        jnp.where(sub < 4, jnp.broadcast_to(s[0], (8, BZ)), jnp.broadcast_to(s[1], (8, BZ)))
        for s in sides
    ]
    tile = None
    for g in range(4):
        shift = g % 2 + 64 * (g // 2)
        a = high if shift == 0 else pltpu.roll(high, -shift % BZ, 1)
        b = low if shift == 1 else pltpu.roll(low, (1 - shift) % BZ, 1)
        part = jnp.where(lane % 2 == 0, a, b)
        tile = part if tile is None else jnp.where(sub % 4 == g, part, tile)
    return tile


def send_fields(geo, lay, f_refs, zs, work, scalars, send_ref, xs, ys, fields, extra=None):
    rows = lay.slot_rows(fields)
    base = [scalars[:, i * 128 : (i + 1) * 128] for i in range(lay.scalar_rows)]
    used = lay.scalar_rows
    if extra is not None:
        base.append(jnp.zeros((2 * fields, 128), F32))
        base += [extra[:, i * 128 : (i + 1) * 128] for i in range(lay.scalar_rows)]
        used += 2 * fields + lay.scalar_rows
    base.append(jnp.zeros((rows - used, 128), F32))
    base = jnp.concatenate([b for b in base if b.shape[0]], axis=0)
    send_ref[...] = jnp.broadcast_to(base[None], (lay.devices, rows, 128))
    for k, f_ref in enumerate(f_refs):
        at = lay.scalar_rows + 2 * k
        pairs = pack_z_faces(zs[k], work)
        for dz in (-1, 1):
            pair = pairs[0 if dz < 0 else 1]
            for dx in (-1, 0, 1):
                for dy in (-1, 0, 1):
                    there = geo.neighbour(dx, dy, dz)
                    send_ref[there, at : at + 1, :] = pair[0]
                    send_ref[there, at + 1 : at + 2, :] = pair[1]
        for dx in (-1, 1):
            for dy in (-1, 1):
                row = (BX - 1 if dx > 0 else 0) * BY + (BY - 1 if dy > 0 else 0)
                send_ref[geo.neighbour(dx, dy, 0), at : at + 1, :] = f_ref[row : row + 1, :]
        lowx, highx = f_ref[0:BY, :], f_ref[ROWS - BY : ROWS, :]
        for ref, face in zip(xs, pick_faces(geo, 0, lay.sizes[0], lowx, highx)):
            ref[k * BY : (k + 1) * BY, :] = face
        lowy = f_ref[pl.ds(0, BX, stride=BY), :]
        highy = f_ref[pl.ds(BY - 1, BX, stride=BY), :]
        for ref, face in zip(ys, pick_faces(geo, 1, lay.sizes[1], lowy, highy)):
            ref[k * BX : (k + 1) * BX, :] = face
    send_ref[geo.me] = base


def came_from(geo, axis, n, refs, k, size):
    if n == 2:
        face = refs[0][k * size : (k + 1) * size, :]
        return (
            jnp.where(geo.low[axis], face, 0.0),
            jnp.where(geo.high[axis], face, 0.0),
        )
    up = refs[0][k * size : (k + 1) * size, :]
    down = refs[1][k * size : (k + 1) * size, :]
    return jnp.where(geo.low[axis], up, 0.0), jnp.where(geo.high[axis], down, 0.0)


def received(geo, lay, f, recv_ref, xs, ys, w_ref, k):
    at = lay.scalar_rows + 2 * k
    line = lax.broadcasted_iota(jnp.int32, (1, BZ), 1)
    sides = []
    for dz in (-1, 1):
        pair = []
        for r in range(2):
            total = None
            for dy in (0, 1 if r else -1):
                for dx in (0, -1, 1):
                    source = 1 - r if dy else r
                    part = recv_ref[geo.neighbour(dx, dy, dz), at + source : at + source + 1, :]
                    keep = None
                    if dx:
                        keep = line % 64 >= 60 if dx > 0 else line % 64 < 4
                    if dy > 0:
                        want = (line >= 64) & (line % 4 == 3)
                        keep = want if keep is None else keep & want
                    if dy < 0:
                        want = (line < 64) & (line % 4 == 0)
                        keep = want if keep is None else keep & want
                    if keep is not None:
                        part = jnp.where(keep, pltpu.roll(part, (60 * dx + 67 * dy) % BZ, 1), 0.0)
                    total = part if total is None else total + part
            pair.append(total)
        sides.append(pair)
    tile = unpack_z_faces(sides)
    _, lane = tile_iota()
    ends = (lane == 0) | (lane == BZ - 1)
    parts = []
    for q in range(ROWS // 8):
        part = pltpu.roll(tile, (BZ - 1 - 2 * q) % BZ, 1)
        parts.append(f[8 * q : 8 * q + 8] + jnp.where(ends, part, 0.0))
    w_ref[...] = jnp.concatenate(parts, axis=0)
    lowx, highx = came_from(geo, 0, lay.sizes[0], xs, k, BY)
    w_ref[0:BY, :] += lowx
    w_ref[ROWS - BY : ROWS, :] += highx
    lowy, highy = came_from(geo, 1, lay.sizes[1], ys, k, BX)
    w_ref[pl.ds(0, BX, stride=BY), :] += lowy
    w_ref[pl.ds(BY - 1, BX, stride=BY), :] += highy
    for dx in (-1, 1):
        for dy in (-1, 1):
            row = (BX - 1 if dx > 0 else 0) * BY + (BY - 1 if dy > 0 else 0)
            w_ref[row : row + 1, :] += recv_ref[geo.neighbour(dx, dy, 0), at : at + 1, :]


def received_scalars(lay, recv_ref):
    total = jnp.sum(recv_ref[...], axis=0)
    return jnp.concatenate([total[i : i + 1] for i in range(lay.scalar_rows)], axis=1)


def coarse_tables(geo, lay, places):
    out = []
    for half in range(2):
        size = 32 if half else 16
        row = lax.broadcasted_iota(jnp.int32, (size, lay.lanes), 0)
        steps = [
            jnp.broadcast_to(places[3 * half + a : 3 * half + a + 1, :], row.shape)
            - geo.at[a].astype(F32)
            for a in range(3)
        ]
        if half:
            row_dx = jnp.where(row < 24, row // 8 - 1, (row - 24) // 2 - 1)
            row_dy = jnp.where(row < 24, 0, row % 2 * 2 - 1)
            row_dx = jnp.where(row < 30, row_dx, 1000)
        else:
            row_dx, row_dy = row // 3 - 1, row % 3 - 1
            row_dx = jnp.where(row < 9, row_dx, 1000)
        near = (steps[0] == row_dx.astype(F32)) & (steps[1] == row_dy.astype(F32))
        for dz in (-1.0, 0.0, 1.0):
            out.append(jnp.where(near & (steps[2] == dz), 1.0, 0.0))
    row = lax.broadcasted_iota(jnp.int32, (24, lay.lanes), 0)
    lane = lax.broadcasted_iota(jnp.int32, (24, lay.lanes), 1)
    out.append(jnp.where(lane == lay.plain + row // 8, 1.0, 0.0))
    return jnp.concatenate(out, axis=0)


HOT_ROWS = 48 + 96 + 24


def partial_sums(geo, v, sums, q_ref, hot_ref):
    first, last = v[0:BY], v[ROWS - BY : ROWS]
    middle = first * geo.x_share(0) + last * geo.x_share(BX - 1)
    for x in range(1, BX - 1):
        middle = middle + v[x * BY : (x + 1) * BY]
    share = geo.y_share()
    for i, part in enumerate((0.5 * first, middle, 0.5 * last)):
        shared = part * share
        q_ref[8 * i : 8 * i + 8, :] = shared[0:8] + shared[8:16]
        q_ref[24 + 2 * i : 25 + 2 * i, :] = 0.5 * part[0:1]
        q_ref[25 + 2 * i : 26 + 2 * i, :] = 0.5 * part[BY - 1 : BY]
    q_ref[30:32, :] = jnp.zeros((2, BZ), F32)
    q = q_ref[...]
    own = jnp.sum(q * geo.z_share(q.shape, 1), axis=1, keepdims=True)
    below, above = 0.5 * q[:, 0:1], 0.5 * q[:, BZ - 1 : BZ]
    rows = hot_ref[48:80, :] * below + hot_ref[80:112, :] * own + hot_ref[112:144, :] * above
    rows = rows[0:8] + rows[8:16] + rows[16:24] + rows[24:32]
    for i, total in enumerate(sums):
        at = 144 + 8 * i
        rows = rows + hot_ref[at : at + 8, :] * jnp.sum(total, axis=1, keepdims=True)
    return jnp.sum(rows, axis=0, keepdims=True)


def spread(geo, values, hot_ref):
    below, own, above = [
        jnp.sum(hot_ref[16 * i : 16 * i + 16, :] * values, axis=1, keepdims=True) for i in range(3)
    ]
    lane = lax.broadcasted_iota(jnp.int32, (16, BZ), 1)
    rows = own * geo.z_share((16, BZ), 1)
    rows = rows + jnp.where(lane == 0, 0.5 * below, 0.0)
    rows = rows + jnp.where(lane == BZ - 1, 0.5 * above, 0.0)
    y = lax.broadcasted_iota(jnp.int32, (BY, BZ), 0)
    share = geo.y_share()
    planes = []
    for i in range(3):
        plane = share * rows[3 * i + 1 : 3 * i + 2]
        plane = plane + jnp.where(y == 0, 0.5 * rows[3 * i : 3 * i + 1], 0.0)
        planes.append(plane + jnp.where(y == BY - 1, 0.5 * rows[3 * i + 2 : 3 * i + 3], 0.0))
    out = [planes[1]] * BX
    out[0] = planes[1] * geo.x_share(0) + 0.5 * planes[0]
    out[BX - 1] = planes[1] * geo.x_share(BX - 1) + 0.5 * planes[2]
    return out


def with_coarse(lay, row, gram_ref):
    return row + jnp.dot(row, gram_ref[...], precision=HIGHEST, preferred_element_type=F32)


def coarse_inner(lay, row):
    lane = lax.broadcasted_iota(jnp.int32, row.shape, 1)
    both = row * pltpu.roll(row, lay.offset, 1)
    return jnp.sum(jnp.where(lane >= lay.offset, both, 0.0), axis=1, keepdims=True)


def all_rows(v):
    total = v[0:8]
    for i in range(1, ROWS // 8):
        total = total + v[8 * i : 8 * i + 8]
    return total


def weighted_rows(geo, v):
    yz = geo.yz_weight()
    total = None
    for x in range(BX):
        weight = geo.x_weight(x)
        part = v[x * BY : (x + 1) * BY]
        if not (isinstance(weight, float) and weight == 1.0):
            part = part * weight
        total = part if total is None else total + part
    total = total * yz
    return total[0:8] + total[8:16]


def weak_form(level, tab, zt, work):
    gx, gy, gz = along_x(level, "d"), along_y(level, "d", tab, work.at[0]), along_z(level, "d", zt)
    inv_norm = lax.rsqrt(1.0 + gx * gx + gy * gy + gz * gz)
    coef = bmass_of(tab) * (level * (1.0 - level) * inv_norm - INTERFACE_WIDTH)
    out = along_x(coef * gx, "t") + along_y(coef * gy, "t", tab, work.at[1])
    return out + along_z(coef * gz, "t", zt)


def stiffness(v, scaled, tab, zt, work):
    out = bmass_of(tab) * v
    out = out + along_x(scaled * along_x(v, "d"), "t")
    out = out + along_y(scaled * along_y(v, "d", tab, work.at[0]), "t", tab, work.at[1])
    return out + along_z(scaled * along_z(v, "d", zt), "t", zt)


def local_step(geo, lay, residual, dinv, scaled, state, p_old, refs):
    tab, zt, hot, u_ref, f_ref, send_ref, xs, ys, q_ref, state_ref, work, zwork, final = refs
    s_row, ts_row, gamma, curvature = state
    jacobi = residual * dinv
    planes = spread(geo, s_row, hot)
    u = jnp.concatenate([jacobi[x * BY : (x + 1) * BY] + planes[x] for x in range(BX)], axis=0)
    u_ref[...] = u
    local = stiffness(u, scaled, tab, zt, work)
    sums = [weighted_rows(geo, residual * jacobi), all_rows(u * local)]
    if p_old is not None:
        sums.append(all_rows(p_old * local))
    scalars = partial_sums(geo, local, sums, q_ref, hot)
    ones = jnp.ones_like(s_row)
    coarse = coarse_inner(lay, s_row)
    state_ref[...] = jnp.concatenate(
        [s_row, ts_row, ones * gamma, ones * curvature, ones * coarse, jnp.zeros((3, lay.lanes), F32)],
        axis=0,
    )
    if final:
        rows = [scalars[:, i * 128 : (i + 1) * 128] for i in range(lay.scalar_rows)]
        rows = jnp.concatenate(rows, axis=0)
        send_ref[...] = jnp.broadcast_to(rows[None], send_ref.shape)
        return
    local = local_sum_xy(local)
    f_ref[...] = local_sum_z(local)
    send_fields(geo, lay, [f_ref], [local], zwork, scalars, send_ref, xs, ys, 1)


def step_sizes(lay, recv_ref, state_ref, first):
    row = received_scalars(lay, recv_ref)
    lane = lax.broadcasted_iota(jnp.int32, row.shape, 1)

    def pick(which):
        return jnp.sum(jnp.where(lane == lay.plain + which, row, 0.0), axis=1, keepdims=True)

    gamma = pick(0) + state_ref[4:5, 0:1]
    if first:
        curvature = pick(1)
        beta = None
    else:
        beta = gamma / state_ref[2:3, 0:1]
        curvature = pick(1) + beta * (2.0 * pick(2) + beta * state_ref[3:4, 0:1])
    return row, gamma, curvature, beta, gamma / curvature


def build(mesh):
    sizes = tuple(int(mesh.shape[a]) for a in AXES)
    lay = Layout(sizes)
    steps = [face_steps(sizes[0]), face_steps(sizes[1])]
    nx, ny = len(steps[0]), len(steps[1])
    tab_np, zt_np = const_tables(), z_tables()
    number = np.arange(lay.lanes)
    places_np = np.full((8, lay.lanes), -9.0, np.float32)
    for half in range(2):
        lanes = slice(half * lay.offset, half * lay.offset + lay.devices)
        for a, place in enumerate(np.unravel_index(np.arange(lay.devices), sizes)):
            places_np[3 * half + a, lanes] = place
    block = jax.ShapeDtypeStruct((ROWS, BZ), F32)

    def like(*shape):
        return jax.ShapeDtypeStruct(shape, F32)

    def outgoing(fields):
        return (
            [like(lay.devices, lay.slot_rows(fields), 128)]
            + [like(BY * fields, BZ)] * nx
            + [like(BX * fields, BZ)] * ny
        )

    def call(kernel, ins, outs, scratch, name, space=pltpu.VMEM, limit=48):
        spec = pl.BlockSpec(memory_space=pltpu.VMEM)
        if space == pltpu.HBM:
            ins = [pltpu.with_memory_space_constraint(v, pltpu.HBM) for v in ins]
        return pl.pallas_call(
            kernel,
            out_shape=outs,
            in_specs=[pl.BlockSpec(memory_space=space)] * len(ins),
            out_specs=[spec] * len(outs),
            scratch_shapes=scratch,
            compiler_params=pltpu.CompilerParams(vmem_limit_bytes=limit * 1024 * 1024),
            name=name,
        )(*ins)

    work = pltpu.VMEM((ROWS, BZ), F32)
    qrows = pltpu.VMEM((32, BZ), F32)
    pair = pltpu.VMEM((2, ROWS, BZ), F32)
    tiles = pltpu.VMEM((48, BZ), F32)

    def ring(v, axis, n, step):
        if step == "swap":
            pairs = [(0, 1), (1, 0)]
        else:
            d = 1 if step == "up" else n - 1
            pairs = [(i, (i + d) % n) for i in range(n)]
        return lax.ppermute(v, axis, pairs)

    def exchange(out):
        send, faces = out[0], out[1:]
        recv = lax.all_to_all(send, AXES, 0, 0, tiled=True)
        xs = [ring(faces[i], "gx", sizes[0], s) for i, s in enumerate(steps[0])]
        ys = [ring(faces[nx + i], "gy", sizes[1], s) for i, s in enumerate(steps[1])]
        return [recv, *xs, *ys]

    n_out = 1 + nx + ny

    def split(refs):
        return refs[0], refs[1 : 1 + nx], refs[1 + nx : 1 + nx + ny]

    def start_kernel(level_any, vel_any, source_any, factor_any, tab_any, zt_any, places_any, *rest):
        send, xs, ys = split(rest[:n_out])
        fa_ref, fd_ref, hot_ref, q_ref, work, zwork = rest[n_out : n_out + 6]
        buffers, sems = rest[n_out + 6 : -1], rest[-1]
        sources = (level_any, zt_any, tab_any, vel_any, source_any, places_any, factor_any)
        copies = [
            pltpu.make_async_copy(source, target, sems.at[i])
            for i, (source, target) in enumerate(zip(sources, buffers))
        ]
        for copy in copies:
            copy.start()
        for copy in copies:
            copy.wait()
        level_ref, zt_ref, tab_ref, vel_ref, source_ref, places_ref, factor_ref = buffers
        geo = Geometry(sizes)
        level = level_ref[...]
        bm = bmass_of(tab_ref)
        advect = vel_ref[0] * along_x(level, "d")
        advect = advect + vel_ref[1] * along_y(level, "d", tab_ref, work.at[0])
        advect = advect + vel_ref[2] * along_z(level, "d", zt_ref)
        advect = local_sum_xy(bm * advect)
        fa_ref[...] = local_sum_z(advect)
        div = bm * source_ref[...] + along_x(bm * vel_ref[0], "t")
        div = div + along_y(bm * vel_ref[1], "t", tab_ref, work.at[1])
        div = div + along_z(bm * vel_ref[2], "t", zt_ref)
        hot_ref[...] = coarse_tables(geo, lay, places_ref)
        scalars = partial_sums(geo, div, [], q_ref, hot_ref)
        div = local_sum_xy(div)
        fd_ref[...] = local_sum_z(div)
        factor = factor_ref[...]
        if lay.lanes > lay.devices:
            pad = jnp.zeros((1, lay.lanes - lay.devices), F32)
            factor = jnp.concatenate([factor, pad], axis=1)
        send_fields(
            geo, lay, [fa_ref, fd_ref], [advect, div], zwork, scalars, send, xs, ys, 2, factor
        )

    def finish(geo, v, f_ref, zwork, send, xs, ys):
        v = local_sum_xy(v)
        f_ref[...] = local_sum_z(v)
        nothing = jnp.zeros((1, lay.lanes), F32)
        send_fields(geo, lay, [f_ref], [v], zwork, nothing, send, xs, ys, 1)

    def first_kernel(recv, *rest):
        xs, ys = rest[:nx], rest[nx : nx + ny]
        level_ref, fa_ref, fd_ref, tab_ref, zt_ref, hot_ref = rest[nx + ny : nx + ny + 6]
        out = rest[nx + ny + 6 :]
        send, oxs, oys = split(out[:n_out])
        level_out, f_ref, r_ref, s_ref, hot_out, w_ref, work, zwork, gram_ref = out[n_out:]
        geo = Geometry(sizes)
        at = lay.scalar_rows + 4
        factor = [recv[:, at + i, :] for i in range(lay.scalar_rows)]
        factor = jnp.concatenate(factor, axis=1)
        after = lay.lanes - lay.offset - lay.devices
        shifted = [jnp.zeros((lay.offset, lay.lanes), F32), factor]
        if after:
            shifted.append(jnp.zeros((after, lay.lanes), F32))
        plain = [factor, jnp.zeros((lay.lanes - lay.devices, lay.lanes), F32)]
        gram_ref[...] = lax.dot_general(
            jnp.concatenate(shifted, axis=0),
            jnp.concatenate(plain, axis=0),
            (((1,), (1,)), ((), ())),
            precision=HIGHEST,
            preferred_element_type=F32,
        )
        received(geo, lay, fd_ref[...], recv, xs, ys, w_ref, 1)
        r_ref[...] = SOURCE_SCALE * w_ref[...]
        row = received_scalars(lay, recv)
        row = with_coarse(lay, SOURCE_SCALE * row, gram_ref)
        s_ref[...] = jnp.broadcast_to(row, s_ref.shape)
        hot_out[...] = hot_ref[...]
        hot_out[48:144, :] = with_coarse(lay, hot_ref[48:144, :], gram_ref)
        received(geo, lay, fa_ref[...], recv, xs, ys, w_ref, 0)
        level = level_ref[...] - TIME_STEP * w_ref[...] * inverse_mass(geo, tab_ref)
        level_out[...] = level
        finish(geo, weak_form(level, tab_ref, zt_ref, work), f_ref, zwork, send, oxs, oys)

    def new_level(geo, recv, xs, ys, level_ref, f_ref, tab_ref, w_ref):
        received(geo, lay, f_ref[...], recv, xs, ys, w_ref, 0)
        return level_ref[...] + PSEUDO_STEP * w_ref[...] * inverse_mass(geo, tab_ref)

    def sweep_kernel(recv, *rest):
        xs, ys = rest[:nx], rest[nx : nx + ny]
        level_ref, fin_ref, tab_ref, zt_ref = rest[nx + ny : nx + ny + 4]
        out = rest[nx + ny + 4 :]
        send, oxs, oys = split(out[:n_out])
        level_out, f_ref, w_ref, work, zwork = out[n_out:]
        geo = Geometry(sizes)
        level = new_level(geo, recv, xs, ys, level_ref, fin_ref, tab_ref, w_ref)
        level_out[...] = level
        finish(geo, weak_form(level, tab_ref, zt_ref, work), f_ref, zwork, send, oxs, oys)

    def diagonal_kernel(recv, *rest):
        xs, ys = rest[:nx], rest[nx : nx + ny]
        level_ref, fin_ref, tab_ref, zt_ref = rest[nx + ny : nx + ny + 4]
        out = rest[nx + ny + 4 :]
        send, oxs, oys = split(out[:n_out])
        level_out, f_ref, scaled_ref, w_ref, work, zwork = out[n_out:]
        geo = Geometry(sizes)
        level = new_level(geo, recv, xs, ys, level_ref, fin_ref, tab_ref, w_ref)
        level_out[...] = level
        bm = bmass_of(tab_ref)
        scaled = bm / (GAS_DENSITY + (1.0 - GAS_DENSITY) * jnp.clip(level, 0.0, 1.0))
        scaled_ref[...] = scaled
        diag = bm + along_x(scaled, "s") + along_y(scaled, "s", tab_ref, work.at[0])
        diag = diag + along_z(scaled, "s", zt_ref)
        finish(geo, diag, f_ref, zwork, send, oxs, oys)

    def solve_kernel(recv, *rest):
        xs, ys = rest[:nx], rest[nx : nx + ny]
        fin_ref, r_ref, scaled_ref, s_ref, tab_ref, zt_ref, hot_ref = rest[nx + ny : nx + ny + 7]
        out = rest[nx + ny + 7 :]
        send, oxs, oys = split(out[:n_out])
        dinv_ref, u_ref, f_ref, state_ref, w_ref, work, zwork, q_ref = out[n_out:]
        geo = Geometry(sizes)
        received(geo, lay, fin_ref[...], recv, xs, ys, w_ref, 0)
        dinv = 1.0 / w_ref[...]
        dinv_ref[...] = dinv
        zero = jnp.zeros((1, 1), F32)
        s_row = s_ref[0:1, :]
        state = (s_row, jnp.zeros_like(s_row), zero, zero)
        refs = (tab_ref, zt_ref, hot_ref, u_ref, f_ref, send, oxs, oys)
        local_step(
            geo, lay, r_ref[...], dinv, scaled_ref[...], state, None, (*refs, q_ref, state_ref, work, zwork, False)
        )

    def make_iterate(first, final):
        def iterate_kernel(recv, *rest):
            xs, ys = rest[:nx], rest[nx : nx + ny]
            n_in = 9 + (0 if first else 3)
            ins = rest[nx + ny : nx + ny + n_in]
            fin_ref, r_ref, u_in, dinv_ref, scaled_ref, state_in = ins[:6]
            tab_ref, zt_ref, hot_ref = ins[6:9]
            p_in, si_in, x_in = (None, None, None) if first else ins[9:12]
            out = rest[nx + ny + n_in :]
            if final:
                send, oxs, oys = out[0], (), ()
                out = out[1:]
                u_ref, state_ref, p_ref, x_ref, w_ref, work, zwork, q_ref = out
                f_ref = r_out = si_ref = None
            else:
                send, oxs, oys = split(out[:n_out])
                u_ref, state_ref, p_ref, x_ref, r_out, si_ref, f_ref, w_ref, work, zwork, q_ref = out[
                    n_out:
                ]
            geo = Geometry(sizes)
            row, gamma, curvature, beta, alpha = step_sizes(lay, recv, state_in, first)
            received(geo, lay, fin_ref[...], recv, xs, ys, w_ref, 0)
            image = w_ref[...]
            p = u_in[...]
            s_row, ts_row = state_in[0:1, :], row
            if not first:
                p = p + beta * p_in[...]
                image = image + beta * si_in[...]
                ts_row = ts_row + beta * state_in[1:2, :]
            p_ref[...] = p
            x_ref[...] = alpha * p if first else x_in[...] + alpha * p
            residual = r_ref[...] - alpha * image
            if not final:
                si_ref[...] = image
                r_out[...] = residual
            lane = lax.broadcasted_iota(jnp.int32, row.shape, 1)
            ts_row = jnp.where((lane < lay.devices) | (lane >= lay.offset), ts_row, 0.0)
            state = (s_row - alpha * ts_row, ts_row, gamma, curvature)
            refs = (tab_ref, zt_ref, hot_ref, u_ref, f_ref, send)
            local_step(
                geo,
                lay,
                residual,
                dinv_ref[...],
                scaled_ref[...],
                state,
                p,
                (*refs, oxs, oys, q_ref, state_ref, work, zwork, final),
            )

        return iterate_kernel

    def last_kernel(recv, state_in, u_in, p_in, x_in, out_ref):
        _, _, _, beta, alpha = step_sizes(lay, recv, state_in, False)
        out_ref[...] = x_in[...] + alpha * (u_in[...] + beta * p_in[...])

    def body(level_set, velocity, source, coarse_factor):
        level = level_set.reshape(ROWS, BZ)
        vel = velocity.reshape(3, ROWS, BZ)
        src = source.reshape(ROWS, BZ)
        tab, zt, places = jnp.asarray(tab_np), jnp.asarray(zt_np), jnp.asarray(places_np)
        out = call(
            start_kernel,
            [level, vel, src, coarse_factor, tab, zt, places],
            outgoing(2) + [block, block, like(HOT_ROWS, lay.lanes)],
            [qrows, pair, tiles]
            + [pltpu.VMEM(a.shape, a.dtype) for a in (level, zt, tab, vel, src, places, coarse_factor)]
            + [pltpu.SemaphoreType.DMA((7,))],
            "advect",
            pltpu.HBM,
        )
        fa, fd, hot = out[n_out:]
        got = exchange(out[:n_out])
        out = call(
            first_kernel,
            [*got, level, fa, fd, tab, zt, hot],
            outgoing(1) + [block, block, block, like(8, lay.lanes), like(HOT_ROWS, lay.lanes)],
            [work, pair, tiles, pltpu.VMEM((lay.lanes, lay.lanes), F32)],
            "sweep_first",
        )
        level, f, residual, s_rows, hot = out[n_out:]
        for _ in range(RSWEEPS - 1):
            got = exchange(out[:n_out])
            out = call(
                sweep_kernel, [*got, level, f, tab, zt], outgoing(1) + [block, block], [work, pair, tiles], "sweep"
            )
            level, f = out[n_out:]
        got = exchange(out[:n_out])
        out = call(
            diagonal_kernel,
            [*got, level, f, tab, zt],
            outgoing(1) + [block, block, block],
            [work, pair, tiles],
            "diagonal",
        )
        level, f, scaled = out[n_out:]
        got = exchange(out[:n_out])
        out = call(
            solve_kernel,
            [*got, f, residual, scaled, s_rows, tab, zt, hot],
            outgoing(1) + [block, block, block, like(8, lay.lanes)],
            [work, pair, tiles, qrows],
            "solve_start",
        )
        dinv, u, f, state = out[n_out:]
        p = image = x = None
        for step in range(ITERS - 1):
            first, final = step == 0, step == ITERS - 2
            got = exchange(out[:n_out])
            ins = [*got, f, residual, u, dinv, scaled, state, tab, zt, hot]
            if not first:
                ins += [p, image, x]
            fields = [block, like(8, lay.lanes), block, block]
            if final:
                outs = [like(lay.devices, lay.scalar_rows, 128)] + fields
            else:
                outs = outgoing(1) + fields + [block, block, block]
            out = call(make_iterate(first, final), ins, outs, [work, pair, tiles, qrows], "iterate")
            if final:
                u, state, p, x = out[1:]
            else:
                u, state, p, x, residual, image, f = out[n_out:]
        recv = lax.all_to_all(out[0], AXES, 0, 0, tiled=True)
        (x,) = call(last_kernel, [recv, state, u, p, x], [block], [], "pressure")
        return level.reshape(BX, BY, BZ), x.reshape(BX, BY, BZ)

    return body


def solution(mesh):
    in_specs = (
        P("gx", "gy", "gz"),
        P(None, "gx", "gy", "gz"),
        P("gx", "gy", "gz"),
        P(("gx", "gy", "gz"), None),
    )
    out_specs = (P("gx", "gy", "gz"), P("gx", "gy", "gz"))
    return jax.shard_map(
        build(mesh), mesh=mesh, in_specs=in_specs, out_specs=out_specs, check_vma=False
    )
```

time: 134 us -> 123 us (0.918)
  Pallas kernels: 21.7 us -> 16.4 us
  local copies, waits for them, and re-layouts: 5.32 us -> 0.02 us
    pallas_call x11, Pallas kernels: 21.7 us -> 16.4 us  [call(): pl.pallas_call(kernel, out_shape=outs, in_specs=[pl.BlockSpec(memory_spac...]
    unnamed x18 -> x6, local copies, waits for them, and re-layouts: 4.65 us -> 0.02 us
where the time goes in v2:
time: 123 us
  starting transfers between devices  59.2 us (48%)
  waiting for transfers between devices  37.1 us (30%)
  Pallas kernels  16.4 us (13%)
  blocking collectives  9.31 us (8%)
    ppermute x27, starting transfers between devices, ring(): return lax.ppermute(v, axis, pairs)  31.3 us
    all_to_all x9, starting transfers between devices, exchange(): recv = lax.all_to_all(send, AXES, 0, 0, tiled=True)  27.9 us
    all_to_all x9, waiting for transfers between devices, exchange(): recv = lax.all_to_all(send, AXES, 0, 0, tiled=True)  24.6 us
    pallas_call x11, Pallas kernels, call(): pl.pallas_call(kernel, out_shape=outs, in_specs=[pl.BlockSpec(memory_spac...  16.4 us
    ppermute x27, waiting for transfers between devices, ring(): return lax.ppermute(v, axis, pairs)  12.4 us
    all_to_all x1, blocking collectives, body(): recv = lax.all_to_all(out[0], AXES, 0, 0, tiled=True)  9.31 us
  transfers between devices with their start and end apart: 36, of which 27 were waited for; matrix products, arithmetic and copies ran while one was open for 0% of the time, Pallas kernels for 0%

profile of v2, /device:TPU:0, one launch (start us, length us, event | category | flops | bytes accessed | tf_op | source)
XLA Modules:
  0.0 122.7 jit_solution(17200794908544654911)
XLA Ops:
  0.6 2.7 %advect.1 = (f32[32,8,128]{2,1,0:T(8,128)}, f32[32,128]{1,0:T(8,128)S(1)}, f32[32,128]{1,0:T(8,128)S(1)}, f32[32,128]{1,0:T(8,128)S(1)}, f32[256,128]{1,0:T(8,12...) custom-call(f32[256,128]{1,0:T(8,128)} %bitcast.5, f32[3,256,128]{2,1,0:T(8,128)} %bitcast.7, f32[256,128]{1,0:T(8,128)} %bitcast.9, ...), custom_call_target="tpu_custom_call" | custom-call | tf_op jit(solution)/shard_map/advect/pallas_call | solution.py:607
  3.4 7.3 %all-to-all-start = ((f32[32,8,128]{2,1,0:T(8,128)}), f32[32,8,128]{2,1,0:T(8,128)S(1)}, u32[]{:S(2)}, u32[]{:S(2)}) async-start(f32[32,8,128]{2,1,0:T(8,128)} %get-tuple-element.88), calls=%async_computation | async-start | bytes 262144 | tf_op jit(solution)/shard_map/all_to_all | solution.py:632
  10.7 1.8 %collective-permute-start = (f32[32,128]{1,0:T(8,128)S(1)}, f32[32,128]{1,0:T(8,128)S(1)}, u32[]{:S(2)}, u32[]{:S(2)}) collective-permute-start(f32[32,128]{1,0:T(8,128)S(1)} %get-tuple-element.89), channel_id=1, source_target_pairs={{0,16},{16,0},{1,17},{17,1},{2,18},{18,2},{3,19},{19,3},{4,20},{20... | collective-permute-start | bytes 49160 | tf_op jit(solution)/shard_map/ppermute | solution.py:628
  12.5 1.7 %collective-permute-start.2 = (f32[32,128]{1,0:T(8,128)S(1)}, f32[32,128]{1,0:T(8,128)S(1)}, u32[]{:S(2)}, u32[]{:S(2)}) collective-permute-start(f32[32,128]{1,0:T(8,128)S(1)} %get-tuple-element.91), channel_id=1, source_target_pairs={{0,12},{4,0},{8,4},{12,8},{1,13},{5,1},{9,5},{13,9},{2,14},{6,2},{... | collective-permute-start | bytes 49160 | tf_op jit(solution)/shard_map/ppermute | solution.py:628
  14.5 1.3 %collective-permute-done.1.rest_1_ = f32[32,128]{1,0:T(8,128)S(1)} collective-permute-done((f32[32,128]{1,0:T(8,128)S(1)}, f32[32,128]{1,0:T(8,128)S(1)}, u32[]{:S(2)}, u32[]{:S(2)}) %collective-permute-start.1) | collective-permute-done | bytes 16416 | tf_op jit(solution)/shard_map/ppermute | solution.py:628
  15.8 3.3 %all-to-all-done.recv = f32[32,8,128]{2,1,0:T(8,128)S(1)} async-done(((f32[32,8,128]{2,1,0:T(8,128)}), f32[32,8,128]{2,1,0:T(8,128)S(1)}, u32[]{:S(2)}, u32[]{:S(2)}) %all-to-all-start) | async-done | bytes 131104 | tf_op jit(solution)/shard_map/all_to_all | solution.py:632
  19.1 1.6 %sweep_first.1 = (f32[32,4,128]{2,1,0:T(4,128)}, f32[16,128]{1,0:T(8,128)S(1)}, f32[16,128]{1,0:T(8,128)S(1)}, f32[16,128]{1,0:T(8,128)S(1)}, f32[256,128]{1,0:T...) custom-call(f32[32,8,128]{2,1,0:T(8,128)S(1)} %all-to-all-done.recv,, ...), custom_call_target="tpu_custom_call" | custom-call | tf_op jit(solution)/shard_map/sweep_first/pallas_call | solution.py:607
  20.7 2.6 %all-to-all-start.1 = ((f32[32,4,128]{2,1,0:T(4,128)}), f32[32,4,128]{2,1,0:T(4,128)S(1)}, u32[]{:S(2)}, u32[]{:S(2)}) async-start(f32[32,4,128]{2,1,0:T(4,128)} %get-tuple-element.95), calls=%async_computation.1 | async-start | bytes 131072 | tf_op jit(solution)/shard_map/all_to_all | solution.py:632
  23.3 1.7 %collective-permute-start.3 = (f32[16,128]{1,0:T(8,128)S(1)}, f32[16,128]{1,0:T(8,128)S(1)}, u32[]{:S(2)}, u32[]{:S(2)}) collective-permute-start(f32[16,128]{1,0:T(8,128)S(1)} %get-tuple-element.96), channel_id=1, source_target_pairs={{0,16},{16,0},{1,17},{17,1},{2,18},{18,2},{3,19},{19,3},{4,20},{20... | collective-permute-start | bytes 24584 | tf_op jit(solution)/shard_map/ppermute | solution.py:628
  25.0 1.7 %collective-permute-start.5 = (f32[16,128]{1,0:T(8,128)S(1)}, f32[16,128]{1,0:T(8,128)S(1)}, u32[]{:S(2)}, u32[]{:S(2)}) collective-permute-start(f32[16,128]{1,0:T(8,128)S(1)} %get-tuple-element.98), channel_id=1, source_target_pairs={{0,12},{4,0},{8,4},{12,8},{1,13},{5,1},{9,5},{13,9},{2,14},{6,2},{... | collective-permute-start | bytes 24584 | tf_op jit(solution)/shard_map/ppermute | solution.py:628
  26.7 0.3 collective-permute-done.3.rest_0_
  27.0 1.1 collective-permute-done.4.rest_1_
  28.1 2.7 %all-to-all-done.1.recv = f32[32,4,128]{2,1,0:T(4,128)S(1)} async-done(((f32[32,4,128]{2,1,0:T(4,128)}), f32[32,4,128]{2,1,0:T(4,128)S(1)}, u32[]{:S(2)}, u32[]{:S(2)}) %all-to-all-start.1) | async-done | bytes 65568 | tf_op jit(solution)/shard_map/all_to_all | solution.py:632
  30.7 1.5 %sweep.1 = (f32[32,4,128]{2,1,0:T(4,128)}, f32[16,128]{1,0:T(8,128)S(1)}, f32[16,128]{1,0:T(8,128)S(1)}, f32[16,128]{1,0:T(8,128)S(1)}, f32[256,128]{1,0:T(8,128)S(1)}, /*index=5*/f32[256,128]{1,0:T(8,128)S(1)}) custom-call(f32[32,4,128]{2,1,0:T(4,128)S(1)} %all-to-all-done.1.recv, f32[16,128]{1,0:T(8,128)S(1)} %collective-permute-done.3.rest_0_, ...), custom_call_target="tpu_custom_call" | custom-call | tf_op jit(solution)/shard_map/sweep/pallas_call | solution.py:607
  32.2 2.6 %all-to-all-start.2 = ((f32[32,4,128]{2,1,0:T(4,128)}), f32[32,4,128]{2,1,0:T(4,128)S(1)}, u32[]{:S(2)}, u32[]{:S(2)}) async-start(f32[32,4,128]{2,1,0:T(4,128)} %get-tuple-element.101), calls=%async_computation.2 | async-start | bytes 131072 | tf_op jit(solution)/shard_map/all_to_all | solution.py:632
  34.8 1.7 %collective-permute-start.6 = (f32[16,128]{1,0:T(8,128)S(1)}, f32[16,128]{1,0:T(8,128)S(1)}, u32[]{:S(2)}, u32[]{:S(2)}) collective-permute-start(f32[16,128]{1,0:T(8,128)S(1)} %get-tuple-element.102), channel_id=1, source_target_pairs={{0,16},{16,0},{1,17},{17,1},{2,18},{18,2},{3,19},{19,3},{4,20},{20... | collective-permute-start | bytes 24584 | tf_op jit(solution)/shard_map/ppermute | solution.py:628
  36.5 1.7 %collective-permute-start.8 = (f32[16,128]{1,0:T(8,128)S(1)}, f32[16,128]{1,0:T(8,128)S(1)}, u32[]{:S(2)}, u32[]{:S(2)}) collective-permute-start(f32[16,128]{1,0:T(8,128)S(1)} %get-tuple-element.104), channel_id=1, source_target_pairs={{0,12},{4,0},{8,4},{12,8},{1,13},{5,1},{9,5},{13,9},{2,14},{6,2},{... | collective-permute-start | bytes 24584 | tf_op jit(solution)/shard_map/ppermute | solution.py:628
  38.2 0.3 collective-permute-done.6.rest_0_
  38.5 1.1 collective-permute-done.7.rest_1_
  39.6 2.7 %all-to-all-done.2.recv = f32[32,4,128]{2,1,0:T(4,128)S(1)} async-done(((f32[32,4,128]{2,1,0:T(4,128)}), f32[32,4,128]{2,1,0:T(4,128)S(1)}, u32[]{:S(2)}, u32[]{:S(2)}) %all-to-all-start.2) | async-done | bytes 65568 | tf_op jit(solution)/shard_map/all_to_all | solution.py:632
  42.3 1.3 %diagonal.1 = (f32[32,4,128]{2,1,0:T(4,128)}, f32[16,128]{1,0:T(8,128)S(1)}, f32[16,128]{1,0:T(8,128)S(1)}, f32[16,128]{1,0:T(8,128)S(1)}, f32[256,128]{1,0:T(8,...) custom-call(f32[32,4,128]{2,1,0:T(4,128)S(1)} %all-to-all-done.2.recv, ...), custom_call_target="tpu_custom_call" | custom-call | tf_op jit(solution)/shard_map/diagonal/pallas_call | solution.py:607
  43.6 2.6 %all-to-all-start.3 = ((f32[32,4,128]{2,1,0:T(4,128)}), f32[32,4,128]{2,1,0:T(4,128)S(1)}, u32[]{:S(2)}, u32[]{:S(2)}) async-start(f32[32,4,128]{2,1,0:T(4,128)} %get-tuple-element.108), calls=%async_computation.3 | async-start | bytes 131072 | tf_op jit(solution)/shard_map/all_to_all | solution.py:632
  46.2 1.7 %collective-permute-start.9 = (f32[16,128]{1,0:T(8,128)S(1)}, f32[16,128]{1,0:T(8,128)S(1)}, u32[]{:S(2)}, u32[]{:S(2)}) collective-permute-start(f32[16,128]{1,0:T(8,128)S(1)} %get-tuple-element.109), channel_id=1, source_target_pairs={{0,16},{16,0},{1,17},{17,1},{2,18},{18,2},{3,19},{19,3},{4,20},{20... | collective-permute-start | bytes 24584 | tf_op jit(solution)/shard_map/ppermute | solution.py:628
  47.9 1.7 %collective-permute-start.11 = (f32[16,128]{1,0:T(8,128)S(1)}, f32[16,128]{1,0:T(8,128)S(1)}, u32[]{:S(2)}, u32[]{:S(2)}) collective-permute-start(f32[16,128]{1,0:T(8,128)S(1)} %get-tuple-element.111), channel_id=1, source_target_pairs={{0,12},{4,0},{8,4},{12,8},{1,13},{5,1},{9,5},{13,9},{2,14},{6,2},{... | collective-permute-start | bytes 24584 | tf_op jit(solution)/shard_map/ppermute | solution.py:628
  49.6 0.3 collective-permute-done.9.rest_0_
  49.9 1.1 collective-permute-done.10.rest_1_
  51.0 2.7 %all-to-all-done.3.recv = f32[32,4,128]{2,1,0:T(4,128)S(1)} async-done(((f32[32,4,128]{2,1,0:T(4,128)}), f32[32,4,128]{2,1,0:T(4,128)S(1)}, u32[]{:S(2)}, u32[]{:S(2)}) %all-to-all-start.3) | async-done | bytes 65568 | tf_op jit(solution)/shard_map/all_to_all | solution.py:632
  53.7 1.5 %solve_start.1 = (f32[32,4,128]{2,1,0:T(4,128)}, f32[16,128]{1,0:T(8,128)S(1)}, f32[16,128]{1,0:T(8,128)S(1)}, f32[16,128]{1,0:T(8,128)S(1)}, f32[256,128]{1,0:T...) custom-call(f32[32,4,128]{2,1,0:T(4,128)S(1)} %all-to-all-done.3.recv, ...), custom_call_target="tpu_custom_call" | custom-call | tf_op jit(solution)/shard_map/solve_start/pallas_call | solution.py:607
  55.2 2.6 %all-to-all-start.4 = ((f32[32,4,128]{2,1,0:T(4,128)}), f32[32,4,128]{2,1,0:T(4,128)S(1)}, u32[]{:S(2)}, u32[]{:S(2)}) async-start(f32[32,4,128]{2,1,0:T(4,128)} %get-tuple-element.117), calls=%async_computation.4 | async-start | bytes 131072 | tf_op jit(solution)/shard_map/all_to_all | solution.py:632
  57.7 1.7 %collective-permute-start.12 = (f32[16,128]{1,0:T(8,128)S(1)}, f32[16,128]{1,0:T(8,128)S(1)}, u32[]{:S(2)}, u32[]{:S(2)}) collective-permute-start(f32[16,128]{1,0:T(8,128)S(1)} %get-tuple-element.118), channel_id=1, source_target_pairs={{0,16},{16,0},{1,17},{17,1},{2,18},{18,2},{3,19},{19,3},{4,20},{20... | collective-permute-start | bytes 24584 | tf_op jit(solution)/shard_map/ppermute | solution.py:628
  59.5 1.7 %collective-permute-start.14 = (f32[16,128]{1,0:T(8,128)S(1)}, f32[16,128]{1,0:T(8,128)S(1)}, u32[]{:S(2)}, u32[]{:S(2)}) collective-permute-start(f32[16,128]{1,0:T(8,128)S(1)} %get-tuple-element.120), channel_id=1, source_target_pairs={{0,12},{4,0},{8,4},{12,8},{1,13},{5,1},{9,5},{13,9},{2,14},{6,2},{... | collective-permute-start | bytes 24584 | tf_op jit(solution)/shard_map/ppermute | solution.py:628
  61.2 0.3 collective-permute-done.12.rest_0_
  61.5 1.1 collective-permute-done.13.rest_1_
  62.6 2.7 %all-to-all-done.4.recv = f32[32,4,128]{2,1,0:T(4,128)S(1)} async-done(((f32[32,4,128]{2,1,0:T(4,128)}), f32[32,4,128]{2,1,0:T(4,128)S(1)}, u32[]{:S(2)}, u32[]{:S(2)}) %all-to-all-start.4) | async-done | bytes 65568 | tf_op jit(solution)/shard_map/all_to_all | solution.py:632
  65.2 1.5 %iterate.5 = (f32[32,4,128]{2,1,0:T(4,128)}, f32[16,128]{1,0:T(8,128)S(1)}, f32[16,128]{1,0:T(8,128)S(1)}, f32[16,128]{1,0:T(8,128)S(1)}, f32[256,128]{1,0:T(8,1...) custom-call(f32[32,4,128]{2,1,0:T(4,128)S(1)} %all-to-all-done.4.rec, ...), custom_call_target="tpu_custom_call" | custom-call | tf_op jit(solution)/shard_map/iterate/pallas_call | solution.py:607
  66.8 2.6 %all-to-all-start.5 = ((f32[32,4,128]{2,1,0:T(4,128)}), f32[32,4,128]{2,1,0:T(4,128)S(1)}, u32[]{:S(2)}, u32[]{:S(2)}) async-start(f32[32,4,128]{2,1,0:T(4,128)} %get-tuple-element.125), calls=%async_computation.5 | async-start | bytes 131072 | tf_op jit(solution)/shard_map/all_to_all | solution.py:632
  69.3 1.7 %collective-permute-start.15 = (f32[16,128]{1,0:T(8,128)S(1)}, f32[16,128]{1,0:T(8,128)S(1)}, u32[]{:S(2)}, u32[]{:S(2)}) collective-permute-start(f32[16,128]{1,0:T(8,128)S(1)} %get-tuple-element.126), channel_id=1, source_target_pairs={{0,16},{16,0},{1,17},{17,1},{2,18},{18,2},{3,19},{19,3},{4,20},{20... | collective-permute-start | bytes 24584 | tf_op jit(solution)/shard_map/ppermute | solution.py:628
  71.1 1.7 %collective-permute-start.17 = (f32[16,128]{1,0:T(8,128)S(1)}, f32[16,128]{1,0:T(8,128)S(1)}, u32[]{:S(2)}, u32[]{:S(2)}) collective-permute-start(f32[16,128]{1,0:T(8,128)S(1)} %get-tuple-element.128), channel_id=1, source_target_pairs={{0,12},{4,0},{8,4},{12,8},{1,13},{5,1},{9,5},{13,9},{2,14},{6,2},{... | collective-permute-start | bytes 24584 | tf_op jit(solution)/shard_map/ppermute | solution.py:628
  72.8 0.3 collective-permute-done.15.rest_0_
  73.1 1.1 collective-permute-done.16.rest_1_
  74.2 2.7 %all-to-all-done.5.recv = f32[32,4,128]{2,1,0:T(4,128)S(1)} async-done(((f32[32,4,128]{2,1,0:T(4,128)}), f32[32,4,128]{2,1,0:T(4,128)S(1)}, u32[]{:S(2)}, u32[]{:S(2)}) %all-to-all-start.5) | async-done | bytes 65568 | tf_op jit(solution)/shard_map/all_to_all | solution.py:632
  76.8 1.6 %iterate.6 = (f32[32,4,128]{2,1,0:T(4,128)}, f32[16,128]{1,0:T(8,128)S(1)}, f32[16,128]{1,0:T(8,128)S(1)}, f32[16,128]{1,0:T(8,128)S(1)}, f32[256,128]{1,0:T(8,1...) custom-call(f32[32,4,128]{2,1,0:T(4,128)S(1)} %all-to-all-done.5.rec, ...), custom_call_target="tpu_custom_call" | custom-call | tf_op jit(solution)/shard_map/iterate/pallas_call | solution.py:607
  78.4 2.6 %all-to-all-start.6 = ((f32[32,4,128]{2,1,0:T(4,128)}), f32[32,4,128]{2,1,0:T(4,128)S(1)}, u32[]{:S(2)}, u32[]{:S(2)}) async-start(f32[32,4,128]{2,1,0:T(4,128)} %get-tuple-element.136), calls=%async_computation.6 | async-start | bytes 131072 | tf_op jit(solution)/shard_map/all_to_all | solution.py:632
  81.0 1.7 %collective-permute-start.18 = (f32[16,128]{1,0:T(8,128)S(1)}, f32[16,128]{1,0:T(8,128)S(1)}, u32[]{:S(2)}, u32[]{:S(2)}) collective-permute-start(f32[16,128]{1,0:T(8,128)S(1)} %get-tuple-element.137), channel_id=1, source_target_pairs={{0,16},{16,0},{1,17},{17,1},{2,18},{18,2},{3,19},{19,3},{4,20},{20... | collective-permute-start | bytes 24584 | tf_op jit(solution)/shard_map/ppermute | solution.py:628
  82.7 1.7 %collective-permute-start.20 = (f32[16,128]{1,0:T(8,128)S(1)}, f32[16,128]{1,0:T(8,128)S(1)}, u32[]{:S(2)}, u32[]{:S(2)}) collective-permute-start(f32[16,128]{1,0:T(8,128)S(1)} %get-tuple-element.139), channel_id=1, source_target_pairs={{0,12},{4,0},{8,4},{12,8},{1,13},{5,1},{9,5},{13,9},{2,14},{6,2},{... | collective-permute-start | bytes 24584 | tf_op jit(solution)/shard_map/ppermute | solution.py:628
  84.4 0.3 collective-permute-done.18.rest_0_
  84.7 1.1 collective-permute-done.19.rest_1_
  85.8 2.7 %all-to-all-done.6.recv = f32[32,4,128]{2,1,0:T(4,128)S(1)} async-done(((f32[32,4,128]{2,1,0:T(4,128)}), f32[32,4,128]{2,1,0:T(4,128)S(1)}, u32[]{:S(2)}, u32[]{:S(2)}) %all-to-all-start.6) | async-done | bytes 65568 | tf_op jit(solution)/shard_map/all_to_all | solution.py:632
  88.5 1.6 %iterate.7 = (f32[32,4,128]{2,1,0:T(4,128)}, f32[16,128]{1,0:T(8,128)S(1)}, f32[16,128]{1,0:T(8,128)S(1)}, f32[16,128]{1,0:T(8,128)S(1)}, f32[256,128]{1,0:T(8,1...) custom-call(f32[32,4,128]{2,1,0:T(4,128)S(1)} %all-to-all-done.6.rec, ...), custom_call_target="tpu_custom_call" | custom-call | tf_op jit(solution)/shard_map/iterate/pallas_call | solution.py:607
  90.0 2.6 %all-to-all-start.7 = ((f32[32,4,128]{2,1,0:T(4,128)}), f32[32,4,128]{2,1,0:T(4,128)S(1)}, u32[]{:S(2)}, u32[]{:S(2)}) async-start(f32[32,4,128]{2,1,0:T(4,128)} %get-tuple-element.147), calls=%async_computation.7 | async-start | bytes 131072 | tf_op jit(solution)/shard_map/all_to_all | solution.py:632
  92.6 1.7 %collective-permute-start.21 = (f32[16,128]{1,0:T(8,128)S(1)}, f32[16,128]{1,0:T(8,128)S(1)}, u32[]{:S(2)}, u32[]{:S(2)}) collective-permute-start(f32[16,128]{1,0:T(8,128)S(1)} %get-tuple-element.148), channel_id=1, source_target_pairs={{0,16},{16,0},{1,17},{17,1},{2,18},{18,2},{3,19},{19,3},{4,20},{20... | collective-permute-start | bytes 24584 | tf_op jit(solution)/shard_map/ppermute | solution.py:628
  94.3 1.7 %collective-permute-start.23 = (f32[16,128]{1,0:T(8,128)S(1)}, f32[16,128]{1,0:T(8,128)S(1)}, u32[]{:S(2)}, u32[]{:S(2)}) collective-permute-start(f32[16,128]{1,0:T(8,128)S(1)} %get-tuple-element.150), channel_id=1, source_target_pairs={{0,12},{4,0},{8,4},{12,8},{1,13},{5,1},{9,5},{13,9},{2,14},{6,2},{... | collective-permute-start | bytes 24584 | tf_op jit(solution)/shard_map/ppermute | solution.py:628
  96.1 0.3 collective-permute-done.21.rest_0_
  96.3 1.1 collective-permute-done.22.rest_1_
  97.4 2.7 %all-to-all-done.7.recv = f32[32,4,128]{2,1,0:T(4,128)S(1)} async-done(((f32[32,4,128]{2,1,0:T(4,128)}), f32[32,4,128]{2,1,0:T(4,128)S(1)}, u32[]{:S(2)}, u32[]{:S(2)}) %all-to-all-start.7) | async-done | bytes 65568 | tf_op jit(solution)/shard_map/all_to_all | solution.py:632
  100.1 1.6 %iterate.8 = (f32[32,4,128]{2,1,0:T(4,128)}, f32[16,128]{1,0:T(8,128)S(1)}, f32[16,128]{1,0:T(8,128)S(1)}, f32[16,128]{1,0:T(8,128)S(1)}, f32[256,128]{1,0:T(8,1...) custom-call(f32[32,4,128]{2,1,0:T(4,128)S(1)} %all-to-all-done.7.rec, ...), custom_call_target="tpu_custom_call" | custom-call | tf_op jit(solution)/shard_map/iterate/pallas_call | solution.py:607
  101.6 2.6 %all-to-all-start.8 = ((f32[32,4,128]{2,1,0:T(4,128)}), f32[32,4,128]{2,1,0:T(4,128)S(1)}, u32[]{:S(2)}, u32[]{:S(2)}) async-start(f32[32,4,128]{2,1,0:T(4,128)} %get-tuple-element.158), calls=%async_computation.8 | async-start | bytes 131072 | tf_op jit(solution)/shard_map/all_to_all | solution.py:632
  104.2 1.7 %collective-permute-start.24 = (f32[16,128]{1,0:T(8,128)S(1)}, f32[16,128]{1,0:T(8,128)S(1)}, u32[]{:S(2)}, u32[]{:S(2)}) collective-permute-start(f32[16,128]{1,0:T(8,128)S(1)} %get-tuple-element.159), channel_id=1, source_target_pairs={{0,16},{16,0},{1,17},{17,1},{2,18},{18,2},{3,19},{19,3},{4,20},{20... | collective-permute-start | bytes 24584 | tf_op jit(solution)/shard_map/ppermute | solution.py:628
  105.9 1.7 %collective-permute-start.26 = (f32[16,128]{1,0:T(8,128)S(1)}, f32[16,128]{1,0:T(8,128)S(1)}, u32[]{:S(2)}, u32[]{:S(2)}) collective-permute-start(f32[16,128]{1,0:T(8,128)S(1)} %get-tuple-element.161), channel_id=1, source_target_pairs={{0,12},{4,0},{8,4},{12,8},{1,13},{5,1},{9,5},{13,9},{2,14},{6,2},{... | collective-permute-start | bytes 24584 | tf_op jit(solution)/shard_map/ppermute | solution.py:628
  108.0 1.1 collective-permute-done.25.rest_1_
  109.1 2.7 %all-to-all-done.8.recv = f32[32,4,128]{2,1,0:T(4,128)S(1)} async-done(((f32[32,4,128]{2,1,0:T(4,128)}), f32[32,4,128]{2,1,0:T(4,128)S(1)}, u32[]{:S(2)}, u32[]{:S(2)}) %all-to-all-start.8) | async-done | bytes 65568 | tf_op jit(solution)/shard_map/all_to_all | solution.py:632
  111.7 0.9 iterate.9
  112.6 9.3 %all_to_all.50.recv = f32[32,1,128]{2,1,0:T(1,128)S(1)} all-to-all(f32[32,1,128]{2,1,0:T(1,128)S(1)} %get-tuple-element.169), channel_id=1, replica_groups=mesh['gx'=2,'gy'=4,'gz'=4] {'gx','gy','gz'}, dimensions={0} | all-to-all | bytes 32768 | tf_op jit(solution)/shard_map/all_to_all | solution.py:890
  121.9 0.8 pressure.1
  (26 shorter events, 0.7 us)
Async XLA Ops:
  0.6 18.4 %copy-start = (bf16[768,256]{1,0:T(8,128)(2,1)S(1)}, bf16[768,256]{1,0:T(8,128)(2,1)}, u32[]{:S(2)}) copy-start(bf16[768,256]{1,0:T(8,128)(2,1)} %constant.7.clone.zt_any.rest_7_.rest_6_.rest_8_.rest_10_) | copy-start | bytes 1179652
  3.3 15.7 %copy-start.1 = (f32[224,128]{1,0:T(8,128)S(1)}, f32[224,128]{1,0:T(8,128)}, u32[]{:S(2)}) copy-start(f32[224,128]{1,0:T(8,128)} %constant.6.clone.tab_any.rest_6_.rest_5_.rest_7_.rest_9_) | copy-start | bytes 344068
  3.3 15.7 %copy-start.2 = (f32[16,16,128]{2,1,0:T(8,128)S(1)}, f32[16,16,128]{2,1,0:T(8,128)}, u32[]{:S(2)}) copy-start(f32[16,16,128]{2,1,0:T(8,128)} %param.7) | copy-start | bytes 393220
  3.4 15.7 %all-to-all-start = ((f32[32,8,128]{2,1,0:T(8,128)}), f32[32,8,128]{2,1,0:T(8,128)S(1)}, u32[]{:S(2)}, u32[]{:S(2)}) async-start(f32[32,8,128]{2,1,0:T(8,128)} %get-tuple-element.88), calls=%async_computation | async-start | bytes 262144 | tf_op jit(solution)/shard_map/all_to_all | solution.py:632
  10.7 3.8 %collective-permute-start = (f32[32,128]{1,0:T(8,128)S(1)}, f32[32,128]{1,0:T(8,128)S(1)}, u32[]{:S(2)}, u32[]{:S(2)}) collective-permute-start(f32[32,128]{1,0:T(8,128)S(1)} %get-tuple-element.89), channel_id=1, source_target_pairs={{0,16},{16,0},{1,17},{17,1},{2,18},{18,2},{3,19},{19,3},{4,20},{20... | collective-permute-start | bytes 49160 | tf_op jit(solution)/shard_map/ppermute | solution.py:628
  12.5 3.3 %collective-permute-start.1 = (f32[32,128]{1,0:T(8,128)S(1)}, f32[32,128]{1,0:T(8,128)S(1)}, u32[]{:S(2)}, u32[]{:S(2)}) collective-permute-start(f32[32,128]{1,0:T(8,128)S(1)} %get-tuple-element.90), channel_id=1, source_target_pairs={{0,4},{4,8},{8,12},{12,0},{1,5},{5,9},{9,13},{13,1},{2,6},{6,10},{... | collective-permute-start | bytes 49160 | tf_op jit(solution)/shard_map/ppermute | solution.py:628
  12.5 3.3 %collective-permute-start.2 = (f32[32,128]{1,0:T(8,128)S(1)}, f32[32,128]{1,0:T(8,128)S(1)}, u32[]{:S(2)}, u32[]{:S(2)}) collective-permute-start(f32[32,128]{1,0:T(8,128)S(1)} %get-tuple-element.91), channel_id=1, source_target_pairs={{0,12},{4,0},{8,4},{12,8},{1,13},{5,1},{9,5},{13,9},{2,14},{6,2},{... | collective-permute-start | bytes 49160 | tf_op jit(solution)/shard_map/ppermute | solution.py:628
  20.7 10.1 %all-to-all-start.1 = ((f32[32,4,128]{2,1,0:T(4,128)}), f32[32,4,128]{2,1,0:T(4,128)S(1)}, u32[]{:S(2)}, u32[]{:S(2)}) async-start(f32[32,4,128]{2,1,0:T(4,128)} %get-tuple-element.95), calls=%async_computation.1 | async-start | bytes 131072 | tf_op jit(solution)/shard_map/all_to_all | solution.py:632
  23.3 3.7 %collective-permute-start.3 = (f32[16,128]{1,0:T(8,128)S(1)}, f32[16,128]{1,0:T(8,128)S(1)}, u32[]{:S(2)}, u32[]{:S(2)}) collective-permute-start(f32[16,128]{1,0:T(8,128)S(1)} %get-tuple-element.96), channel_id=1, source_target_pairs={{0,16},{16,0},{1,17},{17,1},{2,18},{18,2},{3,19},{19,3},{4,20},{20... | collective-permute-start | bytes 24584 | tf_op jit(solution)/shard_map/ppermute | solution.py:628
  25.0 3.1 %collective-permute-start.4 = (f32[16,128]{1,0:T(8,128)S(1)}, f32[16,128]{1,0:T(8,128)S(1)}, u32[]{:S(2)}, u32[]{:S(2)}) collective-permute-start(f32[16,128]{1,0:T(8,128)S(1)} %get-tuple-element.97), channel_id=1, source_target_pairs={{0,4},{4,8},{8,12},{12,0},{1,5},{5,9},{9,13},{13,1},{2,6},{6,10},{... | collective-permute-start | bytes 24584 | tf_op jit(solution)/shard_map/ppermute | solution.py:628
  25.0 3.1 %collective-permute-start.5 = (f32[16,128]{1,0:T(8,128)S(1)}, f32[16,128]{1,0:T(8,128)S(1)}, u32[]{:S(2)}, u32[]{:S(2)}) collective-permute-start(f32[16,128]{1,0:T(8,128)S(1)} %get-tuple-element.98), channel_id=1, source_target_pairs={{0,12},{4,0},{8,4},{12,8},{1,13},{5,1},{9,5},{13,9},{2,14},{6,2},{... | collective-permute-start | bytes 24584 | tf_op jit(solution)/shard_map/ppermute | solution.py:628
  32.2 10.1 %all-to-all-start.2 = ((f32[32,4,128]{2,1,0:T(4,128)}), f32[32,4,128]{2,1,0:T(4,128)S(1)}, u32[]{:S(2)}, u32[]{:S(2)}) async-start(f32[32,4,128]{2,1,0:T(4,128)} %get-tuple-element.101), calls=%async_computation.2 | async-start | bytes 131072 | tf_op jit(solution)/shard_map/all_to_all | solution.py:632
  34.8 3.7 %collective-permute-start.6 = (f32[16,128]{1,0:T(8,128)S(1)}, f32[16,128]{1,0:T(8,128)S(1)}, u32[]{:S(2)}, u32[]{:S(2)}) collective-permute-start(f32[16,128]{1,0:T(8,128)S(1)} %get-tuple-element.102), channel_id=1, source_target_pairs={{0,16},{16,0},{1,17},{17,1},{2,18},{18,2},{3,19},{19,3},{4,20},{20... | collective-permute-start | bytes 24584 | tf_op jit(solution)/shard_map/ppermute | solution.py:628
  36.5 3.1 %collective-permute-start.7 = (f32[16,128]{1,0:T(8,128)S(1)}, f32[16,128]{1,0:T(8,128)S(1)}, u32[]{:S(2)}, u32[]{:S(2)}) collective-permute-start(f32[16,128]{1,0:T(8,128)S(1)} %get-tuple-element.103), channel_id=1, source_target_pairs={{0,4},{4,8},{8,12},{12,0},{1,5},{5,9},{9,13},{13,1},{2,6},{6,10},{... | collective-permute-start | bytes 24584 | tf_op jit(solution)/shard_map/ppermute | solution.py:628
  36.5 3.1 %collective-permute-start.8 = (f32[16,128]{1,0:T(8,128)S(1)}, f32[16,128]{1,0:T(8,128)S(1)}, u32[]{:S(2)}, u32[]{:S(2)}) collective-permute-start(f32[16,128]{1,0:T(8,128)S(1)} %get-tuple-element.104), channel_id=1, source_target_pairs={{0,12},{4,0},{8,4},{12,8},{1,13},{5,1},{9,5},{13,9},{2,14},{6,2},{... | collective-permute-start | bytes 24584 | tf_op jit(solution)/shard_map/ppermute | solution.py:628
  43.6 10.1 %all-to-all-start.3 = ((f32[32,4,128]{2,1,0:T(4,128)}), f32[32,4,128]{2,1,0:T(4,128)S(1)}, u32[]{:S(2)}, u32[]{:S(2)}) async-start(f32[32,4,128]{2,1,0:T(4,128)} %get-tuple-element.108), calls=%async_computation.3 | async-start | bytes 131072 | tf_op jit(solution)/shard_map/all_to_all | solution.py:632
  46.2 3.7 %collective-permute-start.9 = (f32[16,128]{1,0:T(8,128)S(1)}, f32[16,128]{1,0:T(8,128)S(1)}, u32[]{:S(2)}, u32[]{:S(2)}) collective-permute-start(f32[16,128]{1,0:T(8,128)S(1)} %get-tuple-element.109), channel_id=1, source_target_pairs={{0,16},{16,0},{1,17},{17,1},{2,18},{18,2},{3,19},{19,3},{4,20},{20... | collective-permute-start | bytes 24584 | tf_op jit(solution)/shard_map/ppermute | solution.py:628
  47.9 3.1 %collective-permute-start.10 = (f32[16,128]{1,0:T(8,128)S(1)}, f32[16,128]{1,0:T(8,128)S(1)}, u32[]{:S(2)}, u32[]{:S(2)}) collective-permute-start(f32[16,128]{1,0:T(8,128)S(1)} %get-tuple-element.110), channel_id=1, source_target_pairs={{0,4},{4,8},{8,12},{12,0},{1,5},{5,9},{9,13},{13,1},{2,6},{6,10},{... | collective-permute-start | bytes 24584 | tf_op jit(solution)/shard_map/ppermute | solution.py:628
  47.9 3.1 %collective-permute-start.11 = (f32[16,128]{1,0:T(8,128)S(1)}, f32[16,128]{1,0:T(8,128)S(1)}, u32[]{:S(2)}, u32[]{:S(2)}) collective-permute-start(f32[16,128]{1,0:T(8,128)S(1)} %get-tuple-element.111), channel_id=1, source_target_pairs={{0,12},{4,0},{8,4},{12,8},{1,13},{5,1},{9,5},{13,9},{2,14},{6,2},{... | collective-permute-start | bytes 24584 | tf_op jit(solution)/shard_map/ppermute | solution.py:628
  55.2 10.1 %all-to-all-start.4 = ((f32[32,4,128]{2,1,0:T(4,128)}), f32[32,4,128]{2,1,0:T(4,128)S(1)}, u32[]{:S(2)}, u32[]{:S(2)}) async-start(f32[32,4,128]{2,1,0:T(4,128)} %get-tuple-element.117), calls=%async_computation.4 | async-start | bytes 131072 | tf_op jit(solution)/shard_map/all_to_all | solution.py:632
  57.7 3.7 %collective-permute-start.12 = (f32[16,128]{1,0:T(8,128)S(1)}, f32[16,128]{1,0:T(8,128)S(1)}, u32[]{:S(2)}, u32[]{:S(2)}) collective-permute-start(f32[16,128]{1,0:T(8,128)S(1)} %get-tuple-element.118), channel_id=1, source_target_pairs={{0,16},{16,0},{1,17},{17,1},{2,18},{18,2},{3,19},{19,3},{4,20},{20... | collective-permute-start | bytes 24584 | tf_op jit(solution)/shard_map/ppermute | solution.py:628
  59.5 3.1 %collective-permute-start.13 = (f32[16,128]{1,0:T(8,128)S(1)}, f32[16,128]{1,0:T(8,128)S(1)}, u32[]{:S(2)}, u32[]{:S(2)}) collective-permute-start(f32[16,128]{1,0:T(8,128)S(1)} %get-tuple-element.119), channel_id=1, source_target_pairs={{0,4},{4,8},{8,12},{12,0},{1,5},{5,9},{9,13},{13,1},{2,6},{6,10},{... | collective-permute-start | bytes 24584 | tf_op jit(solution)/shard_map/ppermute | solution.py:628
  59.5 3.1 %collective-permute-start.14 = (f32[16,128]{1,0:T(8,128)S(1)}, f32[16,128]{1,0:T(8,128)S(1)}, u32[]{:S(2)}, u32[]{:S(2)}) collective-permute-start(f32[16,128]{1,0:T(8,128)S(1)} %get-tuple-element.120), channel_id=1, source_target_pairs={{0,12},{4,0},{8,4},{12,8},{1,13},{5,1},{9,5},{13,9},{2,14},{6,2},{... | collective-permute-start | bytes 24584 | tf_op jit(solution)/shard_map/ppermute | solution.py:628
  66.8 10.1 %all-to-all-start.5 = ((f32[32,4,128]{2,1,0:T(4,128)}), f32[32,4,128]{2,1,0:T(4,128)S(1)}, u32[]{:S(2)}, u32[]{:S(2)}) async-start(f32[32,4,128]{2,1,0:T(4,128)} %get-tuple-element.125), calls=%async_computation.5 | async-start | bytes 131072 | tf_op jit(solution)/shard_map/all_to_all | solution.py:632
  69.3 3.7 %collective-permute-start.15 = (f32[16,128]{1,0:T(8,128)S(1)}, f32[16,128]{1,0:T(8,128)S(1)}, u32[]{:S(2)}, u32[]{:S(2)}) collective-permute-start(f32[16,128]{1,0:T(8,128)S(1)} %get-tuple-element.126), channel_id=1, source_target_pairs={{0,16},{16,0},{1,17},{17,1},{2,18},{18,2},{3,19},{19,3},{4,20},{20... | collective-permute-start | bytes 24584 | tf_op jit(solution)/shard_map/ppermute | solution.py:628
  71.1 3.1 %collective-permute-start.16 = (f32[16,128]{1,0:T(8,128)S(1)}, f32[16,128]{1,0:T(8,128)S(1)}, u32[]{:S(2)}, u32[]{:S(2)}) collective-permute-start(f32[16,128]{1,0:T(8,128)S(1)} %get-tuple-element.127), channel_id=1, source_target_pairs={{0,4},{4,8},{8,12},{12,0},{1,5},{5,9},{9,13},{13,1},{2,6},{6,10},{... | collective-permute-start | bytes 24584 | tf_op jit(solution)/shard_map/ppermute | solution.py:628
  71.1 3.1 %collective-permute-start.17 = (f32[16,128]{1,0:T(8,128)S(1)}, f32[16,128]{1,0:T(8,128)S(1)}, u32[]{:S(2)}, u32[]{:S(2)}) collective-permute-start(f32[16,128]{1,0:T(8,128)S(1)} %get-tuple-element.128), channel_id=1, source_target_pairs={{0,12},{4,0},{8,4},{12,8},{1,13},{5,1},{9,5},{13,9},{2,14},{6,2},{... | collective-permute-start | bytes 24584 | tf_op jit(solution)/shard_map/ppermute | solution.py:628
  78.4 10.1 %all-to-all-start.6 = ((f32[32,4,128]{2,1,0:T(4,128)}), f32[32,4,128]{2,1,0:T(4,128)S(1)}, u32[]{:S(2)}, u32[]{:S(2)}) async-start(f32[32,4,128]{2,1,0:T(4,128)} %get-tuple-element.136), calls=%async_computation.6 | async-start | bytes 131072 | tf_op jit(solution)/shard_map/all_to_all | solution.py:632
  81.0 3.7 %collective-permute-start.18 = (f32[16,128]{1,0:T(8,128)S(1)}, f32[16,128]{1,0:T(8,128)S(1)}, u32[]{:S(2)}, u32[]{:S(2)}) collective-permute-start(f32[16,128]{1,0:T(8,128)S(1)} %get-tuple-element.137), channel_id=1, source_target_pairs={{0,16},{16,0},{1,17},{17,1},{2,18},{18,2},{3,19},{19,3},{4,20},{20... | collective-permute-start | bytes 24584 | tf_op jit(solution)/shard_map/ppermute | solution.py:628
  82.7 3.1 %collective-permute-start.19 = (f32[16,128]{1,0:T(8,128)S(1)}, f32[16,128]{1,0:T(8,128)S(1)}, u32[]{:S(2)}, u32[]{:S(2)}) collective-permute-start(f32[16,128]{1,0:T(8,128)S(1)} %get-tuple-element.138), channel_id=1, source_target_pairs={{0,4},{4,8},{8,12},{12,0},{1,5},{5,9},{9,13},{13,1},{2,6},{6,10},{... | collective-permute-start | bytes 24584 | tf_op jit(solution)/shard_map/ppermute | solution.py:628
  82.7 3.1 %collective-permute-start.20 = (f32[16,128]{1,0:T(8,128)S(1)}, f32[16,128]{1,0:T(8,128)S(1)}, u32[]{:S(2)}, u32[]{:S(2)}) collective-permute-start(f32[16,128]{1,0:T(8,128)S(1)} %get-tuple-element.139), channel_id=1, source_target_pairs={{0,12},{4,0},{8,4},{12,8},{1,13},{5,1},{9,5},{13,9},{2,14},{6,2},{... | collective-permute-start | bytes 24584 | tf_op jit(solution)/shard_map/ppermute | solution.py:628
  90.0 10.1 %all-to-all-start.7 = ((f32[32,4,128]{2,1,0:T(4,128)}), f32[32,4,128]{2,1,0:T(4,128)S(1)}, u32[]{:S(2)}, u32[]{:S(2)}) async-start(f32[32,4,128]{2,1,0:T(4,128)} %get-tuple-element.147), calls=%async_computation.7 | async-start | bytes 131072 | tf_op jit(solution)/shard_map/all_to_all | solution.py:632
  92.6 3.7 %collective-permute-start.21 = (f32[16,128]{1,0:T(8,128)S(1)}, f32[16,128]{1,0:T(8,128)S(1)}, u32[]{:S(2)}, u32[]{:S(2)}) collective-permute-start(f32[16,128]{1,0:T(8,128)S(1)} %get-tuple-element.148), channel_id=1, source_target_pairs={{0,16},{16,0},{1,17},{17,1},{2,18},{18,2},{3,19},{19,3},{4,20},{20... | collective-permute-start | bytes 24584 | tf_op jit(solution)/shard_map/ppermute | solution.py:628
  94.3 3.1 %collective-permute-start.22 = (f32[16,128]{1,0:T(8,128)S(1)}, f32[16,128]{1,0:T(8,128)S(1)}, u32[]{:S(2)}, u32[]{:S(2)}) collective-permute-start(f32[16,128]{1,0:T(8,128)S(1)} %get-tuple-element.149), channel_id=1, source_target_pairs={{0,4},{4,8},{8,12},{12,0},{1,5},{5,9},{9,13},{13,1},{2,6},{6,10},{... | collective-permute-start | bytes 24584 | tf_op jit(solution)/shard_map/ppermute | solution.py:628
  94.3 3.1 %collective-permute-start.23 = (f32[16,128]{1,0:T(8,128)S(1)}, f32[16,128]{1,0:T(8,128)S(1)}, u32[]{:S(2)}, u32[]{:S(2)}) collective-permute-start(f32[16,128]{1,0:T(8,128)S(1)} %get-tuple-element.150), channel_id=1, source_target_pairs={{0,12},{4,0},{8,4},{12,8},{1,13},{5,1},{9,5},{13,9},{2,14},{6,2},{... | collective-permute-start | bytes 24584 | tf_op jit(solution)/shard_map/ppermute | solution.py:628
  101.6 10.1 %all-to-all-start.8 = ((f32[32,4,128]{2,1,0:T(4,128)}), f32[32,4,128]{2,1,0:T(4,128)S(1)}, u32[]{:S(2)}, u32[]{:S(2)}) async-start(f32[32,4,128]{2,1,0:T(4,128)} %get-tuple-element.158), calls=%async_computation.8 | async-start | bytes 131072 | tf_op jit(solution)/shard_map/all_to_all | solution.py:632
  104.2 3.7 %collective-permute-start.24 = (f32[16,128]{1,0:T(8,128)S(1)}, f32[16,128]{1,0:T(8,128)S(1)}, u32[]{:S(2)}, u32[]{:S(2)}) collective-permute-start(f32[16,128]{1,0:T(8,128)S(1)} %get-tuple-element.159), channel_id=1, source_target_pairs={{0,16},{16,0},{1,17},{17,1},{2,18},{18,2},{3,19},{19,3},{4,20},{20... | collective-permute-start | bytes 24584 | tf_op jit(solution)/shard_map/ppermute | solution.py:628
  105.9 3.1 %collective-permute-start.25 = (f32[16,128]{1,0:T(8,128)S(1)}, f32[16,128]{1,0:T(8,128)S(1)}, u32[]{:S(2)}, u32[]{:S(2)}) collective-permute-start(f32[16,128]{1,0:T(8,128)S(1)} %get-tuple-element.160), channel_id=1, source_target_pairs={{0,4},{4,8},{8,12},{12,0},{1,5},{5,9},{9,13},{13,1},{2,6},{6,10},{... | collective-permute-start | bytes 24584 | tf_op jit(solution)/shard_map/ppermute | solution.py:628
  105.9 3.1 %collective-permute-start.26 = (f32[16,128]{1,0:T(8,128)S(1)}, f32[16,128]{1,0:T(8,128)S(1)}, u32[]{:S(2)}, u32[]{:S(2)}) collective-permute-start(f32[16,128]{1,0:T(8,128)S(1)} %get-tuple-element.161), channel_id=1, source_target_pairs={{0,12},{4,0},{8,4},{12,8},{1,13},{5,1},{9,5},{13,9},{2,14},{6,2},{... | collective-permute-start | bytes 24584 | tf_op jit(solution)/shard_map/ppermute | solution.py:628

commit v3 on v2

--- a/solution.py
+++ b/solution.py
@@ -171,11 +171,20 @@
     lane = lax.broadcasted_iota(jnp.int32, (NP, BZ), 1)
     last = (lane % NP == NP - 1) & (lane < BZ - 1)
     first = (lane % NP == 0) & (lane > 0)
-    v3 = v.reshape(ROWS // NP, NP, BZ)
-    up = pltpu.roll(v3, BZ - 1, 2)
-    down = pltpu.roll(v3, 1, 2)
-    v3 = v3 + jnp.where(last[None], up, jnp.where(first[None], down, 0.0))
-    return v3.reshape(ROWS, BZ)
+    swap = jnp.where(last, lane + 1, jnp.where(first, lane - 1, lane))
+    out = []
+    for q in range(v.shape[0] // NP):
+        part = v[NP * q : NP * q + NP]
+        other = jnp.take_along_axis(part, swap, axis=1, mode="promise_in_bounds")
+        out.append(part + jnp.where(last | first, other, 0.0))
+    return jnp.concatenate(out, axis=0)
+
+
+def tree(parts):
+    while len(parts) > 1:
+        rest = parts[len(parts) // 2 * 2 :]
+        parts = [a + b for a, b in zip(parts[0::2], parts[1::2])] + rest
+    return parts[0]
 
 
 class Geometry:
@@ -272,13 +281,13 @@
 
 def pack_z_faces(v, work):
     sub, lane = tile_iota()
-    tile = None
-    for q in range(ROWS // 8):
-        part = pltpu.roll(v[8 * q : 8 * q + 8], (2 * q + 1) % BZ, 1)
-        if tile is None:
-            tile = part
-        else:
-            tile = jnp.where(lane >= 2 * q, part, tile)
+    parts = [pltpu.roll(v[8 * q : 8 * q + 8], (2 * q + 1) % BZ, 1) for q in range(ROWS // 8)]
+    width = 2
+    while len(parts) > 1:
+        pairs = zip(parts[0::2], parts[1::2])
+        parts = [jnp.where(lane & width == 0, a, b) for a, b in pairs]
+        width *= 2
+    tile = parts[0]
     turns = (-1, 0, 1, 63, 64, 65)
     for i, a in enumerate(turns):
         work[8 * i : 8 * i + 8, :] = tile if a == 0 else pltpu.roll(tile, a % BZ, 1)
@@ -315,7 +324,7 @@
     return tile
 
 
-def send_fields(geo, lay, f_refs, zs, work, scalars, send_ref, xs, ys, fields, extra=None):
+def send_fields(geo, lay, f_ref, z, work, scalars, send_ref, xs, ys, fields=1, extra=None):
     rows = lay.slot_rows(fields)
     base = [scalars[:, i * 128 : (i + 1) * 128] for i in range(lay.scalar_rows)]
     used = lay.scalar_rows
@@ -326,28 +335,35 @@
     base.append(jnp.zeros((rows - used, 128), F32))
     base = jnp.concatenate([b for b in base if b.shape[0]], axis=0)
     send_ref[...] = jnp.broadcast_to(base[None], (lay.devices, rows, 128))
-    for k, f_ref in enumerate(f_refs):
-        at = lay.scalar_rows + 2 * k
-        pairs = pack_z_faces(zs[k], work)
-        for dz in (-1, 1):
-            pair = pairs[0 if dz < 0 else 1]
-            for dx in (-1, 0, 1):
-                for dy in (-1, 0, 1):
-                    there = geo.neighbour(dx, dy, dz)
-                    send_ref[there, at : at + 1, :] = pair[0]
-                    send_ref[there, at + 1 : at + 2, :] = pair[1]
-        for dx in (-1, 1):
-            for dy in (-1, 1):
-                row = (BX - 1 if dx > 0 else 0) * BY + (BY - 1 if dy > 0 else 0)
-                send_ref[geo.neighbour(dx, dy, 0), at : at + 1, :] = f_ref[row : row + 1, :]
-        lowx, highx = f_ref[0:BY, :], f_ref[ROWS - BY : ROWS, :]
-        for ref, face in zip(xs, pick_faces(geo, 0, lay.sizes[0], lowx, highx)):
-            ref[k * BY : (k + 1) * BY, :] = face
-        lowy = f_ref[pl.ds(0, BX, stride=BY), :]
-        highy = f_ref[pl.ds(BY - 1, BX, stride=BY), :]
-        for ref, face in zip(ys, pick_faces(geo, 1, lay.sizes[1], lowy, highy)):
-            ref[k * BX : (k + 1) * BX, :] = face
+    fill_field(geo, lay, f_ref, z, work, send_ref, fields - 1)
+    fill_faces(geo, lay, f_ref, xs, ys)
     send_ref[geo.me] = base
+
+
+def fill_field(geo, lay, f_ref, z, work, send_ref, k):
+    at = lay.scalar_rows + 2 * k
+    pairs = pack_z_faces(z, work)
+    for dz in (-1, 1):
+        pair = pairs[0 if dz < 0 else 1]
+        for dx in (-1, 0, 1):
+            for dy in (-1, 0, 1):
+                there = geo.neighbour(dx, dy, dz)
+                send_ref[there, at : at + 1, :] = pair[0]
+                send_ref[there, at + 1 : at + 2, :] = pair[1]
+    for dx in (-1, 1):
+        for dy in (-1, 1):
+            row = (BX - 1 if dx > 0 else 0) * BY + (BY - 1 if dy > 0 else 0)
+            send_ref[geo.neighbour(dx, dy, 0), at : at + 1, :] = f_ref[row : row + 1, :]
+
+
+def fill_faces(geo, lay, f_ref, xs, ys):
+    lowx, highx = f_ref[0:BY, :], f_ref[ROWS - BY : ROWS, :]
+    for ref, face in zip(xs, pick_faces(geo, 0, lay.sizes[0], lowx, highx)):
+        ref[0:BY, :] = face
+    lowy = f_ref[pl.ds(0, BX, stride=BY), :]
+    highy = f_ref[pl.ds(BY - 1, BX, stride=BY), :]
+    for ref, face in zip(ys, pick_faces(geo, 1, lay.sizes[1], lowy, highy)):
+        ref[0:BX, :] = face
 
 
 def came_from(geo, axis, n, refs, k, size):
@@ -409,7 +425,11 @@
 
 
 def received_scalars(lay, recv_ref):
-    total = jnp.sum(recv_ref[...], axis=0)
+    total = recv_ref[...]
+    while total.shape[0] % 2 == 0:
+        half = total.shape[0] // 2
+        total = total[:half] + total[half:]
+    total = jnp.sum(total, axis=0)
     return jnp.concatenate([total[i : i + 1] for i in range(lay.scalar_rows)], axis=1)
 
 
@@ -444,9 +464,8 @@
 
 def partial_sums(geo, v, sums, q_ref, hot_ref):
     first, last = v[0:BY], v[ROWS - BY : ROWS]
-    middle = first * geo.x_share(0) + last * geo.x_share(BX - 1)
-    for x in range(1, BX - 1):
-        middle = middle + v[x * BY : (x + 1) * BY]
+    inner = [v[x * BY : (x + 1) * BY] for x in range(1, BX - 1)]
+    middle = tree([first * geo.x_share(0), last * geo.x_share(BX - 1), *inner])
     share = geo.y_share()
     for i, part in enumerate((0.5 * first, middle, 0.5 * last)):
         shared = part * share
@@ -459,10 +478,17 @@
     below, above = 0.5 * q[:, 0:1], 0.5 * q[:, BZ - 1 : BZ]
     rows = hot_ref[48:80, :] * below + hot_ref[80:112, :] * own + hot_ref[112:144, :] * above
     rows = rows[0:8] + rows[8:16] + rows[16:24] + rows[24:32]
+    if sums:
+        rows = rows + plain_sums(sums, hot_ref)
+    return jnp.sum(rows, axis=0, keepdims=True)
+
+
+def plain_sums(sums, hot_ref):
+    parts = []
     for i, total in enumerate(sums):
         at = 144 + 8 * i
-        rows = rows + hot_ref[at : at + 8, :] * jnp.sum(total, axis=1, keepdims=True)
-    return jnp.sum(rows, axis=0, keepdims=True)
+        parts.append(hot_ref[at : at + 8, :] * jnp.sum(total, axis=1, keepdims=True))
+    return tree(parts)
 
 
 def spread(geo, values, hot_ref):
@@ -497,21 +523,19 @@
 
 
 def all_rows(v):
-    total = v[0:8]
-    for i in range(1, ROWS // 8):
-        total = total + v[8 * i : 8 * i + 8]
-    return total
+    return tree([v[8 * i : 8 * i + 8] for i in range(ROWS // 8)])
 
 
 def weighted_rows(geo, v):
     yz = geo.yz_weight()
-    total = None
+    parts = []
     for x in range(BX):
         weight = geo.x_weight(x)
         part = v[x * BY : (x + 1) * BY]
         if not (isinstance(weight, float) and weight == 1.0):
             part = part * weight
-        total = part if total is None else total + part
+        parts.append(part)
+    total = tree(parts)
     total = total * yz
     return total[0:8] + total[8:16]
 
@@ -524,25 +548,28 @@
     return out + along_z(coef * gz, "t", zt)
 
 
-def stiffness(v, scaled, tab, zt, work):
-    out = bmass_of(tab) * v
-    out = out + along_x(scaled * along_x(v, "d"), "t")
-    out = out + along_y(scaled * along_y(v, "d", tab, work.at[0]), "t", tab, work.at[1])
-    return out + along_z(scaled * along_z(v, "d", zt), "t", zt)
-
-
-def local_step(geo, lay, residual, dinv, scaled, state, p_old, refs):
+def stiffness(v, scaled, tab, zt, work, final):
+    bm = bmass_of(tab)
+    gx, gy, gz = along_x(v, "d"), along_y(v, "d", tab, work.at[0]), along_z(v, "d", zt)
+    tx, ty, tz = scaled * gx, scaled * gy, scaled * gz
+    energy = all_rows(bm * v * v + (tx * gx + ty * gy + tz * gz))
+    if final:
+        return None, energy
+    out = bm * v + along_x(tx, "t") + along_y(ty, "t", tab, work.at[1])
+    return out + along_z(tz, "t", zt), energy
+
+
+def local_step(geo, lay, residual, dinv, scaled, state, image, refs):
     tab, zt, hot, u_ref, f_ref, send_ref, xs, ys, q_ref, state_ref, work, zwork, final = refs
     s_row, ts_row, gamma, curvature = state
     jacobi = residual * dinv
     planes = spread(geo, s_row, hot)
     u = jnp.concatenate([jacobi[x * BY : (x + 1) * BY] + planes[x] for x in range(BX)], axis=0)
     u_ref[...] = u
-    local = stiffness(u, scaled, tab, zt, work)
-    sums = [weighted_rows(geo, residual * jacobi), all_rows(u * local)]
-    if p_old is not None:
-        sums.append(all_rows(p_old * local))
-    scalars = partial_sums(geo, local, sums, q_ref, hot)
+    local, energy = stiffness(u, scaled, tab, zt, work, final)
+    sums = [weighted_rows(geo, residual * jacobi), energy]
+    if image is not None:
+        sums.append(weighted_rows(geo, u * image))
     ones = jnp.ones_like(s_row)
     coarse = coarse_inner(lay, s_row)
     state_ref[...] = jnp.concatenate(
@@ -550,13 +577,15 @@
         axis=0,
     )
     if final:
+        scalars = jnp.sum(plain_sums(sums, hot), axis=0, keepdims=True)
         rows = [scalars[:, i * 128 : (i + 1) * 128] for i in range(lay.scalar_rows)]
         rows = jnp.concatenate(rows, axis=0)
         send_ref[...] = jnp.broadcast_to(rows[None], send_ref.shape)
         return
+    scalars = partial_sums(geo, local, sums, q_ref, hot)
     local = local_sum_xy(local)
     f_ref[...] = local_sum_z(local)
-    send_fields(geo, lay, [f_ref], [local], zwork, scalars, send_ref, xs, ys, 1)
+    send_fields(geo, lay, f_ref, local, zwork, scalars, send_ref, xs, ys)
 
 
 def step_sizes(lay, recv_ref, state_ref, first):
@@ -600,17 +629,18 @@
             + [like(BX * fields, BZ)] * ny
         )
 
-    def call(kernel, ins, outs, scratch, name, space=pltpu.VMEM, limit=48):
+    def call(kernel, ins, outs, scratch, name, from_hbm=()):
         spec = pl.BlockSpec(memory_space=pltpu.VMEM)
-        if space == pltpu.HBM:
-            ins = [pltpu.with_memory_space_constraint(v, pltpu.HBM) for v in ins]
+        hbm = pl.BlockSpec(memory_space=pltpu.HBM)
+        ins = [pltpu.with_memory_space_constraint(v, pltpu.HBM) if i in from_hbm else v for i, v in enumerate(ins)]
         return pl.pallas_call(
             kernel,
             out_shape=outs,
-            in_specs=[pl.BlockSpec(memory_space=space)] * len(ins),
+            in_specs=[hbm if i in from_hbm else spec for i in range(len(ins))],
             out_specs=[spec] * len(outs),
             scratch_shapes=scratch,
-            compiler_params=pltpu.CompilerParams(vmem_limit_bytes=limit * 1024 * 1024),
+            compiler_params=pltpu.CompilerParams(vmem_limit_bytes=48 * 1024 * 1024),
+            cost_estimate=pl.CostEstimate(flops=4000000, bytes_accessed=1000000, transcendentals=0),
             name=name,
         )(*ins)
 
@@ -639,55 +669,73 @@
     def split(refs):
         return refs[0], refs[1 : 1 + nx], refs[1 + nx : 1 + nx + ny]
 
-    def start_kernel(level_any, vel_any, source_any, factor_any, tab_any, zt_any, places_any, *rest):
+    def start_kernel(level_any, vel_any, tab_any, zt_any, *rest):
         send, xs, ys = split(rest[:n_out])
-        fa_ref, fd_ref, hot_ref, q_ref, work, zwork = rest[n_out : n_out + 6]
-        buffers, sems = rest[n_out + 6 : -1], rest[-1]
-        sources = (level_any, zt_any, tab_any, vel_any, source_any, places_any, factor_any)
+        f_ref, work, zwork = rest[n_out : n_out + 3]
+        level_ref, zt_ref, tab_ref, vel_ref, sems = rest[n_out + 3 :]
+        sources = (level_any, zt_any.at[0 : 2 * BZ], tab_any, vel_any)
         copies = [
             pltpu.make_async_copy(source, target, sems.at[i])
-            for i, (source, target) in enumerate(zip(sources, buffers))
+            for i, (source, target) in enumerate(zip(sources, (level_ref, zt_ref, tab_ref, vel_ref)))
         ]
         for copy in copies:
             copy.start()
-        for copy in copies:
+        for copy in copies[:3]:
             copy.wait()
-        level_ref, zt_ref, tab_ref, vel_ref, source_ref, places_ref, factor_ref = buffers
         geo = Geometry(sizes)
         level = level_ref[...]
+        gx, gy, gz = along_x(level, "d"), along_y(level, "d", tab_ref, work.at[0]), along_z(level, "d", zt_ref)
+        copies[3].wait()
+        advect = bmass_of(tab_ref) * (vel_ref[0] * gx + vel_ref[1] * gy + vel_ref[2] * gz)
+        finish(geo, advect, f_ref, zwork, send, xs, ys)
+
+    def finish(geo, v, f_ref, zwork, send, xs, ys):
+        v = local_sum_xy(v)
+        f_ref[...] = local_sum_z(v)
+        nothing = jnp.zeros((1, lay.lanes), F32)
+        send_fields(geo, lay, f_ref, v, zwork, nothing, send, xs, ys)
+
+    def source_kernel(vel_ref, source_ref, factor_ref, tab_ref, zt_ref, places_ref, _, *rest):
+        slots, xs, ys = split(rest[:n_out])
+        f_ref, hot_ref, q_ref, work, zwork = rest[n_out:]
+        geo = Geometry(sizes)
         bm = bmass_of(tab_ref)
-        advect = vel_ref[0] * along_x(level, "d")
-        advect = advect + vel_ref[1] * along_y(level, "d", tab_ref, work.at[0])
-        advect = advect + vel_ref[2] * along_z(level, "d", zt_ref)
-        advect = local_sum_xy(bm * advect)
-        fa_ref[...] = local_sum_z(advect)
         div = bm * source_ref[...] + along_x(bm * vel_ref[0], "t")
         div = div + along_y(bm * vel_ref[1], "t", tab_ref, work.at[1])
         div = div + along_z(bm * vel_ref[2], "t", zt_ref)
         hot_ref[...] = coarse_tables(geo, lay, places_ref)
         scalars = partial_sums(geo, div, [], q_ref, hot_ref)
         div = local_sum_xy(div)
-        fd_ref[...] = local_sum_z(div)
+        f_ref[...] = local_sum_z(div)
         factor = factor_ref[...]
         if lay.lanes > lay.devices:
             pad = jnp.zeros((1, lay.lanes - lay.devices), F32)
             factor = jnp.concatenate([factor, pad], axis=1)
-        send_fields(
-            geo, lay, [fa_ref, fd_ref], [advect, div], zwork, scalars, send, xs, ys, 2, factor
-        )
-
-    def finish(geo, v, f_ref, zwork, send, xs, ys):
-        v = local_sum_xy(v)
-        f_ref[...] = local_sum_z(v)
-        nothing = jnp.zeros((1, lay.lanes), F32)
-        send_fields(geo, lay, [f_ref], [v], zwork, nothing, send, xs, ys, 1)
+        send_fields(geo, lay, f_ref, div, zwork, scalars, slots, xs, ys, 2, factor)
 
     def first_kernel(recv, *rest):
         xs, ys = rest[:nx], rest[nx : nx + ny]
-        level_ref, fa_ref, fd_ref, tab_ref, zt_ref, hot_ref = rest[nx + ny : nx + ny + 6]
-        out = rest[nx + ny + 6 :]
+        level_ref, fa_ref, tab_ref, zt_ref = rest[nx + ny : nx + ny + 4]
+        slots, sxs, sys = split(rest[nx + ny + 4 : nx + ny + 4 + n_out])
+        out = rest[nx + ny + 4 + n_out :]
         send, oxs, oys = split(out[:n_out])
-        level_out, f_ref, r_ref, s_ref, hot_out, w_ref, work, zwork, gram_ref = out[n_out:]
+        level_out, f_ref, w_ref, work, zwork = out[n_out:]
+        geo = Geometry(sizes)
+        received(geo, lay, fa_ref[...], recv, xs, ys, w_ref, 0)
+        level = level_ref[...] - TIME_STEP * w_ref[...] * inverse_mass(geo, tab_ref)
+        level_out[...] = level
+        v = local_sum_xy(weak_form(level, tab_ref, zt_ref, work))
+        f_ref[...] = local_sum_z(v)
+        send[...] = slots[...]
+        fill_field(geo, lay, f_ref, v, zwork, send, 0)
+        send[geo.me] = slots[geo.me]
+        fill_faces(geo, lay, f_ref, oxs, oys)
+        for to, part in zip((*oxs, *oys), (*sxs, *sys)):
+            to[BY : 2 * BY, :] = part[...]
+
+    def rhs_kernel(recv, *rest):
+        xs, ys = rest[:nx], rest[nx : nx + ny]
+        fd_ref, hot_ref, r_ref, s_ref, hot_out, w_ref, gram_ref = rest[nx + ny :]
         geo = Geometry(sizes)
         at = lay.scalar_rows + 4
         factor = [recv[:, at + i, :] for i in range(lay.scalar_rows)]
@@ -706,15 +754,10 @@
         )
         received(geo, lay, fd_ref[...], recv, xs, ys, w_ref, 1)
         r_ref[...] = SOURCE_SCALE * w_ref[...]
-        row = received_scalars(lay, recv)
-        row = with_coarse(lay, SOURCE_SCALE * row, gram_ref)
+        row = with_coarse(lay, SOURCE_SCALE * received_scalars(lay, recv), gram_ref)
         s_ref[...] = jnp.broadcast_to(row, s_ref.shape)
         hot_out[...] = hot_ref[...]
         hot_out[48:144, :] = with_coarse(lay, hot_ref[48:144, :], gram_ref)
-        received(geo, lay, fa_ref[...], recv, xs, ys, w_ref, 0)
-        level = level_ref[...] - TIME_STEP * w_ref[...] * inverse_mass(geo, tab_ref)
-        level_out[...] = level
-        finish(geo, weak_form(level, tab_ref, zt_ref, work), f_ref, zwork, send, oxs, oys)
 
     def new_level(geo, recv, xs, ys, level_ref, f_ref, tab_ref, w_ref):
         received(geo, lay, f_ref[...], recv, xs, ys, w_ref, 0)
@@ -811,7 +854,7 @@
                 dinv_ref[...],
                 scaled_ref[...],
                 state,
-                p,
+                image,
                 (*refs, oxs, oys, q_ref, state_ref, work, zwork, final),
             )
 
@@ -828,31 +871,46 @@
         tab, zt, places = jnp.asarray(tab_np), jnp.asarray(zt_np), jnp.asarray(places_np)
         out = call(
             start_kernel,
-            [level, vel, src, coarse_factor, tab, zt, places],
-            outgoing(2) + [block, block, like(HOT_ROWS, lay.lanes)],
-            [qrows, pair, tiles]
-            + [pltpu.VMEM(a.shape, a.dtype) for a in (level, zt, tab, vel, src, places, coarse_factor)]
-            + [pltpu.SemaphoreType.DMA((7,))],
+            [level, vel, tab, zt],
+            outgoing(1) + [block],
+            [pair, tiles]
+            + [pltpu.VMEM(a, d) for a, d in ((level.shape, F32), ((2 * BZ, 2 * BZ), BF16), (tab.shape, F32), (vel.shape, F32))]
+            + [pltpu.SemaphoreType.DMA((4,))],
             "advect",
-            pltpu.HBM,
+            range(4),
         )
-        fa, fd, hot = out[n_out:]
+        fa = out[n_out]
         got = exchange(out[:n_out])
+        side = call(
+            source_kernel,
+            [vel, src, coarse_factor, tab, zt, places, fa],
+            [like(lay.devices, lay.slot_rows(2), 128), *outgoing(1)[1:], block, like(HOT_ROWS, lay.lanes)],
+            [qrows, pair, tiles],
+            "source",
+        )
+        fd, hot = side[n_out:]
         out = call(
             first_kernel,
-            [*got, level, fa, fd, tab, zt, hot],
-            outgoing(1) + [block, block, block, like(8, lay.lanes), like(HOT_ROWS, lay.lanes)],
-            [work, pair, tiles, pltpu.VMEM((lay.lanes, lay.lanes), F32)],
+            [*got, level, fa, tab, zt, *side[:n_out]],
+            outgoing(2) + [block, block],
+            [work, pair, tiles],
             "sweep_first",
         )
-        level, f, residual, s_rows, hot = out[n_out:]
+        level, f = out[n_out:]
+        got = exchange(out[:n_out])
+        residual, s_rows, hot = call(
+            rhs_kernel,
+            [*got, fd, hot],
+            [block, like(8, lay.lanes), like(HOT_ROWS, lay.lanes)],
+            [work, pltpu.VMEM((lay.lanes, lay.lanes), F32)],
+            "rhs",
+        )
         for _ in range(RSWEEPS - 1):
-            got = exchange(out[:n_out])
             out = call(
                 sweep_kernel, [*got, level, f, tab, zt], outgoing(1) + [block, block], [work, pair, tiles], "sweep"
             )
             level, f = out[n_out:]
-        got = exchange(out[:n_out])
+            got = exchange(out[:n_out])
         out = call(
             diagonal_kernel,
             [*got, level, f, tab, zt],

time: 123 us -> 123 us (level)
  waiting for transfers between devices: 37.1 us -> 35.5 us
    ppermute x27, waiting for transfers between devices: 12.4 us -> 10.9 us  [ring(): return lax.ppermute(v, axis, pairs)]
    pallas_call x11 -> x13, Pallas kernels: 16.4 us -> 16.5 us  [call(): pl.pallas_call(kernel, out_shape=outs, in_specs=[hbm if i in from_hbm els...]
  transfers between devices with their start and end apart: 36 -> 36, of which waited for: 27 -> 25; matrix products, arithmetic and copies ran while one was open for 0% -> 0% of each run, Pallas kernels for 0% -> 1%
where the time goes in v3:
time: 123 us; the launch traced here: 122 us
  starting transfers between devices  59.2 us (48%)
  waiting for transfers between devices  35.5 us (29%)
  Pallas kernels  16.5 us (13%)
  blocking collectives  9.31 us (8%)
    ppermute x27, starting transfers between devices, ring(): return lax.ppermute(v, axis, pairs)  31.3 us
    all_to_all x9, starting transfers between devices, exchange(): recv = lax.all_to_all(send, AXES, 0, 0, tiled=True)  27.9 us
    all_to_all x9, waiting for transfers between devices, exchange(): recv = lax.all_to_all(send, AXES, 0, 0, tiled=True)  24.6 us
    pallas_call x13, Pallas kernels, call(): pl.pallas_call(kernel, out_shape=outs, in_specs=[hbm if i in from_hbm els...  16.5 us
    ppermute x27, waiting for transfers between devices, ring(): return lax.ppermute(v, axis, pairs)  10.9 us
    all_to_all x1, blocking collectives, body(): recv = lax.all_to_all(out[0], AXES, 0, 0, tiled=True)  9.31 us
  transfers between devices with their start and end apart: 36, of which 25 were waited for; matrix products, arithmetic and copies ran while one was open for 0% of the time, Pallas kernels for 1%

profile of v3, /device:TPU:0, one launch (start us, length us, event | category | flops | bytes accessed | tf_op | source)
XLA Modules:
  0.0 121.9 jit_solution(492565593514248075)
XLA Ops:
  0.7 2.3 %advect.1 = (f32[32,4,128]{2,1,0:T(4,128)}, f32[16,128]{1,0:T(8,128)S(1)}, f32[16,128]{1,0:T(8,128)S(1)}, f32[16,128]{1,0:T(8,128)S(1)}, f32[256,128]{1,0:T(8,128)S(1)}) custom-call(f32[256,128]{1,0:T(8,128)} %bitcast.7, f32[3,256,128]{2,1,0:T(8,128)} %bitcast.5, f32[224,128]{1,0:T(8,128)} %constant.6.clone.tab_any.tab_ref.rest_5_.rest_7_.rest_9_, ...), custom_call_target="tpu_custom_call" | custom-call | flops 4000000 | bytes 1000000 | tf_op jit(solution)/shard_map/advect/pallas_call | solution.py:636
  2.9 7.3 %all-to-all-start = ((f32[32,4,128]{2,1,0:T(4,128)}), f32[32,4,128]{2,1,0:T(4,128)S(1)}, u32[]{:S(2)}, u32[]{:S(2)}) async-start(f32[32,4,128]{2,1,0:T(4,128)} %get-tuple-element.92), calls=%async_computation | async-start | bytes 131072 | tf_op jit(solution)/shard_map/all_to_all | solution.py:662
  10.3 1.8 %collective-permute-start = (f32[16,128]{1,0:T(8,128)S(1)}, f32[16,128]{1,0:T(8,128)S(1)}, u32[]{:S(2)}, u32[]{:S(2)}) collective-permute-start(f32[16,128]{1,0:T(8,128)S(1)} %get-tuple-element.93), channel_id=1, source_target_pairs={{0,16},{16,0},{1,17},{17,1},{2,18},{18,2},{3,19},{19,3},{4,20},{20... | collective-permute-start | bytes 24584 | tf_op jit(solution)/shard_map/ppermute | solution.py:658
  12.1 1.7 %collective-permute-start.2 = (f32[16,128]{1,0:T(8,128)S(1)}, f32[16,128]{1,0:T(8,128)S(1)}, u32[]{:S(2)}, u32[]{:S(2)}) collective-permute-start(f32[16,128]{1,0:T(8,128)S(1)} %get-tuple-element.95), channel_id=1, source_target_pairs={{0,12},{4,0},{8,4},{12,8},{1,13},{5,1},{9,5},{13,9},{2,14},{6,2},{... | collective-permute-start | bytes 24584 | tf_op jit(solution)/shard_map/ppermute | solution.py:658
  13.9 0.6 copy-done.6
  14.5 0.5 source.1
  15.2 2.5 %all-to-all-done.recv = f32[32,4,128]{2,1,0:T(4,128)S(1)} async-done(((f32[32,4,128]{2,1,0:T(4,128)}), f32[32,4,128]{2,1,0:T(4,128)S(1)}, u32[]{:S(2)}, u32[]{:S(2)}) %all-to-all-start) | async-done | bytes 65568 | tf_op jit(solution)/shard_map/all_to_all | solution.py:662
  17.8 1.5 %sweep_first.1 = (f32[32,8,128]{2,1,0:T(8,128)}, f32[32,128]{1,0:T(8,128)S(1)}, f32[32,128]{1,0:T(8,128)S(1)}, f32[32,128]{1,0:T(8,128)S(1)}, f32[256,128]{1,0:T(8,128)S(1)}, /*index=5*/f32[256,128]{1,0:T(8,128)S(1)}) custom-call(f32[32,4,128]{2,1,0:T(4,128)S(1)} %all-to-all-done.recv, f32[16,128]{1,0:T(8,128)S(1)} %collective-permute-done.rest_0_, ...), custom_call_target="tpu_custom_call" | custom-call | flops 4000000 | bytes 1000000 | tf_op jit(solution)/shard_map/sweep_first/pallas_call | solution.py:636
  19.2 2.6 %all-to-all-start.1 = ((f32[32,8,128]{2,1,0:T(8,128)}), f32[32,8,128]{2,1,0:T(8,128)S(1)}, u32[]{:S(2)}, u32[]{:S(2)}) async-start(f32[32,8,128]{2,1,0:T(8,128)} %get-tuple-element.101), calls=%async_computation.1 | async-start | bytes 262144 | tf_op jit(solution)/shard_map/all_to_all | solution.py:662
  21.8 1.7 %collective-permute-start.3 = (f32[32,128]{1,0:T(8,128)S(1)}, f32[32,128]{1,0:T(8,128)S(1)}, u32[]{:S(2)}, u32[]{:S(2)}) collective-permute-start(f32[32,128]{1,0:T(8,128)S(1)} %get-tuple-element.102), channel_id=1, source_target_pairs={{0,16},{16,0},{1,17},{17,1},{2,18},{18,2},{3,19},{19,3},{4,20},{20... | collective-permute-start | bytes 49160 | tf_op jit(solution)/shard_map/ppermute | solution.py:658
  23.5 1.7 %collective-permute-start.5 = (f32[32,128]{1,0:T(8,128)S(1)}, f32[32,128]{1,0:T(8,128)S(1)}, u32[]{:S(2)}, u32[]{:S(2)}) collective-permute-start(f32[32,128]{1,0:T(8,128)S(1)} %get-tuple-element.104), channel_id=1, source_target_pairs={{0,12},{4,0},{8,4},{12,8},{1,13},{5,1},{9,5},{13,9},{2,14},{6,2},{... | collective-permute-start | bytes 49160 | tf_op jit(solution)/shard_map/ppermute | solution.py:658
  25.3 0.3 collective-permute-done.3.rest_0_
  25.6 1.2 collective-permute-done.4.rest_1_
  26.8 3.4 %all-to-all-done.1.recv = f32[32,8,128]{2,1,0:T(8,128)S(1)} async-done(((f32[32,8,128]{2,1,0:T(8,128)}), f32[32,8,128]{2,1,0:T(8,128)S(1)}, u32[]{:S(2)}, u32[]{:S(2)}) %all-to-all-start.1) | async-done | bytes 131104 | tf_op jit(solution)/shard_map/all_to_all | solution.py:662
  30.2 1.4 %sweep.1 = (f32[32,4,128]{2,1,0:T(4,128)}, f32[16,128]{1,0:T(8,128)S(1)}, f32[16,128]{1,0:T(8,128)S(1)}, f32[16,128]{1,0:T(8,128)S(1)}, f32[256,128]{1,0:T(8,128)S(1)}, /*index=5*/f32[256,128]{1,0:T(8,128)S(1)}) custom-call(f32[32,8,128]{2,1,0:T(8,128)S(1)} %all-to-all-done.1.recv, f32[32,128]{1,0:T(8,128)S(1)} %collective-permute-done.3.rest_0_, ...), custom_call_target="tpu_custom_call" | custom-call | flops 4000000 | bytes 1000000 | tf_op jit(solution)/shard_map/sweep/pallas_call | solution.py:636
  31.7 2.6 %all-to-all-start.2 = ((f32[32,4,128]{2,1,0:T(4,128)}), f32[32,4,128]{2,1,0:T(4,128)S(1)}, u32[]{:S(2)}, u32[]{:S(2)}) async-start(f32[32,4,128]{2,1,0:T(4,128)} %get-tuple-element.107), calls=%async_computation.2 | async-start | bytes 131072 | tf_op jit(solution)/shard_map/all_to_all | solution.py:662
  34.2 1.7 %collective-permute-start.6 = (f32[16,128]{1,0:T(8,128)S(1)}, f32[16,128]{1,0:T(8,128)S(1)}, u32[]{:S(2)}, u32[]{:S(2)}) collective-permute-start(f32[16,128]{1,0:T(8,128)S(1)} %get-tuple-element.108), channel_id=1, source_target_pairs={{0,16},{16,0},{1,17},{17,1},{2,18},{18,2},{3,19},{19,3},{4,20},{20... | collective-permute-start | bytes 24584 | tf_op jit(solution)/shard_map/ppermute | solution.py:658
  36.0 1.7 %collective-permute-start.8 = (f32[16,128]{1,0:T(8,128)S(1)}, f32[16,128]{1,0:T(8,128)S(1)}, u32[]{:S(2)}, u32[]{:S(2)}) collective-permute-start(f32[16,128]{1,0:T(8,128)S(1)} %get-tuple-element.110), channel_id=1, source_target_pairs={{0,12},{4,0},{8,4},{12,8},{1,13},{5,1},{9,5},{13,9},{2,14},{6,2},{... | collective-permute-start | bytes 24584 | tf_op jit(solution)/shard_map/ppermute | solution.py:658
  37.7 0.3 collective-permute-done.6.rest_0_
  38.0 1.1 collective-permute-done.7.rest_1_
  39.1 2.7 %all-to-all-done.2.recv = f32[32,4,128]{2,1,0:T(4,128)S(1)} async-done(((f32[32,4,128]{2,1,0:T(4,128)}), f32[32,4,128]{2,1,0:T(4,128)S(1)}, u32[]{:S(2)}, u32[]{:S(2)}) %all-to-all-start.2) | async-done | bytes 65568 | tf_op jit(solution)/shard_map/all_to_all | solution.py:662
  41.7 1.3 %diagonal.1 = (f32[32,4,128]{2,1,0:T(4,128)}, f32[16,128]{1,0:T(8,128)S(1)}, f32[16,128]{1,0:T(8,128)S(1)}, f32[16,128]{1,0:T(8,128)S(1)}, f32[256,128]{1,0:T(8,...) custom-call(f32[32,4,128]{2,1,0:T(4,128)S(1)} %all-to-all-done.2.recv, ...), custom_call_target="tpu_custom_call" | custom-call | flops 4000000 | bytes 1000000 | tf_op jit(solution)/shard_map/diagonal/pallas_call | solution.py:636
  43.0 2.6 %all-to-all-start.3 = ((f32[32,4,128]{2,1,0:T(4,128)}), f32[32,4,128]{2,1,0:T(4,128)S(1)}, u32[]{:S(2)}, u32[]{:S(2)}) async-start(f32[32,4,128]{2,1,0:T(4,128)} %get-tuple-element.114), calls=%async_computation.3 | async-start | bytes 131072 | tf_op jit(solution)/shard_map/all_to_all | solution.py:662
  45.6 1.7 %collective-permute-start.9 = (f32[16,128]{1,0:T(8,128)S(1)}, f32[16,128]{1,0:T(8,128)S(1)}, u32[]{:S(2)}, u32[]{:S(2)}) collective-permute-start(f32[16,128]{1,0:T(8,128)S(1)} %get-tuple-element.115), channel_id=1, source_target_pairs={{0,16},{16,0},{1,17},{17,1},{2,18},{18,2},{3,19},{19,3},{4,20},{20... | collective-permute-start | bytes 24584 | tf_op jit(solution)/shard_map/ppermute | solution.py:658
  47.3 1.7 %collective-permute-start.11 = (f32[16,128]{1,0:T(8,128)S(1)}, f32[16,128]{1,0:T(8,128)S(1)}, u32[]{:S(2)}, u32[]{:S(2)}) collective-permute-start(f32[16,128]{1,0:T(8,128)S(1)} %get-tuple-element.117), channel_id=1, source_target_pairs={{0,12},{4,0},{8,4},{12,8},{1,13},{5,1},{9,5},{13,9},{2,14},{6,2},{... | collective-permute-start | bytes 24584 | tf_op jit(solution)/shard_map/ppermute | solution.py:658
  49.1 0.4 rhs.1
  49.5 0.9 collective-permute-done.10.rest_1_
  50.5 2.7 %all-to-all-done.3.recv = f32[32,4,128]{2,1,0:T(4,128)S(1)} async-done(((f32[32,4,128]{2,1,0:T(4,128)}), f32[32,4,128]{2,1,0:T(4,128)S(1)}, u32[]{:S(2)}, u32[]{:S(2)}) %all-to-all-start.3) | async-done | bytes 65568 | tf_op jit(solution)/shard_map/all_to_all | solution.py:662
  53.1 1.5 %solve_start.1 = (f32[32,4,128]{2,1,0:T(4,128)}, f32[16,128]{1,0:T(8,128)S(1)}, f32[16,128]{1,0:T(8,128)S(1)}, f32[16,128]{1,0:T(8,128)S(1)}, f32[256,128]{1,0:T...) custom-call(f32[32,4,128]{2,1,0:T(4,128)S(1)} %all-to-all-done.3.recv, ...), custom_call_target="tpu_custom_call" | custom-call | flops 4000000 | bytes 1000000 | tf_op jit(solution)/shard_map/solve_start/pallas_call | solution.py:636
  54.6 2.6 %all-to-all-start.4 = ((f32[32,4,128]{2,1,0:T(4,128)}), f32[32,4,128]{2,1,0:T(4,128)S(1)}, u32[]{:S(2)}, u32[]{:S(2)}) async-start(f32[32,4,128]{2,1,0:T(4,128)} %get-tuple-element.125), calls=%async_computation.4 | async-start | bytes 131072 | tf_op jit(solution)/shard_map/all_to_all | solution.py:662
  57.2 1.7 %collective-permute-start.12 = (f32[16,128]{1,0:T(8,128)S(1)}, f32[16,128]{1,0:T(8,128)S(1)}, u32[]{:S(2)}, u32[]{:S(2)}) collective-permute-start(f32[16,128]{1,0:T(8,128)S(1)} %get-tuple-element.126), channel_id=1, source_target_pairs={{0,16},{16,0},{1,17},{17,1},{2,18},{18,2},{3,19},{19,3},{4,20},{20... | collective-permute-start | bytes 24584 | tf_op jit(solution)/shard_map/ppermute | solution.py:658
  58.9 1.7 %collective-permute-start.14 = (f32[16,128]{1,0:T(8,128)S(1)}, f32[16,128]{1,0:T(8,128)S(1)}, u32[]{:S(2)}, u32[]{:S(2)}) collective-permute-start(f32[16,128]{1,0:T(8,128)S(1)} %get-tuple-element.128), channel_id=1, source_target_pairs={{0,12},{4,0},{8,4},{12,8},{1,13},{5,1},{9,5},{13,9},{2,14},{6,2},{... | collective-permute-start | bytes 24584 | tf_op jit(solution)/shard_map/ppermute | solution.py:658
  60.7 0.3 collective-permute-done.12.rest_0_
  60.9 1.1 collective-permute-done.13.rest_1_
  62.0 2.7 %all-to-all-done.4.recv = f32[32,4,128]{2,1,0:T(4,128)S(1)} async-done(((f32[32,4,128]{2,1,0:T(4,128)}), f32[32,4,128]{2,1,0:T(4,128)S(1)}, u32[]{:S(2)}, u32[]{:S(2)}) %all-to-all-start.4) | async-done | bytes 65568 | tf_op jit(solution)/shard_map/all_to_all | solution.py:662
  64.7 1.5 %iterate.5 = (f32[32,4,128]{2,1,0:T(4,128)}, f32[16,128]{1,0:T(8,128)S(1)}, f32[16,128]{1,0:T(8,128)S(1)}, f32[16,128]{1,0:T(8,128)S(1)}, f32[256,128]{1,0:T(8,1...) custom-call(f32[32,4,128]{2,1,0:T(4,128)S(1)} %all-to-all-done.4.rec, ...), custom_call_target="tpu_custom_call" | custom-call | flops 4000000 | bytes 1000000 | tf_op jit(solution)/shard_map/iterate/pallas_call | solution.py:636
  66.3 2.6 %all-to-all-start.5 = ((f32[32,4,128]{2,1,0:T(4,128)}), f32[32,4,128]{2,1,0:T(4,128)S(1)}, u32[]{:S(2)}, u32[]{:S(2)}) async-start(f32[32,4,128]{2,1,0:T(4,128)} %get-tuple-element.133), calls=%async_computation.5 | async-start | bytes 131072 | tf_op jit(solution)/shard_map/all_to_all | solution.py:662
  68.8 1.7 %collective-permute-start.15 = (f32[16,128]{1,0:T(8,128)S(1)}, f32[16,128]{1,0:T(8,128)S(1)}, u32[]{:S(2)}, u32[]{:S(2)}) collective-permute-start(f32[16,128]{1,0:T(8,128)S(1)} %get-tuple-element.134), channel_id=1, source_target_pairs={{0,16},{16,0},{1,17},{17,1},{2,18},{18,2},{3,19},{19,3},{4,20},{20... | collective-permute-start | bytes 24584 | tf_op jit(solution)/shard_map/ppermute | solution.py:658
  70.6 1.7 %collective-permute-start.17 = (f32[16,128]{1,0:T(8,128)S(1)}, f32[16,128]{1,0:T(8,128)S(1)}, u32[]{:S(2)}, u32[]{:S(2)}) collective-permute-start(f32[16,128]{1,0:T(8,128)S(1)} %get-tuple-element.136), channel_id=1, source_target_pairs={{0,12},{4,0},{8,4},{12,8},{1,13},{5,1},{9,5},{13,9},{2,14},{6,2},{... | collective-permute-start | bytes 24584 | tf_op jit(solution)/shard_map/ppermute | solution.py:658
  72.3 0.3 collective-permute-done.15.rest_0_
  72.6 1.1 collective-permute-done.16.rest_1_
  73.7 2.7 %all-to-all-done.5.recv = f32[32,4,128]{2,1,0:T(4,128)S(1)} async-done(((f32[32,4,128]{2,1,0:T(4,128)}), f32[32,4,128]{2,1,0:T(4,128)S(1)}, u32[]{:S(2)}, u32[]{:S(2)}) %all-to-all-start.5) | async-done | bytes 65568 | tf_op jit(solution)/shard_map/all_to_all | solution.py:662
  76.3 1.5 %iterate.6 = (f32[32,4,128]{2,1,0:T(4,128)}, f32[16,128]{1,0:T(8,128)S(1)}, f32[16,128]{1,0:T(8,128)S(1)}, f32[16,128]{1,0:T(8,128)S(1)}, f32[256,128]{1,0:T(8,1...) custom-call(f32[32,4,128]{2,1,0:T(4,128)S(1)} %all-to-all-done.5.rec, ...), custom_call_target="tpu_custom_call" | custom-call | flops 4000000 | bytes 1000000 | tf_op jit(solution)/shard_map/iterate/pallas_call | solution.py:636
  77.9 2.6 %all-to-all-start.6 = ((f32[32,4,128]{2,1,0:T(4,128)}), f32[32,4,128]{2,1,0:T(4,128)S(1)}, u32[]{:S(2)}, u32[]{:S(2)}) async-start(f32[32,4,128]{2,1,0:T(4,128)} %get-tuple-element.144), calls=%async_computation.6 | async-start | bytes 131072 | tf_op jit(solution)/shard_map/all_to_all | solution.py:662
  80.4 1.7 %collective-permute-start.18 = (f32[16,128]{1,0:T(8,128)S(1)}, f32[16,128]{1,0:T(8,128)S(1)}, u32[]{:S(2)}, u32[]{:S(2)}) collective-permute-start(f32[16,128]{1,0:T(8,128)S(1)} %get-tuple-element.145), channel_id=1, source_target_pairs={{0,16},{16,0},{1,17},{17,1},{2,18},{18,2},{3,19},{19,3},{4,20},{20... | collective-permute-start | bytes 24584 | tf_op jit(solution)/shard_map/ppermute | solution.py:658
  82.2 1.7 %collective-permute-start.20 = (f32[16,128]{1,0:T(8,128)S(1)}, f32[16,128]{1,0:T(8,128)S(1)}, u32[]{:S(2)}, u32[]{:S(2)}) collective-permute-start(f32[16,128]{1,0:T(8,128)S(1)} %get-tuple-element.147), channel_id=1, source_target_pairs={{0,12},{4,0},{8,4},{12,8},{1,13},{5,1},{9,5},{13,9},{2,14},{6,2},{... | collective-permute-start | bytes 24584 | tf_op jit(solution)/shard_map/ppermute | solution.py:658
  83.9 0.3 collective-permute-done.18.rest_0_
  84.2 1.1 collective-permute-done.19.rest_1_
  85.3 2.7 %all-to-all-done.6.recv = f32[32,4,128]{2,1,0:T(4,128)S(1)} async-done(((f32[32,4,128]{2,1,0:T(4,128)}), f32[32,4,128]{2,1,0:T(4,128)S(1)}, u32[]{:S(2)}, u32[]{:S(2)}) %all-to-all-start.6) | async-done | bytes 65568 | tf_op jit(solution)/shard_map/all_to_all | solution.py:662
  87.9 1.5 %iterate.7 = (f32[32,4,128]{2,1,0:T(4,128)}, f32[16,128]{1,0:T(8,128)S(1)}, f32[16,128]{1,0:T(8,128)S(1)}, f32[16,128]{1,0:T(8,128)S(1)}, f32[256,128]{1,0:T(8,1...) custom-call(f32[32,4,128]{2,1,0:T(4,128)S(1)} %all-to-all-done.6.rec, ...), custom_call_target="tpu_custom_call" | custom-call | flops 4000000 | bytes 1000000 | tf_op jit(solution)/shard_map/iterate/pallas_call | solution.py:636
  89.5 2.6 %all-to-all-start.7 = ((f32[32,4,128]{2,1,0:T(4,128)}), f32[32,4,128]{2,1,0:T(4,128)S(1)}, u32[]{:S(2)}, u32[]{:S(2)}) async-start(f32[32,4,128]{2,1,0:T(4,128)} %get-tuple-element.155), calls=%async_computation.7 | async-start | bytes 131072 | tf_op jit(solution)/shard_map/all_to_all | solution.py:662
  92.1 1.7 %collective-permute-start.21 = (f32[16,128]{1,0:T(8,128)S(1)}, f32[16,128]{1,0:T(8,128)S(1)}, u32[]{:S(2)}, u32[]{:S(2)}) collective-permute-start(f32[16,128]{1,0:T(8,128)S(1)} %get-tuple-element.156), channel_id=1, source_target_pairs={{0,16},{16,0},{1,17},{17,1},{2,18},{18,2},{3,19},{19,3},{4,20},{20... | collective-permute-start | bytes 24584 | tf_op jit(solution)/shard_map/ppermute | solution.py:658
  93.8 1.7 %collective-permute-start.23 = (f32[16,128]{1,0:T(8,128)S(1)}, f32[16,128]{1,0:T(8,128)S(1)}, u32[]{:S(2)}, u32[]{:S(2)}) collective-permute-start(f32[16,128]{1,0:T(8,128)S(1)} %get-tuple-element.158), channel_id=1, source_target_pairs={{0,12},{4,0},{8,4},{12,8},{1,13},{5,1},{9,5},{13,9},{2,14},{6,2},{... | collective-permute-start | bytes 24584 | tf_op jit(solution)/shard_map/ppermute | solution.py:658
  95.8 1.1 collective-permute-done.22.rest_1_
  96.9 2.7 %all-to-all-done.7.recv = f32[32,4,128]{2,1,0:T(4,128)S(1)} async-done(((f32[32,4,128]{2,1,0:T(4,128)}), f32[32,4,128]{2,1,0:T(4,128)S(1)}, u32[]{:S(2)}, u32[]{:S(2)}) %all-to-all-start.7) | async-done | bytes 65568 | tf_op jit(solution)/shard_map/all_to_all | solution.py:662
  99.6 1.5 %iterate.8 = (f32[32,4,128]{2,1,0:T(4,128)}, f32[16,128]{1,0:T(8,128)S(1)}, f32[16,128]{1,0:T(8,128)S(1)}, f32[16,128]{1,0:T(8,128)S(1)}, f32[256,128]{1,0:T(8,1...) custom-call(f32[32,4,128]{2,1,0:T(4,128)S(1)} %all-to-all-done.7.rec, ...), custom_call_target="tpu_custom_call" | custom-call | flops 4000000 | bytes 1000000 | tf_op jit(solution)/shard_map/iterate/pallas_call | solution.py:636
  101.1 2.6 %all-to-all-start.8 = ((f32[32,4,128]{2,1,0:T(4,128)}), f32[32,4,128]{2,1,0:T(4,128)S(1)}, u32[]{:S(2)}, u32[]{:S(2)}) async-start(f32[32,4,128]{2,1,0:T(4,128)} %get-tuple-element.166), calls=%async_computation.8 | async-start | bytes 131072 | tf_op jit(solution)/shard_map/all_to_all | solution.py:662
  103.7 1.7 %collective-permute-start.24 = (f32[16,128]{1,0:T(8,128)S(1)}, f32[16,128]{1,0:T(8,128)S(1)}, u32[]{:S(2)}, u32[]{:S(2)}) collective-permute-start(f32[16,128]{1,0:T(8,128)S(1)} %get-tuple-element.167), channel_id=1, source_target_pairs={{0,16},{16,0},{1,17},{17,1},{2,18},{18,2},{3,19},{19,3},{4,20},{20... | collective-permute-start | bytes 24584 | tf_op jit(solution)/shard_map/ppermute | solution.py:658
  105.4 1.7 %collective-permute-start.26 = (f32[16,128]{1,0:T(8,128)S(1)}, f32[16,128]{1,0:T(8,128)S(1)}, u32[]{:S(2)}, u32[]{:S(2)}) collective-permute-start(f32[16,128]{1,0:T(8,128)S(1)} %get-tuple-element.169), channel_id=1, source_target_pairs={{0,12},{4,0},{8,4},{12,8},{1,13},{5,1},{9,5},{13,9},{2,14},{6,2},{... | collective-permute-start | bytes 24584 | tf_op jit(solution)/shard_map/ppermute | solution.py:658
  107.4 1.1 collective-permute-done.25.rest_1_
  108.5 2.7 %all-to-all-done.8.recv = f32[32,4,128]{2,1,0:T(4,128)S(1)} async-done(((f32[32,4,128]{2,1,0:T(4,128)}), f32[32,4,128]{2,1,0:T(4,128)S(1)}, u32[]{:S(2)}, u32[]{:S(2)}) %all-to-all-start.8) | async-done | bytes 65568 | tf_op jit(solution)/shard_map/all_to_all | solution.py:662
  111.2 0.7 iterate.9
  111.8 9.3 %all_to_all.50.recv = f32[32,1,128]{2,1,0:T(1,128)S(1)} all-to-all(f32[32,1,128]{2,1,0:T(1,128)S(1)} %get-tuple-element.177), channel_id=1, replica_groups=mesh['gx'=2,'gy'=4,'gz'=4] {'gx','gy','gz'}, dimensions={0} | all-to-all | bytes 32768 | tf_op jit(solution)/shard_map/all_to_all | solution.py:948
  121.1 0.8 pressure.1
  (36 shorter events, 1.0 us)
Async XLA Ops:
  0.6 13.2 %copy-start = (bf16[768,256]{1,0:T(8,128)(2,1)S(1)}, bf16[768,256]{1,0:T(8,128)(2,1)}, u32[]{:S(2)}) copy-start(bf16[768,256]{1,0:T(8,128)(2,1)} %constant.7.clone.zt_any.zt_ref.rest_6_.rest_8_.rest_10_) | copy-start | bytes 1179652
  0.6 13.2 %copy-start.2 = (f32[3,16,16,128]{3,2,1,0:T(8,128)S(1)}, f32[3,16,16,128]{3,2,1,0:T(8,128)}, u32[]{:S(2)}) copy-start(f32[3,16,16,128]{3,2,1,0:T(8,128)} %param.8) | copy-start | bytes 1179652
  0.7 13.2 %copy-start.4 = (f32[16,16,128]{2,1,0:T(8,128)S(1)}, f32[16,16,128]{2,1,0:T(8,128)}, u32[]{:S(2)}) copy-start(f32[16,16,128]{2,1,0:T(8,128)} %param.9) | copy-start | bytes 393220
  2.9 10.9 %copy-start.1 = (f32[224,128]{1,0:T(8,128)S(1)}, f32[224,128]{1,0:T(8,128)}, u32[]{:S(2)}) copy-start(f32[224,128]{1,0:T(8,128)} %constant.6.clone.tab_any.tab_ref.rest_5_.rest_7_.rest_9_) | copy-start | bytes 344068
  2.9 14.8 %all-to-all-start = ((f32[32,4,128]{2,1,0:T(4,128)}), f32[32,4,128]{2,1,0:T(4,128)S(1)}, u32[]{:S(2)}, u32[]{:S(2)}) async-start(f32[32,4,128]{2,1,0:T(4,128)} %get-tuple-element.92), calls=%async_computation | async-start | bytes 131072 | tf_op jit(solution)/shard_map/all_to_all | solution.py:662
  10.3 3.6 %copy-start.5 = (f32[8,128]{1,0:T(8,128)S(1)}, f32[8,128]{1,0:T(8,128)}, u32[]{:S(2)}) copy-start(f32[8,128]{1,0:T(8,128)} %constant.8.clone.places_ref) | copy-start | bytes 12292
  10.3 4.7 %collective-permute-start = (f32[16,128]{1,0:T(8,128)S(1)}, f32[16,128]{1,0:T(8,128)S(1)}, u32[]{:S(2)}, u32[]{:S(2)}) collective-permute-start(f32[16,128]{1,0:T(8,128)S(1)} %get-tuple-element.93), channel_id=1, source_target_pairs={{0,16},{16,0},{1,17},{17,1},{2,18},{18,2},{3,19},{19,3},{4,20},{20... | collective-permute-start | bytes 24584 | tf_op jit(solution)/shard_map/ppermute | solution.py:658
  12.1 3.1 %collective-permute-start.1 = (f32[16,128]{1,0:T(8,128)S(1)}, f32[16,128]{1,0:T(8,128)S(1)}, u32[]{:S(2)}, u32[]{:S(2)}) collective-permute-start(f32[16,128]{1,0:T(8,128)S(1)} %get-tuple-element.94), channel_id=1, source_target_pairs={{0,4},{4,8},{8,12},{12,0},{1,5},{5,9},{9,13},{13,1},{2,6},{6,10},{... | collective-permute-start | bytes 24584 | tf_op jit(solution)/shard_map/ppermute | solution.py:658
  12.1 3.1 %collective-permute-start.2 = (f32[16,128]{1,0:T(8,128)S(1)}, f32[16,128]{1,0:T(8,128)S(1)}, u32[]{:S(2)}, u32[]{:S(2)}) collective-permute-start(f32[16,128]{1,0:T(8,128)S(1)} %get-tuple-element.95), channel_id=1, source_target_pairs={{0,12},{4,0},{8,4},{12,8},{1,13},{5,1},{9,5},{13,9},{2,14},{6,2},{... | collective-permute-start | bytes 24584 | tf_op jit(solution)/shard_map/ppermute | solution.py:658
  13.9 0.7 copy-start.6
  14.5 3.2 %copy-start.3 = (f32[16,16,128]{2,1,0:T(8,128)S(1)}, f32[16,16,128]{2,1,0:T(8,128)}, u32[]{:S(2)}) copy-start(f32[16,16,128]{2,1,0:T(8,128)} %param.7) | copy-start | bytes 393220
  19.2 11.0 %all-to-all-start.1 = ((f32[32,8,128]{2,1,0:T(8,128)}), f32[32,8,128]{2,1,0:T(8,128)S(1)}, u32[]{:S(2)}, u32[]{:S(2)}) async-start(f32[32,8,128]{2,1,0:T(8,128)} %get-tuple-element.101), calls=%async_computation.1 | async-start | bytes 262144 | tf_op jit(solution)/shard_map/all_to_all | solution.py:662
  21.8 3.8 %collective-permute-start.3 = (f32[32,128]{1,0:T(8,128)S(1)}, f32[32,128]{1,0:T(8,128)S(1)}, u32[]{:S(2)}, u32[]{:S(2)}) collective-permute-start(f32[32,128]{1,0:T(8,128)S(1)} %get-tuple-element.102), channel_id=1, source_target_pairs={{0,16},{16,0},{1,17},{17,1},{2,18},{18,2},{3,19},{19,3},{4,20},{20... | collective-permute-start | bytes 49160 | tf_op jit(solution)/shard_map/ppermute | solution.py:658
  23.5 3.2 %collective-permute-start.4 = (f32[32,128]{1,0:T(8,128)S(1)}, f32[32,128]{1,0:T(8,128)S(1)}, u32[]{:S(2)}, u32[]{:S(2)}) collective-permute-start(f32[32,128]{1,0:T(8,128)S(1)} %get-tuple-element.103), channel_id=1, source_target_pairs={{0,4},{4,8},{8,12},{12,0},{1,5},{5,9},{9,13},{13,1},{2,6},{6,10},{... | collective-permute-start | bytes 49160 | tf_op jit(solution)/shard_map/ppermute | solution.py:658
  23.5 3.2 %collective-permute-start.5 = (f32[32,128]{1,0:T(8,128)S(1)}, f32[32,128]{1,0:T(8,128)S(1)}, u32[]{:S(2)}, u32[]{:S(2)}) collective-permute-start(f32[32,128]{1,0:T(8,128)S(1)} %get-tuple-element.104), channel_id=1, source_target_pairs={{0,12},{4,0},{8,4},{12,8},{1,13},{5,1},{9,5},{13,9},{2,14},{6,2},{... | collective-permute-start | bytes 49160 | tf_op jit(solution)/shard_map/ppermute | solution.py:658
  31.7 10.1 %all-to-all-start.2 = ((f32[32,4,128]{2,1,0:T(4,128)}), f32[32,4,128]{2,1,0:T(4,128)S(1)}, u32[]{:S(2)}, u32[]{:S(2)}) async-start(f32[32,4,128]{2,1,0:T(4,128)} %get-tuple-element.107), calls=%async_computation.2 | async-start | bytes 131072 | tf_op jit(solution)/shard_map/all_to_all | solution.py:662
  34.2 3.7 %collective-permute-start.6 = (f32[16,128]{1,0:T(8,128)S(1)}, f32[16,128]{1,0:T(8,128)S(1)}, u32[]{:S(2)}, u32[]{:S(2)}) collective-permute-start(f32[16,128]{1,0:T(8,128)S(1)} %get-tuple-element.108), channel_id=1, source_target_pairs={{0,16},{16,0},{1,17},{17,1},{2,18},{18,2},{3,19},{19,3},{4,20},{20... | collective-permute-start | bytes 24584 | tf_op jit(solution)/shard_map/ppermute | solution.py:658
  36.0 3.1 %collective-permute-start.7 = (f32[16,128]{1,0:T(8,128)S(1)}, f32[16,128]{1,0:T(8,128)S(1)}, u32[]{:S(2)}, u32[]{:S(2)}) collective-permute-start(f32[16,128]{1,0:T(8,128)S(1)} %get-tuple-element.109), channel_id=1, source_target_pairs={{0,4},{4,8},{8,12},{12,0},{1,5},{5,9},{9,13},{13,1},{2,6},{6,10},{... | collective-permute-start | bytes 24584 | tf_op jit(solution)/shard_map/ppermute | solution.py:658
  36.0 3.1 %collective-permute-start.8 = (f32[16,128]{1,0:T(8,128)S(1)}, f32[16,128]{1,0:T(8,128)S(1)}, u32[]{:S(2)}, u32[]{:S(2)}) collective-permute-start(f32[16,128]{1,0:T(8,128)S(1)} %get-tuple-element.110), channel_id=1, source_target_pairs={{0,12},{4,0},{8,4},{12,8},{1,13},{5,1},{9,5},{13,9},{2,14},{6,2},{... | collective-permute-start | bytes 24584 | tf_op jit(solution)/shard_map/ppermute | solution.py:658
  43.0 10.1 %all-to-all-start.3 = ((f32[32,4,128]{2,1,0:T(4,128)}), f32[32,4,128]{2,1,0:T(4,128)S(1)}, u32[]{:S(2)}, u32[]{:S(2)}) async-start(f32[32,4,128]{2,1,0:T(4,128)} %get-tuple-element.114), calls=%async_computation.3 | async-start | bytes 131072 | tf_op jit(solution)/shard_map/all_to_all | solution.py:662
  45.6 3.9 %collective-permute-start.9 = (f32[16,128]{1,0:T(8,128)S(1)}, f32[16,128]{1,0:T(8,128)S(1)}, u32[]{:S(2)}, u32[]{:S(2)}) collective-permute-start(f32[16,128]{1,0:T(8,128)S(1)} %get-tuple-element.115), channel_id=1, source_target_pairs={{0,16},{16,0},{1,17},{17,1},{2,18},{18,2},{3,19},{19,3},{4,20},{20... | collective-permute-start | bytes 24584 | tf_op jit(solution)/shard_map/ppermute | solution.py:658
  47.3 3.1 %collective-permute-start.10 = (f32[16,128]{1,0:T(8,128)S(1)}, f32[16,128]{1,0:T(8,128)S(1)}, u32[]{:S(2)}, u32[]{:S(2)}) collective-permute-start(f32[16,128]{1,0:T(8,128)S(1)} %get-tuple-element.116), channel_id=1, source_target_pairs={{0,4},{4,8},{8,12},{12,0},{1,5},{5,9},{9,13},{13,1},{2,6},{6,10},{... | collective-permute-start | bytes 24584 | tf_op jit(solution)/shard_map/ppermute | solution.py:658
  47.3 3.1 %collective-permute-start.11 = (f32[16,128]{1,0:T(8,128)S(1)}, f32[16,128]{1,0:T(8,128)S(1)}, u32[]{:S(2)}, u32[]{:S(2)}) collective-permute-start(f32[16,128]{1,0:T(8,128)S(1)} %get-tuple-element.117), channel_id=1, source_target_pairs={{0,12},{4,0},{8,4},{12,8},{1,13},{5,1},{9,5},{13,9},{2,14},{6,2},{... | collective-permute-start | bytes 24584 | tf_op jit(solution)/shard_map/ppermute | solution.py:658
  54.6 10.1 %all-to-all-start.4 = ((f32[32,4,128]{2,1,0:T(4,128)}), f32[32,4,128]{2,1,0:T(4,128)S(1)}, u32[]{:S(2)}, u32[]{:S(2)}) async-start(f32[32,4,128]{2,1,0:T(4,128)} %get-tuple-element.125), calls=%async_computation.4 | async-start | bytes 131072 | tf_op jit(solution)/shard_map/all_to_all | solution.py:662
  57.2 3.7 %collective-permute-start.12 = (f32[16,128]{1,0:T(8,128)S(1)}, f32[16,128]{1,0:T(8,128)S(1)}, u32[]{:S(2)}, u32[]{:S(2)}) collective-permute-start(f32[16,128]{1,0:T(8,128)S(1)} %get-tuple-element.126), channel_id=1, source_target_pairs={{0,16},{16,0},{1,17},{17,1},{2,18},{18,2},{3,19},{19,3},{4,20},{20... | collective-permute-start | bytes 24584 | tf_op jit(solution)/shard_map/ppermute | solution.py:658
  58.9 3.1 %collective-permute-start.13 = (f32[16,128]{1,0:T(8,128)S(1)}, f32[16,128]{1,0:T(8,128)S(1)}, u32[]{:S(2)}, u32[]{:S(2)}) collective-permute-start(f32[16,128]{1,0:T(8,128)S(1)} %get-tuple-element.127), channel_id=1, source_target_pairs={{0,4},{4,8},{8,12},{12,0},{1,5},{5,9},{9,13},{13,1},{2,6},{6,10},{... | collective-permute-start | bytes 24584 | tf_op jit(solution)/shard_map/ppermute | solution.py:658
  58.9 3.1 %collective-permute-start.14 = (f32[16,128]{1,0:T(8,128)S(1)}, f32[16,128]{1,0:T(8,128)S(1)}, u32[]{:S(2)}, u32[]{:S(2)}) collective-permute-start(f32[16,128]{1,0:T(8,128)S(1)} %get-tuple-element.128), channel_id=1, source_target_pairs={{0,12},{4,0},{8,4},{12,8},{1,13},{5,1},{9,5},{13,9},{2,14},{6,2},{... | collective-permute-start | bytes 24584 | tf_op jit(solution)/shard_map/ppermute | solution.py:658
  66.3 10.1 %all-to-all-start.5 = ((f32[32,4,128]{2,1,0:T(4,128)}), f32[32,4,128]{2,1,0:T(4,128)S(1)}, u32[]{:S(2)}, u32[]{:S(2)}) async-start(f32[32,4,128]{2,1,0:T(4,128)} %get-tuple-element.133), calls=%async_computation.5 | async-start | bytes 131072 | tf_op jit(solution)/shard_map/all_to_all | solution.py:662
  68.8 3.7 %collective-permute-start.15 = (f32[16,128]{1,0:T(8,128)S(1)}, f32[16,128]{1,0:T(8,128)S(1)}, u32[]{:S(2)}, u32[]{:S(2)}) collective-permute-start(f32[16,128]{1,0:T(8,128)S(1)} %get-tuple-element.134), channel_id=1, source_target_pairs={{0,16},{16,0},{1,17},{17,1},{2,18},{18,2},{3,19},{19,3},{4,20},{20... | collective-permute-start | bytes 24584 | tf_op jit(solution)/shard_map/ppermute | solution.py:658
  70.5 3.1 %collective-permute-start.16 = (f32[16,128]{1,0:T(8,128)S(1)}, f32[16,128]{1,0:T(8,128)S(1)}, u32[]{:S(2)}, u32[]{:S(2)}) collective-permute-start(f32[16,128]{1,0:T(8,128)S(1)} %get-tuple-element.135), channel_id=1, source_target_pairs={{0,4},{4,8},{8,12},{12,0},{1,5},{5,9},{9,13},{13,1},{2,6},{6,10},{... | collective-permute-start | bytes 24584 | tf_op jit(solution)/shard_map/ppermute | solution.py:658
  70.6 3.1 %collective-permute-start.17 = (f32[16,128]{1,0:T(8,128)S(1)}, f32[16,128]{1,0:T(8,128)S(1)}, u32[]{:S(2)}, u32[]{:S(2)}) collective-permute-start(f32[16,128]{1,0:T(8,128)S(1)} %get-tuple-element.136), channel_id=1, source_target_pairs={{0,12},{4,0},{8,4},{12,8},{1,13},{5,1},{9,5},{13,9},{2,14},{6,2},{... | collective-permute-start | bytes 24584 | tf_op jit(solution)/shard_map/ppermute | solution.py:658
  77.9 10.1 %all-to-all-start.6 = ((f32[32,4,128]{2,1,0:T(4,128)}), f32[32,4,128]{2,1,0:T(4,128)S(1)}, u32[]{:S(2)}, u32[]{:S(2)}) async-start(f32[32,4,128]{2,1,0:T(4,128)} %get-tuple-element.144), calls=%async_computation.6 | async-start | bytes 131072 | tf_op jit(solution)/shard_map/all_to_all | solution.py:662
  80.4 3.7 %collective-permute-start.18 = (f32[16,128]{1,0:T(8,128)S(1)}, f32[16,128]{1,0:T(8,128)S(1)}, u32[]{:S(2)}, u32[]{:S(2)}) collective-permute-start(f32[16,128]{1,0:T(8,128)S(1)} %get-tuple-element.145), channel_id=1, source_target_pairs={{0,16},{16,0},{1,17},{17,1},{2,18},{18,2},{3,19},{19,3},{4,20},{20... | collective-permute-start | bytes 24584 | tf_op jit(solution)/shard_map/ppermute | solution.py:658
  82.2 3.1 %collective-permute-start.19 = (f32[16,128]{1,0:T(8,128)S(1)}, f32[16,128]{1,0:T(8,128)S(1)}, u32[]{:S(2)}, u32[]{:S(2)}) collective-permute-start(f32[16,128]{1,0:T(8,128)S(1)} %get-tuple-element.146), channel_id=1, source_target_pairs={{0,4},{4,8},{8,12},{12,0},{1,5},{5,9},{9,13},{13,1},{2,6},{6,10},{... | collective-permute-start | bytes 24584 | tf_op jit(solution)/shard_map/ppermute | solution.py:658
  82.2 3.1 %collective-permute-start.20 = (f32[16,128]{1,0:T(8,128)S(1)}, f32[16,128]{1,0:T(8,128)S(1)}, u32[]{:S(2)}, u32[]{:S(2)}) collective-permute-start(f32[16,128]{1,0:T(8,128)S(1)} %get-tuple-element.147), channel_id=1, source_target_pairs={{0,12},{4,0},{8,4},{12,8},{1,13},{5,1},{9,5},{13,9},{2,14},{6,2},{... | collective-permute-start | bytes 24584 | tf_op jit(solution)/shard_map/ppermute | solution.py:658
  89.5 10.1 %all-to-all-start.7 = ((f32[32,4,128]{2,1,0:T(4,128)}), f32[32,4,128]{2,1,0:T(4,128)S(1)}, u32[]{:S(2)}, u32[]{:S(2)}) async-start(f32[32,4,128]{2,1,0:T(4,128)} %get-tuple-element.155), calls=%async_computation.7 | async-start | bytes 131072 | tf_op jit(solution)/shard_map/all_to_all | solution.py:662
  92.1 3.7 %collective-permute-start.21 = (f32[16,128]{1,0:T(8,128)S(1)}, f32[16,128]{1,0:T(8,128)S(1)}, u32[]{:S(2)}, u32[]{:S(2)}) collective-permute-start(f32[16,128]{1,0:T(8,128)S(1)} %get-tuple-element.156), channel_id=1, source_target_pairs={{0,16},{16,0},{1,17},{17,1},{2,18},{18,2},{3,19},{19,3},{4,20},{20... | collective-permute-start | bytes 24584 | tf_op jit(solution)/shard_map/ppermute | solution.py:658
  93.8 3.1 %collective-permute-start.22 = (f32[16,128]{1,0:T(8,128)S(1)}, f32[16,128]{1,0:T(8,128)S(1)}, u32[]{:S(2)}, u32[]{:S(2)}) collective-permute-start(f32[16,128]{1,0:T(8,128)S(1)} %get-tuple-element.157), channel_id=1, source_target_pairs={{0,4},{4,8},{8,12},{12,0},{1,5},{5,9},{9,13},{13,1},{2,6},{6,10},{... | collective-permute-start | bytes 24584 | tf_op jit(solution)/shard_map/ppermute | solution.py:658
  93.8 3.1 %collective-permute-start.23 = (f32[16,128]{1,0:T(8,128)S(1)}, f32[16,128]{1,0:T(8,128)S(1)}, u32[]{:S(2)}, u32[]{:S(2)}) collective-permute-start(f32[16,128]{1,0:T(8,128)S(1)} %get-tuple-element.158), channel_id=1, source_target_pairs={{0,12},{4,0},{8,4},{12,8},{1,13},{5,1},{9,5},{13,9},{2,14},{6,2},{... | collective-permute-start | bytes 24584 | tf_op jit(solution)/shard_map/ppermute | solution.py:658
  101.1 10.1 %all-to-all-start.8 = ((f32[32,4,128]{2,1,0:T(4,128)}), f32[32,4,128]{2,1,0:T(4,128)S(1)}, u32[]{:S(2)}, u32[]{:S(2)}) async-start(f32[32,4,128]{2,1,0:T(4,128)} %get-tuple-element.166), calls=%async_computation.8 | async-start | bytes 131072 | tf_op jit(solution)/shard_map/all_to_all | solution.py:662
  103.7 3.7 %collective-permute-start.24 = (f32[16,128]{1,0:T(8,128)S(1)}, f32[16,128]{1,0:T(8,128)S(1)}, u32[]{:S(2)}, u32[]{:S(2)}) collective-permute-start(f32[16,128]{1,0:T(8,128)S(1)} %get-tuple-element.167), channel_id=1, source_target_pairs={{0,16},{16,0},{1,17},{17,1},{2,18},{18,2},{3,19},{19,3},{4,20},{20... | collective-permute-start | bytes 24584 | tf_op jit(solution)/shard_map/ppermute | solution.py:658
  105.4 3.1 %collective-permute-start.25 = (f32[16,128]{1,0:T(8,128)S(1)}, f32[16,128]{1,0:T(8,128)S(1)}, u32[]{:S(2)}, u32[]{:S(2)}) collective-permute-start(f32[16,128]{1,0:T(8,128)S(1)} %get-tuple-element.168), channel_id=1, source_target_pairs={{0,4},{4,8},{8,12},{12,0},{1,5},{5,9},{9,13},{13,1},{2,6},{6,10},{... | collective-permute-start | bytes 24584 | tf_op jit(solution)/shard_map/ppermute | solution.py:658
  105.4 3.1 %collective-permute-start.26 = (f32[16,128]{1,0:T(8,128)S(1)}, f32[16,128]{1,0:T(8,128)S(1)}, u32[]{:S(2)}, u32[]{:S(2)}) collective-permute-start(f32[16,128]{1,0:T(8,128)S(1)} %get-tuple-element.169), channel_id=1, source_target_pairs={{0,12},{4,0},{8,4},{12,8},{1,13},{5,1},{9,5},{13,9},{2,14},{6,2},{... | collective-permute-start | bytes 24584 | tf_op jit(solution)/shard_map/ppermute | solution.py:658

commit v4 on v3

--- a/solution.py
+++ b/solution.py
@@ -8,7 +8,6 @@
 from jax.sharding import PartitionSpec as P
 
 NP = 8
-RSWEEPS = 2
 ITERS = 6
 AXES = ("gx", "gy", "gz")
 
@@ -262,11 +261,11 @@
         self.lanes = -(-(self.offset + self.devices) // 128) * 128
         self.scalar_rows = self.lanes // 128
 
-    def slot_rows(self, fields):
-        need = self.scalar_rows + 2 * fields
-        if fields == 2:
-            need += self.scalar_rows
-        return 4 if need <= 4 else -(-need // 8) * 8
+        need = 2 * self.scalar_rows + 2
+        self.slot_rows = 4 if need <= 4 else -(-need // 8) * 8
+
+    def field_rows(self, k):
+        return (0, self.scalar_rows + 2) if k else (self.scalar_rows, self.scalar_rows + 1)
 
 
 def pick_faces(geo, axis, n, low, high):
@@ -324,36 +323,36 @@
     return tile
 
 
-def send_fields(geo, lay, f_ref, z, work, scalars, send_ref, xs, ys, fields=1, extra=None):
-    rows = lay.slot_rows(fields)
+def send_field(geo, lay, f_ref, z, work, scalars, send_ref, xs, ys, extra=None):
+    rows = lay.slot_rows
     base = [scalars[:, i * 128 : (i + 1) * 128] for i in range(lay.scalar_rows)]
-    used = lay.scalar_rows
+    base.append(jnp.zeros((2, 128), F32))
     if extra is not None:
-        base.append(jnp.zeros((2 * fields, 128), F32))
         base += [extra[:, i * 128 : (i + 1) * 128] for i in range(lay.scalar_rows)]
-        used += 2 * fields + lay.scalar_rows
-    base.append(jnp.zeros((rows - used, 128), F32))
-    base = jnp.concatenate([b for b in base if b.shape[0]], axis=0)
+    used = sum(b.shape[0] for b in base)
+    if used < rows:
+        base.append(jnp.zeros((rows - used, 128), F32))
+    base = jnp.concatenate(base, axis=0)
     send_ref[...] = jnp.broadcast_to(base[None], (lay.devices, rows, 128))
-    fill_field(geo, lay, f_ref, z, work, send_ref, fields - 1)
+    fill_field(geo, lay, f_ref, z, work, send_ref, 0)
     fill_faces(geo, lay, f_ref, xs, ys)
     send_ref[geo.me] = base
 
 
 def fill_field(geo, lay, f_ref, z, work, send_ref, k):
-    at = lay.scalar_rows + 2 * k
+    row0, row1 = lay.field_rows(k)
     pairs = pack_z_faces(z, work)
     for dz in (-1, 1):
         pair = pairs[0 if dz < 0 else 1]
         for dx in (-1, 0, 1):
             for dy in (-1, 0, 1):
                 there = geo.neighbour(dx, dy, dz)
-                send_ref[there, at : at + 1, :] = pair[0]
-                send_ref[there, at + 1 : at + 2, :] = pair[1]
+                send_ref[there, row0 : row0 + 1, :] = pair[0]
+                send_ref[there, row1 : row1 + 1, :] = pair[1]
     for dx in (-1, 1):
         for dy in (-1, 1):
             row = (BX - 1 if dx > 0 else 0) * BY + (BY - 1 if dy > 0 else 0)
-            send_ref[geo.neighbour(dx, dy, 0), at : at + 1, :] = f_ref[row : row + 1, :]
+            send_ref[geo.neighbour(dx, dy, 0), row0 : row0 + 1, :] = f_ref[row : row + 1, :]
 
 
 def fill_faces(geo, lay, f_ref, xs, ys):
@@ -379,7 +378,7 @@
 
 
 def received(geo, lay, f, recv_ref, xs, ys, w_ref, k):
-    at = lay.scalar_rows + 2 * k
+    at = lay.field_rows(k)
     line = lax.broadcasted_iota(jnp.int32, (1, BZ), 1)
     sides = []
     for dz in (-1, 1):
@@ -389,7 +388,7 @@
             for dy in (0, 1 if r else -1):
                 for dx in (0, -1, 1):
                     source = 1 - r if dy else r
-                    part = recv_ref[geo.neighbour(dx, dy, dz), at + source : at + source + 1, :]
+                    part = recv_ref[geo.neighbour(dx, dy, dz), at[source] : at[source] + 1, :]
                     keep = None
                     if dx:
                         keep = line % 64 >= 60 if dx > 0 else line % 64 < 4
@@ -421,7 +420,7 @@
     for dx in (-1, 1):
         for dy in (-1, 1):
             row = (BX - 1 if dx > 0 else 0) * BY + (BY - 1 if dy > 0 else 0)
-            w_ref[row : row + 1, :] += recv_ref[geo.neighbour(dx, dy, 0), at : at + 1, :]
+            w_ref[row : row + 1, :] += recv_ref[geo.neighbour(dx, dy, 0), at[0] : at[0] + 1, :]
 
 
 def received_scalars(lay, recv_ref):
@@ -585,7 +584,7 @@
     scalars = partial_sums(geo, local, sums, q_ref, hot)
     local = local_sum_xy(local)
     f_ref[...] = local_sum_z(local)
-    send_fields(geo, lay, f_ref, local, zwork, scalars, send_ref, xs, ys)
+    send_field(geo, lay, f_ref, local, zwork, scalars, send_ref, xs, ys)
 
 
 def step_sizes(lay, recv_ref, state_ref, first):
@@ -624,7 +623,7 @@
 
     def outgoing(fields):
         return (
-            [like(lay.devices, lay.slot_rows(fields), 128)]
+            [like(lay.devices, lay.slot_rows, 128)]
             + [like(BY * fields, BZ)] * nx
             + [like(BX * fields, BZ)] * ny
         )
@@ -689,56 +688,55 @@
         advect = bmass_of(tab_ref) * (vel_ref[0] * gx + vel_ref[1] * gy + vel_ref[2] * gz)
         finish(geo, advect, f_ref, zwork, send, xs, ys)
 
-    def finish(geo, v, f_ref, zwork, send, xs, ys):
+    def finish(geo, v, f_ref, zwork, send, xs, ys, scalars=None, extra=None):
         v = local_sum_xy(v)
         f_ref[...] = local_sum_z(v)
-        nothing = jnp.zeros((1, lay.lanes), F32)
-        send_fields(geo, lay, f_ref, v, zwork, nothing, send, xs, ys)
+        if scalars is None:
+            scalars = jnp.zeros((1, lay.lanes), F32)
+        send_field(geo, lay, f_ref, v, zwork, scalars, send, xs, ys, extra)
 
     def source_kernel(vel_ref, source_ref, factor_ref, tab_ref, zt_ref, places_ref, _, *rest):
         slots, xs, ys = split(rest[:n_out])
-        f_ref, hot_ref, q_ref, work, zwork = rest[n_out:]
+        f_ref, hot_ref, row_ref, q_ref, work, zwork = rest[n_out:]
         geo = Geometry(sizes)
         bm = bmass_of(tab_ref)
         div = bm * source_ref[...] + along_x(bm * vel_ref[0], "t")
         div = div + along_y(bm * vel_ref[1], "t", tab_ref, work.at[1])
         div = div + along_z(bm * vel_ref[2], "t", zt_ref)
         hot_ref[...] = coarse_tables(geo, lay, places_ref)
-        scalars = partial_sums(geo, div, [], q_ref, hot_ref)
-        div = local_sum_xy(div)
-        f_ref[...] = local_sum_z(div)
+        row_ref[0:1, :] = partial_sums(geo, div, [], q_ref, hot_ref)
         factor = factor_ref[...]
         if lay.lanes > lay.devices:
             pad = jnp.zeros((1, lay.lanes - lay.devices), F32)
             factor = jnp.concatenate([factor, pad], axis=1)
-        send_fields(geo, lay, f_ref, div, zwork, scalars, slots, xs, ys, 2, factor)
+        row_ref[1:2, :] = factor
+        row_ref[2:8, :] = jnp.zeros((6, lay.lanes), F32)
+        div = local_sum_xy(div)
+        f_ref[...] = local_sum_z(div)
+        slots[...] = jnp.zeros(slots.shape, F32)
+        fill_field(geo, lay, f_ref, div, zwork, slots, 1)
+        slots[geo.me] = jnp.zeros(slots.shape[1:], F32)
+        fill_faces(geo, lay, f_ref, xs, ys)
 
     def first_kernel(recv, *rest):
         xs, ys = rest[:nx], rest[nx : nx + ny]
-        level_ref, fa_ref, tab_ref, zt_ref = rest[nx + ny : nx + ny + 4]
-        slots, sxs, sys = split(rest[nx + ny + 4 : nx + ny + 4 + n_out])
-        out = rest[nx + ny + 4 + n_out :]
+        level_ref, fa_ref, tab_ref, zt_ref, row_ref = rest[nx + ny : nx + ny + 5]
+        out = rest[nx + ny + 5 :]
         send, oxs, oys = split(out[:n_out])
         level_out, f_ref, w_ref, work, zwork = out[n_out:]
         geo = Geometry(sizes)
         received(geo, lay, fa_ref[...], recv, xs, ys, w_ref, 0)
         level = level_ref[...] - TIME_STEP * w_ref[...] * inverse_mass(geo, tab_ref)
         level_out[...] = level
-        v = local_sum_xy(weak_form(level, tab_ref, zt_ref, work))
-        f_ref[...] = local_sum_z(v)
-        send[...] = slots[...]
-        fill_field(geo, lay, f_ref, v, zwork, send, 0)
-        send[geo.me] = slots[geo.me]
-        fill_faces(geo, lay, f_ref, oxs, oys)
-        for to, part in zip((*oxs, *oys), (*sxs, *sys)):
-            to[BY : 2 * BY, :] = part[...]
+        weak = weak_form(level, tab_ref, zt_ref, work)
+        finish(geo, weak, f_ref, zwork, send, oxs, oys, row_ref[0:1, :], row_ref[1:2, :])
 
     def rhs_kernel(recv, *rest):
         xs, ys = rest[:nx], rest[nx : nx + ny]
-        fd_ref, hot_ref, r_ref, s_ref, hot_out, w_ref, gram_ref = rest[nx + ny :]
+        rows_ref, fd_ref, hot_ref, r_ref, s_ref, hot_out, w_ref, gram_ref = rest[nx + ny :]
         geo = Geometry(sizes)
-        at = lay.scalar_rows + 4
-        factor = [recv[:, at + i, :] for i in range(lay.scalar_rows)]
+        at = lay.scalar_rows + 2
+        factor = [rows_ref[:, at + i, :] for i in range(lay.scalar_rows)]
         factor = jnp.concatenate(factor, axis=1)
         after = lay.lanes - lay.offset - lay.devices
         shifted = [jnp.zeros((lay.offset, lay.lanes), F32), factor]
@@ -754,7 +752,7 @@
         )
         received(geo, lay, fd_ref[...], recv, xs, ys, w_ref, 1)
         r_ref[...] = SOURCE_SCALE * w_ref[...]
-        row = with_coarse(lay, SOURCE_SCALE * received_scalars(lay, recv), gram_ref)
+        row = with_coarse(lay, SOURCE_SCALE * received_scalars(lay, rows_ref), gram_ref)
         s_ref[...] = jnp.broadcast_to(row, s_ref.shape)
         hot_out[...] = hot_ref[...]
         hot_out[48:144, :] = with_coarse(lay, hot_ref[48:144, :], gram_ref)
@@ -766,13 +764,21 @@
     def sweep_kernel(recv, *rest):
         xs, ys = rest[:nx], rest[nx : nx + ny]
         level_ref, fin_ref, tab_ref, zt_ref = rest[nx + ny : nx + ny + 4]
-        out = rest[nx + ny + 4 :]
+        slots, sxs, sys = split(rest[nx + ny + 4 : nx + ny + 4 + n_out])
+        out = rest[nx + ny + 4 + n_out :]
         send, oxs, oys = split(out[:n_out])
         level_out, f_ref, w_ref, work, zwork = out[n_out:]
         geo = Geometry(sizes)
         level = new_level(geo, recv, xs, ys, level_ref, fin_ref, tab_ref, w_ref)
         level_out[...] = level
-        finish(geo, weak_form(level, tab_ref, zt_ref, work), f_ref, zwork, send, oxs, oys)
+        v = local_sum_xy(weak_form(level, tab_ref, zt_ref, work))
+        f_ref[...] = local_sum_z(v)
+        send[...] = slots[...]
+        fill_field(geo, lay, f_ref, v, zwork, send, 0)
+        send[geo.me] = slots[geo.me]
+        fill_faces(geo, lay, f_ref, oxs, oys)
+        for to, part in zip((*oxs, *oys), (*sxs, *sys)):
+            to[BY : 2 * BY, :] = part[...]
 
     def diagonal_kernel(recv, *rest):
         xs, ys = rest[:nx], rest[nx : nx + ny]
@@ -884,33 +890,36 @@
         side = call(
             source_kernel,
             [vel, src, coarse_factor, tab, zt, places, fa],
-            [like(lay.devices, lay.slot_rows(2), 128), *outgoing(1)[1:], block, like(HOT_ROWS, lay.lanes)],
+            outgoing(1) + [block, like(HOT_ROWS, lay.lanes), like(8, lay.lanes)],
             [qrows, pair, tiles],
             "source",
         )
-        fd, hot = side[n_out:]
+        fd, hot, row = side[n_out:]
         out = call(
             first_kernel,
-            [*got, level, fa, tab, zt, *side[:n_out]],
+            [*got, level, fa, tab, zt, row],
+            outgoing(1) + [block, block],
+            [work, pair, tiles],
+            "sweep_first",
+        )
+        level, f = out[n_out:]
+        got = rows = exchange(out[:n_out])
+        out = call(
+            sweep_kernel,
+            [*got, level, f, tab, zt, *side[:n_out]],
             outgoing(2) + [block, block],
             [work, pair, tiles],
-            "sweep_first",
+            "sweep",
         )
         level, f = out[n_out:]
         got = exchange(out[:n_out])
         residual, s_rows, hot = call(
             rhs_kernel,
-            [*got, fd, hot],
+            [*got, rows[0], fd, hot],
             [block, like(8, lay.lanes), like(HOT_ROWS, lay.lanes)],
             [work, pltpu.VMEM((lay.lanes, lay.lanes), F32)],
             "rhs",
         )
-        for _ in range(RSWEEPS - 1):
-            out = call(
-                sweep_kernel, [*got, level, f, tab, zt], outgoing(1) + [block, block], [work, pair, tiles], "sweep"
-            )
-            level, f = out[n_out:]
-            got = exchange(out[:n_out])
         out = call(
             diagonal_kernel,
             [*got, level, f, tab, zt],

time: 123 us -> 122 us (level)
  no operation moved by 1% of the time
where the time goes in v4:
time: 122 us; the launch traced here: 121 us
  starting transfers between devices  59.2 us (49%)
  waiting for transfers between devices  34.6 us (28%)
  Pallas kernels  16.5 us (14%)
  blocking collectives  9.31 us (8%)
    ppermute x27, starting transfers between devices, ring(): return lax.ppermute(v, axis, pairs)  31.3 us
    all_to_all x9, starting transfers between devices, exchange(): recv = lax.all_to_all(send, AXES, 0, 0, tiled=True)  27.9 us
    all_to_all x9, waiting for transfers between devices, exchange(): recv = lax.all_to_all(send, AXES, 0, 0, tiled=True)  23.7 us
    pallas_call x13, Pallas kernels, call(): pl.pallas_call(kernel, out_shape=outs, in_specs=[hbm if i in from_hbm els...  16.5 us
    ppermute x27, waiting for transfers between devices, ring(): return lax.ppermute(v, axis, pairs)  10.8 us
    all_to_all x1, blocking collectives, body(): recv = lax.all_to_all(out[0], AXES, 0, 0, tiled=True)  9.31 us
  transfers between devices with their start and end apart: 36, of which 25 were waited for; matrix products, arithmetic and copies ran while one was open for 0% of the time, Pallas kernels for 1%

profile of v4, /device:TPU:0, one launch (start us, length us, event | category | flops | bytes accessed | tf_op | source)
XLA Modules:
  0.0 121.0 jit_solution(3862442271660185206)
XLA Ops:
  0.7 2.3 %advect.1 = (f32[32,4,128]{2,1,0:T(4,128)}, f32[16,128]{1,0:T(8,128)S(1)}, f32[16,128]{1,0:T(8,128)S(1)}, f32[16,128]{1,0:T(8,128)S(1)}, f32[256,128]{1,0:T(8,128)S(1)}) custom-call(f32[256,128]{1,0:T(8,128)} %bitcast.7, f32[3,256,128]{2,1,0:T(8,128)} %bitcast.5, f32[224,128]{1,0:T(8,128)} %constant.6.clone.tab_any.tab_ref.rest_5_.rest_7_.rest_9_, ...), custom_call_target="tpu_custom_call" | custom-call | flops 4000000 | bytes 1000000 | tf_op jit(solution)/shard_map/advect/pallas_call | solution.py:635
  2.9 7.3 %all-to-all-start = ((f32[32,4,128]{2,1,0:T(4,128)}), f32[32,4,128]{2,1,0:T(4,128)S(1)}, u32[]{:S(2)}, u32[]{:S(2)}) async-start(f32[32,4,128]{2,1,0:T(4,128)} %get-tuple-element.93), calls=%async_computation | async-start | bytes 131072 | tf_op jit(solution)/shard_map/all_to_all | solution.py:661
  10.3 1.8 %collective-permute-start = (f32[16,128]{1,0:T(8,128)S(1)}, f32[16,128]{1,0:T(8,128)S(1)}, u32[]{:S(2)}, u32[]{:S(2)}) collective-permute-start(f32[16,128]{1,0:T(8,128)S(1)} %get-tuple-element.94), channel_id=1, source_target_pairs={{0,16},{16,0},{1,17},{17,1},{2,18},{18,2},{3,19},{19,3},{4,20},{20... | collective-permute-start | bytes 24584 | tf_op jit(solution)/shard_map/ppermute | solution.py:657
  12.1 1.7 %collective-permute-start.2 = (f32[16,128]{1,0:T(8,128)S(1)}, f32[16,128]{1,0:T(8,128)S(1)}, u32[]{:S(2)}, u32[]{:S(2)}) collective-permute-start(f32[16,128]{1,0:T(8,128)S(1)} %get-tuple-element.96), channel_id=1, source_target_pairs={{0,12},{4,0},{8,4},{12,8},{1,13},{5,1},{9,5},{13,9},{2,14},{6,2},{... | collective-permute-start | bytes 24584 | tf_op jit(solution)/shard_map/ppermute | solution.py:657
  13.9 0.6 copy-done.6
  14.5 0.5 source.1
  15.2 2.5 %all-to-all-done.recv = f32[32,4,128]{2,1,0:T(4,128)S(1)} async-done(((f32[32,4,128]{2,1,0:T(4,128)}), f32[32,4,128]{2,1,0:T(4,128)S(1)}, u32[]{:S(2)}, u32[]{:S(2)}) %all-to-all-start) | async-done | bytes 65568 | tf_op jit(solution)/shard_map/all_to_all | solution.py:661
  17.8 1.4 %sweep_first.1 = (f32[32,4,128]{2,1,0:T(4,128)}, f32[16,128]{1,0:T(8,128)S(1)}, f32[16,128]{1,0:T(8,128)S(1)}, f32[16,128]{1,0:T(8,128)S(1)}, f32[256,128]{1,0:T(8,128)S(1)}, /*index=5*/f32[256,128]{1,0:T(8,128)S(1)}) custom-call(f32[32,4,128]{2,1,0:T(4,128)S(1)} %all-to-all-done.recv, f32[16,128]{1,0:T(8,128)S(1)} %collective-permute-done.rest_0_, ...), custom_call_target="tpu_custom_call" | custom-call | flops 4000000 | bytes 1000000 | tf_op jit(solution)/shard_map/sweep_first/pallas_call | solution.py:635
  19.2 2.6 %all-to-all-start.1 = ((f32[32,4,128]{2,1,0:T(4,128)}), f32[32,4,128]{2,1,0:T(4,128)S(1)}, u32[]{:S(2)}, u32[]{:S(2)}) async-start(f32[32,4,128]{2,1,0:T(4,128)} %get-tuple-element.99), calls=%async_computation.1 | async-start | bytes 131072 | tf_op jit(solution)/shard_map/all_to_all | solution.py:661
  21.8 1.7 %collective-permute-start.3 = (f32[16,128]{1,0:T(8,128)S(1)}, f32[16,128]{1,0:T(8,128)S(1)}, u32[]{:S(2)}, u32[]{:S(2)}) collective-permute-start(f32[16,128]{1,0:T(8,128)S(1)} %get-tuple-element.100), channel_id=1, source_target_pairs={{0,16},{16,0},{1,17},{17,1},{2,18},{18,2},{3,19},{19,3},{4,20},{20... | collective-permute-start | bytes 24584 | tf_op jit(solution)/shard_map/ppermute | solution.py:657
  23.5 1.7 %collective-permute-start.5 = (f32[16,128]{1,0:T(8,128)S(1)}, f32[16,128]{1,0:T(8,128)S(1)}, u32[]{:S(2)}, u32[]{:S(2)}) collective-permute-start(f32[16,128]{1,0:T(8,128)S(1)} %get-tuple-element.102), channel_id=1, source_target_pairs={{0,12},{4,0},{8,4},{12,8},{1,13},{5,1},{9,5},{13,9},{2,14},{6,2},{... | collective-permute-start | bytes 24584 | tf_op jit(solution)/shard_map/ppermute | solution.py:657
  25.3 0.3 collective-permute-done.3.rest_0_
  25.5 1.1 collective-permute-done.4.rest_1_
  26.6 2.7 %all-to-all-done.1.recv.rest_3_ = f32[32,4,128]{2,1,0:T(4,128)S(1)} async-done(((f32[32,4,128]{2,1,0:T(4,128)}), f32[32,4,128]{2,1,0:T(4,128)S(1)}, u32[]{:S(2)}, u32[]{:S(2)}) %all-to-all-start.1) | async-done | bytes 65568 | tf_op jit(solution)/shard_map/all_to_all | solution.py:661
  29.3 1.4 %sweep.1 = (f32[32,4,128]{2,1,0:T(4,128)}, f32[32,128]{1,0:T(8,128)S(1)}, f32[32,128]{1,0:T(8,128)S(1)}, f32[32,128]{1,0:T(8,128)S(1)}, f32[256,128]{1,0:T(8,128)S(1)}, /*index=5*/f32[256,128]{1,0:T(8,128)S(1)}) custom-call(f32[32,4,128]{2,1,0:T(4,128)S(1)} %all-to-all-done.1.recv.rest_3_, f32[16,128]{1,0:T(8,128)S(1)} %collective-permute-done.3.rest_0_, ...), custom_call_target="tpu_custom_call" | custom-call | flops 4000000 | bytes 1000000 | tf_op jit(solution)/shard_map/sweep/pallas_call | solution.py:635
  30.7 2.6 %all-to-all-start.2 = ((f32[32,4,128]{2,1,0:T(4,128)}), f32[32,4,128]{2,1,0:T(4,128)S(1)}, u32[]{:S(2)}, u32[]{:S(2)}) async-start(f32[32,4,128]{2,1,0:T(4,128)} %get-tuple-element.109), calls=%async_computation.2 | async-start | bytes 131072 | tf_op jit(solution)/shard_map/all_to_all | solution.py:661
  33.3 1.7 %collective-permute-start.6 = (f32[32,128]{1,0:T(8,128)S(1)}, f32[32,128]{1,0:T(8,128)S(1)}, u32[]{:S(2)}, u32[]{:S(2)}) collective-permute-start(f32[32,128]{1,0:T(8,128)S(1)} %get-tuple-element.110), channel_id=1, source_target_pairs={{0,16},{16,0},{1,17},{17,1},{2,18},{18,2},{3,19},{19,3},{4,20},{20... | collective-permute-start | bytes 49160 | tf_op jit(solution)/shard_map/ppermute | solution.py:657
  35.0 1.7 %collective-permute-start.8 = (f32[32,128]{1,0:T(8,128)S(1)}, f32[32,128]{1,0:T(8,128)S(1)}, u32[]{:S(2)}, u32[]{:S(2)}) collective-permute-start(f32[32,128]{1,0:T(8,128)S(1)} %get-tuple-element.112), channel_id=1, source_target_pairs={{0,12},{4,0},{8,4},{12,8},{1,13},{5,1},{9,5},{13,9},{2,14},{6,2},{... | collective-permute-start | bytes 49160 | tf_op jit(solution)/shard_map/ppermute | solution.py:657
  36.8 0.4 collective-permute-done.6.rest_0_
  37.2 1.0 collective-permute-done.7.rest_1_
  38.2 2.6 %all-to-all-done.2.recv = f32[32,4,128]{2,1,0:T(4,128)S(1)} async-done(((f32[32,4,128]{2,1,0:T(4,128)}), f32[32,4,128]{2,1,0:T(4,128)S(1)}, u32[]{:S(2)}, u32[]{:S(2)}) %all-to-all-start.2) | async-done | bytes 65568 | tf_op jit(solution)/shard_map/all_to_all | solution.py:661
  40.8 1.3 %diagonal.1 = (f32[32,4,128]{2,1,0:T(4,128)}, f32[16,128]{1,0:T(8,128)S(1)}, f32[16,128]{1,0:T(8,128)S(1)}, f32[16,128]{1,0:T(8,128)S(1)}, f32[256,128]{1,0:T(8,...) custom-call(f32[32,4,128]{2,1,0:T(4,128)S(1)} %all-to-all-done.2.recv, ...), custom_call_target="tpu_custom_call" | custom-call | flops 4000000 | bytes 1000000 | tf_op jit(solution)/shard_map/diagonal/pallas_call | solution.py:635
  42.1 2.6 %all-to-all-start.3 = ((f32[32,4,128]{2,1,0:T(4,128)}), f32[32,4,128]{2,1,0:T(4,128)S(1)}, u32[]{:S(2)}, u32[]{:S(2)}) async-start(f32[32,4,128]{2,1,0:T(4,128)} %get-tuple-element.116), calls=%async_computation.3 | async-start | bytes 131072 | tf_op jit(solution)/shard_map/all_to_all | solution.py:661
  44.7 1.7 %collective-permute-start.9 = (f32[16,128]{1,0:T(8,128)S(1)}, f32[16,128]{1,0:T(8,128)S(1)}, u32[]{:S(2)}, u32[]{:S(2)}) collective-permute-start(f32[16,128]{1,0:T(8,128)S(1)} %get-tuple-element.117), channel_id=1, source_target_pairs={{0,16},{16,0},{1,17},{17,1},{2,18},{18,2},{3,19},{19,3},{4,20},{20... | collective-permute-start | bytes 24584 | tf_op jit(solution)/shard_map/ppermute | solution.py:657
  46.4 1.7 %collective-permute-start.11 = (f32[16,128]{1,0:T(8,128)S(1)}, f32[16,128]{1,0:T(8,128)S(1)}, u32[]{:S(2)}, u32[]{:S(2)}) collective-permute-start(f32[16,128]{1,0:T(8,128)S(1)} %get-tuple-element.119), channel_id=1, source_target_pairs={{0,12},{4,0},{8,4},{12,8},{1,13},{5,1},{9,5},{13,9},{2,14},{6,2},{... | collective-permute-start | bytes 24584 | tf_op jit(solution)/shard_map/ppermute | solution.py:657
  48.2 0.4 rhs.1
  48.6 0.9 collective-permute-done.10.rest_1_
  49.5 2.7 %all-to-all-done.3.recv = f32[32,4,128]{2,1,0:T(4,128)S(1)} async-done(((f32[32,4,128]{2,1,0:T(4,128)}), f32[32,4,128]{2,1,0:T(4,128)S(1)}, u32[]{:S(2)}, u32[]{:S(2)}) %all-to-all-start.3) | async-done | bytes 65568 | tf_op jit(solution)/shard_map/all_to_all | solution.py:661
  52.2 1.5 %solve_start.1 = (f32[32,4,128]{2,1,0:T(4,128)}, f32[16,128]{1,0:T(8,128)S(1)}, f32[16,128]{1,0:T(8,128)S(1)}, f32[16,128]{1,0:T(8,128)S(1)}, f32[256,128]{1,0:T...) custom-call(f32[32,4,128]{2,1,0:T(4,128)S(1)} %all-to-all-done.3.recv, ...), custom_call_target="tpu_custom_call" | custom-call | flops 4000000 | bytes 1000000 | tf_op jit(solution)/shard_map/solve_start/pallas_call | solution.py:635
  53.7 2.6 %all-to-all-start.4 = ((f32[32,4,128]{2,1,0:T(4,128)}), f32[32,4,128]{2,1,0:T(4,128)S(1)}, u32[]{:S(2)}, u32[]{:S(2)}) async-start(f32[32,4,128]{2,1,0:T(4,128)} %get-tuple-element.127), calls=%async_computation.4 | async-start | bytes 131072 | tf_op jit(solution)/shard_map/all_to_all | solution.py:661
  56.3 1.7 %collective-permute-start.12 = (f32[16,128]{1,0:T(8,128)S(1)}, f32[16,128]{1,0:T(8,128)S(1)}, u32[]{:S(2)}, u32[]{:S(2)}) collective-permute-start(f32[16,128]{1,0:T(8,128)S(1)} %get-tuple-element.128), channel_id=1, source_target_pairs={{0,16},{16,0},{1,17},{17,1},{2,18},{18,2},{3,19},{19,3},{4,20},{20... | collective-permute-start | bytes 24584 | tf_op jit(solution)/shard_map/ppermute | solution.py:657
  58.0 1.7 %collective-permute-start.14 = (f32[16,128]{1,0:T(8,128)S(1)}, f32[16,128]{1,0:T(8,128)S(1)}, u32[]{:S(2)}, u32[]{:S(2)}) collective-permute-start(f32[16,128]{1,0:T(8,128)S(1)} %get-tuple-element.130), channel_id=1, source_target_pairs={{0,12},{4,0},{8,4},{12,8},{1,13},{5,1},{9,5},{13,9},{2,14},{6,2},{... | collective-permute-start | bytes 24584 | tf_op jit(solution)/shard_map/ppermute | solution.py:657
  59.7 0.3 collective-permute-done.12.rest_0_
  60.0 1.1 collective-permute-done.13.rest_1_
  61.1 2.7 %all-to-all-done.4.recv = f32[32,4,128]{2,1,0:T(4,128)S(1)} async-done(((f32[32,4,128]{2,1,0:T(4,128)}), f32[32,4,128]{2,1,0:T(4,128)S(1)}, u32[]{:S(2)}, u32[]{:S(2)}) %all-to-all-start.4) | async-done | bytes 65568 | tf_op jit(solution)/shard_map/all_to_all | solution.py:661
  63.8 1.5 %iterate.5 = (f32[32,4,128]{2,1,0:T(4,128)}, f32[16,128]{1,0:T(8,128)S(1)}, f32[16,128]{1,0:T(8,128)S(1)}, f32[16,128]{1,0:T(8,128)S(1)}, f32[256,128]{1,0:T(8,1...) custom-call(f32[32,4,128]{2,1,0:T(4,128)S(1)} %all-to-all-done.4.rec, ...), custom_call_target="tpu_custom_call" | custom-call | flops 4000000 | bytes 1000000 | tf_op jit(solution)/shard_map/iterate/pallas_call | solution.py:635
  65.3 2.6 %all-to-all-start.5 = ((f32[32,4,128]{2,1,0:T(4,128)}), f32[32,4,128]{2,1,0:T(4,128)S(1)}, u32[]{:S(2)}, u32[]{:S(2)}) async-start(f32[32,4,128]{2,1,0:T(4,128)} %get-tuple-element.135), calls=%async_computation.5 | async-start | bytes 131072 | tf_op jit(solution)/shard_map/all_to_all | solution.py:661
  67.9 1.7 %collective-permute-start.15 = (f32[16,128]{1,0:T(8,128)S(1)}, f32[16,128]{1,0:T(8,128)S(1)}, u32[]{:S(2)}, u32[]{:S(2)}) collective-permute-start(f32[16,128]{1,0:T(8,128)S(1)} %get-tuple-element.136), channel_id=1, source_target_pairs={{0,16},{16,0},{1,17},{17,1},{2,18},{18,2},{3,19},{19,3},{4,20},{20... | collective-permute-start | bytes 24584 | tf_op jit(solution)/shard_map/ppermute | solution.py:657
  69.6 1.7 %collective-permute-start.17 = (f32[16,128]{1,0:T(8,128)S(1)}, f32[16,128]{1,0:T(8,128)S(1)}, u32[]{:S(2)}, u32[]{:S(2)}) collective-permute-start(f32[16,128]{1,0:T(8,128)S(1)} %get-tuple-element.138), channel_id=1, source_target_pairs={{0,12},{4,0},{8,4},{12,8},{1,13},{5,1},{9,5},{13,9},{2,14},{6,2},{... | collective-permute-start | bytes 24584 | tf_op jit(solution)/shard_map/ppermute | solution.py:657
  71.4 0.3 collective-permute-done.15.rest_0_
  71.6 1.1 collective-permute-done.16.rest_1_
  72.7 2.7 %all-to-all-done.5.recv = f32[32,4,128]{2,1,0:T(4,128)S(1)} async-done(((f32[32,4,128]{2,1,0:T(4,128)}), f32[32,4,128]{2,1,0:T(4,128)S(1)}, u32[]{:S(2)}, u32[]{:S(2)}) %all-to-all-start.5) | async-done | bytes 65568 | tf_op jit(solution)/shard_map/all_to_all | solution.py:661
  75.4 1.5 %iterate.6 = (f32[32,4,128]{2,1,0:T(4,128)}, f32[16,128]{1,0:T(8,128)S(1)}, f32[16,128]{1,0:T(8,128)S(1)}, f32[16,128]{1,0:T(8,128)S(1)}, f32[256,128]{1,0:T(8,1...) custom-call(f32[32,4,128]{2,1,0:T(4,128)S(1)} %all-to-all-done.5.rec, ...), custom_call_target="tpu_custom_call" | custom-call | flops 4000000 | bytes 1000000 | tf_op jit(solution)/shard_map/iterate/pallas_call | solution.py:635
  76.9 2.6 %all-to-all-start.6 = ((f32[32,4,128]{2,1,0:T(4,128)}), f32[32,4,128]{2,1,0:T(4,128)S(1)}, u32[]{:S(2)}, u32[]{:S(2)}) async-start(f32[32,4,128]{2,1,0:T(4,128)} %get-tuple-element.146), calls=%async_computation.6 | async-start | bytes 131072 | tf_op jit(solution)/shard_map/all_to_all | solution.py:661
  79.5 1.7 %collective-permute-start.18 = (f32[16,128]{1,0:T(8,128)S(1)}, f32[16,128]{1,0:T(8,128)S(1)}, u32[]{:S(2)}, u32[]{:S(2)}) collective-permute-start(f32[16,128]{1,0:T(8,128)S(1)} %get-tuple-element.147), channel_id=1, source_target_pairs={{0,16},{16,0},{1,17},{17,1},{2,18},{18,2},{3,19},{19,3},{4,20},{20... | collective-permute-start | bytes 24584 | tf_op jit(solution)/shard_map/ppermute | solution.py:657
  81.2 1.7 %collective-permute-start.20 = (f32[16,128]{1,0:T(8,128)S(1)}, f32[16,128]{1,0:T(8,128)S(1)}, u32[]{:S(2)}, u32[]{:S(2)}) collective-permute-start(f32[16,128]{1,0:T(8,128)S(1)} %get-tuple-element.149), channel_id=1, source_target_pairs={{0,12},{4,0},{8,4},{12,8},{1,13},{5,1},{9,5},{13,9},{2,14},{6,2},{... | collective-permute-start | bytes 24584 | tf_op jit(solution)/shard_map/ppermute | solution.py:657
  83.0 0.3 collective-permute-done.18.rest_0_
  83.2 1.1 collective-permute-done.19.rest_1_
  84.3 2.7 %all-to-all-done.6.recv = f32[32,4,128]{2,1,0:T(4,128)S(1)} async-done(((f32[32,4,128]{2,1,0:T(4,128)}), f32[32,4,128]{2,1,0:T(4,128)S(1)}, u32[]{:S(2)}, u32[]{:S(2)}) %all-to-all-start.6) | async-done | bytes 65568 | tf_op jit(solution)/shard_map/all_to_all | solution.py:661
  87.0 1.5 %iterate.7 = (f32[32,4,128]{2,1,0:T(4,128)}, f32[16,128]{1,0:T(8,128)S(1)}, f32[16,128]{1,0:T(8,128)S(1)}, f32[16,128]{1,0:T(8,128)S(1)}, f32[256,128]{1,0:T(8,1...) custom-call(f32[32,4,128]{2,1,0:T(4,128)S(1)} %all-to-all-done.6.rec, ...), custom_call_target="tpu_custom_call" | custom-call | flops 4000000 | bytes 1000000 | tf_op jit(solution)/shard_map/iterate/pallas_call | solution.py:635
  88.5 2.6 %all-to-all-start.7 = ((f32[32,4,128]{2,1,0:T(4,128)}), f32[32,4,128]{2,1,0:T(4,128)S(1)}, u32[]{:S(2)}, u32[]{:S(2)}) async-start(f32[32,4,128]{2,1,0:T(4,128)} %get-tuple-element.157), calls=%async_computation.7 | async-start | bytes 131072 | tf_op jit(solution)/shard_map/all_to_all | solution.py:661
  91.1 1.7 %collective-permute-start.21 = (f32[16,128]{1,0:T(8,128)S(1)}, f32[16,128]{1,0:T(8,128)S(1)}, u32[]{:S(2)}, u32[]{:S(2)}) collective-permute-start(f32[16,128]{1,0:T(8,128)S(1)} %get-tuple-element.158), channel_id=1, source_target_pairs={{0,16},{16,0},{1,17},{17,1},{2,18},{18,2},{3,19},{19,3},{4,20},{20... | collective-permute-start | bytes 24584 | tf_op jit(solution)/shard_map/ppermute | solution.py:657
  92.8 1.7 %collective-permute-start.23 = (f32[16,128]{1,0:T(8,128)S(1)}, f32[16,128]{1,0:T(8,128)S(1)}, u32[]{:S(2)}, u32[]{:S(2)}) collective-permute-start(f32[16,128]{1,0:T(8,128)S(1)} %get-tuple-element.160), channel_id=1, source_target_pairs={{0,12},{4,0},{8,4},{12,8},{1,13},{5,1},{9,5},{13,9},{2,14},{6,2},{... | collective-permute-start | bytes 24584 | tf_op jit(solution)/shard_map/ppermute | solution.py:657
  94.8 1.1 collective-permute-done.22.rest_1_
  95.9 2.7 %all-to-all-done.7.recv = f32[32,4,128]{2,1,0:T(4,128)S(1)} async-done(((f32[32,4,128]{2,1,0:T(4,128)}), f32[32,4,128]{2,1,0:T(4,128)S(1)}, u32[]{:S(2)}, u32[]{:S(2)}) %all-to-all-start.7) | async-done | bytes 65568 | tf_op jit(solution)/shard_map/all_to_all | solution.py:661
  98.6 1.5 %iterate.8 = (f32[32,4,128]{2,1,0:T(4,128)}, f32[16,128]{1,0:T(8,128)S(1)}, f32[16,128]{1,0:T(8,128)S(1)}, f32[16,128]{1,0:T(8,128)S(1)}, f32[256,128]{1,0:T(8,1...) custom-call(f32[32,4,128]{2,1,0:T(4,128)S(1)} %all-to-all-done.7.rec, ...), custom_call_target="tpu_custom_call" | custom-call | flops 4000000 | bytes 1000000 | tf_op jit(solution)/shard_map/iterate/pallas_call | solution.py:635
  100.1 2.6 %all-to-all-start.8 = ((f32[32,4,128]{2,1,0:T(4,128)}), f32[32,4,128]{2,1,0:T(4,128)S(1)}, u32[]{:S(2)}, u32[]{:S(2)}) async-start(f32[32,4,128]{2,1,0:T(4,128)} %get-tuple-element.168), calls=%async_computation.8 | async-start | bytes 131072 | tf_op jit(solution)/shard_map/all_to_all | solution.py:661
  102.7 1.7 %collective-permute-start.24 = (f32[16,128]{1,0:T(8,128)S(1)}, f32[16,128]{1,0:T(8,128)S(1)}, u32[]{:S(2)}, u32[]{:S(2)}) collective-permute-start(f32[16,128]{1,0:T(8,128)S(1)} %get-tuple-element.169), channel_id=1, source_target_pairs={{0,16},{16,0},{1,17},{17,1},{2,18},{18,2},{3,19},{19,3},{4,20},{20... | collective-permute-start | bytes 24584 | tf_op jit(solution)/shard_map/ppermute | solution.py:657
  104.4 1.7 %collective-permute-start.26 = (f32[16,128]{1,0:T(8,128)S(1)}, f32[16,128]{1,0:T(8,128)S(1)}, u32[]{:S(2)}, u32[]{:S(2)}) collective-permute-start(f32[16,128]{1,0:T(8,128)S(1)} %get-tuple-element.171), channel_id=1, source_target_pairs={{0,12},{4,0},{8,4},{12,8},{1,13},{5,1},{9,5},{13,9},{2,14},{6,2},{... | collective-permute-start | bytes 24584 | tf_op jit(solution)/shard_map/ppermute | solution.py:657
  106.5 1.1 collective-permute-done.25.rest_1_
  107.6 2.7 %all-to-all-done.8.recv = f32[32,4,128]{2,1,0:T(4,128)S(1)} async-done(((f32[32,4,128]{2,1,0:T(4,128)}), f32[32,4,128]{2,1,0:T(4,128)S(1)}, u32[]{:S(2)}, u32[]{:S(2)}) %all-to-all-start.8) | async-done | bytes 65568 | tf_op jit(solution)/shard_map/all_to_all | solution.py:661
  110.2 0.7 iterate.9
  110.9 9.3 %all_to_all.50.recv = f32[32,1,128]{2,1,0:T(1,128)S(1)} all-to-all(f32[32,1,128]{2,1,0:T(1,128)S(1)} %get-tuple-element.179), channel_id=1, replica_groups=mesh['gx'=2,'gy'=4,'gz'=4] {'gx','gy','gz'}, dimensions={0} | all-to-all | bytes 32768 | tf_op jit(solution)/shard_map/all_to_all | solution.py:957
  120.2 0.8 pressure.1
  (36 shorter events, 1.0 us)
Async XLA Ops:
  0.6 13.2 %copy-start = (bf16[768,256]{1,0:T(8,128)(2,1)S(1)}, bf16[768,256]{1,0:T(8,128)(2,1)}, u32[]{:S(2)}) copy-start(bf16[768,256]{1,0:T(8,128)(2,1)} %constant.7.clone.zt_any.zt_ref.rest_6_.rest_8_.rest_10_) | copy-start | bytes 1179652
  0.6 13.2 %copy-start.2 = (f32[3,16,16,128]{3,2,1,0:T(8,128)S(1)}, f32[3,16,16,128]{3,2,1,0:T(8,128)}, u32[]{:S(2)}) copy-start(f32[3,16,16,128]{3,2,1,0:T(8,128)} %param.8) | copy-start | bytes 1179652
  0.7 13.2 %copy-start.4 = (f32[16,16,128]{2,1,0:T(8,128)S(1)}, f32[16,16,128]{2,1,0:T(8,128)}, u32[]{:S(2)}) copy-start(f32[16,16,128]{2,1,0:T(8,128)} %param.9) | copy-start | bytes 393220
  2.9 10.9 %copy-start.1 = (f32[224,128]{1,0:T(8,128)S(1)}, f32[224,128]{1,0:T(8,128)}, u32[]{:S(2)}) copy-start(f32[224,128]{1,0:T(8,128)} %constant.6.clone.tab_any.tab_ref.rest_5_.rest_7_.rest_9_) | copy-start | bytes 344068
  2.9 14.8 %all-to-all-start = ((f32[32,4,128]{2,1,0:T(4,128)}), f32[32,4,128]{2,1,0:T(4,128)S(1)}, u32[]{:S(2)}, u32[]{:S(2)}) async-start(f32[32,4,128]{2,1,0:T(4,128)} %get-tuple-element.93), calls=%async_computation | async-start | bytes 131072 | tf_op jit(solution)/shard_map/all_to_all | solution.py:661
  10.3 3.6 %copy-start.5 = (f32[8,128]{1,0:T(8,128)S(1)}, f32[8,128]{1,0:T(8,128)}, u32[]{:S(2)}) copy-start(f32[8,128]{1,0:T(8,128)} %constant.8.clone.places_ref) | copy-start | bytes 12292
  10.3 4.7 %collective-permute-start = (f32[16,128]{1,0:T(8,128)S(1)}, f32[16,128]{1,0:T(8,128)S(1)}, u32[]{:S(2)}, u32[]{:S(2)}) collective-permute-start(f32[16,128]{1,0:T(8,128)S(1)} %get-tuple-element.94), channel_id=1, source_target_pairs={{0,16},{16,0},{1,17},{17,1},{2,18},{18,2},{3,19},{19,3},{4,20},{20... | collective-permute-start | bytes 24584 | tf_op jit(solution)/shard_map/ppermute | solution.py:657
  12.1 3.1 %collective-permute-start.1 = (f32[16,128]{1,0:T(8,128)S(1)}, f32[16,128]{1,0:T(8,128)S(1)}, u32[]{:S(2)}, u32[]{:S(2)}) collective-permute-start(f32[16,128]{1,0:T(8,128)S(1)} %get-tuple-element.95), channel_id=1, source_target_pairs={{0,4},{4,8},{8,12},{12,0},{1,5},{5,9},{9,13},{13,1},{2,6},{6,10},{... | collective-permute-start | bytes 24584 | tf_op jit(solution)/shard_map/ppermute | solution.py:657
  12.1 3.1 %collective-permute-start.2 = (f32[16,128]{1,0:T(8,128)S(1)}, f32[16,128]{1,0:T(8,128)S(1)}, u32[]{:S(2)}, u32[]{:S(2)}) collective-permute-start(f32[16,128]{1,0:T(8,128)S(1)} %get-tuple-element.96), channel_id=1, source_target_pairs={{0,12},{4,0},{8,4},{12,8},{1,13},{5,1},{9,5},{13,9},{2,14},{6,2},{... | collective-permute-start | bytes 24584 | tf_op jit(solution)/shard_map/ppermute | solution.py:657
  13.9 0.7 copy-start.6
  14.5 3.2 %copy-start.3 = (f32[16,16,128]{2,1,0:T(8,128)S(1)}, f32[16,16,128]{2,1,0:T(8,128)}, u32[]{:S(2)}) copy-start(f32[16,16,128]{2,1,0:T(8,128)} %param.7) | copy-start | bytes 393220
  19.2 10.1 %all-to-all-start.1 = ((f32[32,4,128]{2,1,0:T(4,128)}), f32[32,4,128]{2,1,0:T(4,128)S(1)}, u32[]{:S(2)}, u32[]{:S(2)}) async-start(f32[32,4,128]{2,1,0:T(4,128)} %get-tuple-element.99), calls=%async_computation.1 | async-start | bytes 131072 | tf_op jit(solution)/shard_map/all_to_all | solution.py:661
  21.8 3.7 %collective-permute-start.3 = (f32[16,128]{1,0:T(8,128)S(1)}, f32[16,128]{1,0:T(8,128)S(1)}, u32[]{:S(2)}, u32[]{:S(2)}) collective-permute-start(f32[16,128]{1,0:T(8,128)S(1)} %get-tuple-element.100), channel_id=1, source_target_pairs={{0,16},{16,0},{1,17},{17,1},{2,18},{18,2},{3,19},{19,3},{4,20},{20... | collective-permute-start | bytes 24584 | tf_op jit(solution)/shard_map/ppermute | solution.py:657
  23.5 3.1 %collective-permute-start.4 = (f32[16,128]{1,0:T(8,128)S(1)}, f32[16,128]{1,0:T(8,128)S(1)}, u32[]{:S(2)}, u32[]{:S(2)}) collective-permute-start(f32[16,128]{1,0:T(8,128)S(1)} %get-tuple-element.101), channel_id=1, source_target_pairs={{0,4},{4,8},{8,12},{12,0},{1,5},{5,9},{9,13},{13,1},{2,6},{6,10},{... | collective-permute-start | bytes 24584 | tf_op jit(solution)/shard_map/ppermute | solution.py:657
  23.5 3.1 %collective-permute-start.5 = (f32[16,128]{1,0:T(8,128)S(1)}, f32[16,128]{1,0:T(8,128)S(1)}, u32[]{:S(2)}, u32[]{:S(2)}) collective-permute-start(f32[16,128]{1,0:T(8,128)S(1)} %get-tuple-element.102), channel_id=1, source_target_pairs={{0,12},{4,0},{8,4},{12,8},{1,13},{5,1},{9,5},{13,9},{2,14},{6,2},{... | collective-permute-start | bytes 24584 | tf_op jit(solution)/shard_map/ppermute | solution.py:657
  30.7 10.1 %all-to-all-start.2 = ((f32[32,4,128]{2,1,0:T(4,128)}), f32[32,4,128]{2,1,0:T(4,128)S(1)}, u32[]{:S(2)}, u32[]{:S(2)}) async-start(f32[32,4,128]{2,1,0:T(4,128)} %get-tuple-element.109), calls=%async_computation.2 | async-start | bytes 131072 | tf_op jit(solution)/shard_map/all_to_all | solution.py:661
  33.3 3.9 %collective-permute-start.6 = (f32[32,128]{1,0:T(8,128)S(1)}, f32[32,128]{1,0:T(8,128)S(1)}, u32[]{:S(2)}, u32[]{:S(2)}) collective-permute-start(f32[32,128]{1,0:T(8,128)S(1)} %get-tuple-element.110), channel_id=1, source_target_pairs={{0,16},{16,0},{1,17},{17,1},{2,18},{18,2},{3,19},{19,3},{4,20},{20... | collective-permute-start | bytes 49160 | tf_op jit(solution)/shard_map/ppermute | solution.py:657
  35.0 3.2 %collective-permute-start.7 = (f32[32,128]{1,0:T(8,128)S(1)}, f32[32,128]{1,0:T(8,128)S(1)}, u32[]{:S(2)}, u32[]{:S(2)}) collective-permute-start(f32[32,128]{1,0:T(8,128)S(1)} %get-tuple-element.111), channel_id=1, source_target_pairs={{0,4},{4,8},{8,12},{12,0},{1,5},{5,9},{9,13},{13,1},{2,6},{6,10},{... | collective-permute-start | bytes 49160 | tf_op jit(solution)/shard_map/ppermute | solution.py:657
  35.0 3.2 %collective-permute-start.8 = (f32[32,128]{1,0:T(8,128)S(1)}, f32[32,128]{1,0:T(8,128)S(1)}, u32[]{:S(2)}, u32[]{:S(2)}) collective-permute-start(f32[32,128]{1,0:T(8,128)S(1)} %get-tuple-element.112), channel_id=1, source_target_pairs={{0,12},{4,0},{8,4},{12,8},{1,13},{5,1},{9,5},{13,9},{2,14},{6,2},{... | collective-permute-start | bytes 49160 | tf_op jit(solution)/shard_map/ppermute | solution.py:657
  42.1 10.1 %all-to-all-start.3 = ((f32[32,4,128]{2,1,0:T(4,128)}), f32[32,4,128]{2,1,0:T(4,128)S(1)}, u32[]{:S(2)}, u32[]{:S(2)}) async-start(f32[32,4,128]{2,1,0:T(4,128)} %get-tuple-element.116), calls=%async_computation.3 | async-start | bytes 131072 | tf_op jit(solution)/shard_map/all_to_all | solution.py:661
  44.7 3.9 %collective-permute-start.9 = (f32[16,128]{1,0:T(8,128)S(1)}, f32[16,128]{1,0:T(8,128)S(1)}, u32[]{:S(2)}, u32[]{:S(2)}) collective-permute-start(f32[16,128]{1,0:T(8,128)S(1)} %get-tuple-element.117), channel_id=1, source_target_pairs={{0,16},{16,0},{1,17},{17,1},{2,18},{18,2},{3,19},{19,3},{4,20},{20... | collective-permute-start | bytes 24584 | tf_op jit(solution)/shard_map/ppermute | solution.py:657
  46.4 3.1 %collective-permute-start.10 = (f32[16,128]{1,0:T(8,128)S(1)}, f32[16,128]{1,0:T(8,128)S(1)}, u32[]{:S(2)}, u32[]{:S(2)}) collective-permute-start(f32[16,128]{1,0:T(8,128)S(1)} %get-tuple-element.118), channel_id=1, source_target_pairs={{0,4},{4,8},{8,12},{12,0},{1,5},{5,9},{9,13},{13,1},{2,6},{6,10},{... | collective-permute-start | bytes 24584 | tf_op jit(solution)/shard_map/ppermute | solution.py:657
  46.4 3.1 %collective-permute-start.11 = (f32[16,128]{1,0:T(8,128)S(1)}, f32[16,128]{1,0:T(8,128)S(1)}, u32[]{:S(2)}, u32[]{:S(2)}) collective-permute-start(f32[16,128]{1,0:T(8,128)S(1)} %get-tuple-element.119), channel_id=1, source_target_pairs={{0,12},{4,0},{8,4},{12,8},{1,13},{5,1},{9,5},{13,9},{2,14},{6,2},{... | collective-permute-start | bytes 24584 | tf_op jit(solution)/shard_map/ppermute | solution.py:657
  53.7 10.1 %all-to-all-start.4 = ((f32[32,4,128]{2,1,0:T(4,128)}), f32[32,4,128]{2,1,0:T(4,128)S(1)}, u32[]{:S(2)}, u32[]{:S(2)}) async-start(f32[32,4,128]{2,1,0:T(4,128)} %get-tuple-element.127), calls=%async_computation.4 | async-start | bytes 131072 | tf_op jit(solution)/shard_map/all_to_all | solution.py:661
  56.3 3.7 %collective-permute-start.12 = (f32[16,128]{1,0:T(8,128)S(1)}, f32[16,128]{1,0:T(8,128)S(1)}, u32[]{:S(2)}, u32[]{:S(2)}) collective-permute-start(f32[16,128]{1,0:T(8,128)S(1)} %get-tuple-element.128), channel_id=1, source_target_pairs={{0,16},{16,0},{1,17},{17,1},{2,18},{18,2},{3,19},{19,3},{4,20},{20... | collective-permute-start | bytes 24584 | tf_op jit(solution)/shard_map/ppermute | solution.py:657
  58.0 3.1 %collective-permute-start.13 = (f32[16,128]{1,0:T(8,128)S(1)}, f32[16,128]{1,0:T(8,128)S(1)}, u32[]{:S(2)}, u32[]{:S(2)}) collective-permute-start(f32[16,128]{1,0:T(8,128)S(1)} %get-tuple-element.129), channel_id=1, source_target_pairs={{0,4},{4,8},{8,12},{12,0},{1,5},{5,9},{9,13},{13,1},{2,6},{6,10},{... | collective-permute-start | bytes 24584 | tf_op jit(solution)/shard_map/ppermute | solution.py:657
  58.0 3.1 %collective-permute-start.14 = (f32[16,128]{1,0:T(8,128)S(1)}, f32[16,128]{1,0:T(8,128)S(1)}, u32[]{:S(2)}, u32[]{:S(2)}) collective-permute-start(f32[16,128]{1,0:T(8,128)S(1)} %get-tuple-element.130), channel_id=1, source_target_pairs={{0,12},{4,0},{8,4},{12,8},{1,13},{5,1},{9,5},{13,9},{2,14},{6,2},{... | collective-permute-start | bytes 24584 | tf_op jit(solution)/shard_map/ppermute | solution.py:657
  65.3 10.1 %all-to-all-start.5 = ((f32[32,4,128]{2,1,0:T(4,128)}), f32[32,4,128]{2,1,0:T(4,128)S(1)}, u32[]{:S(2)}, u32[]{:S(2)}) async-start(f32[32,4,128]{2,1,0:T(4,128)} %get-tuple-element.135), calls=%async_computation.5 | async-start | bytes 131072 | tf_op jit(solution)/shard_map/all_to_all | solution.py:661
  67.9 3.7 %collective-permute-start.15 = (f32[16,128]{1,0:T(8,128)S(1)}, f32[16,128]{1,0:T(8,128)S(1)}, u32[]{:S(2)}, u32[]{:S(2)}) collective-permute-start(f32[16,128]{1,0:T(8,128)S(1)} %get-tuple-element.136), channel_id=1, source_target_pairs={{0,16},{16,0},{1,17},{17,1},{2,18},{18,2},{3,19},{19,3},{4,20},{20... | collective-permute-start | bytes 24584 | tf_op jit(solution)/shard_map/ppermute | solution.py:657
  69.6 3.1 %collective-permute-start.16 = (f32[16,128]{1,0:T(8,128)S(1)}, f32[16,128]{1,0:T(8,128)S(1)}, u32[]{:S(2)}, u32[]{:S(2)}) collective-permute-start(f32[16,128]{1,0:T(8,128)S(1)} %get-tuple-element.137), channel_id=1, source_target_pairs={{0,4},{4,8},{8,12},{12,0},{1,5},{5,9},{9,13},{13,1},{2,6},{6,10},{... | collective-permute-start | bytes 24584 | tf_op jit(solution)/shard_map/ppermute | solution.py:657
  69.6 3.1 %collective-permute-start.17 = (f32[16,128]{1,0:T(8,128)S(1)}, f32[16,128]{1,0:T(8,128)S(1)}, u32[]{:S(2)}, u32[]{:S(2)}) collective-permute-start(f32[16,128]{1,0:T(8,128)S(1)} %get-tuple-element.138), channel_id=1, source_target_pairs={{0,12},{4,0},{8,4},{12,8},{1,13},{5,1},{9,5},{13,9},{2,14},{6,2},{... | collective-permute-start | bytes 24584 | tf_op jit(solution)/shard_map/ppermute | solution.py:657
  76.9 10.1 %all-to-all-start.6 = ((f32[32,4,128]{2,1,0:T(4,128)}), f32[32,4,128]{2,1,0:T(4,128)S(1)}, u32[]{:S(2)}, u32[]{:S(2)}) async-start(f32[32,4,128]{2,1,0:T(4,128)} %get-tuple-element.146), calls=%async_computation.6 | async-start | bytes 131072 | tf_op jit(solution)/shard_map/all_to_all | solution.py:661
  79.5 3.7 %collective-permute-start.18 = (f32[16,128]{1,0:T(8,128)S(1)}, f32[16,128]{1,0:T(8,128)S(1)}, u32[]{:S(2)}, u32[]{:S(2)}) collective-permute-start(f32[16,128]{1,0:T(8,128)S(1)} %get-tuple-element.147), channel_id=1, source_target_pairs={{0,16},{16,0},{1,17},{17,1},{2,18},{18,2},{3,19},{19,3},{4,20},{20... | collective-permute-start | bytes 24584 | tf_op jit(solution)/shard_map/ppermute | solution.py:657
  81.2 3.1 %collective-permute-start.19 = (f32[16,128]{1,0:T(8,128)S(1)}, f32[16,128]{1,0:T(8,128)S(1)}, u32[]{:S(2)}, u32[]{:S(2)}) collective-permute-start(f32[16,128]{1,0:T(8,128)S(1)} %get-tuple-element.148), channel_id=1, source_target_pairs={{0,4},{4,8},{8,12},{12,0},{1,5},{5,9},{9,13},{13,1},{2,6},{6,10},{... | collective-permute-start | bytes 24584 | tf_op jit(solution)/shard_map/ppermute | solution.py:657
  81.2 3.1 %collective-permute-start.20 = (f32[16,128]{1,0:T(8,128)S(1)}, f32[16,128]{1,0:T(8,128)S(1)}, u32[]{:S(2)}, u32[]{:S(2)}) collective-permute-start(f32[16,128]{1,0:T(8,128)S(1)} %get-tuple-element.149), channel_id=1, source_target_pairs={{0,12},{4,0},{8,4},{12,8},{1,13},{5,1},{9,5},{13,9},{2,14},{6,2},{... | collective-permute-start | bytes 24584 | tf_op jit(solution)/shard_map/ppermute | solution.py:657
  88.5 10.1 %all-to-all-start.7 = ((f32[32,4,128]{2,1,0:T(4,128)}), f32[32,4,128]{2,1,0:T(4,128)S(1)}, u32[]{:S(2)}, u32[]{:S(2)}) async-start(f32[32,4,128]{2,1,0:T(4,128)} %get-tuple-element.157), calls=%async_computation.7 | async-start | bytes 131072 | tf_op jit(solution)/shard_map/all_to_all | solution.py:661
  91.1 3.7 %collective-permute-start.21 = (f32[16,128]{1,0:T(8,128)S(1)}, f32[16,128]{1,0:T(8,128)S(1)}, u32[]{:S(2)}, u32[]{:S(2)}) collective-permute-start(f32[16,128]{1,0:T(8,128)S(1)} %get-tuple-element.158), channel_id=1, source_target_pairs={{0,16},{16,0},{1,17},{17,1},{2,18},{18,2},{3,19},{19,3},{4,20},{20... | collective-permute-start | bytes 24584 | tf_op jit(solution)/shard_map/ppermute | solution.py:657
  92.8 3.1 %collective-permute-start.22 = (f32[16,128]{1,0:T(8,128)S(1)}, f32[16,128]{1,0:T(8,128)S(1)}, u32[]{:S(2)}, u32[]{:S(2)}) collective-permute-start(f32[16,128]{1,0:T(8,128)S(1)} %get-tuple-element.159), channel_id=1, source_target_pairs={{0,4},{4,8},{8,12},{12,0},{1,5},{5,9},{9,13},{13,1},{2,6},{6,10},{... | collective-permute-start | bytes 24584 | tf_op jit(solution)/shard_map/ppermute | solution.py:657
  92.8 3.1 %collective-permute-start.23 = (f32[16,128]{1,0:T(8,128)S(1)}, f32[16,128]{1,0:T(8,128)S(1)}, u32[]{:S(2)}, u32[]{:S(2)}) collective-permute-start(f32[16,128]{1,0:T(8,128)S(1)} %get-tuple-element.160), channel_id=1, source_target_pairs={{0,12},{4,0},{8,4},{12,8},{1,13},{5,1},{9,5},{13,9},{2,14},{6,2},{... | collective-permute-start | bytes 24584 | tf_op jit(solution)/shard_map/ppermute | solution.py:657
  100.1 10.1 %all-to-all-start.8 = ((f32[32,4,128]{2,1,0:T(4,128)}), f32[32,4,128]{2,1,0:T(4,128)S(1)}, u32[]{:S(2)}, u32[]{:S(2)}) async-start(f32[32,4,128]{2,1,0:T(4,128)} %get-tuple-element.168), calls=%async_computation.8 | async-start | bytes 131072 | tf_op jit(solution)/shard_map/all_to_all | solution.py:661
  102.7 3.7 %collective-permute-start.24 = (f32[16,128]{1,0:T(8,128)S(1)}, f32[16,128]{1,0:T(8,128)S(1)}, u32[]{:S(2)}, u32[]{:S(2)}) collective-permute-start(f32[16,128]{1,0:T(8,128)S(1)} %get-tuple-element.169), channel_id=1, source_target_pairs={{0,16},{16,0},{1,17},{17,1},{2,18},{18,2},{3,19},{19,3},{4,20},{20... | collective-permute-start | bytes 24584 | tf_op jit(solution)/shard_map/ppermute | solution.py:657
  104.4 3.1 %collective-permute-start.25 = (f32[16,128]{1,0:T(8,128)S(1)}, f32[16,128]{1,0:T(8,128)S(1)}, u32[]{:S(2)}, u32[]{:S(2)}) collective-permute-start(f32[16,128]{1,0:T(8,128)S(1)} %get-tuple-element.170), channel_id=1, source_target_pairs={{0,4},{4,8},{8,12},{12,0},{1,5},{5,9},{9,13},{13,1},{2,6},{6,10},{... | collective-permute-start | bytes 24584 | tf_op jit(solution)/shard_map/ppermute | solution.py:657
  104.4 3.1 %collective-permute-start.26 = (f32[16,128]{1,0:T(8,128)S(1)}, f32[16,128]{1,0:T(8,128)S(1)}, u32[]{:S(2)}, u32[]{:S(2)}) collective-permute-start(f32[16,128]{1,0:T(8,128)S(1)} %get-tuple-element.171), channel_id=1, source_target_pairs={{0,12},{4,0},{8,4},{12,8},{1,13},{5,1},{9,5},{13,9},{2,14},{6,2},{... | collective-permute-start | bytes 24584 | tf_op jit(solution)/shard_map/ppermute | solution.py:657

commit v5 on v4

--- a/solution.py
+++ b/solution.py
@@ -205,6 +205,18 @@
                 number = number + step[a] * strides[a]
         return jnp.where(ok, number, self.me)
 
+    def across(self, dy, dz):
+        plane = self.sizes[1] * self.sizes[2]
+        there = self.neighbour(0, dy, dz)
+        other = jnp.where(self.at[0] == 0, there + plane, there - plane)
+        return other if dy == 0 and dz == 0 else jnp.where(there == self.me, self.me, other)
+
+    def x_sides(self):
+        return (2,) if self.sizes[0] == 2 else (-1, 1)
+
+    def beside(self, dx, dy, dz):
+        return self.across(dy, dz) if dx == 2 else self.neighbour(dx, dy, dz)
+
     def half(self, flag):
         return jnp.where(flag, 0.5, 1.0).astype(F32)
 
@@ -344,15 +356,21 @@
     pairs = pack_z_faces(z, work)
     for dz in (-1, 1):
         pair = pairs[0 if dz < 0 else 1]
-        for dx in (-1, 0, 1):
+        for dx in (0, *geo.x_sides()):
             for dy in (-1, 0, 1):
-                there = geo.neighbour(dx, dy, dz)
+                there = geo.beside(dx, dy, dz)
                 send_ref[there, row0 : row0 + 1, :] = pair[0]
                 send_ref[there, row1 : row1 + 1, :] = pair[1]
-    for dx in (-1, 1):
+    for dx in geo.x_sides():
         for dy in (-1, 1):
-            row = (BX - 1 if dx > 0 else 0) * BY + (BY - 1 if dy > 0 else 0)
-            send_ref[geo.neighbour(dx, dy, 0), row0 : row0 + 1, :] = f_ref[row : row + 1, :]
+            low = BY - 1 if dy > 0 else 0
+            high = low + (BX - 1) * BY
+            if dx == 2:
+                edge = jnp.where(geo.at[0] == 0, f_ref[high : high + 1, :], f_ref[low : low + 1, :])
+            else:
+                row = high if dx > 0 else low
+                edge = f_ref[row : row + 1, :]
+            send_ref[geo.beside(dx, dy, 0), row0 : row0 + 1, :] = edge
 
 
 def fill_faces(geo, lay, f_ref, xs, ys):
@@ -386,11 +404,16 @@
         for r in range(2):
             total = None
             for dy in (0, 1 if r else -1):
-                for dx in (0, -1, 1):
+                for dx in (0, *geo.x_sides()):
                     source = 1 - r if dy else r
-                    part = recv_ref[geo.neighbour(dx, dy, dz), at[source] : at[source] + 1, :]
+                    part = recv_ref[geo.beside(dx, dy, dz), at[source] : at[source] + 1, :]
                     keep = None
-                    if dx:
+                    shift = (60 * dx + 67 * dy) % BZ
+                    if dx == 2:
+                        first = jnp.where(geo.at[0] == 0, 60, 0)
+                        keep = (line % 64 >= first) & (line % 64 < first + 4)
+                        shift = jnp.where(geo.at[0] == 0, (60 + 67 * dy) % BZ, (67 * dy - 60) % BZ)
+                    elif dx:
                         keep = line % 64 >= 60 if dx > 0 else line % 64 < 4
                     if dy > 0:
                         want = (line >= 64) & (line % 4 == 3)
@@ -399,7 +422,7 @@
                         want = (line < 64) & (line % 4 == 0)
                         keep = want if keep is None else keep & want
                     if keep is not None:
-                        part = jnp.where(keep, pltpu.roll(part, (60 * dx + 67 * dy) % BZ, 1), 0.0)
+                        part = jnp.where(keep, pltpu.roll(part, shift, 1), 0.0)
                     total = part if total is None else total + part
             pair.append(total)
         sides.append(pair)
@@ -417,10 +440,17 @@
     lowy, highy = came_from(geo, 1, lay.sizes[1], ys, k, BX)
     w_ref[pl.ds(0, BX, stride=BY), :] += lowy
     w_ref[pl.ds(BY - 1, BX, stride=BY), :] += highy
-    for dx in (-1, 1):
+    for dx in geo.x_sides():
         for dy in (-1, 1):
-            row = (BX - 1 if dx > 0 else 0) * BY + (BY - 1 if dy > 0 else 0)
-            w_ref[row : row + 1, :] += recv_ref[geo.neighbour(dx, dy, 0), at[0] : at[0] + 1, :]
+            edge = recv_ref[geo.beside(dx, dy, 0), at[0] : at[0] + 1, :]
+            low = BY - 1 if dy > 0 else 0
+            high = low + (BX - 1) * BY
+            if dx == 2:
+                w_ref[low : low + 1, :] += jnp.where(geo.at[0] == 0, 0.0, edge)
+                w_ref[high : high + 1, :] += jnp.where(geo.at[0] == 0, edge, 0.0)
+            else:
+                row = high if dx > 0 else low
+                w_ref[row : row + 1, :] += edge
 
 
 def received_scalars(lay, recv_ref):
@@ -551,11 +581,11 @@
     bm = bmass_of(tab)
     gx, gy, gz = along_x(v, "d"), along_y(v, "d", tab, work.at[0]), along_z(v, "d", zt)
     tx, ty, tz = scaled * gx, scaled * gy, scaled * gz
-    energy = all_rows(bm * v * v + (tx * gx + ty * gy + tz * gz))
     if final:
-        return None, energy
+        return None, all_rows(bm * v * v + (tx * gx + ty * gy + tz * gz))
     out = bm * v + along_x(tx, "t") + along_y(ty, "t", tab, work.at[1])
-    return out + along_z(tz, "t", zt), energy
+    out = out + along_z(tz, "t", zt)
+    return out, all_rows(v * out)
 
 
 def local_step(geo, lay, residual, dinv, scaled, state, image, refs):

time: 122 us -> 121 us (level)
  no operation moved by 1% of the time
where the time goes in v5:
time: 121 us
  starting transfers between devices  59.2 us (49%)
  waiting for transfers between devices  34.6 us (29%)
  Pallas kernels  16.1 us (13%)
  blocking collectives  9.31 us (8%)
    ppermute x27, starting transfers between devices, ring(): return lax.ppermute(v, axis, pairs)  31.3 us
    all_to_all x9, starting transfers between devices, exchange(): recv = lax.all_to_all(send, AXES, 0, 0, tiled=True)  27.9 us
    all_to_all x9, waiting for transfers between devices, exchange(): recv = lax.all_to_all(send, AXES, 0, 0, tiled=True)  23.7 us
    pallas_call x13, Pallas kernels, call(): pl.pallas_call(kernel, out_shape=outs, in_specs=[hbm if i in from_hbm els...  16.1 us
    ppermute x27, waiting for transfers between devices, ring(): return lax.ppermute(v, axis, pairs)  10.8 us
    all_to_all x1, blocking collectives, body(): recv = lax.all_to_all(out[0], AXES, 0, 0, tiled=True)  9.31 us
  transfers between devices with their start and end apart: 36, of which 25 were waited for; matrix products, arithmetic and copies ran while one was open for 0% of the time, Pallas kernels for 1%

profile of v5, /device:TPU:0, one launch (start us, length us, event | category | flops | bytes accessed | tf_op | source)
XLA Modules:
  0.0 120.7 jit_solution(9867740224581945087)
XLA Ops:
  0.7 2.2 %advect.1 = (f32[32,4,128]{2,1,0:T(4,128)}, f32[16,128]{1,0:T(8,128)S(1)}, f32[16,128]{1,0:T(8,128)S(1)}, f32[16,128]{1,0:T(8,128)S(1)}, f32[256,128]{1,0:T(8,128)S(1)}) custom-call(f32[256,128]{1,0:T(8,128)} %bitcast.7, f32[3,256,128]{2,1,0:T(8,128)} %bitcast.5, f32[224,128]{1,0:T(8,128)} %constant.6.clone.tab_any.tab_ref.rest_5_.rest_7_.rest_9_, ...), custom_call_target="tpu_custom_call" | custom-call | flops 4000000 | bytes 1000000 | tf_op jit(solution)/shard_map/advect/pallas_call | solution.py:665
  2.9 7.3 %all-to-all-start = ((f32[32,4,128]{2,1,0:T(4,128)}), f32[32,4,128]{2,1,0:T(4,128)S(1)}, u32[]{:S(2)}, u32[]{:S(2)}) async-start(f32[32,4,128]{2,1,0:T(4,128)} %get-tuple-element.93), calls=%async_computation | async-start | bytes 131072 | tf_op jit(solution)/shard_map/all_to_all | solution.py:691
  10.2 1.8 %collective-permute-start = (f32[16,128]{1,0:T(8,128)S(1)}, f32[16,128]{1,0:T(8,128)S(1)}, u32[]{:S(2)}, u32[]{:S(2)}) collective-permute-start(f32[16,128]{1,0:T(8,128)S(1)} %get-tuple-element.94), channel_id=1, source_target_pairs={{0,16},{16,0},{1,17},{17,1},{2,18},{18,2},{3,19},{19,3},{4,20},{20... | collective-permute-start | bytes 24584 | tf_op jit(solution)/shard_map/ppermute | solution.py:687
  12.1 1.7 %collective-permute-start.2 = (f32[16,128]{1,0:T(8,128)S(1)}, f32[16,128]{1,0:T(8,128)S(1)}, u32[]{:S(2)}, u32[]{:S(2)}) collective-permute-start(f32[16,128]{1,0:T(8,128)S(1)} %get-tuple-element.96), channel_id=1, source_target_pairs={{0,12},{4,0},{8,4},{12,8},{1,13},{5,1},{9,5},{13,9},{2,14},{6,2},{... | collective-permute-start | bytes 24584 | tf_op jit(solution)/shard_map/ppermute | solution.py:687
  13.8 0.6 copy-done.6
  14.5 0.5 source.1
  15.2 2.5 %all-to-all-done.recv = f32[32,4,128]{2,1,0:T(4,128)S(1)} async-done(((f32[32,4,128]{2,1,0:T(4,128)}), f32[32,4,128]{2,1,0:T(4,128)S(1)}, u32[]{:S(2)}, u32[]{:S(2)}) %all-to-all-start) | async-done | bytes 65568 | tf_op jit(solution)/shard_map/all_to_all | solution.py:691
  17.7 1.4 %sweep_first.1 = (f32[32,4,128]{2,1,0:T(4,128)}, f32[16,128]{1,0:T(8,128)S(1)}, f32[16,128]{1,0:T(8,128)S(1)}, f32[16,128]{1,0:T(8,128)S(1)}, f32[256,128]{1,0:T(8,128)S(1)}, /*index=5*/f32[256,128]{1,0:T(8,128)S(1)}) custom-call(f32[32,4,128]{2,1,0:T(4,128)S(1)} %all-to-all-done.recv, f32[16,128]{1,0:T(8,128)S(1)} %collective-permute-done.rest_0_, ...), custom_call_target="tpu_custom_call" | custom-call | flops 4000000 | bytes 1000000 | tf_op jit(solution)/shard_map/sweep_first/pallas_call | solution.py:665
  19.1 2.6 %all-to-all-start.1 = ((f32[32,4,128]{2,1,0:T(4,128)}), f32[32,4,128]{2,1,0:T(4,128)S(1)}, u32[]{:S(2)}, u32[]{:S(2)}) async-start(f32[32,4,128]{2,1,0:T(4,128)} %get-tuple-element.99), calls=%async_computation.1 | async-start | bytes 131072 | tf_op jit(solution)/shard_map/all_to_all | solution.py:691
  21.7 1.7 %collective-permute-start.3 = (f32[16,128]{1,0:T(8,128)S(1)}, f32[16,128]{1,0:T(8,128)S(1)}, u32[]{:S(2)}, u32[]{:S(2)}) collective-permute-start(f32[16,128]{1,0:T(8,128)S(1)} %get-tuple-element.100), channel_id=1, source_target_pairs={{0,16},{16,0},{1,17},{17,1},{2,18},{18,2},{3,19},{19,3},{4,20},{20... | collective-permute-start | bytes 24584 | tf_op jit(solution)/shard_map/ppermute | solution.py:687
  23.4 1.7 %collective-permute-start.5 = (f32[16,128]{1,0:T(8,128)S(1)}, f32[16,128]{1,0:T(8,128)S(1)}, u32[]{:S(2)}, u32[]{:S(2)}) collective-permute-start(f32[16,128]{1,0:T(8,128)S(1)} %get-tuple-element.102), channel_id=1, source_target_pairs={{0,12},{4,0},{8,4},{12,8},{1,13},{5,1},{9,5},{13,9},{2,14},{6,2},{... | collective-permute-start | bytes 24584 | tf_op jit(solution)/shard_map/ppermute | solution.py:687
  25.2 0.3 collective-permute-done.3.rest_0_
  25.4 1.1 collective-permute-done.4.rest_1_
  26.6 2.7 %all-to-all-done.1.recv.rest_3_ = f32[32,4,128]{2,1,0:T(4,128)S(1)} async-done(((f32[32,4,128]{2,1,0:T(4,128)}), f32[32,4,128]{2,1,0:T(4,128)S(1)}, u32[]{:S(2)}, u32[]{:S(2)}) %all-to-all-start.1) | async-done | bytes 65568 | tf_op jit(solution)/shard_map/all_to_all | solution.py:691
  29.2 1.4 %sweep.1 = (f32[32,4,128]{2,1,0:T(4,128)}, f32[32,128]{1,0:T(8,128)S(1)}, f32[32,128]{1,0:T(8,128)S(1)}, f32[32,128]{1,0:T(8,128)S(1)}, f32[256,128]{1,0:T(8,128)S(1)}, /*index=5*/f32[256,128]{1,0:T(8,128)S(1)}) custom-call(f32[32,4,128]{2,1,0:T(4,128)S(1)} %all-to-all-done.1.recv.rest_3_, f32[16,128]{1,0:T(8,128)S(1)} %collective-permute-done.3.rest_0_, ...), custom_call_target="tpu_custom_call" | custom-call | flops 4000000 | bytes 1000000 | tf_op jit(solution)/shard_map/sweep/pallas_call | solution.py:665
  30.6 2.6 %all-to-all-start.2 = ((f32[32,4,128]{2,1,0:T(4,128)}), f32[32,4,128]{2,1,0:T(4,128)S(1)}, u32[]{:S(2)}, u32[]{:S(2)}) async-start(f32[32,4,128]{2,1,0:T(4,128)} %get-tuple-element.109), calls=%async_computation.2 | async-start | bytes 131072 | tf_op jit(solution)/shard_map/all_to_all | solution.py:691
  33.2 1.7 %collective-permute-start.6 = (f32[32,128]{1,0:T(8,128)S(1)}, f32[32,128]{1,0:T(8,128)S(1)}, u32[]{:S(2)}, u32[]{:S(2)}) collective-permute-start(f32[32,128]{1,0:T(8,128)S(1)} %get-tuple-element.110), channel_id=1, source_target_pairs={{0,16},{16,0},{1,17},{17,1},{2,18},{18,2},{3,19},{19,3},{4,20},{20... | collective-permute-start | bytes 49160 | tf_op jit(solution)/shard_map/ppermute | solution.py:687
  34.9 1.7 %collective-permute-start.8 = (f32[32,128]{1,0:T(8,128)S(1)}, f32[32,128]{1,0:T(8,128)S(1)}, u32[]{:S(2)}, u32[]{:S(2)}) collective-permute-start(f32[32,128]{1,0:T(8,128)S(1)} %get-tuple-element.112), channel_id=1, source_target_pairs={{0,12},{4,0},{8,4},{12,8},{1,13},{5,1},{9,5},{13,9},{2,14},{6,2},{... | collective-permute-start | bytes 49160 | tf_op jit(solution)/shard_map/ppermute | solution.py:687
  36.7 0.4 collective-permute-done.6.rest_0_
  37.1 1.0 collective-permute-done.7.rest_1_
  38.2 2.6 %all-to-all-done.2.recv = f32[32,4,128]{2,1,0:T(4,128)S(1)} async-done(((f32[32,4,128]{2,1,0:T(4,128)}), f32[32,4,128]{2,1,0:T(4,128)S(1)}, u32[]{:S(2)}, u32[]{:S(2)}) %all-to-all-start.2) | async-done | bytes 65568 | tf_op jit(solution)/shard_map/all_to_all | solution.py:691
  40.7 1.3 %diagonal.1 = (f32[32,4,128]{2,1,0:T(4,128)}, f32[16,128]{1,0:T(8,128)S(1)}, f32[16,128]{1,0:T(8,128)S(1)}, f32[16,128]{1,0:T(8,128)S(1)}, f32[256,128]{1,0:T(8,...) custom-call(f32[32,4,128]{2,1,0:T(4,128)S(1)} %all-to-all-done.2.recv, ...), custom_call_target="tpu_custom_call" | custom-call | flops 4000000 | bytes 1000000 | tf_op jit(solution)/shard_map/diagonal/pallas_call | solution.py:665
  42.0 2.6 %all-to-all-start.3 = ((f32[32,4,128]{2,1,0:T(4,128)}), f32[32,4,128]{2,1,0:T(4,128)S(1)}, u32[]{:S(2)}, u32[]{:S(2)}) async-start(f32[32,4,128]{2,1,0:T(4,128)} %get-tuple-element.116), calls=%async_computation.3 | async-start | bytes 131072 | tf_op jit(solution)/shard_map/all_to_all | solution.py:691
  44.6 1.7 %collective-permute-start.9 = (f32[16,128]{1,0:T(8,128)S(1)}, f32[16,128]{1,0:T(8,128)S(1)}, u32[]{:S(2)}, u32[]{:S(2)}) collective-permute-start(f32[16,128]{1,0:T(8,128)S(1)} %get-tuple-element.117), channel_id=1, source_target_pairs={{0,16},{16,0},{1,17},{17,1},{2,18},{18,2},{3,19},{19,3},{4,20},{20... | collective-permute-start | bytes 24584 | tf_op jit(solution)/shard_map/ppermute | solution.py:687
  46.3 1.7 %collective-permute-start.11 = (f32[16,128]{1,0:T(8,128)S(1)}, f32[16,128]{1,0:T(8,128)S(1)}, u32[]{:S(2)}, u32[]{:S(2)}) collective-permute-start(f32[16,128]{1,0:T(8,128)S(1)} %get-tuple-element.119), channel_id=1, source_target_pairs={{0,12},{4,0},{8,4},{12,8},{1,13},{5,1},{9,5},{13,9},{2,14},{6,2},{... | collective-permute-start | bytes 24584 | tf_op jit(solution)/shard_map/ppermute | solution.py:687
  48.1 0.4 rhs.1
  48.5 0.9 collective-permute-done.10.rest_1_
  49.4 2.7 %all-to-all-done.3.recv = f32[32,4,128]{2,1,0:T(4,128)S(1)} async-done(((f32[32,4,128]{2,1,0:T(4,128)}), f32[32,4,128]{2,1,0:T(4,128)S(1)}, u32[]{:S(2)}, u32[]{:S(2)}) %all-to-all-start.3) | async-done | bytes 65568 | tf_op jit(solution)/shard_map/all_to_all | solution.py:691
  52.1 1.5 %solve_start.1 = (f32[32,4,128]{2,1,0:T(4,128)}, f32[16,128]{1,0:T(8,128)S(1)}, f32[16,128]{1,0:T(8,128)S(1)}, f32[16,128]{1,0:T(8,128)S(1)}, f32[256,128]{1,0:T...) custom-call(f32[32,4,128]{2,1,0:T(4,128)S(1)} %all-to-all-done.3.recv, ...), custom_call_target="tpu_custom_call" | custom-call | flops 4000000 | bytes 1000000 | tf_op jit(solution)/shard_map/solve_start/pallas_call | solution.py:665
  53.6 2.6 %all-to-all-start.4 = ((f32[32,4,128]{2,1,0:T(4,128)}), f32[32,4,128]{2,1,0:T(4,128)S(1)}, u32[]{:S(2)}, u32[]{:S(2)}) async-start(f32[32,4,128]{2,1,0:T(4,128)} %get-tuple-element.127), calls=%async_computation.4 | async-start | bytes 131072 | tf_op jit(solution)/shard_map/all_to_all | solution.py:691
  56.1 1.7 %collective-permute-start.12 = (f32[16,128]{1,0:T(8,128)S(1)}, f32[16,128]{1,0:T(8,128)S(1)}, u32[]{:S(2)}, u32[]{:S(2)}) collective-permute-start(f32[16,128]{1,0:T(8,128)S(1)} %get-tuple-element.128), channel_id=1, source_target_pairs={{0,16},{16,0},{1,17},{17,1},{2,18},{18,2},{3,19},{19,3},{4,20},{20... | collective-permute-start | bytes 24584 | tf_op jit(solution)/shard_map/ppermute | solution.py:687
  57.9 1.7 %collective-permute-start.14 = (f32[16,128]{1,0:T(8,128)S(1)}, f32[16,128]{1,0:T(8,128)S(1)}, u32[]{:S(2)}, u32[]{:S(2)}) collective-permute-start(f32[16,128]{1,0:T(8,128)S(1)} %get-tuple-element.130), channel_id=1, source_target_pairs={{0,12},{4,0},{8,4},{12,8},{1,13},{5,1},{9,5},{13,9},{2,14},{6,2},{... | collective-permute-start | bytes 24584 | tf_op jit(solution)/shard_map/ppermute | solution.py:687
  59.6 0.3 collective-permute-done.12.rest_0_
  59.9 1.1 collective-permute-done.13.rest_1_
  61.0 2.7 %all-to-all-done.4.recv = f32[32,4,128]{2,1,0:T(4,128)S(1)} async-done(((f32[32,4,128]{2,1,0:T(4,128)}), f32[32,4,128]{2,1,0:T(4,128)S(1)}, u32[]{:S(2)}, u32[]{:S(2)}) %all-to-all-start.4) | async-done | bytes 65568 | tf_op jit(solution)/shard_map/all_to_all | solution.py:691
  63.6 1.6 %iterate.5 = (f32[32,4,128]{2,1,0:T(4,128)}, f32[16,128]{1,0:T(8,128)S(1)}, f32[16,128]{1,0:T(8,128)S(1)}, f32[16,128]{1,0:T(8,128)S(1)}, f32[256,128]{1,0:T(8,1...) custom-call(f32[32,4,128]{2,1,0:T(4,128)S(1)} %all-to-all-done.4.rec, ...), custom_call_target="tpu_custom_call" | custom-call | flops 4000000 | bytes 1000000 | tf_op jit(solution)/shard_map/iterate/pallas_call | solution.py:665
  65.2 2.6 %all-to-all-start.5 = ((f32[32,4,128]{2,1,0:T(4,128)}), f32[32,4,128]{2,1,0:T(4,128)S(1)}, u32[]{:S(2)}, u32[]{:S(2)}) async-start(f32[32,4,128]{2,1,0:T(4,128)} %get-tuple-element.135), calls=%async_computation.5 | async-start | bytes 131072 | tf_op jit(solution)/shard_map/all_to_all | solution.py:691
  67.8 1.7 %collective-permute-start.15 = (f32[16,128]{1,0:T(8,128)S(1)}, f32[16,128]{1,0:T(8,128)S(1)}, u32[]{:S(2)}, u32[]{:S(2)}) collective-permute-start(f32[16,128]{1,0:T(8,128)S(1)} %get-tuple-element.136), channel_id=1, source_target_pairs={{0,16},{16,0},{1,17},{17,1},{2,18},{18,2},{3,19},{19,3},{4,20},{20... | collective-permute-start | bytes 24584 | tf_op jit(solution)/shard_map/ppermute | solution.py:687
  69.5 1.7 %collective-permute-start.17 = (f32[16,128]{1,0:T(8,128)S(1)}, f32[16,128]{1,0:T(8,128)S(1)}, u32[]{:S(2)}, u32[]{:S(2)}) collective-permute-start(f32[16,128]{1,0:T(8,128)S(1)} %get-tuple-element.138), channel_id=1, source_target_pairs={{0,12},{4,0},{8,4},{12,8},{1,13},{5,1},{9,5},{13,9},{2,14},{6,2},{... | collective-permute-start | bytes 24584 | tf_op jit(solution)/shard_map/ppermute | solution.py:687
  71.2 0.3 collective-permute-done.15.rest_0_
  71.5 1.1 collective-permute-done.16.rest_1_
  72.6 2.7 %all-to-all-done.5.recv = f32[32,4,128]{2,1,0:T(4,128)S(1)} async-done(((f32[32,4,128]{2,1,0:T(4,128)}), f32[32,4,128]{2,1,0:T(4,128)S(1)}, u32[]{:S(2)}, u32[]{:S(2)}) %all-to-all-start.5) | async-done | bytes 65568 | tf_op jit(solution)/shard_map/all_to_all | solution.py:691
  75.3 1.5 %iterate.6 = (f32[32,4,128]{2,1,0:T(4,128)}, f32[16,128]{1,0:T(8,128)S(1)}, f32[16,128]{1,0:T(8,128)S(1)}, f32[16,128]{1,0:T(8,128)S(1)}, f32[256,128]{1,0:T(8,1...) custom-call(f32[32,4,128]{2,1,0:T(4,128)S(1)} %all-to-all-done.5.rec, ...), custom_call_target="tpu_custom_call" | custom-call | flops 4000000 | bytes 1000000 | tf_op jit(solution)/shard_map/iterate/pallas_call | solution.py:665
  76.7 2.6 %all-to-all-start.6 = ((f32[32,4,128]{2,1,0:T(4,128)}), f32[32,4,128]{2,1,0:T(4,128)S(1)}, u32[]{:S(2)}, u32[]{:S(2)}) async-start(f32[32,4,128]{2,1,0:T(4,128)} %get-tuple-element.146), calls=%async_computation.6 | async-start | bytes 131072 | tf_op jit(solution)/shard_map/all_to_all | solution.py:691
  79.3 1.7 %collective-permute-start.18 = (f32[16,128]{1,0:T(8,128)S(1)}, f32[16,128]{1,0:T(8,128)S(1)}, u32[]{:S(2)}, u32[]{:S(2)}) collective-permute-start(f32[16,128]{1,0:T(8,128)S(1)} %get-tuple-element.147), channel_id=1, source_target_pairs={{0,16},{16,0},{1,17},{17,1},{2,18},{18,2},{3,19},{19,3},{4,20},{20... | collective-permute-start | bytes 24584 | tf_op jit(solution)/shard_map/ppermute | solution.py:687
  81.0 1.7 %collective-permute-start.20 = (f32[16,128]{1,0:T(8,128)S(1)}, f32[16,128]{1,0:T(8,128)S(1)}, u32[]{:S(2)}, u32[]{:S(2)}) collective-permute-start(f32[16,128]{1,0:T(8,128)S(1)} %get-tuple-element.149), channel_id=1, source_target_pairs={{0,12},{4,0},{8,4},{12,8},{1,13},{5,1},{9,5},{13,9},{2,14},{6,2},{... | collective-permute-start | bytes 24584 | tf_op jit(solution)/shard_map/ppermute | solution.py:687
  82.8 0.3 collective-permute-done.18.rest_0_
  83.0 1.1 collective-permute-done.19.rest_1_
  84.1 2.7 %all-to-all-done.6.recv = f32[32,4,128]{2,1,0:T(4,128)S(1)} async-done(((f32[32,4,128]{2,1,0:T(4,128)}), f32[32,4,128]{2,1,0:T(4,128)S(1)}, u32[]{:S(2)}, u32[]{:S(2)}) %all-to-all-start.6) | async-done | bytes 65568 | tf_op jit(solution)/shard_map/all_to_all | solution.py:691
  86.8 1.5 %iterate.7 = (f32[32,4,128]{2,1,0:T(4,128)}, f32[16,128]{1,0:T(8,128)S(1)}, f32[16,128]{1,0:T(8,128)S(1)}, f32[16,128]{1,0:T(8,128)S(1)}, f32[256,128]{1,0:T(8,1...) custom-call(f32[32,4,128]{2,1,0:T(4,128)S(1)} %all-to-all-done.6.rec, ...), custom_call_target="tpu_custom_call" | custom-call | flops 4000000 | bytes 1000000 | tf_op jit(solution)/shard_map/iterate/pallas_call | solution.py:665
  88.3 2.6 %all-to-all-start.7 = ((f32[32,4,128]{2,1,0:T(4,128)}), f32[32,4,128]{2,1,0:T(4,128)S(1)}, u32[]{:S(2)}, u32[]{:S(2)}) async-start(f32[32,4,128]{2,1,0:T(4,128)} %get-tuple-element.157), calls=%async_computation.7 | async-start | bytes 131072 | tf_op jit(solution)/shard_map/all_to_all | solution.py:691
  90.9 1.7 %collective-permute-start.21 = (f32[16,128]{1,0:T(8,128)S(1)}, f32[16,128]{1,0:T(8,128)S(1)}, u32[]{:S(2)}, u32[]{:S(2)}) collective-permute-start(f32[16,128]{1,0:T(8,128)S(1)} %get-tuple-element.158), channel_id=1, source_target_pairs={{0,16},{16,0},{1,17},{17,1},{2,18},{18,2},{3,19},{19,3},{4,20},{20... | collective-permute-start | bytes 24584 | tf_op jit(solution)/shard_map/ppermute | solution.py:687
  92.6 1.7 %collective-permute-start.23 = (f32[16,128]{1,0:T(8,128)S(1)}, f32[16,128]{1,0:T(8,128)S(1)}, u32[]{:S(2)}, u32[]{:S(2)}) collective-permute-start(f32[16,128]{1,0:T(8,128)S(1)} %get-tuple-element.160), channel_id=1, source_target_pairs={{0,12},{4,0},{8,4},{12,8},{1,13},{5,1},{9,5},{13,9},{2,14},{6,2},{... | collective-permute-start | bytes 24584 | tf_op jit(solution)/shard_map/ppermute | solution.py:687
  94.6 1.1 collective-permute-done.22.rest_1_
  95.7 2.7 %all-to-all-done.7.recv = f32[32,4,128]{2,1,0:T(4,128)S(1)} async-done(((f32[32,4,128]{2,1,0:T(4,128)}), f32[32,4,128]{2,1,0:T(4,128)S(1)}, u32[]{:S(2)}, u32[]{:S(2)}) %all-to-all-start.7) | async-done | bytes 65568 | tf_op jit(solution)/shard_map/all_to_all | solution.py:691
  98.4 1.5 %iterate.8 = (f32[32,4,128]{2,1,0:T(4,128)}, f32[16,128]{1,0:T(8,128)S(1)}, f32[16,128]{1,0:T(8,128)S(1)}, f32[16,128]{1,0:T(8,128)S(1)}, f32[256,128]{1,0:T(8,1...) custom-call(f32[32,4,128]{2,1,0:T(4,128)S(1)} %all-to-all-done.7.rec, ...), custom_call_target="tpu_custom_call" | custom-call | flops 4000000 | bytes 1000000 | tf_op jit(solution)/shard_map/iterate/pallas_call | solution.py:665
  99.8 2.6 %all-to-all-start.8 = ((f32[32,4,128]{2,1,0:T(4,128)}), f32[32,4,128]{2,1,0:T(4,128)S(1)}, u32[]{:S(2)}, u32[]{:S(2)}) async-start(f32[32,4,128]{2,1,0:T(4,128)} %get-tuple-element.168), calls=%async_computation.8 | async-start | bytes 131072 | tf_op jit(solution)/shard_map/all_to_all | solution.py:691
  102.4 1.7 %collective-permute-start.24 = (f32[16,128]{1,0:T(8,128)S(1)}, f32[16,128]{1,0:T(8,128)S(1)}, u32[]{:S(2)}, u32[]{:S(2)}) collective-permute-start(f32[16,128]{1,0:T(8,128)S(1)} %get-tuple-element.169), channel_id=1, source_target_pairs={{0,16},{16,0},{1,17},{17,1},{2,18},{18,2},{3,19},{19,3},{4,20},{20... | collective-permute-start | bytes 24584 | tf_op jit(solution)/shard_map/ppermute | solution.py:687
  104.1 1.7 %collective-permute-start.26 = (f32[16,128]{1,0:T(8,128)S(1)}, f32[16,128]{1,0:T(8,128)S(1)}, u32[]{:S(2)}, u32[]{:S(2)}) collective-permute-start(f32[16,128]{1,0:T(8,128)S(1)} %get-tuple-element.171), channel_id=1, source_target_pairs={{0,12},{4,0},{8,4},{12,8},{1,13},{5,1},{9,5},{13,9},{2,14},{6,2},{... | collective-permute-start | bytes 24584 | tf_op jit(solution)/shard_map/ppermute | solution.py:687
  106.1 1.1 collective-permute-done.25.rest_1_
  107.3 2.7 %all-to-all-done.8.recv = f32[32,4,128]{2,1,0:T(4,128)S(1)} async-done(((f32[32,4,128]{2,1,0:T(4,128)}), f32[32,4,128]{2,1,0:T(4,128)S(1)}, u32[]{:S(2)}, u32[]{:S(2)}) %all-to-all-start.8) | async-done | bytes 65568 | tf_op jit(solution)/shard_map/all_to_all | solution.py:691
  109.9 0.6 iterate.9
  110.6 9.3 %all_to_all.50.recv = f32[32,1,128]{2,1,0:T(1,128)S(1)} all-to-all(f32[32,1,128]{2,1,0:T(1,128)S(1)} %get-tuple-element.179), channel_id=1, replica_groups=mesh['gx'=2,'gy'=4,'gz'=4] {'gx','gy','gz'}, dimensions={0} | all-to-all | bytes 32768 | tf_op jit(solution)/shard_map/all_to_all | solution.py:987
  119.9 0.8 pressure.1
  (36 shorter events, 1.0 us)
Async XLA Ops:
  0.6 13.2 %copy-start = (bf16[768,256]{1,0:T(8,128)(2,1)S(1)}, bf16[768,256]{1,0:T(8,128)(2,1)}, u32[]{:S(2)}) copy-start(bf16[768,256]{1,0:T(8,128)(2,1)} %constant.7.clone.zt_any.zt_ref.rest_6_.rest_8_.rest_10_) | copy-start | bytes 1179652
  0.6 13.2 %copy-start.2 = (f32[3,16,16,128]{3,2,1,0:T(8,128)S(1)}, f32[3,16,16,128]{3,2,1,0:T(8,128)}, u32[]{:S(2)}) copy-start(f32[3,16,16,128]{3,2,1,0:T(8,128)} %param.8) | copy-start | bytes 1179652
  0.7 13.2 %copy-start.4 = (f32[16,16,128]{2,1,0:T(8,128)S(1)}, f32[16,16,128]{2,1,0:T(8,128)}, u32[]{:S(2)}) copy-start(f32[16,16,128]{2,1,0:T(8,128)} %param.9) | copy-start | bytes 393220
  2.9 10.9 %copy-start.1 = (f32[224,128]{1,0:T(8,128)S(1)}, f32[224,128]{1,0:T(8,128)}, u32[]{:S(2)}) copy-start(f32[224,128]{1,0:T(8,128)} %constant.6.clone.tab_any.tab_ref.rest_5_.rest_7_.rest_9_) | copy-start | bytes 344068
  2.9 14.8 %all-to-all-start = ((f32[32,4,128]{2,1,0:T(4,128)}), f32[32,4,128]{2,1,0:T(4,128)S(1)}, u32[]{:S(2)}, u32[]{:S(2)}) async-start(f32[32,4,128]{2,1,0:T(4,128)} %get-tuple-element.93), calls=%async_computation | async-start | bytes 131072 | tf_op jit(solution)/shard_map/all_to_all | solution.py:691
  10.2 3.6 %copy-start.5 = (f32[8,128]{1,0:T(8,128)S(1)}, f32[8,128]{1,0:T(8,128)}, u32[]{:S(2)}) copy-start(f32[8,128]{1,0:T(8,128)} %constant.8.clone.places_ref) | copy-start | bytes 12292
  10.2 4.7 %collective-permute-start = (f32[16,128]{1,0:T(8,128)S(1)}, f32[16,128]{1,0:T(8,128)S(1)}, u32[]{:S(2)}, u32[]{:S(2)}) collective-permute-start(f32[16,128]{1,0:T(8,128)S(1)} %get-tuple-element.94), channel_id=1, source_target_pairs={{0,16},{16,0},{1,17},{17,1},{2,18},{18,2},{3,19},{19,3},{4,20},{20... | collective-permute-start | bytes 24584 | tf_op jit(solution)/shard_map/ppermute | solution.py:687
  12.1 3.1 %collective-permute-start.1 = (f32[16,128]{1,0:T(8,128)S(1)}, f32[16,128]{1,0:T(8,128)S(1)}, u32[]{:S(2)}, u32[]{:S(2)}) collective-permute-start(f32[16,128]{1,0:T(8,128)S(1)} %get-tuple-element.95), channel_id=1, source_target_pairs={{0,4},{4,8},{8,12},{12,0},{1,5},{5,9},{9,13},{13,1},{2,6},{6,10},{... | collective-permute-start | bytes 24584 | tf_op jit(solution)/shard_map/ppermute | solution.py:687
  12.1 3.1 %collective-permute-start.2 = (f32[16,128]{1,0:T(8,128)S(1)}, f32[16,128]{1,0:T(8,128)S(1)}, u32[]{:S(2)}, u32[]{:S(2)}) collective-permute-start(f32[16,128]{1,0:T(8,128)S(1)} %get-tuple-element.96), channel_id=1, source_target_pairs={{0,12},{4,0},{8,4},{12,8},{1,13},{5,1},{9,5},{13,9},{2,14},{6,2},{... | collective-permute-start | bytes 24584 | tf_op jit(solution)/shard_map/ppermute | solution.py:687
  13.8 0.7 copy-start.6
  14.5 3.2 %copy-start.3 = (f32[16,16,128]{2,1,0:T(8,128)S(1)}, f32[16,16,128]{2,1,0:T(8,128)}, u32[]{:S(2)}) copy-start(f32[16,16,128]{2,1,0:T(8,128)} %param.7) | copy-start | bytes 393220
  19.1 10.1 %all-to-all-start.1 = ((f32[32,4,128]{2,1,0:T(4,128)}), f32[32,4,128]{2,1,0:T(4,128)S(1)}, u32[]{:S(2)}, u32[]{:S(2)}) async-start(f32[32,4,128]{2,1,0:T(4,128)} %get-tuple-element.99), calls=%async_computation.1 | async-start | bytes 131072 | tf_op jit(solution)/shard_map/all_to_all | solution.py:691
  21.7 3.7 %collective-permute-start.3 = (f32[16,128]{1,0:T(8,128)S(1)}, f32[16,128]{1,0:T(8,128)S(1)}, u32[]{:S(2)}, u32[]{:S(2)}) collective-permute-start(f32[16,128]{1,0:T(8,128)S(1)} %get-tuple-element.100), channel_id=1, source_target_pairs={{0,16},{16,0},{1,17},{17,1},{2,18},{18,2},{3,19},{19,3},{4,20},{20... | collective-permute-start | bytes 24584 | tf_op jit(solution)/shard_map/ppermute | solution.py:687
  23.4 3.1 %collective-permute-start.4 = (f32[16,128]{1,0:T(8,128)S(1)}, f32[16,128]{1,0:T(8,128)S(1)}, u32[]{:S(2)}, u32[]{:S(2)}) collective-permute-start(f32[16,128]{1,0:T(8,128)S(1)} %get-tuple-element.101), channel_id=1, source_target_pairs={{0,4},{4,8},{8,12},{12,0},{1,5},{5,9},{9,13},{13,1},{2,6},{6,10},{... | collective-permute-start | bytes 24584 | tf_op jit(solution)/shard_map/ppermute | solution.py:687
  23.4 3.1 %collective-permute-start.5 = (f32[16,128]{1,0:T(8,128)S(1)}, f32[16,128]{1,0:T(8,128)S(1)}, u32[]{:S(2)}, u32[]{:S(2)}) collective-permute-start(f32[16,128]{1,0:T(8,128)S(1)} %get-tuple-element.102), channel_id=1, source_target_pairs={{0,12},{4,0},{8,4},{12,8},{1,13},{5,1},{9,5},{13,9},{2,14},{6,2},{... | collective-permute-start | bytes 24584 | tf_op jit(solution)/shard_map/ppermute | solution.py:687
  30.6 10.1 %all-to-all-start.2 = ((f32[32,4,128]{2,1,0:T(4,128)}), f32[32,4,128]{2,1,0:T(4,128)S(1)}, u32[]{:S(2)}, u32[]{:S(2)}) async-start(f32[32,4,128]{2,1,0:T(4,128)} %get-tuple-element.109), calls=%async_computation.2 | async-start | bytes 131072 | tf_op jit(solution)/shard_map/all_to_all | solution.py:691
  33.2 3.9 %collective-permute-start.6 = (f32[32,128]{1,0:T(8,128)S(1)}, f32[32,128]{1,0:T(8,128)S(1)}, u32[]{:S(2)}, u32[]{:S(2)}) collective-permute-start(f32[32,128]{1,0:T(8,128)S(1)} %get-tuple-element.110), channel_id=1, source_target_pairs={{0,16},{16,0},{1,17},{17,1},{2,18},{18,2},{3,19},{19,3},{4,20},{20... | collective-permute-start | bytes 49160 | tf_op jit(solution)/shard_map/ppermute | solution.py:687
  34.9 3.2 %collective-permute-start.7 = (f32[32,128]{1,0:T(8,128)S(1)}, f32[32,128]{1,0:T(8,128)S(1)}, u32[]{:S(2)}, u32[]{:S(2)}) collective-permute-start(f32[32,128]{1,0:T(8,128)S(1)} %get-tuple-element.111), channel_id=1, source_target_pairs={{0,4},{4,8},{8,12},{12,0},{1,5},{5,9},{9,13},{13,1},{2,6},{6,10},{... | collective-permute-start | bytes 49160 | tf_op jit(solution)/shard_map/ppermute | solution.py:687
  34.9 3.2 %collective-permute-start.8 = (f32[32,128]{1,0:T(8,128)S(1)}, f32[32,128]{1,0:T(8,128)S(1)}, u32[]{:S(2)}, u32[]{:S(2)}) collective-permute-start(f32[32,128]{1,0:T(8,128)S(1)} %get-tuple-element.112), channel_id=1, source_target_pairs={{0,12},{4,0},{8,4},{12,8},{1,13},{5,1},{9,5},{13,9},{2,14},{6,2},{... | collective-permute-start | bytes 49160 | tf_op jit(solution)/shard_map/ppermute | solution.py:687
  42.0 10.1 %all-to-all-start.3 = ((f32[32,4,128]{2,1,0:T(4,128)}), f32[32,4,128]{2,1,0:T(4,128)S(1)}, u32[]{:S(2)}, u32[]{:S(2)}) async-start(f32[32,4,128]{2,1,0:T(4,128)} %get-tuple-element.116), calls=%async_computation.3 | async-start | bytes 131072 | tf_op jit(solution)/shard_map/all_to_all | solution.py:691
  44.6 3.9 %collective-permute-start.9 = (f32[16,128]{1,0:T(8,128)S(1)}, f32[16,128]{1,0:T(8,128)S(1)}, u32[]{:S(2)}, u32[]{:S(2)}) collective-permute-start(f32[16,128]{1,0:T(8,128)S(1)} %get-tuple-element.117), channel_id=1, source_target_pairs={{0,16},{16,0},{1,17},{17,1},{2,18},{18,2},{3,19},{19,3},{4,20},{20... | collective-permute-start | bytes 24584 | tf_op jit(solution)/shard_map/ppermute | solution.py:687
  46.3 3.1 %collective-permute-start.10 = (f32[16,128]{1,0:T(8,128)S(1)}, f32[16,128]{1,0:T(8,128)S(1)}, u32[]{:S(2)}, u32[]{:S(2)}) collective-permute-start(f32[16,128]{1,0:T(8,128)S(1)} %get-tuple-element.118), channel_id=1, source_target_pairs={{0,4},{4,8},{8,12},{12,0},{1,5},{5,9},{9,13},{13,1},{2,6},{6,10},{... | collective-permute-start | bytes 24584 | tf_op jit(solution)/shard_map/ppermute | solution.py:687
  46.3 3.1 %collective-permute-start.11 = (f32[16,128]{1,0:T(8,128)S(1)}, f32[16,128]{1,0:T(8,128)S(1)}, u32[]{:S(2)}, u32[]{:S(2)}) collective-permute-start(f32[16,128]{1,0:T(8,128)S(1)} %get-tuple-element.119), channel_id=1, source_target_pairs={{0,12},{4,0},{8,4},{12,8},{1,13},{5,1},{9,5},{13,9},{2,14},{6,2},{... | collective-permute-start | bytes 24584 | tf_op jit(solution)/shard_map/ppermute | solution.py:687
  53.6 10.1 %all-to-all-start.4 = ((f32[32,4,128]{2,1,0:T(4,128)}), f32[32,4,128]{2,1,0:T(4,128)S(1)}, u32[]{:S(2)}, u32[]{:S(2)}) async-start(f32[32,4,128]{2,1,0:T(4,128)} %get-tuple-element.127), calls=%async_computation.4 | async-start | bytes 131072 | tf_op jit(solution)/shard_map/all_to_all | solution.py:691
  56.1 3.7 %collective-permute-start.12 = (f32[16,128]{1,0:T(8,128)S(1)}, f32[16,128]{1,0:T(8,128)S(1)}, u32[]{:S(2)}, u32[]{:S(2)}) collective-permute-start(f32[16,128]{1,0:T(8,128)S(1)} %get-tuple-element.128), channel_id=1, source_target_pairs={{0,16},{16,0},{1,17},{17,1},{2,18},{18,2},{3,19},{19,3},{4,20},{20... | collective-permute-start | bytes 24584 | tf_op jit(solution)/shard_map/ppermute | solution.py:687
  57.8 3.1 %collective-permute-start.13 = (f32[16,128]{1,0:T(8,128)S(1)}, f32[16,128]{1,0:T(8,128)S(1)}, u32[]{:S(2)}, u32[]{:S(2)}) collective-permute-start(f32[16,128]{1,0:T(8,128)S(1)} %get-tuple-element.129), channel_id=1, source_target_pairs={{0,4},{4,8},{8,12},{12,0},{1,5},{5,9},{9,13},{13,1},{2,6},{6,10},{... | collective-permute-start | bytes 24584 | tf_op jit(solution)/shard_map/ppermute | solution.py:687
  57.9 3.1 %collective-permute-start.14 = (f32[16,128]{1,0:T(8,128)S(1)}, f32[16,128]{1,0:T(8,128)S(1)}, u32[]{:S(2)}, u32[]{:S(2)}) collective-permute-start(f32[16,128]{1,0:T(8,128)S(1)} %get-tuple-element.130), channel_id=1, source_target_pairs={{0,12},{4,0},{8,4},{12,8},{1,13},{5,1},{9,5},{13,9},{2,14},{6,2},{... | collective-permute-start | bytes 24584 | tf_op jit(solution)/shard_map/ppermute | solution.py:687
  65.2 10.1 %all-to-all-start.5 = ((f32[32,4,128]{2,1,0:T(4,128)}), f32[32,4,128]{2,1,0:T(4,128)S(1)}, u32[]{:S(2)}, u32[]{:S(2)}) async-start(f32[32,4,128]{2,1,0:T(4,128)} %get-tuple-element.135), calls=%async_computation.5 | async-start | bytes 131072 | tf_op jit(solution)/shard_map/all_to_all | solution.py:691
  67.8 3.7 %collective-permute-start.15 = (f32[16,128]{1,0:T(8,128)S(1)}, f32[16,128]{1,0:T(8,128)S(1)}, u32[]{:S(2)}, u32[]{:S(2)}) collective-permute-start(f32[16,128]{1,0:T(8,128)S(1)} %get-tuple-element.136), channel_id=1, source_target_pairs={{0,16},{16,0},{1,17},{17,1},{2,18},{18,2},{3,19},{19,3},{4,20},{20... | collective-permute-start | bytes 24584 | tf_op jit(solution)/shard_map/ppermute | solution.py:687
  69.5 3.1 %collective-permute-start.16 = (f32[16,128]{1,0:T(8,128)S(1)}, f32[16,128]{1,0:T(8,128)S(1)}, u32[]{:S(2)}, u32[]{:S(2)}) collective-permute-start(f32[16,128]{1,0:T(8,128)S(1)} %get-tuple-element.137), channel_id=1, source_target_pairs={{0,4},{4,8},{8,12},{12,0},{1,5},{5,9},{9,13},{13,1},{2,6},{6,10},{... | collective-permute-start | bytes 24584 | tf_op jit(solution)/shard_map/ppermute | solution.py:687
  69.5 3.1 %collective-permute-start.17 = (f32[16,128]{1,0:T(8,128)S(1)}, f32[16,128]{1,0:T(8,128)S(1)}, u32[]{:S(2)}, u32[]{:S(2)}) collective-permute-start(f32[16,128]{1,0:T(8,128)S(1)} %get-tuple-element.138), channel_id=1, source_target_pairs={{0,12},{4,0},{8,4},{12,8},{1,13},{5,1},{9,5},{13,9},{2,14},{6,2},{... | collective-permute-start | bytes 24584 | tf_op jit(solution)/shard_map/ppermute | solution.py:687
  76.7 10.1 %all-to-all-start.6 = ((f32[32,4,128]{2,1,0:T(4,128)}), f32[32,4,128]{2,1,0:T(4,128)S(1)}, u32[]{:S(2)}, u32[]{:S(2)}) async-start(f32[32,4,128]{2,1,0:T(4,128)} %get-tuple-element.146), calls=%async_computation.6 | async-start | bytes 131072 | tf_op jit(solution)/shard_map/all_to_all | solution.py:691
  79.3 3.7 %collective-permute-start.18 = (f32[16,128]{1,0:T(8,128)S(1)}, f32[16,128]{1,0:T(8,128)S(1)}, u32[]{:S(2)}, u32[]{:S(2)}) collective-permute-start(f32[16,128]{1,0:T(8,128)S(1)} %get-tuple-element.147), channel_id=1, source_target_pairs={{0,16},{16,0},{1,17},{17,1},{2,18},{18,2},{3,19},{19,3},{4,20},{20... | collective-permute-start | bytes 24584 | tf_op jit(solution)/shard_map/ppermute | solution.py:687
  81.0 3.1 %collective-permute-start.19 = (f32[16,128]{1,0:T(8,128)S(1)}, f32[16,128]{1,0:T(8,128)S(1)}, u32[]{:S(2)}, u32[]{:S(2)}) collective-permute-start(f32[16,128]{1,0:T(8,128)S(1)} %get-tuple-element.148), channel_id=1, source_target_pairs={{0,4},{4,8},{8,12},{12,0},{1,5},{5,9},{9,13},{13,1},{2,6},{6,10},{... | collective-permute-start | bytes 24584 | tf_op jit(solution)/shard_map/ppermute | solution.py:687
  81.0 3.1 %collective-permute-start.20 = (f32[16,128]{1,0:T(8,128)S(1)}, f32[16,128]{1,0:T(8,128)S(1)}, u32[]{:S(2)}, u32[]{:S(2)}) collective-permute-start(f32[16,128]{1,0:T(8,128)S(1)} %get-tuple-element.149), channel_id=1, source_target_pairs={{0,12},{4,0},{8,4},{12,8},{1,13},{5,1},{9,5},{13,9},{2,14},{6,2},{... | collective-permute-start | bytes 24584 | tf_op jit(solution)/shard_map/ppermute | solution.py:687
  88.3 10.1 %all-to-all-start.7 = ((f32[32,4,128]{2,1,0:T(4,128)}), f32[32,4,128]{2,1,0:T(4,128)S(1)}, u32[]{:S(2)}, u32[]{:S(2)}) async-start(f32[32,4,128]{2,1,0:T(4,128)} %get-tuple-element.157), calls=%async_computation.7 | async-start | bytes 131072 | tf_op jit(solution)/shard_map/all_to_all | solution.py:691
  90.9 3.7 %collective-permute-start.21 = (f32[16,128]{1,0:T(8,128)S(1)}, f32[16,128]{1,0:T(8,128)S(1)}, u32[]{:S(2)}, u32[]{:S(2)}) collective-permute-start(f32[16,128]{1,0:T(8,128)S(1)} %get-tuple-element.158), channel_id=1, source_target_pairs={{0,16},{16,0},{1,17},{17,1},{2,18},{18,2},{3,19},{19,3},{4,20},{20... | collective-permute-start | bytes 24584 | tf_op jit(solution)/shard_map/ppermute | solution.py:687
  92.6 3.1 %collective-permute-start.22 = (f32[16,128]{1,0:T(8,128)S(1)}, f32[16,128]{1,0:T(8,128)S(1)}, u32[]{:S(2)}, u32[]{:S(2)}) collective-permute-start(f32[16,128]{1,0:T(8,128)S(1)} %get-tuple-element.159), channel_id=1, source_target_pairs={{0,4},{4,8},{8,12},{12,0},{1,5},{5,9},{9,13},{13,1},{2,6},{6,10},{... | collective-permute-start | bytes 24584 | tf_op jit(solution)/shard_map/ppermute | solution.py:687
  92.6 3.1 %collective-permute-start.23 = (f32[16,128]{1,0:T(8,128)S(1)}, f32[16,128]{1,0:T(8,128)S(1)}, u32[]{:S(2)}, u32[]{:S(2)}) collective-permute-start(f32[16,128]{1,0:T(8,128)S(1)} %get-tuple-element.160), channel_id=1, source_target_pairs={{0,12},{4,0},{8,4},{12,8},{1,13},{5,1},{9,5},{13,9},{2,14},{6,2},{... | collective-permute-start | bytes 24584 | tf_op jit(solution)/shard_map/ppermute | solution.py:687
  99.8 10.1 %all-to-all-start.8 = ((f32[32,4,128]{2,1,0:T(4,128)}), f32[32,4,128]{2,1,0:T(4,128)S(1)}, u32[]{:S(2)}, u32[]{:S(2)}) async-start(f32[32,4,128]{2,1,0:T(4,128)} %get-tuple-element.168), calls=%async_computation.8 | async-start | bytes 131072 | tf_op jit(solution)/shard_map/all_to_all | solution.py:691
  102.4 3.7 %collective-permute-start.24 = (f32[16,128]{1,0:T(8,128)S(1)}, f32[16,128]{1,0:T(8,128)S(1)}, u32[]{:S(2)}, u32[]{:S(2)}) collective-permute-start(f32[16,128]{1,0:T(8,128)S(1)} %get-tuple-element.169), channel_id=1, source_target_pairs={{0,16},{16,0},{1,17},{17,1},{2,18},{18,2},{3,19},{19,3},{4,20},{20... | collective-permute-start | bytes 24584 | tf_op jit(solution)/shard_map/ppermute | solution.py:687
  104.1 3.1 %collective-permute-start.25 = (f32[16,128]{1,0:T(8,128)S(1)}, f32[16,128]{1,0:T(8,128)S(1)}, u32[]{:S(2)}, u32[]{:S(2)}) collective-permute-start(f32[16,128]{1,0:T(8,128)S(1)} %get-tuple-element.170), channel_id=1, source_target_pairs={{0,4},{4,8},{8,12},{12,0},{1,5},{5,9},{9,13},{13,1},{2,6},{6,10},{... | collective-permute-start | bytes 24584 | tf_op jit(solution)/shard_map/ppermute | solution.py:687
  104.1 3.1 %collective-permute-start.26 = (f32[16,128]{1,0:T(8,128)S(1)}, f32[16,128]{1,0:T(8,128)S(1)}, u32[]{:S(2)}, u32[]{:S(2)}) collective-permute-start(f32[16,128]{1,0:T(8,128)S(1)} %get-tuple-element.171), channel_id=1, source_target_pairs={{0,12},{4,0},{8,4},{12,8},{1,13},{5,1},{9,5},{13,9},{2,14},{6,2},{... | collective-permute-start | bytes 24584 | tf_op jit(solution)/shard_map/ppermute | solution.py:687

commit v6 on v5

--- a/solution.py
+++ b/solution.py
@@ -847,11 +847,11 @@
     def make_iterate(first, final):
         def iterate_kernel(recv, *rest):
             xs, ys = rest[:nx], rest[nx : nx + ny]
-            n_in = 9 + (0 if first else 3)
+            n_in = 9 + (0 if first else 3 if final else 1)
             ins = rest[nx + ny : nx + ny + n_in]
             fin_ref, r_ref, u_in, dinv_ref, scaled_ref, state_in = ins[:6]
             tab_ref, zt_ref, hot_ref = ins[6:9]
-            p_in, si_in, x_in = (None, None, None) if first else ins[9:12]
+            si_in, p_in, x_in = (*ins[9:], None, None, None)[:3]
             out = rest[nx + ny + n_in :]
             if final:
                 send, oxs, oys = out[0], (), ()
@@ -860,21 +860,21 @@
                 f_ref = r_out = si_ref = None
             else:
                 send, oxs, oys = split(out[:n_out])
-                u_ref, state_ref, p_ref, x_ref, r_out, si_ref, f_ref, w_ref, work, zwork, q_ref = out[
+                u_ref, state_ref, r_out, si_ref, f_ref, w_ref, work, zwork, q_ref = out[
                     n_out:
                 ]
             geo = Geometry(sizes)
             row, gamma, curvature, beta, alpha = step_sizes(lay, recv, state_in, first)
             received(geo, lay, fin_ref[...], recv, xs, ys, w_ref, 0)
             image = w_ref[...]
-            p = u_in[...]
             s_row, ts_row = state_in[0:1, :], row
             if not first:
-                p = p + beta * p_in[...]
                 image = image + beta * si_in[...]
                 ts_row = ts_row + beta * state_in[1:2, :]
-            p_ref[...] = p
-            x_ref[...] = alpha * p if first else x_in[...] + alpha * p
+            if final:
+                p = u_in[...] + beta * p_in[...]
+                p_ref[...] = p
+                x_ref[...] = x_in[...] + alpha * p
             residual = r_ref[...] - alpha * image
             if not final:
                 si_ref[...] = image
@@ -895,6 +895,17 @@
             )
 
         return iterate_kernel
+
+    def first_update_kernel(state_ref, u_in, p_ref, x_ref):
+        p = u_in[...]
+        p_ref[...] = p
+        x_ref[...] = state_ref[2:3, 0:1] / state_ref[3:4, 0:1] * p
+
+    def update_kernel(state_ref, u_in, old_ref, p_in, x_in, p_ref, x_ref):
+        gamma = state_ref[2:3, 0:1]
+        p = u_in[...] + gamma / old_ref[2:3, 0:1] * p_in[...]
+        p_ref[...] = p
+        x_ref[...] = x_in[...] + gamma / state_ref[3:4, 0:1] * p
 
     def last_kernel(recv, state_in, u_in, p_in, x_in, out_ref):
         _, _, _, beta, alpha = step_sizes(lay, recv, state_in, False)
@@ -973,17 +984,23 @@
             got = exchange(out[:n_out])
             ins = [*got, f, residual, u, dinv, scaled, state, tab, zt, hot]
             if not first:
-                ins += [p, image, x]
+                ins.append(image)
+            if final:
+                ins += [p, x]
             fields = [block, like(8, lay.lanes), block, block]
             if final:
                 outs = [like(lay.devices, lay.scalar_rows, 128)] + fields
             else:
-                outs = outgoing(1) + fields + [block, block, block]
+                outs = outgoing(1) + fields + [block]
             out = call(make_iterate(first, final), ins, outs, [work, pair, tiles, qrows], "iterate")
             if final:
                 u, state, p, x = out[1:]
             else:
-                u, state, p, x, residual, image, f = out[n_out:]
+                old, u_old = state, u
+                u, state, residual, image, f = out[n_out:]
+                more = [] if first else [old, p, x]
+                kernel = first_update_kernel if first else update_kernel
+                p, x = call(kernel, [state, u_old, *more], [block, block], [], "update")
         recv = lax.all_to_all(out[0], AXES, 0, 0, tiled=True)
         (x,) = call(last_kernel, [recv, state, u, p, x], [block], [], "pressure")
         return level.reshape(BX, BY, BZ), x.reshape(BX, BY, BZ)

time: 121 us -> 121 us (level)
    pallas_call x13 -> x17, Pallas kernels: 16.1 us -> 16.4 us  [call(): pl.pallas_call(kernel, out_shape=outs, in_specs=[hbm if i in from_hbm els...]
  transfers between devices with their start and end apart: 36 -> 36, of which waited for: 25 -> 24; matrix products, arithmetic and copies ran while one was open for 0% -> 0% of each run, Pallas kernels for 1% -> 1%
where the time goes in v6:
time: 121 us
  starting transfers between devices  59.2 us (49%)
  waiting for transfers between devices  34.3 us (28%)
  Pallas kernels  16.4 us (14%)
  blocking collectives  9.31 us (8%)
    ppermute x27, starting transfers between devices, ring(): return lax.ppermute(v, axis, pairs)  31.3 us
    all_to_all x9, starting transfers between devices, exchange(): recv = lax.all_to_all(send, AXES, 0, 0, tiled=True)  27.9 us
    all_to_all x9, waiting for transfers between devices, exchange(): recv = lax.all_to_all(send, AXES, 0, 0, tiled=True)  23.7 us
    pallas_call x17, Pallas kernels, call(): pl.pallas_call(kernel, out_shape=outs, in_specs=[hbm if i in from_hbm els...  16.4 us
    ppermute x27, waiting for transfers between devices, ring(): return lax.ppermute(v, axis, pairs)  10.5 us
    all_to_all x1, blocking collectives, body(): recv = lax.all_to_all(out[0], AXES, 0, 0, tiled=True)  9.31 us
  transfers between devices with their start and end apart: 36, of which 24 were waited for; matrix products, arithmetic and copies ran while one was open for 0% of the time, Pallas kernels for 1%

profile of v6, /device:TPU:0, one launch (start us, length us, event | category | flops | bytes accessed | tf_op | source)
XLA Modules:
  0.0 120.7 jit_solution(10280333959811660486)
XLA Ops:
  0.7 2.2 %advect.1 = (f32[32,4,128]{2,1,0:T(4,128)}, f32[16,128]{1,0:T(8,128)S(1)}, f32[16,128]{1,0:T(8,128)S(1)}, f32[16,128]{1,0:T(8,128)S(1)}, f32[256,128]{1,0:T(8,128)S(1)}) custom-call(f32[256,128]{1,0:T(8,128)} %bitcast.7, f32[3,256,128]{2,1,0:T(8,128)} %bitcast.5, f32[224,128]{1,0:T(8,128)} %constant.6.clone.tab_any.tab_ref.rest_5_.rest_7_.rest_9_, ...), custom_call_target="tpu_custom_call" | custom-call | flops 4000000 | bytes 1000000 | tf_op jit(solution)/shard_map/advect/pallas_call | solution.py:665
  2.9 7.3 %all-to-all-start = ((f32[32,4,128]{2,1,0:T(4,128)}), f32[32,4,128]{2,1,0:T(4,128)S(1)}, u32[]{:S(2)}, u32[]{:S(2)}) async-start(f32[32,4,128]{2,1,0:T(4,128)} %get-tuple-element.93), calls=%async_computation | async-start | bytes 131072 | tf_op jit(solution)/shard_map/all_to_all | solution.py:691
  10.2 1.8 %collective-permute-start = (f32[16,128]{1,0:T(8,128)S(1)}, f32[16,128]{1,0:T(8,128)S(1)}, u32[]{:S(2)}, u32[]{:S(2)}) collective-permute-start(f32[16,128]{1,0:T(8,128)S(1)} %get-tuple-element.94), channel_id=1, source_target_pairs={{0,16},{16,0},{1,17},{17,1},{2,18},{18,2},{3,19},{19,3},{4,20},{20... | collective-permute-start | bytes 24584 | tf_op jit(solution)/shard_map/ppermute | solution.py:687
  12.1 1.7 %collective-permute-start.2 = (f32[16,128]{1,0:T(8,128)S(1)}, f32[16,128]{1,0:T(8,128)S(1)}, u32[]{:S(2)}, u32[]{:S(2)}) collective-permute-start(f32[16,128]{1,0:T(8,128)S(1)} %get-tuple-element.96), channel_id=1, source_target_pairs={{0,12},{4,0},{8,4},{12,8},{1,13},{5,1},{9,5},{13,9},{2,14},{6,2},{... | collective-permute-start | bytes 24584 | tf_op jit(solution)/shard_map/ppermute | solution.py:687
  13.8 0.6 copy-done.6
  14.5 0.5 source.1
  15.2 2.5 %all-to-all-done.recv = f32[32,4,128]{2,1,0:T(4,128)S(1)} async-done(((f32[32,4,128]{2,1,0:T(4,128)}), f32[32,4,128]{2,1,0:T(4,128)S(1)}, u32[]{:S(2)}, u32[]{:S(2)}) %all-to-all-start) | async-done | bytes 65568 | tf_op jit(solution)/shard_map/all_to_all | solution.py:691
  17.7 1.4 %sweep_first.1 = (f32[32,4,128]{2,1,0:T(4,128)}, f32[16,128]{1,0:T(8,128)S(1)}, f32[16,128]{1,0:T(8,128)S(1)}, f32[16,128]{1,0:T(8,128)S(1)}, f32[256,128]{1,0:T(8,128)S(1)}, /*index=5*/f32[256,128]{1,0:T(8,128)S(1)}) custom-call(f32[32,4,128]{2,1,0:T(4,128)S(1)} %all-to-all-done.recv, f32[16,128]{1,0:T(8,128)S(1)} %collective-permute-done.rest_0_, ...), custom_call_target="tpu_custom_call" | custom-call | flops 4000000 | bytes 1000000 | tf_op jit(solution)/shard_map/sweep_first/pallas_call | solution.py:665
  19.1 2.6 %all-to-all-start.1 = ((f32[32,4,128]{2,1,0:T(4,128)}), f32[32,4,128]{2,1,0:T(4,128)S(1)}, u32[]{:S(2)}, u32[]{:S(2)}) async-start(f32[32,4,128]{2,1,0:T(4,128)} %get-tuple-element.99), calls=%async_computation.1 | async-start | bytes 131072 | tf_op jit(solution)/shard_map/all_to_all | solution.py:691
  21.7 1.7 %collective-permute-start.3 = (f32[16,128]{1,0:T(8,128)S(1)}, f32[16,128]{1,0:T(8,128)S(1)}, u32[]{:S(2)}, u32[]{:S(2)}) collective-permute-start(f32[16,128]{1,0:T(8,128)S(1)} %get-tuple-element.100), channel_id=1, source_target_pairs={{0,16},{16,0},{1,17},{17,1},{2,18},{18,2},{3,19},{19,3},{4,20},{20... | collective-permute-start | bytes 24584 | tf_op jit(solution)/shard_map/ppermute | solution.py:687
  23.4 1.7 %collective-permute-start.5 = (f32[16,128]{1,0:T(8,128)S(1)}, f32[16,128]{1,0:T(8,128)S(1)}, u32[]{:S(2)}, u32[]{:S(2)}) collective-permute-start(f32[16,128]{1,0:T(8,128)S(1)} %get-tuple-element.102), channel_id=1, source_target_pairs={{0,12},{4,0},{8,4},{12,8},{1,13},{5,1},{9,5},{13,9},{2,14},{6,2},{... | collective-permute-start | bytes 24584 | tf_op jit(solution)/shard_map/ppermute | solution.py:687
  25.2 0.3 collective-permute-done.3.rest_0_
  25.4 1.1 collective-permute-done.4.rest_1_
  26.6 2.7 %all-to-all-done.1.recv.rest_3_ = f32[32,4,128]{2,1,0:T(4,128)S(1)} async-done(((f32[32,4,128]{2,1,0:T(4,128)}), f32[32,4,128]{2,1,0:T(4,128)S(1)}, u32[]{:S(2)}, u32[]{:S(2)}) %all-to-all-start.1) | async-done | bytes 65568 | tf_op jit(solution)/shard_map/all_to_all | solution.py:691
  29.2 1.4 %sweep.1 = (f32[32,4,128]{2,1,0:T(4,128)}, f32[32,128]{1,0:T(8,128)S(1)}, f32[32,128]{1,0:T(8,128)S(1)}, f32[32,128]{1,0:T(8,128)S(1)}, f32[256,128]{1,0:T(8,128)S(1)}, /*index=5*/f32[256,128]{1,0:T(8,128)S(1)}) custom-call(f32[32,4,128]{2,1,0:T(4,128)S(1)} %all-to-all-done.1.recv.rest_3_, f32[16,128]{1,0:T(8,128)S(1)} %collective-permute-done.3.rest_0_, ...), custom_call_target="tpu_custom_call" | custom-call | flops 4000000 | bytes 1000000 | tf_op jit(solution)/shard_map/sweep/pallas_call | solution.py:665
  30.6 2.6 %all-to-all-start.2 = ((f32[32,4,128]{2,1,0:T(4,128)}), f32[32,4,128]{2,1,0:T(4,128)S(1)}, u32[]{:S(2)}, u32[]{:S(2)}) async-start(f32[32,4,128]{2,1,0:T(4,128)} %get-tuple-element.109), calls=%async_computation.2 | async-start | bytes 131072 | tf_op jit(solution)/shard_map/all_to_all | solution.py:691
  33.2 1.7 %collective-permute-start.6 = (f32[32,128]{1,0:T(8,128)S(1)}, f32[32,128]{1,0:T(8,128)S(1)}, u32[]{:S(2)}, u32[]{:S(2)}) collective-permute-start(f32[32,128]{1,0:T(8,128)S(1)} %get-tuple-element.110), channel_id=1, source_target_pairs={{0,16},{16,0},{1,17},{17,1},{2,18},{18,2},{3,19},{19,3},{4,20},{20... | collective-permute-start | bytes 49160 | tf_op jit(solution)/shard_map/ppermute | solution.py:687
  34.9 1.7 %collective-permute-start.8 = (f32[32,128]{1,0:T(8,128)S(1)}, f32[32,128]{1,0:T(8,128)S(1)}, u32[]{:S(2)}, u32[]{:S(2)}) collective-permute-start(f32[32,128]{1,0:T(8,128)S(1)} %get-tuple-element.112), channel_id=1, source_target_pairs={{0,12},{4,0},{8,4},{12,8},{1,13},{5,1},{9,5},{13,9},{2,14},{6,2},{... | collective-permute-start | bytes 49160 | tf_op jit(solution)/shard_map/ppermute | solution.py:687
  36.7 0.4 collective-permute-done.6.rest_0_
  37.1 1.0 collective-permute-done.7.rest_1_
  38.2 2.6 %all-to-all-done.2.recv = f32[32,4,128]{2,1,0:T(4,128)S(1)} async-done(((f32[32,4,128]{2,1,0:T(4,128)}), f32[32,4,128]{2,1,0:T(4,128)S(1)}, u32[]{:S(2)}, u32[]{:S(2)}) %all-to-all-start.2) | async-done | bytes 65568 | tf_op jit(solution)/shard_map/all_to_all | solution.py:691
  40.7 1.3 %diagonal.1 = (f32[32,4,128]{2,1,0:T(4,128)}, f32[16,128]{1,0:T(8,128)S(1)}, f32[16,128]{1,0:T(8,128)S(1)}, f32[16,128]{1,0:T(8,128)S(1)}, f32[256,128]{1,0:T(8,...) custom-call(f32[32,4,128]{2,1,0:T(4,128)S(1)} %all-to-all-done.2.recv, ...), custom_call_target="tpu_custom_call" | custom-call | flops 4000000 | bytes 1000000 | tf_op jit(solution)/shard_map/diagonal/pallas_call | solution.py:665
  42.0 2.6 %all-to-all-start.3 = ((f32[32,4,128]{2,1,0:T(4,128)}), f32[32,4,128]{2,1,0:T(4,128)S(1)}, u32[]{:S(2)}, u32[]{:S(2)}) async-start(f32[32,4,128]{2,1,0:T(4,128)} %get-tuple-element.116), calls=%async_computation.3 | async-start | bytes 131072 | tf_op jit(solution)/shard_map/all_to_all | solution.py:691
  44.6 1.7 %collective-permute-start.9 = (f32[16,128]{1,0:T(8,128)S(1)}, f32[16,128]{1,0:T(8,128)S(1)}, u32[]{:S(2)}, u32[]{:S(2)}) collective-permute-start(f32[16,128]{1,0:T(8,128)S(1)} %get-tuple-element.117), channel_id=1, source_target_pairs={{0,16},{16,0},{1,17},{17,1},{2,18},{18,2},{3,19},{19,3},{4,20},{20... | collective-permute-start | bytes 24584 | tf_op jit(solution)/shard_map/ppermute | solution.py:687
  46.3 1.7 %collective-permute-start.11 = (f32[16,128]{1,0:T(8,128)S(1)}, f32[16,128]{1,0:T(8,128)S(1)}, u32[]{:S(2)}, u32[]{:S(2)}) collective-permute-start(f32[16,128]{1,0:T(8,128)S(1)} %get-tuple-element.119), channel_id=1, source_target_pairs={{0,12},{4,0},{8,4},{12,8},{1,13},{5,1},{9,5},{13,9},{2,14},{6,2},{... | collective-permute-start | bytes 24584 | tf_op jit(solution)/shard_map/ppermute | solution.py:687
  48.1 0.4 rhs.1
  48.5 0.9 collective-permute-done.10.rest_1_
  49.4 2.7 %all-to-all-done.3.recv = f32[32,4,128]{2,1,0:T(4,128)S(1)} async-done(((f32[32,4,128]{2,1,0:T(4,128)}), f32[32,4,128]{2,1,0:T(4,128)S(1)}, u32[]{:S(2)}, u32[]{:S(2)}) %all-to-all-start.3) | async-done | bytes 65568 | tf_op jit(solution)/shard_map/all_to_all | solution.py:691
  52.1 1.5 %solve_start.1 = (f32[32,4,128]{2,1,0:T(4,128)}, f32[16,128]{1,0:T(8,128)S(1)}, f32[16,128]{1,0:T(8,128)S(1)}, f32[16,128]{1,0:T(8,128)S(1)}, f32[256,128]{1,0:T...) custom-call(f32[32,4,128]{2,1,0:T(4,128)S(1)} %all-to-all-done.3.recv, ...), custom_call_target="tpu_custom_call" | custom-call | flops 4000000 | bytes 1000000 | tf_op jit(solution)/shard_map/solve_start/pallas_call | solution.py:665
  53.6 2.6 %all-to-all-start.4 = ((f32[32,4,128]{2,1,0:T(4,128)}), f32[32,4,128]{2,1,0:T(4,128)S(1)}, u32[]{:S(2)}, u32[]{:S(2)}) async-start(f32[32,4,128]{2,1,0:T(4,128)} %get-tuple-element.127), calls=%async_computation.4 | async-start | bytes 131072 | tf_op jit(solution)/shard_map/all_to_all | solution.py:691
  56.1 1.7 %collective-permute-start.12 = (f32[16,128]{1,0:T(8,128)S(1)}, f32[16,128]{1,0:T(8,128)S(1)}, u32[]{:S(2)}, u32[]{:S(2)}) collective-permute-start(f32[16,128]{1,0:T(8,128)S(1)} %get-tuple-element.128), channel_id=1, source_target_pairs={{0,16},{16,0},{1,17},{17,1},{2,18},{18,2},{3,19},{19,3},{4,20},{20... | collective-permute-start | bytes 24584 | tf_op jit(solution)/shard_map/ppermute | solution.py:687
  57.9 1.7 %collective-permute-start.14 = (f32[16,128]{1,0:T(8,128)S(1)}, f32[16,128]{1,0:T(8,128)S(1)}, u32[]{:S(2)}, u32[]{:S(2)}) collective-permute-start(f32[16,128]{1,0:T(8,128)S(1)} %get-tuple-element.130), channel_id=1, source_target_pairs={{0,12},{4,0},{8,4},{12,8},{1,13},{5,1},{9,5},{13,9},{2,14},{6,2},{... | collective-permute-start | bytes 24584 | tf_op jit(solution)/shard_map/ppermute | solution.py:687
  59.6 0.3 collective-permute-done.12.rest_0_
  59.9 1.1 collective-permute-done.13.rest_1_
  61.0 2.7 %all-to-all-done.4.recv = f32[32,4,128]{2,1,0:T(4,128)S(1)} async-done(((f32[32,4,128]{2,1,0:T(4,128)}), f32[32,4,128]{2,1,0:T(4,128)S(1)}, u32[]{:S(2)}, u32[]{:S(2)}) %all-to-all-start.4) | async-done | bytes 65568 | tf_op jit(solution)/shard_map/all_to_all | solution.py:691
  63.6 1.5 %iterate.5 = (f32[32,4,128]{2,1,0:T(4,128)}, f32[16,128]{1,0:T(8,128)S(1)}, f32[16,128]{1,0:T(8,128)S(1)}, f32[16,128]{1,0:T(8,128)S(1)}, f32[256,128]{1,0:T(8,1...) custom-call(f32[32,4,128]{2,1,0:T(4,128)S(1)} %all-to-all-done.4.recv,, ...), custom_call_target="tpu_custom_call" | custom-call | flops 4000000 | bytes 1000000 | tf_op jit(solution)/shard_map/iterate/pallas_call | solution.py:665
  65.2 2.6 %all-to-all-start.5 = ((f32[32,4,128]{2,1,0:T(4,128)}), f32[32,4,128]{2,1,0:T(4,128)S(1)}, u32[]{:S(2)}, u32[]{:S(2)}) async-start(f32[32,4,128]{2,1,0:T(4,128)} %get-tuple-element.135), calls=%async_computation.5 | async-start | bytes 131072 | tf_op jit(solution)/shard_map/all_to_all | solution.py:691
  67.8 1.7 %collective-permute-start.15 = (f32[16,128]{1,0:T(8,128)S(1)}, f32[16,128]{1,0:T(8,128)S(1)}, u32[]{:S(2)}, u32[]{:S(2)}) collective-permute-start(f32[16,128]{1,0:T(8,128)S(1)} %get-tuple-element.136), channel_id=1, source_target_pairs={{0,16},{16,0},{1,17},{17,1},{2,18},{18,2},{3,19},{19,3},{4,20},{20... | collective-permute-start | bytes 24584 | tf_op jit(solution)/shard_map/ppermute | solution.py:687
  69.5 1.7 %collective-permute-start.17 = (f32[16,128]{1,0:T(8,128)S(1)}, f32[16,128]{1,0:T(8,128)S(1)}, u32[]{:S(2)}, u32[]{:S(2)}) collective-permute-start(f32[16,128]{1,0:T(8,128)S(1)} %get-tuple-element.138), channel_id=1, source_target_pairs={{0,12},{4,0},{8,4},{12,8},{1,13},{5,1},{9,5},{13,9},{2,14},{6,2},{... | collective-permute-start | bytes 24584 | tf_op jit(solution)/shard_map/ppermute | solution.py:687
  71.2 0.3 collective-permute-done.15.rest_0_
  71.5 1.1 collective-permute-done.16.rest_1_
  72.6 2.7 %all-to-all-done.5.recv = f32[32,4,128]{2,1,0:T(4,128)S(1)} async-done(((f32[32,4,128]{2,1,0:T(4,128)}), f32[32,4,128]{2,1,0:T(4,128)S(1)}, u32[]{:S(2)}, u32[]{:S(2)}) %all-to-all-start.5) | async-done | bytes 65568 | tf_op jit(solution)/shard_map/all_to_all | solution.py:691
  75.2 1.5 %iterate.6 = (f32[32,4,128]{2,1,0:T(4,128)}, f32[16,128]{1,0:T(8,128)S(1)}, f32[16,128]{1,0:T(8,128)S(1)}, f32[16,128]{1,0:T(8,128)S(1)}, f32[256,128]{1,0:T(8,1...) custom-call(f32[32,4,128]{2,1,0:T(4,128)S(1)} %all-to-all-done.5.recv,, ...), custom_call_target="tpu_custom_call" | custom-call | flops 4000000 | bytes 1000000 | tf_op jit(solution)/shard_map/iterate/pallas_call | solution.py:665
  76.7 2.6 %all-to-all-start.6 = ((f32[32,4,128]{2,1,0:T(4,128)}), f32[32,4,128]{2,1,0:T(4,128)S(1)}, u32[]{:S(2)}, u32[]{:S(2)}) async-start(f32[32,4,128]{2,1,0:T(4,128)} %get-tuple-element.144), calls=%async_computation.6 | async-start | bytes 131072 | tf_op jit(solution)/shard_map/all_to_all | solution.py:691
  79.3 1.7 %collective-permute-start.18 = (f32[16,128]{1,0:T(8,128)S(1)}, f32[16,128]{1,0:T(8,128)S(1)}, u32[]{:S(2)}, u32[]{:S(2)}) collective-permute-start(f32[16,128]{1,0:T(8,128)S(1)} %get-tuple-element.145), channel_id=1, source_target_pairs={{0,16},{16,0},{1,17},{17,1},{2,18},{18,2},{3,19},{19,3},{4,20},{20... | collective-permute-start | bytes 24584 | tf_op jit(solution)/shard_map/ppermute | solution.py:687
  81.0 1.7 %collective-permute-start.20 = (f32[16,128]{1,0:T(8,128)S(1)}, f32[16,128]{1,0:T(8,128)S(1)}, u32[]{:S(2)}, u32[]{:S(2)}) collective-permute-start(f32[16,128]{1,0:T(8,128)S(1)} %get-tuple-element.147), channel_id=1, source_target_pairs={{0,12},{4,0},{8,4},{12,8},{1,13},{5,1},{9,5},{13,9},{2,14},{6,2},{... | collective-permute-start | bytes 24584 | tf_op jit(solution)/shard_map/ppermute | solution.py:687
  82.8 0.3 collective-permute-done.18.rest_0_
  83.0 1.1 collective-permute-done.19.rest_1_
  84.1 2.7 %all-to-all-done.6.recv = f32[32,4,128]{2,1,0:T(4,128)S(1)} async-done(((f32[32,4,128]{2,1,0:T(4,128)}), f32[32,4,128]{2,1,0:T(4,128)S(1)}, u32[]{:S(2)}, u32[]{:S(2)}) %all-to-all-start.6) | async-done | bytes 65568 | tf_op jit(solution)/shard_map/all_to_all | solution.py:691
  86.8 1.5 %iterate.7 = (f32[32,4,128]{2,1,0:T(4,128)}, f32[16,128]{1,0:T(8,128)S(1)}, f32[16,128]{1,0:T(8,128)S(1)}, f32[16,128]{1,0:T(8,128)S(1)}, f32[256,128]{1,0:T(8,1...) custom-call(f32[32,4,128]{2,1,0:T(4,128)S(1)} %all-to-all-done.6.recv,, ...), custom_call_target="tpu_custom_call" | custom-call | flops 4000000 | bytes 1000000 | tf_op jit(solution)/shard_map/iterate/pallas_call | solution.py:665
  88.3 2.6 %all-to-all-start.7 = ((f32[32,4,128]{2,1,0:T(4,128)}), f32[32,4,128]{2,1,0:T(4,128)S(1)}, u32[]{:S(2)}, u32[]{:S(2)}) async-start(f32[32,4,128]{2,1,0:T(4,128)} %get-tuple-element.153), calls=%async_computation.7 | async-start | bytes 131072 | tf_op jit(solution)/shard_map/all_to_all | solution.py:691
  90.8 1.7 %collective-permute-start.21 = (f32[16,128]{1,0:T(8,128)S(1)}, f32[16,128]{1,0:T(8,128)S(1)}, u32[]{:S(2)}, u32[]{:S(2)}) collective-permute-start(f32[16,128]{1,0:T(8,128)S(1)} %get-tuple-element.154), channel_id=1, source_target_pairs={{0,16},{16,0},{1,17},{17,1},{2,18},{18,2},{3,19},{19,3},{4,20},{20... | collective-permute-start | bytes 24584 | tf_op jit(solution)/shard_map/ppermute | solution.py:687
  92.6 1.7 %collective-permute-start.23 = (f32[16,128]{1,0:T(8,128)S(1)}, f32[16,128]{1,0:T(8,128)S(1)}, u32[]{:S(2)}, u32[]{:S(2)}) collective-permute-start(f32[16,128]{1,0:T(8,128)S(1)} %get-tuple-element.156), channel_id=1, source_target_pairs={{0,12},{4,0},{8,4},{12,8},{1,13},{5,1},{9,5},{13,9},{2,14},{6,2},{... | collective-permute-start | bytes 24584 | tf_op jit(solution)/shard_map/ppermute | solution.py:687
  94.6 1.1 collective-permute-done.22.rest_1_
  95.7 2.7 %all-to-all-done.7.recv = f32[32,4,128]{2,1,0:T(4,128)S(1)} async-done(((f32[32,4,128]{2,1,0:T(4,128)}), f32[32,4,128]{2,1,0:T(4,128)S(1)}, u32[]{:S(2)}, u32[]{:S(2)}) %all-to-all-start.7) | async-done | bytes 65568 | tf_op jit(solution)/shard_map/all_to_all | solution.py:691
  98.3 1.5 %iterate.8 = (f32[32,4,128]{2,1,0:T(4,128)}, f32[16,128]{1,0:T(8,128)S(1)}, f32[16,128]{1,0:T(8,128)S(1)}, f32[16,128]{1,0:T(8,128)S(1)}, f32[256,128]{1,0:T(8,1...) custom-call(f32[32,4,128]{2,1,0:T(4,128)S(1)} %all-to-all-done.7.recv,, ...), custom_call_target="tpu_custom_call" | custom-call | flops 4000000 | bytes 1000000 | tf_op jit(solution)/shard_map/iterate/pallas_call | solution.py:665
  99.8 2.6 %all-to-all-start.8 = ((f32[32,4,128]{2,1,0:T(4,128)}), f32[32,4,128]{2,1,0:T(4,128)S(1)}, u32[]{:S(2)}, u32[]{:S(2)}) async-start(f32[32,4,128]{2,1,0:T(4,128)} %get-tuple-element.162), calls=%async_computation.8 | async-start | bytes 131072 | tf_op jit(solution)/shard_map/all_to_all | solution.py:691
  102.4 1.7 %collective-permute-start.24 = (f32[16,128]{1,0:T(8,128)S(1)}, f32[16,128]{1,0:T(8,128)S(1)}, u32[]{:S(2)}, u32[]{:S(2)}) collective-permute-start(f32[16,128]{1,0:T(8,128)S(1)} %get-tuple-element.163), channel_id=1, source_target_pairs={{0,16},{16,0},{1,17},{17,1},{2,18},{18,2},{3,19},{19,3},{4,20},{20... | collective-permute-start | bytes 24584 | tf_op jit(solution)/shard_map/ppermute | solution.py:687
  104.1 1.7 %collective-permute-start.26 = (f32[16,128]{1,0:T(8,128)S(1)}, f32[16,128]{1,0:T(8,128)S(1)}, u32[]{:S(2)}, u32[]{:S(2)}) collective-permute-start(f32[16,128]{1,0:T(8,128)S(1)} %get-tuple-element.165), channel_id=1, source_target_pairs={{0,12},{4,0},{8,4},{12,8},{1,13},{5,1},{9,5},{13,9},{2,14},{6,2},{... | collective-permute-start | bytes 24584 | tf_op jit(solution)/shard_map/ppermute | solution.py:687
  106.2 1.0 collective-permute-done.25.rest_1_
  107.2 2.7 %all-to-all-done.8.recv = f32[32,4,128]{2,1,0:T(4,128)S(1)} async-done(((f32[32,4,128]{2,1,0:T(4,128)}), f32[32,4,128]{2,1,0:T(4,128)S(1)}, u32[]{:S(2)}, u32[]{:S(2)}) %all-to-all-start.8) | async-done | bytes 65568 | tf_op jit(solution)/shard_map/all_to_all | solution.py:691
  109.9 0.6 iterate.9
  110.5 9.3 %all_to_all.50.recv = f32[32,1,128]{2,1,0:T(1,128)S(1)} all-to-all(f32[32,1,128]{2,1,0:T(1,128)S(1)} %get-tuple-element.179), channel_id=1, replica_groups=mesh['gx'=2,'gy'=4,'gz'=4] {'gx','gy','gz'}, dimensions={0} | all-to-all | bytes 32768 | tf_op jit(solution)/shard_map/all_to_all | solution.py:1004
  119.9 0.8 pressure.1
  (40 shorter events, 1.0 us)
Async XLA Ops:
  0.6 13.2 %copy-start = (bf16[768,256]{1,0:T(8,128)(2,1)S(1)}, bf16[768,256]{1,0:T(8,128)(2,1)}, u32[]{:S(2)}) copy-start(bf16[768,256]{1,0:T(8,128)(2,1)} %constant.7.clone.zt_any.zt_ref.rest_6_.rest_8_.rest_10_) | copy-start | bytes 1179652
  0.6 13.2 %copy-start.2 = (f32[3,16,16,128]{3,2,1,0:T(8,128)S(1)}, f32[3,16,16,128]{3,2,1,0:T(8,128)}, u32[]{:S(2)}) copy-start(f32[3,16,16,128]{3,2,1,0:T(8,128)} %param.8) | copy-start | bytes 1179652
  0.7 13.2 %copy-start.4 = (f32[16,16,128]{2,1,0:T(8,128)S(1)}, f32[16,16,128]{2,1,0:T(8,128)}, u32[]{:S(2)}) copy-start(f32[16,16,128]{2,1,0:T(8,128)} %param.9) | copy-start | bytes 393220
  2.9 10.9 %copy-start.1 = (f32[224,128]{1,0:T(8,128)S(1)}, f32[224,128]{1,0:T(8,128)}, u32[]{:S(2)}) copy-start(f32[224,128]{1,0:T(8,128)} %constant.6.clone.tab_any.tab_ref.rest_5_.rest_7_.rest_9_) | copy-start | bytes 344068
  2.9 14.8 %all-to-all-start = ((f32[32,4,128]{2,1,0:T(4,128)}), f32[32,4,128]{2,1,0:T(4,128)S(1)}, u32[]{:S(2)}, u32[]{:S(2)}) async-start(f32[32,4,128]{2,1,0:T(4,128)} %get-tuple-element.93), calls=%async_computation | async-start | bytes 131072 | tf_op jit(solution)/shard_map/all_to_all | solution.py:691
  10.2 3.6 %copy-start.5 = (f32[8,128]{1,0:T(8,128)S(1)}, f32[8,128]{1,0:T(8,128)}, u32[]{:S(2)}) copy-start(f32[8,128]{1,0:T(8,128)} %constant.8.clone.places_ref) | copy-start | bytes 12292
  10.2 4.7 %collective-permute-start = (f32[16,128]{1,0:T(8,128)S(1)}, f32[16,128]{1,0:T(8,128)S(1)}, u32[]{:S(2)}, u32[]{:S(2)}) collective-permute-start(f32[16,128]{1,0:T(8,128)S(1)} %get-tuple-element.94), channel_id=1, source_target_pairs={{0,16},{16,0},{1,17},{17,1},{2,18},{18,2},{3,19},{19,3},{4,20},{20... | collective-permute-start | bytes 24584 | tf_op jit(solution)/shard_map/ppermute | solution.py:687
  12.1 3.1 %collective-permute-start.1 = (f32[16,128]{1,0:T(8,128)S(1)}, f32[16,128]{1,0:T(8,128)S(1)}, u32[]{:S(2)}, u32[]{:S(2)}) collective-permute-start(f32[16,128]{1,0:T(8,128)S(1)} %get-tuple-element.95), channel_id=1, source_target_pairs={{0,4},{4,8},{8,12},{12,0},{1,5},{5,9},{9,13},{13,1},{2,6},{6,10},{... | collective-permute-start | bytes 24584 | tf_op jit(solution)/shard_map/ppermute | solution.py:687
  12.1 3.1 %collective-permute-start.2 = (f32[16,128]{1,0:T(8,128)S(1)}, f32[16,128]{1,0:T(8,128)S(1)}, u32[]{:S(2)}, u32[]{:S(2)}) collective-permute-start(f32[16,128]{1,0:T(8,128)S(1)} %get-tuple-element.96), channel_id=1, source_target_pairs={{0,12},{4,0},{8,4},{12,8},{1,13},{5,1},{9,5},{13,9},{2,14},{6,2},{... | collective-permute-start | bytes 24584 | tf_op jit(solution)/shard_map/ppermute | solution.py:687
  13.8 0.7 copy-start.6
  14.5 3.2 %copy-start.3 = (f32[16,16,128]{2,1,0:T(8,128)S(1)}, f32[16,16,128]{2,1,0:T(8,128)}, u32[]{:S(2)}) copy-start(f32[16,16,128]{2,1,0:T(8,128)} %param.7) | copy-start | bytes 393220
  19.1 10.1 %all-to-all-start.1 = ((f32[32,4,128]{2,1,0:T(4,128)}), f32[32,4,128]{2,1,0:T(4,128)S(1)}, u32[]{:S(2)}, u32[]{:S(2)}) async-start(f32[32,4,128]{2,1,0:T(4,128)} %get-tuple-element.99), calls=%async_computation.1 | async-start | bytes 131072 | tf_op jit(solution)/shard_map/all_to_all | solution.py:691
  21.7 3.7 %collective-permute-start.3 = (f32[16,128]{1,0:T(8,128)S(1)}, f32[16,128]{1,0:T(8,128)S(1)}, u32[]{:S(2)}, u32[]{:S(2)}) collective-permute-start(f32[16,128]{1,0:T(8,128)S(1)} %get-tuple-element.100), channel_id=1, source_target_pairs={{0,16},{16,0},{1,17},{17,1},{2,18},{18,2},{3,19},{19,3},{4,20},{20... | collective-permute-start | bytes 24584 | tf_op jit(solution)/shard_map/ppermute | solution.py:687
  23.4 3.1 %collective-permute-start.4 = (f32[16,128]{1,0:T(8,128)S(1)}, f32[16,128]{1,0:T(8,128)S(1)}, u32[]{:S(2)}, u32[]{:S(2)}) collective-permute-start(f32[16,128]{1,0:T(8,128)S(1)} %get-tuple-element.101), channel_id=1, source_target_pairs={{0,4},{4,8},{8,12},{12,0},{1,5},{5,9},{9,13},{13,1},{2,6},{6,10},{... | collective-permute-start | bytes 24584 | tf_op jit(solution)/shard_map/ppermute | solution.py:687
  23.4 3.1 %collective-permute-start.5 = (f32[16,128]{1,0:T(8,128)S(1)}, f32[16,128]{1,0:T(8,128)S(1)}, u32[]{:S(2)}, u32[]{:S(2)}) collective-permute-start(f32[16,128]{1,0:T(8,128)S(1)} %get-tuple-element.102), channel_id=1, source_target_pairs={{0,12},{4,0},{8,4},{12,8},{1,13},{5,1},{9,5},{13,9},{2,14},{6,2},{... | collective-permute-start | bytes 24584 | tf_op jit(solution)/shard_map/ppermute | solution.py:687
  30.6 10.1 %all-to-all-start.2 = ((f32[32,4,128]{2,1,0:T(4,128)}), f32[32,4,128]{2,1,0:T(4,128)S(1)}, u32[]{:S(2)}, u32[]{:S(2)}) async-start(f32[32,4,128]{2,1,0:T(4,128)} %get-tuple-element.109), calls=%async_computation.2 | async-start | bytes 131072 | tf_op jit(solution)/shard_map/all_to_all | solution.py:691
  33.2 3.9 %collective-permute-start.6 = (f32[32,128]{1,0:T(8,128)S(1)}, f32[32,128]{1,0:T(8,128)S(1)}, u32[]{:S(2)}, u32[]{:S(2)}) collective-permute-start(f32[32,128]{1,0:T(8,128)S(1)} %get-tuple-element.110), channel_id=1, source_target_pairs={{0,16},{16,0},{1,17},{17,1},{2,18},{18,2},{3,19},{19,3},{4,20},{20... | collective-permute-start | bytes 49160 | tf_op jit(solution)/shard_map/ppermute | solution.py:687
  34.9 3.2 %collective-permute-start.7 = (f32[32,128]{1,0:T(8,128)S(1)}, f32[32,128]{1,0:T(8,128)S(1)}, u32[]{:S(2)}, u32[]{:S(2)}) collective-permute-start(f32[32,128]{1,0:T(8,128)S(1)} %get-tuple-element.111), channel_id=1, source_target_pairs={{0,4},{4,8},{8,12},{12,0},{1,5},{5,9},{9,13},{13,1},{2,6},{6,10},{... | collective-permute-start | bytes 49160 | tf_op jit(solution)/shard_map/ppermute | solution.py:687
  34.9 3.2 %collective-permute-start.8 = (f32[32,128]{1,0:T(8,128)S(1)}, f32[32,128]{1,0:T(8,128)S(1)}, u32[]{:S(2)}, u32[]{:S(2)}) collective-permute-start(f32[32,128]{1,0:T(8,128)S(1)} %get-tuple-element.112), channel_id=1, source_target_pairs={{0,12},{4,0},{8,4},{12,8},{1,13},{5,1},{9,5},{13,9},{2,14},{6,2},{... | collective-permute-start | bytes 49160 | tf_op jit(solution)/shard_map/ppermute | solution.py:687
  42.0 10.1 %all-to-all-start.3 = ((f32[32,4,128]{2,1,0:T(4,128)}), f32[32,4,128]{2,1,0:T(4,128)S(1)}, u32[]{:S(2)}, u32[]{:S(2)}) async-start(f32[32,4,128]{2,1,0:T(4,128)} %get-tuple-element.116), calls=%async_computation.3 | async-start | bytes 131072 | tf_op jit(solution)/shard_map/all_to_all | solution.py:691
  44.6 3.9 %collective-permute-start.9 = (f32[16,128]{1,0:T(8,128)S(1)}, f32[16,128]{1,0:T(8,128)S(1)}, u32[]{:S(2)}, u32[]{:S(2)}) collective-permute-start(f32[16,128]{1,0:T(8,128)S(1)} %get-tuple-element.117), channel_id=1, source_target_pairs={{0,16},{16,0},{1,17},{17,1},{2,18},{18,2},{3,19},{19,3},{4,20},{20... | collective-permute-start | bytes 24584 | tf_op jit(solution)/shard_map/ppermute | solution.py:687
  46.3 3.1 %collective-permute-start.10 = (f32[16,128]{1,0:T(8,128)S(1)}, f32[16,128]{1,0:T(8,128)S(1)}, u32[]{:S(2)}, u32[]{:S(2)}) collective-permute-start(f32[16,128]{1,0:T(8,128)S(1)} %get-tuple-element.118), channel_id=1, source_target_pairs={{0,4},{4,8},{8,12},{12,0},{1,5},{5,9},{9,13},{13,1},{2,6},{6,10},{... | collective-permute-start | bytes 24584 | tf_op jit(solution)/shard_map/ppermute | solution.py:687
  46.3 3.1 %collective-permute-start.11 = (f32[16,128]{1,0:T(8,128)S(1)}, f32[16,128]{1,0:T(8,128)S(1)}, u32[]{:S(2)}, u32[]{:S(2)}) collective-permute-start(f32[16,128]{1,0:T(8,128)S(1)} %get-tuple-element.119), channel_id=1, source_target_pairs={{0,12},{4,0},{8,4},{12,8},{1,13},{5,1},{9,5},{13,9},{2,14},{6,2},{... | collective-permute-start | bytes 24584 | tf_op jit(solution)/shard_map/ppermute | solution.py:687
  53.6 10.1 %all-to-all-start.4 = ((f32[32,4,128]{2,1,0:T(4,128)}), f32[32,4,128]{2,1,0:T(4,128)S(1)}, u32[]{:S(2)}, u32[]{:S(2)}) async-start(f32[32,4,128]{2,1,0:T(4,128)} %get-tuple-element.127), calls=%async_computation.4 | async-start | bytes 131072 | tf_op jit(solution)/shard_map/all_to_all | solution.py:691
  56.1 3.7 %collective-permute-start.12 = (f32[16,128]{1,0:T(8,128)S(1)}, f32[16,128]{1,0:T(8,128)S(1)}, u32[]{:S(2)}, u32[]{:S(2)}) collective-permute-start(f32[16,128]{1,0:T(8,128)S(1)} %get-tuple-element.128), channel_id=1, source_target_pairs={{0,16},{16,0},{1,17},{17,1},{2,18},{18,2},{3,19},{19,3},{4,20},{20... | collective-permute-start | bytes 24584 | tf_op jit(solution)/shard_map/ppermute | solution.py:687
  57.8 3.1 %collective-permute-start.13 = (f32[16,128]{1,0:T(8,128)S(1)}, f32[16,128]{1,0:T(8,128)S(1)}, u32[]{:S(2)}, u32[]{:S(2)}) collective-permute-start(f32[16,128]{1,0:T(8,128)S(1)} %get-tuple-element.129), channel_id=1, source_target_pairs={{0,4},{4,8},{8,12},{12,0},{1,5},{5,9},{9,13},{13,1},{2,6},{6,10},{... | collective-permute-start | bytes 24584 | tf_op jit(solution)/shard_map/ppermute | solution.py:687
  57.9 3.1 %collective-permute-start.14 = (f32[16,128]{1,0:T(8,128)S(1)}, f32[16,128]{1,0:T(8,128)S(1)}, u32[]{:S(2)}, u32[]{:S(2)}) collective-permute-start(f32[16,128]{1,0:T(8,128)S(1)} %get-tuple-element.130), channel_id=1, source_target_pairs={{0,12},{4,0},{8,4},{12,8},{1,13},{5,1},{9,5},{13,9},{2,14},{6,2},{... | collective-permute-start | bytes 24584 | tf_op jit(solution)/shard_map/ppermute | solution.py:687
  65.2 10.1 %all-to-all-start.5 = ((f32[32,4,128]{2,1,0:T(4,128)}), f32[32,4,128]{2,1,0:T(4,128)S(1)}, u32[]{:S(2)}, u32[]{:S(2)}) async-start(f32[32,4,128]{2,1,0:T(4,128)} %get-tuple-element.135), calls=%async_computation.5 | async-start | bytes 131072 | tf_op jit(solution)/shard_map/all_to_all | solution.py:691
  67.8 3.7 %collective-permute-start.15 = (f32[16,128]{1,0:T(8,128)S(1)}, f32[16,128]{1,0:T(8,128)S(1)}, u32[]{:S(2)}, u32[]{:S(2)}) collective-permute-start(f32[16,128]{1,0:T(8,128)S(1)} %get-tuple-element.136), channel_id=1, source_target_pairs={{0,16},{16,0},{1,17},{17,1},{2,18},{18,2},{3,19},{19,3},{4,20},{20... | collective-permute-start | bytes 24584 | tf_op jit(solution)/shard_map/ppermute | solution.py:687
  69.5 3.1 %collective-permute-start.16 = (f32[16,128]{1,0:T(8,128)S(1)}, f32[16,128]{1,0:T(8,128)S(1)}, u32[]{:S(2)}, u32[]{:S(2)}) collective-permute-start(f32[16,128]{1,0:T(8,128)S(1)} %get-tuple-element.137), channel_id=1, source_target_pairs={{0,4},{4,8},{8,12},{12,0},{1,5},{5,9},{9,13},{13,1},{2,6},{6,10},{... | collective-permute-start | bytes 24584 | tf_op jit(solution)/shard_map/ppermute | solution.py:687
  69.5 3.1 %collective-permute-start.17 = (f32[16,128]{1,0:T(8,128)S(1)}, f32[16,128]{1,0:T(8,128)S(1)}, u32[]{:S(2)}, u32[]{:S(2)}) collective-permute-start(f32[16,128]{1,0:T(8,128)S(1)} %get-tuple-element.138), channel_id=1, source_target_pairs={{0,12},{4,0},{8,4},{12,8},{1,13},{5,1},{9,5},{13,9},{2,14},{6,2},{... | collective-permute-start | bytes 24584 | tf_op jit(solution)/shard_map/ppermute | solution.py:687
  76.7 10.1 %all-to-all-start.6 = ((f32[32,4,128]{2,1,0:T(4,128)}), f32[32,4,128]{2,1,0:T(4,128)S(1)}, u32[]{:S(2)}, u32[]{:S(2)}) async-start(f32[32,4,128]{2,1,0:T(4,128)} %get-tuple-element.144), calls=%async_computation.6 | async-start | bytes 131072 | tf_op jit(solution)/shard_map/all_to_all | solution.py:691
  79.3 3.7 %collective-permute-start.18 = (f32[16,128]{1,0:T(8,128)S(1)}, f32[16,128]{1,0:T(8,128)S(1)}, u32[]{:S(2)}, u32[]{:S(2)}) collective-permute-start(f32[16,128]{1,0:T(8,128)S(1)} %get-tuple-element.145), channel_id=1, source_target_pairs={{0,16},{16,0},{1,17},{17,1},{2,18},{18,2},{3,19},{19,3},{4,20},{20... | collective-permute-start | bytes 24584 | tf_op jit(solution)/shard_map/ppermute | solution.py:687
  81.0 3.1 %collective-permute-start.19 = (f32[16,128]{1,0:T(8,128)S(1)}, f32[16,128]{1,0:T(8,128)S(1)}, u32[]{:S(2)}, u32[]{:S(2)}) collective-permute-start(f32[16,128]{1,0:T(8,128)S(1)} %get-tuple-element.146), channel_id=1, source_target_pairs={{0,4},{4,8},{8,12},{12,0},{1,5},{5,9},{9,13},{13,1},{2,6},{6,10},{... | collective-permute-start | bytes 24584 | tf_op jit(solution)/shard_map/ppermute | solution.py:687
  81.0 3.1 %collective-permute-start.20 = (f32[16,128]{1,0:T(8,128)S(1)}, f32[16,128]{1,0:T(8,128)S(1)}, u32[]{:S(2)}, u32[]{:S(2)}) collective-permute-start(f32[16,128]{1,0:T(8,128)S(1)} %get-tuple-element.147), channel_id=1, source_target_pairs={{0,12},{4,0},{8,4},{12,8},{1,13},{5,1},{9,5},{13,9},{2,14},{6,2},{... | collective-permute-start | bytes 24584 | tf_op jit(solution)/shard_map/ppermute | solution.py:687
  88.3 10.1 %all-to-all-start.7 = ((f32[32,4,128]{2,1,0:T(4,128)}), f32[32,4,128]{2,1,0:T(4,128)S(1)}, u32[]{:S(2)}, u32[]{:S(2)}) async-start(f32[32,4,128]{2,1,0:T(4,128)} %get-tuple-element.153), calls=%async_computation.7 | async-start | bytes 131072 | tf_op jit(solution)/shard_map/all_to_all | solution.py:691
  90.8 3.7 %collective-permute-start.21 = (f32[16,128]{1,0:T(8,128)S(1)}, f32[16,128]{1,0:T(8,128)S(1)}, u32[]{:S(2)}, u32[]{:S(2)}) collective-permute-start(f32[16,128]{1,0:T(8,128)S(1)} %get-tuple-element.154), channel_id=1, source_target_pairs={{0,16},{16,0},{1,17},{17,1},{2,18},{18,2},{3,19},{19,3},{4,20},{20... | collective-permute-start | bytes 24584 | tf_op jit(solution)/shard_map/ppermute | solution.py:687
  92.6 3.1 %collective-permute-start.22 = (f32[16,128]{1,0:T(8,128)S(1)}, f32[16,128]{1,0:T(8,128)S(1)}, u32[]{:S(2)}, u32[]{:S(2)}) collective-permute-start(f32[16,128]{1,0:T(8,128)S(1)} %get-tuple-element.155), channel_id=1, source_target_pairs={{0,4},{4,8},{8,12},{12,0},{1,5},{5,9},{9,13},{13,1},{2,6},{6,10},{... | collective-permute-start | bytes 24584 | tf_op jit(solution)/shard_map/ppermute | solution.py:687
  92.6 3.1 %collective-permute-start.23 = (f32[16,128]{1,0:T(8,128)S(1)}, f32[16,128]{1,0:T(8,128)S(1)}, u32[]{:S(2)}, u32[]{:S(2)}) collective-permute-start(f32[16,128]{1,0:T(8,128)S(1)} %get-tuple-element.156), channel_id=1, source_target_pairs={{0,12},{4,0},{8,4},{12,8},{1,13},{5,1},{9,5},{13,9},{2,14},{6,2},{... | collective-permute-start | bytes 24584 | tf_op jit(solution)/shard_map/ppermute | solution.py:687
  99.8 10.1 %all-to-all-start.8 = ((f32[32,4,128]{2,1,0:T(4,128)}), f32[32,4,128]{2,1,0:T(4,128)S(1)}, u32[]{:S(2)}, u32[]{:S(2)}) async-start(f32[32,4,128]{2,1,0:T(4,128)} %get-tuple-element.162), calls=%async_computation.8 | async-start | bytes 131072 | tf_op jit(solution)/shard_map/all_to_all | solution.py:691
  102.4 3.8 %collective-permute-start.24 = (f32[16,128]{1,0:T(8,128)S(1)}, f32[16,128]{1,0:T(8,128)S(1)}, u32[]{:S(2)}, u32[]{:S(2)}) collective-permute-start(f32[16,128]{1,0:T(8,128)S(1)} %get-tuple-element.163), channel_id=1, source_target_pairs={{0,16},{16,0},{1,17},{17,1},{2,18},{18,2},{3,19},{19,3},{4,20},{20... | collective-permute-start | bytes 24584 | tf_op jit(solution)/shard_map/ppermute | solution.py:687
  104.1 3.1 %collective-permute-start.25 = (f32[16,128]{1,0:T(8,128)S(1)}, f32[16,128]{1,0:T(8,128)S(1)}, u32[]{:S(2)}, u32[]{:S(2)}) collective-permute-start(f32[16,128]{1,0:T(8,128)S(1)} %get-tuple-element.164), channel_id=1, source_target_pairs={{0,4},{4,8},{8,12},{12,0},{1,5},{5,9},{9,13},{13,1},{2,6},{6,10},{... | collective-permute-start | bytes 24584 | tf_op jit(solution)/shard_map/ppermute | solution.py:687
  104.1 3.1 %collective-permute-start.26 = (f32[16,128]{1,0:T(8,128)S(1)}, f32[16,128]{1,0:T(8,128)S(1)}, u32[]{:S(2)}, u32[]{:S(2)}) collective-permute-start(f32[16,128]{1,0:T(8,128)S(1)} %get-tuple-element.165), channel_id=1, source_target_pairs={{0,12},{4,0},{8,4},{12,8},{1,13},{5,1},{9,5},{13,9},{2,14},{6,2},{... | collective-permute-start | bytes 24584 | tf_op jit(solution)/shard_map/ppermute | solution.py:687

commit v7 on v6

--- a/solution.py
+++ b/solution.py
@@ -666,7 +666,7 @@
             kernel,
             out_shape=outs,
             in_specs=[hbm if i in from_hbm else spec for i in range(len(ins))],
-            out_specs=[spec] * len(outs),
+            out_specs=[hbm if name == "pressure" else spec] * len(outs),
             scratch_shapes=scratch,
             compiler_params=pltpu.CompilerParams(vmem_limit_bytes=48 * 1024 * 1024),
             cost_estimate=pl.CostEstimate(flops=4000000, bytes_accessed=1000000, transcendentals=0),
@@ -907,9 +907,16 @@
         p_ref[...] = p
         x_ref[...] = x_in[...] + gamma / state_ref[3:4, 0:1] * p
 
-    def last_kernel(recv, state_in, u_in, p_in, x_in, out_ref):
+    def last_kernel(recv, state_in, u_in, p_in, x_in, out_ref, work, sems):
         _, _, _, beta, alpha = step_sizes(lay, recv, state_in, False)
-        out_ref[...] = x_in[...] + alpha * (u_in[...] + beta * p_in[...])
+        copies = []
+        for i in range(2):
+            part = slice(i * ROWS // 2, (i + 1) * ROWS // 2)
+            work[part, :] = x_in[part, :] + alpha * (u_in[part, :] + beta * p_in[part, :])
+            copies.append(pltpu.make_async_copy(work.at[part], out_ref.at[part], sems.at[i]))
+            copies[i].start()
+        for copy in copies:
+            copy.wait()
 
     def body(level_set, velocity, source, coarse_factor):
         level = level_set.reshape(ROWS, BZ)
@@ -1002,7 +1009,7 @@
                 kernel = first_update_kernel if first else update_kernel
                 p, x = call(kernel, [state, u_old, *more], [block, block], [], "update")
         recv = lax.all_to_all(out[0], AXES, 0, 0, tiled=True)
-        (x,) = call(last_kernel, [recv, state, u, p, x], [block], [], "pressure")
+        (x,) = call(last_kernel, [recv, state, u, p, x], [block], [work, pltpu.SemaphoreType.DMA((2,))], "pressure")
         return level.reshape(BX, BY, BZ), x.reshape(BX, BY, BZ)
 
     return body

time: 121 us -> 121 us (level)
  no operation moved by 1% of the time
where the time goes in v7:
time: 121 us
  starting transfers between devices  59.2 us (49%)
  waiting for transfers between devices  34.3 us (28%)
  Pallas kernels  16.4 us (14%)
  blocking collectives  9.31 us (8%)
    ppermute x27, starting transfers between devices, ring(): return lax.ppermute(v, axis, pairs)  31.3 us
    all_to_all x9, starting transfers between devices, exchange(): recv = lax.all_to_all(send, AXES, 0, 0, tiled=True)  27.9 us
    all_to_all x9, waiting for transfers between devices, exchange(): recv = lax.all_to_all(send, AXES, 0, 0, tiled=True)  23.7 us
    pallas_call x17, Pallas kernels, call(): pl.pallas_call(kernel, out_shape=outs, in_specs=[hbm if i in from_hbm els...  16.4 us
    ppermute x27, waiting for transfers between devices, ring(): return lax.ppermute(v, axis, pairs)  10.5 us
    all_to_all x1, blocking collectives, body(): recv = lax.all_to_all(out[0], AXES, 0, 0, tiled=True)  9.31 us
  transfers between devices with their start and end apart: 36, of which 24 were waited for; matrix products, arithmetic and copies ran while one was open for 0% of the time, Pallas kernels for 1%

profile of v7, /device:TPU:0, one launch (start us, length us, event | category | flops | bytes accessed | tf_op | source)
XLA Modules:
  0.0 120.7 jit_solution(9691841863837699266)
XLA Ops:
  0.7 2.2 %advect.1 = (f32[32,4,128]{2,1,0:T(4,128)}, f32[16,128]{1,0:T(8,128)S(1)}, f32[16,128]{1,0:T(8,128)S(1)}, f32[16,128]{1,0:T(8,128)S(1)}, f32[256,128]{1,0:T(8,128)S(1)}) custom-call(f32[256,128]{1,0:T(8,128)} %bitcast.7, f32[3,256,128]{2,1,0:T(8,128)} %bitcast.5, f32[224,128]{1,0:T(8,128)} %constant.6.clone.tab_any.tab_ref.rest_5_.rest_7_.rest_9_, ...), custom_call_target="tpu_custom_call" | custom-call | flops 4000000 | bytes 1000000 | tf_op jit(solution)/shard_map/advect/pallas_call | solution.py:665
  2.9 7.3 %all-to-all-start = ((f32[32,4,128]{2,1,0:T(4,128)}), f32[32,4,128]{2,1,0:T(4,128)S(1)}, u32[]{:S(2)}, u32[]{:S(2)}) async-start(f32[32,4,128]{2,1,0:T(4,128)} %get-tuple-element.93), calls=%async_computation | async-start | bytes 131072 | tf_op jit(solution)/shard_map/all_to_all | solution.py:691
  10.2 1.8 %collective-permute-start = (f32[16,128]{1,0:T(8,128)S(1)}, f32[16,128]{1,0:T(8,128)S(1)}, u32[]{:S(2)}, u32[]{:S(2)}) collective-permute-start(f32[16,128]{1,0:T(8,128)S(1)} %get-tuple-element.94), channel_id=1, source_target_pairs={{0,16},{16,0},{1,17},{17,1},{2,18},{18,2},{3,19},{19,3},{4,20},{20... | collective-permute-start | bytes 24584 | tf_op jit(solution)/shard_map/ppermute | solution.py:687
  12.1 1.7 %collective-permute-start.2 = (f32[16,128]{1,0:T(8,128)S(1)}, f32[16,128]{1,0:T(8,128)S(1)}, u32[]{:S(2)}, u32[]{:S(2)}) collective-permute-start(f32[16,128]{1,0:T(8,128)S(1)} %get-tuple-element.96), channel_id=1, source_target_pairs={{0,12},{4,0},{8,4},{12,8},{1,13},{5,1},{9,5},{13,9},{2,14},{6,2},{... | collective-permute-start | bytes 24584 | tf_op jit(solution)/shard_map/ppermute | solution.py:687
  13.8 0.6 copy-done.6
  14.5 0.5 source.1
  15.2 2.5 %all-to-all-done.recv = f32[32,4,128]{2,1,0:T(4,128)S(1)} async-done(((f32[32,4,128]{2,1,0:T(4,128)}), f32[32,4,128]{2,1,0:T(4,128)S(1)}, u32[]{:S(2)}, u32[]{:S(2)}) %all-to-all-start) | async-done | bytes 65568 | tf_op jit(solution)/shard_map/all_to_all | solution.py:691
  17.7 1.4 %sweep_first.1 = (f32[32,4,128]{2,1,0:T(4,128)}, f32[16,128]{1,0:T(8,128)S(1)}, f32[16,128]{1,0:T(8,128)S(1)}, f32[16,128]{1,0:T(8,128)S(1)}, f32[256,128]{1,0:T(8,128)S(1)}, /*index=5*/f32[256,128]{1,0:T(8,128)S(1)}) custom-call(f32[32,4,128]{2,1,0:T(4,128)S(1)} %all-to-all-done.recv, f32[16,128]{1,0:T(8,128)S(1)} %collective-permute-done.rest_0_, ...), custom_call_target="tpu_custom_call" | custom-call | flops 4000000 | bytes 1000000 | tf_op jit(solution)/shard_map/sweep_first/pallas_call | solution.py:665
  19.1 2.6 %all-to-all-start.1 = ((f32[32,4,128]{2,1,0:T(4,128)}), f32[32,4,128]{2,1,0:T(4,128)S(1)}, u32[]{:S(2)}, u32[]{:S(2)}) async-start(f32[32,4,128]{2,1,0:T(4,128)} %get-tuple-element.99), calls=%async_computation.1 | async-start | bytes 131072 | tf_op jit(solution)/shard_map/all_to_all | solution.py:691
  21.7 1.7 %collective-permute-start.3 = (f32[16,128]{1,0:T(8,128)S(1)}, f32[16,128]{1,0:T(8,128)S(1)}, u32[]{:S(2)}, u32[]{:S(2)}) collective-permute-start(f32[16,128]{1,0:T(8,128)S(1)} %get-tuple-element.100), channel_id=1, source_target_pairs={{0,16},{16,0},{1,17},{17,1},{2,18},{18,2},{3,19},{19,3},{4,20},{20... | collective-permute-start | bytes 24584 | tf_op jit(solution)/shard_map/ppermute | solution.py:687
  23.4 1.7 %collective-permute-start.5 = (f32[16,128]{1,0:T(8,128)S(1)}, f32[16,128]{1,0:T(8,128)S(1)}, u32[]{:S(2)}, u32[]{:S(2)}) collective-permute-start(f32[16,128]{1,0:T(8,128)S(1)} %get-tuple-element.102), channel_id=1, source_target_pairs={{0,12},{4,0},{8,4},{12,8},{1,13},{5,1},{9,5},{13,9},{2,14},{6,2},{... | collective-permute-start | bytes 24584 | tf_op jit(solution)/shard_map/ppermute | solution.py:687
  25.2 0.3 collective-permute-done.3.rest_0_
  25.4 1.1 collective-permute-done.4.rest_1_
  26.6 2.7 %all-to-all-done.1.recv.rest_3_ = f32[32,4,128]{2,1,0:T(4,128)S(1)} async-done(((f32[32,4,128]{2,1,0:T(4,128)}), f32[32,4,128]{2,1,0:T(4,128)S(1)}, u32[]{:S(2)}, u32[]{:S(2)}) %all-to-all-start.1) | async-done | bytes 65568 | tf_op jit(solution)/shard_map/all_to_all | solution.py:691
  29.2 1.4 %sweep.1 = (f32[32,4,128]{2,1,0:T(4,128)}, f32[32,128]{1,0:T(8,128)S(1)}, f32[32,128]{1,0:T(8,128)S(1)}, f32[32,128]{1,0:T(8,128)S(1)}, f32[256,128]{1,0:T(8,128)S(1)}, /*index=5*/f32[256,128]{1,0:T(8,128)S(1)}) custom-call(f32[32,4,128]{2,1,0:T(4,128)S(1)} %all-to-all-done.1.recv.rest_3_, f32[16,128]{1,0:T(8,128)S(1)} %collective-permute-done.3.rest_0_, ...), custom_call_target="tpu_custom_call" | custom-call | flops 4000000 | bytes 1000000 | tf_op jit(solution)/shard_map/sweep/pallas_call | solution.py:665
  30.6 2.6 %all-to-all-start.2 = ((f32[32,4,128]{2,1,0:T(4,128)}), f32[32,4,128]{2,1,0:T(4,128)S(1)}, u32[]{:S(2)}, u32[]{:S(2)}) async-start(f32[32,4,128]{2,1,0:T(4,128)} %get-tuple-element.109), calls=%async_computation.2 | async-start | bytes 131072 | tf_op jit(solution)/shard_map/all_to_all | solution.py:691
  33.2 1.7 %collective-permute-start.6 = (f32[32,128]{1,0:T(8,128)S(1)}, f32[32,128]{1,0:T(8,128)S(1)}, u32[]{:S(2)}, u32[]{:S(2)}) collective-permute-start(f32[32,128]{1,0:T(8,128)S(1)} %get-tuple-element.110), channel_id=1, source_target_pairs={{0,16},{16,0},{1,17},{17,1},{2,18},{18,2},{3,19},{19,3},{4,20},{20... | collective-permute-start | bytes 49160 | tf_op jit(solution)/shard_map/ppermute | solution.py:687
  34.9 1.7 %collective-permute-start.8 = (f32[32,128]{1,0:T(8,128)S(1)}, f32[32,128]{1,0:T(8,128)S(1)}, u32[]{:S(2)}, u32[]{:S(2)}) collective-permute-start(f32[32,128]{1,0:T(8,128)S(1)} %get-tuple-element.112), channel_id=1, source_target_pairs={{0,12},{4,0},{8,4},{12,8},{1,13},{5,1},{9,5},{13,9},{2,14},{6,2},{... | collective-permute-start | bytes 49160 | tf_op jit(solution)/shard_map/ppermute | solution.py:687
  36.7 0.4 collective-permute-done.6.rest_0_
  37.1 1.0 collective-permute-done.7.rest_1_
  38.2 2.6 %all-to-all-done.2.recv = f32[32,4,128]{2,1,0:T(4,128)S(1)} async-done(((f32[32,4,128]{2,1,0:T(4,128)}), f32[32,4,128]{2,1,0:T(4,128)S(1)}, u32[]{:S(2)}, u32[]{:S(2)}) %all-to-all-start.2) | async-done | bytes 65568 | tf_op jit(solution)/shard_map/all_to_all | solution.py:691
  40.7 1.3 %diagonal.1 = (f32[32,4,128]{2,1,0:T(4,128)}, f32[16,128]{1,0:T(8,128)S(1)}, f32[16,128]{1,0:T(8,128)S(1)}, f32[16,128]{1,0:T(8,128)S(1)}, f32[256,128]{1,0:T(8,...) custom-call(f32[32,4,128]{2,1,0:T(4,128)S(1)} %all-to-all-done.2.recv, ...), custom_call_target="tpu_custom_call" | custom-call | flops 4000000 | bytes 1000000 | tf_op jit(solution)/shard_map/diagonal/pallas_call | solution.py:665
  42.0 2.6 %all-to-all-start.3 = ((f32[32,4,128]{2,1,0:T(4,128)}), f32[32,4,128]{2,1,0:T(4,128)S(1)}, u32[]{:S(2)}, u32[]{:S(2)}) async-start(f32[32,4,128]{2,1,0:T(4,128)} %get-tuple-element.116), calls=%async_computation.3 | async-start | bytes 131072 | tf_op jit(solution)/shard_map/all_to_all | solution.py:691
  44.6 1.7 %collective-permute-start.9 = (f32[16,128]{1,0:T(8,128)S(1)}, f32[16,128]{1,0:T(8,128)S(1)}, u32[]{:S(2)}, u32[]{:S(2)}) collective-permute-start(f32[16,128]{1,0:T(8,128)S(1)} %get-tuple-element.117), channel_id=1, source_target_pairs={{0,16},{16,0},{1,17},{17,1},{2,18},{18,2},{3,19},{19,3},{4,20},{20... | collective-permute-start | bytes 24584 | tf_op jit(solution)/shard_map/ppermute | solution.py:687
  46.3 1.7 %collective-permute-start.11 = (f32[16,128]{1,0:T(8,128)S(1)}, f32[16,128]{1,0:T(8,128)S(1)}, u32[]{:S(2)}, u32[]{:S(2)}) collective-permute-start(f32[16,128]{1,0:T(8,128)S(1)} %get-tuple-element.119), channel_id=1, source_target_pairs={{0,12},{4,0},{8,4},{12,8},{1,13},{5,1},{9,5},{13,9},{2,14},{6,2},{... | collective-permute-start | bytes 24584 | tf_op jit(solution)/shard_map/ppermute | solution.py:687
  48.1 0.4 rhs.1
  48.5 0.9 collective-permute-done.10.rest_1_
  49.4 2.7 %all-to-all-done.3.recv = f32[32,4,128]{2,1,0:T(4,128)S(1)} async-done(((f32[32,4,128]{2,1,0:T(4,128)}), f32[32,4,128]{2,1,0:T(4,128)S(1)}, u32[]{:S(2)}, u32[]{:S(2)}) %all-to-all-start.3) | async-done | bytes 65568 | tf_op jit(solution)/shard_map/all_to_all | solution.py:691
  52.1 1.5 %solve_start.1 = (f32[32,4,128]{2,1,0:T(4,128)}, f32[16,128]{1,0:T(8,128)S(1)}, f32[16,128]{1,0:T(8,128)S(1)}, f32[16,128]{1,0:T(8,128)S(1)}, f32[256,128]{1,0:T...) custom-call(f32[32,4,128]{2,1,0:T(4,128)S(1)} %all-to-all-done.3.recv, ...), custom_call_target="tpu_custom_call" | custom-call | flops 4000000 | bytes 1000000 | tf_op jit(solution)/shard_map/solve_start/pallas_call | solution.py:665
  53.6 2.6 %all-to-all-start.4 = ((f32[32,4,128]{2,1,0:T(4,128)}), f32[32,4,128]{2,1,0:T(4,128)S(1)}, u32[]{:S(2)}, u32[]{:S(2)}) async-start(f32[32,4,128]{2,1,0:T(4,128)} %get-tuple-element.127), calls=%async_computation.4 | async-start | bytes 131072 | tf_op jit(solution)/shard_map/all_to_all | solution.py:691
  56.1 1.7 %collective-permute-start.12 = (f32[16,128]{1,0:T(8,128)S(1)}, f32[16,128]{1,0:T(8,128)S(1)}, u32[]{:S(2)}, u32[]{:S(2)}) collective-permute-start(f32[16,128]{1,0:T(8,128)S(1)} %get-tuple-element.128), channel_id=1, source_target_pairs={{0,16},{16,0},{1,17},{17,1},{2,18},{18,2},{3,19},{19,3},{4,20},{20... | collective-permute-start | bytes 24584 | tf_op jit(solution)/shard_map/ppermute | solution.py:687
  57.9 1.7 %collective-permute-start.14 = (f32[16,128]{1,0:T(8,128)S(1)}, f32[16,128]{1,0:T(8,128)S(1)}, u32[]{:S(2)}, u32[]{:S(2)}) collective-permute-start(f32[16,128]{1,0:T(8,128)S(1)} %get-tuple-element.130), channel_id=1, source_target_pairs={{0,12},{4,0},{8,4},{12,8},{1,13},{5,1},{9,5},{13,9},{2,14},{6,2},{... | collective-permute-start | bytes 24584 | tf_op jit(solution)/shard_map/ppermute | solution.py:687
  59.6 0.3 collective-permute-done.12.rest_0_
  59.9 1.1 collective-permute-done.13.rest_1_
  61.0 2.7 %all-to-all-done.4.recv = f32[32,4,128]{2,1,0:T(4,128)S(1)} async-done(((f32[32,4,128]{2,1,0:T(4,128)}), f32[32,4,128]{2,1,0:T(4,128)S(1)}, u32[]{:S(2)}, u32[]{:S(2)}) %all-to-all-start.4) | async-done | bytes 65568 | tf_op jit(solution)/shard_map/all_to_all | solution.py:691
  63.6 1.5 %iterate.5 = (f32[32,4,128]{2,1,0:T(4,128)}, f32[16,128]{1,0:T(8,128)S(1)}, f32[16,128]{1,0:T(8,128)S(1)}, f32[16,128]{1,0:T(8,128)S(1)}, f32[256,128]{1,0:T(8,1...) custom-call(f32[32,4,128]{2,1,0:T(4,128)S(1)} %all-to-all-done.4.recv,, ...), custom_call_target="tpu_custom_call" | custom-call | flops 4000000 | bytes 1000000 | tf_op jit(solution)/shard_map/iterate/pallas_call | solution.py:665
  65.2 2.6 %all-to-all-start.5 = ((f32[32,4,128]{2,1,0:T(4,128)}), f32[32,4,128]{2,1,0:T(4,128)S(1)}, u32[]{:S(2)}, u32[]{:S(2)}) async-start(f32[32,4,128]{2,1,0:T(4,128)} %get-tuple-element.135), calls=%async_computation.5 | async-start | bytes 131072 | tf_op jit(solution)/shard_map/all_to_all | solution.py:691
  67.8 1.7 %collective-permute-start.15 = (f32[16,128]{1,0:T(8,128)S(1)}, f32[16,128]{1,0:T(8,128)S(1)}, u32[]{:S(2)}, u32[]{:S(2)}) collective-permute-start(f32[16,128]{1,0:T(8,128)S(1)} %get-tuple-element.136), channel_id=1, source_target_pairs={{0,16},{16,0},{1,17},{17,1},{2,18},{18,2},{3,19},{19,3},{4,20},{20... | collective-permute-start | bytes 24584 | tf_op jit(solution)/shard_map/ppermute | solution.py:687
  69.5 1.7 %collective-permute-start.17 = (f32[16,128]{1,0:T(8,128)S(1)}, f32[16,128]{1,0:T(8,128)S(1)}, u32[]{:S(2)}, u32[]{:S(2)}) collective-permute-start(f32[16,128]{1,0:T(8,128)S(1)} %get-tuple-element.138), channel_id=1, source_target_pairs={{0,12},{4,0},{8,4},{12,8},{1,13},{5,1},{9,5},{13,9},{2,14},{6,2},{... | collective-permute-start | bytes 24584 | tf_op jit(solution)/shard_map/ppermute | solution.py:687
  71.2 0.3 collective-permute-done.15.rest_0_
  71.5 1.1 collective-permute-done.16.rest_1_
  72.6 2.7 %all-to-all-done.5.recv = f32[32,4,128]{2,1,0:T(4,128)S(1)} async-done(((f32[32,4,128]{2,1,0:T(4,128)}), f32[32,4,128]{2,1,0:T(4,128)S(1)}, u32[]{:S(2)}, u32[]{:S(2)}) %all-to-all-start.5) | async-done | bytes 65568 | tf_op jit(solution)/shard_map/all_to_all | solution.py:691
  75.2 1.5 %iterate.6 = (f32[32,4,128]{2,1,0:T(4,128)}, f32[16,128]{1,0:T(8,128)S(1)}, f32[16,128]{1,0:T(8,128)S(1)}, f32[16,128]{1,0:T(8,128)S(1)}, f32[256,128]{1,0:T(8,1...) custom-call(f32[32,4,128]{2,1,0:T(4,128)S(1)} %all-to-all-done.5.recv,, ...), custom_call_target="tpu_custom_call" | custom-call | flops 4000000 | bytes 1000000 | tf_op jit(solution)/shard_map/iterate/pallas_call | solution.py:665
  76.7 2.6 %all-to-all-start.6 = ((f32[32,4,128]{2,1,0:T(4,128)}), f32[32,4,128]{2,1,0:T(4,128)S(1)}, u32[]{:S(2)}, u32[]{:S(2)}) async-start(f32[32,4,128]{2,1,0:T(4,128)} %get-tuple-element.144), calls=%async_computation.6 | async-start | bytes 131072 | tf_op jit(solution)/shard_map/all_to_all | solution.py:691
  79.3 1.7 %collective-permute-start.18 = (f32[16,128]{1,0:T(8,128)S(1)}, f32[16,128]{1,0:T(8,128)S(1)}, u32[]{:S(2)}, u32[]{:S(2)}) collective-permute-start(f32[16,128]{1,0:T(8,128)S(1)} %get-tuple-element.145), channel_id=1, source_target_pairs={{0,16},{16,0},{1,17},{17,1},{2,18},{18,2},{3,19},{19,3},{4,20},{20... | collective-permute-start | bytes 24584 | tf_op jit(solution)/shard_map/ppermute | solution.py:687
  81.0 1.7 %collective-permute-start.20 = (f32[16,128]{1,0:T(8,128)S(1)}, f32[16,128]{1,0:T(8,128)S(1)}, u32[]{:S(2)}, u32[]{:S(2)}) collective-permute-start(f32[16,128]{1,0:T(8,128)S(1)} %get-tuple-element.147), channel_id=1, source_target_pairs={{0,12},{4,0},{8,4},{12,8},{1,13},{5,1},{9,5},{13,9},{2,14},{6,2},{... | collective-permute-start | bytes 24584 | tf_op jit(solution)/shard_map/ppermute | solution.py:687
  82.8 0.3 collective-permute-done.18.rest_0_
  83.0 1.1 collective-permute-done.19.rest_1_
  84.1 2.7 %all-to-all-done.6.recv = f32[32,4,128]{2,1,0:T(4,128)S(1)} async-done(((f32[32,4,128]{2,1,0:T(4,128)}), f32[32,4,128]{2,1,0:T(4,128)S(1)}, u32[]{:S(2)}, u32[]{:S(2)}) %all-to-all-start.6) | async-done | bytes 65568 | tf_op jit(solution)/shard_map/all_to_all | solution.py:691
  86.8 1.5 %iterate.7 = (f32[32,4,128]{2,1,0:T(4,128)}, f32[16,128]{1,0:T(8,128)S(1)}, f32[16,128]{1,0:T(8,128)S(1)}, f32[16,128]{1,0:T(8,128)S(1)}, f32[256,128]{1,0:T(8,1...) custom-call(f32[32,4,128]{2,1,0:T(4,128)S(1)} %all-to-all-done.6.recv,, ...), custom_call_target="tpu_custom_call" | custom-call | flops 4000000 | bytes 1000000 | tf_op jit(solution)/shard_map/iterate/pallas_call | solution.py:665
  88.3 2.6 %all-to-all-start.7 = ((f32[32,4,128]{2,1,0:T(4,128)}), f32[32,4,128]{2,1,0:T(4,128)S(1)}, u32[]{:S(2)}, u32[]{:S(2)}) async-start(f32[32,4,128]{2,1,0:T(4,128)} %get-tuple-element.153), calls=%async_computation.7 | async-start | bytes 131072 | tf_op jit(solution)/shard_map/all_to_all | solution.py:691
  90.8 1.7 %collective-permute-start.21 = (f32[16,128]{1,0:T(8,128)S(1)}, f32[16,128]{1,0:T(8,128)S(1)}, u32[]{:S(2)}, u32[]{:S(2)}) collective-permute-start(f32[16,128]{1,0:T(8,128)S(1)} %get-tuple-element.154), channel_id=1, source_target_pairs={{0,16},{16,0},{1,17},{17,1},{2,18},{18,2},{3,19},{19,3},{4,20},{20... | collective-permute-start | bytes 24584 | tf_op jit(solution)/shard_map/ppermute | solution.py:687
  92.6 1.7 %collective-permute-start.23 = (f32[16,128]{1,0:T(8,128)S(1)}, f32[16,128]{1,0:T(8,128)S(1)}, u32[]{:S(2)}, u32[]{:S(2)}) collective-permute-start(f32[16,128]{1,0:T(8,128)S(1)} %get-tuple-element.156), channel_id=1, source_target_pairs={{0,12},{4,0},{8,4},{12,8},{1,13},{5,1},{9,5},{13,9},{2,14},{6,2},{... | collective-permute-start | bytes 24584 | tf_op jit(solution)/shard_map/ppermute | solution.py:687
  94.6 1.1 collective-permute-done.22.rest_1_
  95.7 2.7 %all-to-all-done.7.recv = f32[32,4,128]{2,1,0:T(4,128)S(1)} async-done(((f32[32,4,128]{2,1,0:T(4,128)}), f32[32,4,128]{2,1,0:T(4,128)S(1)}, u32[]{:S(2)}, u32[]{:S(2)}) %all-to-all-start.7) | async-done | bytes 65568 | tf_op jit(solution)/shard_map/all_to_all | solution.py:691
  98.3 1.5 %iterate.8 = (f32[32,4,128]{2,1,0:T(4,128)}, f32[16,128]{1,0:T(8,128)S(1)}, f32[16,128]{1,0:T(8,128)S(1)}, f32[16,128]{1,0:T(8,128)S(1)}, f32[256,128]{1,0:T(8,1...) custom-call(f32[32,4,128]{2,1,0:T(4,128)S(1)} %all-to-all-done.7.recv,, ...), custom_call_target="tpu_custom_call" | custom-call | flops 4000000 | bytes 1000000 | tf_op jit(solution)/shard_map/iterate/pallas_call | solution.py:665
  99.8 2.6 %all-to-all-start.8 = ((f32[32,4,128]{2,1,0:T(4,128)}), f32[32,4,128]{2,1,0:T(4,128)S(1)}, u32[]{:S(2)}, u32[]{:S(2)}) async-start(f32[32,4,128]{2,1,0:T(4,128)} %get-tuple-element.162), calls=%async_computation.8 | async-start | bytes 131072 | tf_op jit(solution)/shard_map/all_to_all | solution.py:691
  102.4 1.7 %collective-permute-start.24 = (f32[16,128]{1,0:T(8,128)S(1)}, f32[16,128]{1,0:T(8,128)S(1)}, u32[]{:S(2)}, u32[]{:S(2)}) collective-permute-start(f32[16,128]{1,0:T(8,128)S(1)} %get-tuple-element.163), channel_id=1, source_target_pairs={{0,16},{16,0},{1,17},{17,1},{2,18},{18,2},{3,19},{19,3},{4,20},{20... | collective-permute-start | bytes 24584 | tf_op jit(solution)/shard_map/ppermute | solution.py:687
  104.1 1.7 %collective-permute-start.26 = (f32[16,128]{1,0:T(8,128)S(1)}, f32[16,128]{1,0:T(8,128)S(1)}, u32[]{:S(2)}, u32[]{:S(2)}) collective-permute-start(f32[16,128]{1,0:T(8,128)S(1)} %get-tuple-element.165), channel_id=1, source_target_pairs={{0,12},{4,0},{8,4},{12,8},{1,13},{5,1},{9,5},{13,9},{2,14},{6,2},{... | collective-permute-start | bytes 24584 | tf_op jit(solution)/shard_map/ppermute | solution.py:687
  106.2 1.0 collective-permute-done.25.rest_1_
  107.2 2.7 %all-to-all-done.8.recv = f32[32,4,128]{2,1,0:T(4,128)S(1)} async-done(((f32[32,4,128]{2,1,0:T(4,128)}), f32[32,4,128]{2,1,0:T(4,128)S(1)}, u32[]{:S(2)}, u32[]{:S(2)}) %all-to-all-start.8) | async-done | bytes 65568 | tf_op jit(solution)/shard_map/all_to_all | solution.py:691
  109.9 0.6 iterate.9
  110.5 9.3 %all_to_all.50.recv = f32[32,1,128]{2,1,0:T(1,128)S(1)} all-to-all(f32[32,1,128]{2,1,0:T(1,128)S(1)} %get-tuple-element.179), channel_id=1, replica_groups=mesh['gx'=2,'gy'=4,'gz'=4] {'gx','gy','gz'}, dimensions={0} | all-to-all | bytes 32768 | tf_op jit(solution)/shard_map/all_to_all | solution.py:1011
  119.9 0.8 pressure.1
  (40 shorter events, 1.0 us)
Async XLA Ops:
  0.6 13.2 %copy-start = (bf16[768,256]{1,0:T(8,128)(2,1)S(1)}, bf16[768,256]{1,0:T(8,128)(2,1)}, u32[]{:S(2)}) copy-start(bf16[768,256]{1,0:T(8,128)(2,1)} %constant.7.clone.zt_any.zt_ref.rest_6_.rest_8_.rest_10_) | copy-start | bytes 1179652
  0.6 13.2 %copy-start.2 = (f32[3,16,16,128]{3,2,1,0:T(8,128)S(1)}, f32[3,16,16,128]{3,2,1,0:T(8,128)}, u32[]{:S(2)}) copy-start(f32[3,16,16,128]{3,2,1,0:T(8,128)} %param.8) | copy-start | bytes 1179652
  0.7 13.2 %copy-start.4 = (f32[16,16,128]{2,1,0:T(8,128)S(1)}, f32[16,16,128]{2,1,0:T(8,128)}, u32[]{:S(2)}) copy-start(f32[16,16,128]{2,1,0:T(8,128)} %param.9) | copy-start | bytes 393220
  2.9 10.9 %copy-start.1 = (f32[224,128]{1,0:T(8,128)S(1)}, f32[224,128]{1,0:T(8,128)}, u32[]{:S(2)}) copy-start(f32[224,128]{1,0:T(8,128)} %constant.6.clone.tab_any.tab_ref.rest_5_.rest_7_.rest_9_) | copy-start | bytes 344068
  2.9 14.8 %all-to-all-start = ((f32[32,4,128]{2,1,0:T(4,128)}), f32[32,4,128]{2,1,0:T(4,128)S(1)}, u32[]{:S(2)}, u32[]{:S(2)}) async-start(f32[32,4,128]{2,1,0:T(4,128)} %get-tuple-element.93), calls=%async_computation | async-start | bytes 131072 | tf_op jit(solution)/shard_map/all_to_all | solution.py:691
  10.2 3.6 %copy-start.5 = (f32[8,128]{1,0:T(8,128)S(1)}, f32[8,128]{1,0:T(8,128)}, u32[]{:S(2)}) copy-start(f32[8,128]{1,0:T(8,128)} %constant.8.clone.places_ref) | copy-start | bytes 12292
  10.2 4.7 %collective-permute-start = (f32[16,128]{1,0:T(8,128)S(1)}, f32[16,128]{1,0:T(8,128)S(1)}, u32[]{:S(2)}, u32[]{:S(2)}) collective-permute-start(f32[16,128]{1,0:T(8,128)S(1)} %get-tuple-element.94), channel_id=1, source_target_pairs={{0,16},{16,0},{1,17},{17,1},{2,18},{18,2},{3,19},{19,3},{4,20},{20... | collective-permute-start | bytes 24584 | tf_op jit(solution)/shard_map/ppermute | solution.py:687
  12.1 3.1 %collective-permute-start.1 = (f32[16,128]{1,0:T(8,128)S(1)}, f32[16,128]{1,0:T(8,128)S(1)}, u32[]{:S(2)}, u32[]{:S(2)}) collective-permute-start(f32[16,128]{1,0:T(8,128)S(1)} %get-tuple-element.95), channel_id=1, source_target_pairs={{0,4},{4,8},{8,12},{12,0},{1,5},{5,9},{9,13},{13,1},{2,6},{6,10},{... | collective-permute-start | bytes 24584 | tf_op jit(solution)/shard_map/ppermute | solution.py:687
  12.1 3.1 %collective-permute-start.2 = (f32[16,128]{1,0:T(8,128)S(1)}, f32[16,128]{1,0:T(8,128)S(1)}, u32[]{:S(2)}, u32[]{:S(2)}) collective-permute-start(f32[16,128]{1,0:T(8,128)S(1)} %get-tuple-element.96), channel_id=1, source_target_pairs={{0,12},{4,0},{8,4},{12,8},{1,13},{5,1},{9,5},{13,9},{2,14},{6,2},{... | collective-permute-start | bytes 24584 | tf_op jit(solution)/shard_map/ppermute | solution.py:687
  13.8 0.7 copy-start.6
  14.5 3.2 %copy-start.3 = (f32[16,16,128]{2,1,0:T(8,128)S(1)}, f32[16,16,128]{2,1,0:T(8,128)}, u32[]{:S(2)}) copy-start(f32[16,16,128]{2,1,0:T(8,128)} %param.7) | copy-start | bytes 393220
  19.1 10.1 %all-to-all-start.1 = ((f32[32,4,128]{2,1,0:T(4,128)}), f32[32,4,128]{2,1,0:T(4,128)S(1)}, u32[]{:S(2)}, u32[]{:S(2)}) async-start(f32[32,4,128]{2,1,0:T(4,128)} %get-tuple-element.99), calls=%async_computation.1 | async-start | bytes 131072 | tf_op jit(solution)/shard_map/all_to_all | solution.py:691
  21.7 3.7 %collective-permute-start.3 = (f32[16,128]{1,0:T(8,128)S(1)}, f32[16,128]{1,0:T(8,128)S(1)}, u32[]{:S(2)}, u32[]{:S(2)}) collective-permute-start(f32[16,128]{1,0:T(8,128)S(1)} %get-tuple-element.100), channel_id=1, source_target_pairs={{0,16},{16,0},{1,17},{17,1},{2,18},{18,2},{3,19},{19,3},{4,20},{20... | collective-permute-start | bytes 24584 | tf_op jit(solution)/shard_map/ppermute | solution.py:687
  23.4 3.1 %collective-permute-start.4 = (f32[16,128]{1,0:T(8,128)S(1)}, f32[16,128]{1,0:T(8,128)S(1)}, u32[]{:S(2)}, u32[]{:S(2)}) collective-permute-start(f32[16,128]{1,0:T(8,128)S(1)} %get-tuple-element.101), channel_id=1, source_target_pairs={{0,4},{4,8},{8,12},{12,0},{1,5},{5,9},{9,13},{13,1},{2,6},{6,10},{... | collective-permute-start | bytes 24584 | tf_op jit(solution)/shard_map/ppermute | solution.py:687
  23.4 3.1 %collective-permute-start.5 = (f32[16,128]{1,0:T(8,128)S(1)}, f32[16,128]{1,0:T(8,128)S(1)}, u32[]{:S(2)}, u32[]{:S(2)}) collective-permute-start(f32[16,128]{1,0:T(8,128)S(1)} %get-tuple-element.102), channel_id=1, source_target_pairs={{0,12},{4,0},{8,4},{12,8},{1,13},{5,1},{9,5},{13,9},{2,14},{6,2},{... | collective-permute-start | bytes 24584 | tf_op jit(solution)/shard_map/ppermute | solution.py:687
  30.6 10.1 %all-to-all-start.2 = ((f32[32,4,128]{2,1,0:T(4,128)}), f32[32,4,128]{2,1,0:T(4,128)S(1)}, u32[]{:S(2)}, u32[]{:S(2)}) async-start(f32[32,4,128]{2,1,0:T(4,128)} %get-tuple-element.109), calls=%async_computation.2 | async-start | bytes 131072 | tf_op jit(solution)/shard_map/all_to_all | solution.py:691
  33.2 3.9 %collective-permute-start.6 = (f32[32,128]{1,0:T(8,128)S(1)}, f32[32,128]{1,0:T(8,128)S(1)}, u32[]{:S(2)}, u32[]{:S(2)}) collective-permute-start(f32[32,128]{1,0:T(8,128)S(1)} %get-tuple-element.110), channel_id=1, source_target_pairs={{0,16},{16,0},{1,17},{17,1},{2,18},{18,2},{3,19},{19,3},{4,20},{20... | collective-permute-start | bytes 49160 | tf_op jit(solution)/shard_map/ppermute | solution.py:687
  34.9 3.2 %collective-permute-start.7 = (f32[32,128]{1,0:T(8,128)S(1)}, f32[32,128]{1,0:T(8,128)S(1)}, u32[]{:S(2)}, u32[]{:S(2)}) collective-permute-start(f32[32,128]{1,0:T(8,128)S(1)} %get-tuple-element.111), channel_id=1, source_target_pairs={{0,4},{4,8},{8,12},{12,0},{1,5},{5,9},{9,13},{13,1},{2,6},{6,10},{... | collective-permute-start | bytes 49160 | tf_op jit(solution)/shard_map/ppermute | solution.py:687
  34.9 3.2 %collective-permute-start.8 = (f32[32,128]{1,0:T(8,128)S(1)}, f32[32,128]{1,0:T(8,128)S(1)}, u32[]{:S(2)}, u32[]{:S(2)}) collective-permute-start(f32[32,128]{1,0:T(8,128)S(1)} %get-tuple-element.112), channel_id=1, source_target_pairs={{0,12},{4,0},{8,4},{12,8},{1,13},{5,1},{9,5},{13,9},{2,14},{6,2},{... | collective-permute-start | bytes 49160 | tf_op jit(solution)/shard_map/ppermute | solution.py:687
  42.0 10.1 %all-to-all-start.3 = ((f32[32,4,128]{2,1,0:T(4,128)}), f32[32,4,128]{2,1,0:T(4,128)S(1)}, u32[]{:S(2)}, u32[]{:S(2)}) async-start(f32[32,4,128]{2,1,0:T(4,128)} %get-tuple-element.116), calls=%async_computation.3 | async-start | bytes 131072 | tf_op jit(solution)/shard_map/all_to_all | solution.py:691
  44.6 3.9 %collective-permute-start.9 = (f32[16,128]{1,0:T(8,128)S(1)}, f32[16,128]{1,0:T(8,128)S(1)}, u32[]{:S(2)}, u32[]{:S(2)}) collective-permute-start(f32[16,128]{1,0:T(8,128)S(1)} %get-tuple-element.117), channel_id=1, source_target_pairs={{0,16},{16,0},{1,17},{17,1},{2,18},{18,2},{3,19},{19,3},{4,20},{20... | collective-permute-start | bytes 24584 | tf_op jit(solution)/shard_map/ppermute | solution.py:687
  46.3 3.1 %collective-permute-start.10 = (f32[16,128]{1,0:T(8,128)S(1)}, f32[16,128]{1,0:T(8,128)S(1)}, u32[]{:S(2)}, u32[]{:S(2)}) collective-permute-start(f32[16,128]{1,0:T(8,128)S(1)} %get-tuple-element.118), channel_id=1, source_target_pairs={{0,4},{4,8},{8,12},{12,0},{1,5},{5,9},{9,13},{13,1},{2,6},{6,10},{... | collective-permute-start | bytes 24584 | tf_op jit(solution)/shard_map/ppermute | solution.py:687
  46.3 3.1 %collective-permute-start.11 = (f32[16,128]{1,0:T(8,128)S(1)}, f32[16,128]{1,0:T(8,128)S(1)}, u32[]{:S(2)}, u32[]{:S(2)}) collective-permute-start(f32[16,128]{1,0:T(8,128)S(1)} %get-tuple-element.119), channel_id=1, source_target_pairs={{0,12},{4,0},{8,4},{12,8},{1,13},{5,1},{9,5},{13,9},{2,14},{6,2},{... | collective-permute-start | bytes 24584 | tf_op jit(solution)/shard_map/ppermute | solution.py:687
  53.6 10.1 %all-to-all-start.4 = ((f32[32,4,128]{2,1,0:T(4,128)}), f32[32,4,128]{2,1,0:T(4,128)S(1)}, u32[]{:S(2)}, u32[]{:S(2)}) async-start(f32[32,4,128]{2,1,0:T(4,128)} %get-tuple-element.127), calls=%async_computation.4 | async-start | bytes 131072 | tf_op jit(solution)/shard_map/all_to_all | solution.py:691
  56.1 3.7 %collective-permute-start.12 = (f32[16,128]{1,0:T(8,128)S(1)}, f32[16,128]{1,0:T(8,128)S(1)}, u32[]{:S(2)}, u32[]{:S(2)}) collective-permute-start(f32[16,128]{1,0:T(8,128)S(1)} %get-tuple-element.128), channel_id=1, source_target_pairs={{0,16},{16,0},{1,17},{17,1},{2,18},{18,2},{3,19},{19,3},{4,20},{20... | collective-permute-start | bytes 24584 | tf_op jit(solution)/shard_map/ppermute | solution.py:687
  57.8 3.1 %collective-permute-start.13 = (f32[16,128]{1,0:T(8,128)S(1)}, f32[16,128]{1,0:T(8,128)S(1)}, u32[]{:S(2)}, u32[]{:S(2)}) collective-permute-start(f32[16,128]{1,0:T(8,128)S(1)} %get-tuple-element.129), channel_id=1, source_target_pairs={{0,4},{4,8},{8,12},{12,0},{1,5},{5,9},{9,13},{13,1},{2,6},{6,10},{... | collective-permute-start | bytes 24584 | tf_op jit(solution)/shard_map/ppermute | solution.py:687
  57.9 3.1 %collective-permute-start.14 = (f32[16,128]{1,0:T(8,128)S(1)}, f32[16,128]{1,0:T(8,128)S(1)}, u32[]{:S(2)}, u32[]{:S(2)}) collective-permute-start(f32[16,128]{1,0:T(8,128)S(1)} %get-tuple-element.130), channel_id=1, source_target_pairs={{0,12},{4,0},{8,4},{12,8},{1,13},{5,1},{9,5},{13,9},{2,14},{6,2},{... | collective-permute-start | bytes 24584 | tf_op jit(solution)/shard_map/ppermute | solution.py:687
  65.2 10.1 %all-to-all-start.5 = ((f32[32,4,128]{2,1,0:T(4,128)}), f32[32,4,128]{2,1,0:T(4,128)S(1)}, u32[]{:S(2)}, u32[]{:S(2)}) async-start(f32[32,4,128]{2,1,0:T(4,128)} %get-tuple-element.135), calls=%async_computation.5 | async-start | bytes 131072 | tf_op jit(solution)/shard_map/all_to_all | solution.py:691
  67.8 3.7 %collective-permute-start.15 = (f32[16,128]{1,0:T(8,128)S(1)}, f32[16,128]{1,0:T(8,128)S(1)}, u32[]{:S(2)}, u32[]{:S(2)}) collective-permute-start(f32[16,128]{1,0:T(8,128)S(1)} %get-tuple-element.136), channel_id=1, source_target_pairs={{0,16},{16,0},{1,17},{17,1},{2,18},{18,2},{3,19},{19,3},{4,20},{20... | collective-permute-start | bytes 24584 | tf_op jit(solution)/shard_map/ppermute | solution.py:687
  69.5 3.1 %collective-permute-start.16 = (f32[16,128]{1,0:T(8,128)S(1)}, f32[16,128]{1,0:T(8,128)S(1)}, u32[]{:S(2)}, u32[]{:S(2)}) collective-permute-start(f32[16,128]{1,0:T(8,128)S(1)} %get-tuple-element.137), channel_id=1, source_target_pairs={{0,4},{4,8},{8,12},{12,0},{1,5},{5,9},{9,13},{13,1},{2,6},{6,10},{... | collective-permute-start | bytes 24584 | tf_op jit(solution)/shard_map/ppermute | solution.py:687
  69.5 3.1 %collective-permute-start.17 = (f32[16,128]{1,0:T(8,128)S(1)}, f32[16,128]{1,0:T(8,128)S(1)}, u32[]{:S(2)}, u32[]{:S(2)}) collective-permute-start(f32[16,128]{1,0:T(8,128)S(1)} %get-tuple-element.138), channel_id=1, source_target_pairs={{0,12},{4,0},{8,4},{12,8},{1,13},{5,1},{9,5},{13,9},{2,14},{6,2},{... | collective-permute-start | bytes 24584 | tf_op jit(solution)/shard_map/ppermute | solution.py:687
  76.7 10.1 %all-to-all-start.6 = ((f32[32,4,128]{2,1,0:T(4,128)}), f32[32,4,128]{2,1,0:T(4,128)S(1)}, u32[]{:S(2)}, u32[]{:S(2)}) async-start(f32[32,4,128]{2,1,0:T(4,128)} %get-tuple-element.144), calls=%async_computation.6 | async-start | bytes 131072 | tf_op jit(solution)/shard_map/all_to_all | solution.py:691
  79.3 3.7 %collective-permute-start.18 = (f32[16,128]{1,0:T(8,128)S(1)}, f32[16,128]{1,0:T(8,128)S(1)}, u32[]{:S(2)}, u32[]{:S(2)}) collective-permute-start(f32[16,128]{1,0:T(8,128)S(1)} %get-tuple-element.145), channel_id=1, source_target_pairs={{0,16},{16,0},{1,17},{17,1},{2,18},{18,2},{3,19},{19,3},{4,20},{20... | collective-permute-start | bytes 24584 | tf_op jit(solution)/shard_map/ppermute | solution.py:687
  81.0 3.1 %collective-permute-start.19 = (f32[16,128]{1,0:T(8,128)S(1)}, f32[16,128]{1,0:T(8,128)S(1)}, u32[]{:S(2)}, u32[]{:S(2)}) collective-permute-start(f32[16,128]{1,0:T(8,128)S(1)} %get-tuple-element.146), channel_id=1, source_target_pairs={{0,4},{4,8},{8,12},{12,0},{1,5},{5,9},{9,13},{13,1},{2,6},{6,10},{... | collective-permute-start | bytes 24584 | tf_op jit(solution)/shard_map/ppermute | solution.py:687
  81.0 3.1 %collective-permute-start.20 = (f32[16,128]{1,0:T(8,128)S(1)}, f32[16,128]{1,0:T(8,128)S(1)}, u32[]{:S(2)}, u32[]{:S(2)}) collective-permute-start(f32[16,128]{1,0:T(8,128)S(1)} %get-tuple-element.147), channel_id=1, source_target_pairs={{0,12},{4,0},{8,4},{12,8},{1,13},{5,1},{9,5},{13,9},{2,14},{6,2},{... | collective-permute-start | bytes 24584 | tf_op jit(solution)/shard_map/ppermute | solution.py:687
  88.3 10.1 %all-to-all-start.7 = ((f32[32,4,128]{2,1,0:T(4,128)}), f32[32,4,128]{2,1,0:T(4,128)S(1)}, u32[]{:S(2)}, u32[]{:S(2)}) async-start(f32[32,4,128]{2,1,0:T(4,128)} %get-tuple-element.153), calls=%async_computation.7 | async-start | bytes 131072 | tf_op jit(solution)/shard_map/all_to_all | solution.py:691
  90.8 3.7 %collective-permute-start.21 = (f32[16,128]{1,0:T(8,128)S(1)}, f32[16,128]{1,0:T(8,128)S(1)}, u32[]{:S(2)}, u32[]{:S(2)}) collective-permute-start(f32[16,128]{1,0:T(8,128)S(1)} %get-tuple-element.154), channel_id=1, source_target_pairs={{0,16},{16,0},{1,17},{17,1},{2,18},{18,2},{3,19},{19,3},{4,20},{20... | collective-permute-start | bytes 24584 | tf_op jit(solution)/shard_map/ppermute | solution.py:687
  92.6 3.1 %collective-permute-start.22 = (f32[16,128]{1,0:T(8,128)S(1)}, f32[16,128]{1,0:T(8,128)S(1)}, u32[]{:S(2)}, u32[]{:S(2)}) collective-permute-start(f32[16,128]{1,0:T(8,128)S(1)} %get-tuple-element.155), channel_id=1, source_target_pairs={{0,4},{4,8},{8,12},{12,0},{1,5},{5,9},{9,13},{13,1},{2,6},{6,10},{... | collective-permute-start | bytes 24584 | tf_op jit(solution)/shard_map/ppermute | solution.py:687
  92.6 3.1 %collective-permute-start.23 = (f32[16,128]{1,0:T(8,128)S(1)}, f32[16,128]{1,0:T(8,128)S(1)}, u32[]{:S(2)}, u32[]{:S(2)}) collective-permute-start(f32[16,128]{1,0:T(8,128)S(1)} %get-tuple-element.156), channel_id=1, source_target_pairs={{0,12},{4,0},{8,4},{12,8},{1,13},{5,1},{9,5},{13,9},{2,14},{6,2},{... | collective-permute-start | bytes 24584 | tf_op jit(solution)/shard_map/ppermute | solution.py:687
  99.8 10.1 %all-to-all-start.8 = ((f32[32,4,128]{2,1,0:T(4,128)}), f32[32,4,128]{2,1,0:T(4,128)S(1)}, u32[]{:S(2)}, u32[]{:S(2)}) async-start(f32[32,4,128]{2,1,0:T(4,128)} %get-tuple-element.162), calls=%async_computation.8 | async-start | bytes 131072 | tf_op jit(solution)/shard_map/all_to_all | solution.py:691
  102.4 3.8 %collective-permute-start.24 = (f32[16,128]{1,0:T(8,128)S(1)}, f32[16,128]{1,0:T(8,128)S(1)}, u32[]{:S(2)}, u32[]{:S(2)}) collective-permute-start(f32[16,128]{1,0:T(8,128)S(1)} %get-tuple-element.163), channel_id=1, source_target_pairs={{0,16},{16,0},{1,17},{17,1},{2,18},{18,2},{3,19},{19,3},{4,20},{20... | collective-permute-start | bytes 24584 | tf_op jit(solution)/shard_map/ppermute | solution.py:687
  104.1 3.1 %collective-permute-start.25 = (f32[16,128]{1,0:T(8,128)S(1)}, f32[16,128]{1,0:T(8,128)S(1)}, u32[]{:S(2)}, u32[]{:S(2)}) collective-permute-start(f32[16,128]{1,0:T(8,128)S(1)} %get-tuple-element.164), channel_id=1, source_target_pairs={{0,4},{4,8},{8,12},{12,0},{1,5},{5,9},{9,13},{13,1},{2,6},{6,10},{... | collective-permute-start | bytes 24584 | tf_op jit(solution)/shard_map/ppermute | solution.py:687
  104.1 3.1 %collective-permute-start.26 = (f32[16,128]{1,0:T(8,128)S(1)}, f32[16,128]{1,0:T(8,128)S(1)}, u32[]{:S(2)}, u32[]{:S(2)}) collective-permute-start(f32[16,128]{1,0:T(8,128)S(1)} %get-tuple-element.165), channel_id=1, source_target_pairs={{0,12},{4,0},{8,4},{12,8},{1,13},{5,1},{9,5},{13,9},{2,14},{6,2},{... | collective-permute-start | bytes 24584 | tf_op jit(solution)/shard_map/ppermute | solution.py:687
